TPU v7x, 256 devices: a whole 4x4x8 slice. The times are simulated.
256 devices in a mesh: mem: 8 (over x, core), row: 4 (over z_lo), col: 8 (over y, z_hi).
Axes of the slice: x: 4, y: 4, z: 8 (z_hi: 2, z_lo: 4; z = z_hi * 4 + z_lo), core: 2. Of those that a mesh axis runs over, the one named last changes fastest.
Arguments:
- fields: bfloat16 [32, 16, 256, 256], P('mem', 'row', 'col'), may hold values from -6 to 6
- norm_gain: float32 [256], replicated, may hold values from 0.5 to 1.5
- w_query: bfloat16 [256, 256], replicated, may hold values from -11 to 11
- w_key: bfloat16 [256, 256], replicated, may hold values from -6 to 6
- w_value: bfloat16 [256, 256], replicated, may hold values from -0.375 to 0.375
- w_out: bfloat16 [256, 256], replicated, may hold values from -0.375 to 0.375
- mix_kernel: float32 [3, 3, 256], replicated, may hold values from -1.5 to 1.5
- cotangent: bfloat16 [32, 16, 256, 256], P('mem', 'row', 'col'), may hold values from -6 to 6
Outputs:
- grad_fields: bfloat16 [32, 16, 256, 256], P('mem', 'row', 'col')
- grad_gain: float32 [256], replicated
- grad_query: float32 [256, 256], replicated
- grad_key: float32 [256, 256], replicated
- grad_value: float32 [256, 256], replicated
- grad_out: float32 [256, 256], replicated
- grad_kernel: float32 [3, 3, 256], replicated
All inputs are finite; a program needn't handle non-finite values.
Results may differ from a plain program's by a relative error of at most 0.015.
The roundings to bfloat16 on the way count: a program that leaves them out, or rounds other values in their place, can miss the bound.
Values may be sent and summed in bfloat16 or wider, within the bound.
No kernel may reach another device: no remote copies, remote signals or barrier semaphores. Data moves between devices by JAX's collectives and lax.ppermute only.
A program may use at most 64 MiB of HBM per device.

v0:
```python
import math

import jax
import jax.numpy as jnp
from jax import lax
from jax.sharding import PartitionSpec as P

HEADS = 8
CELLB = 64


epsilon = 1e-06


def with_halo(x, sides, width):
    for axis, dim in sides:
        size, length = (lax.axis_size(axis), x.shape[dim])
        up = [(i, (i + 1) % size) for i in range(size - 1)]
        down = [(j, i) for i, j in up]
        last = lax.slice_in_dim(x, length - width, length, axis=dim)
        first = lax.slice_in_dim(x, 0, width, axis=dim)
        before = lax.ppermute(last, axis, up)
        after = lax.ppermute(first, axis, down)
        x = jnp.concatenate([before, x, after], axis=dim)
    return x


def project(values, weight):
    shape = values.shape
    flat_in = values.reshape(-1, shape[-1])
    return jnp.dot(flat_in, weight, preferred_element_type=jnp.float32).reshape(
        shape[:-1] + (weight.shape[1],)
    )


def local(fields, norm_gain, w_query, w_key, w_value, w_out, mix_kernel, cotangent):
    members, tile_rows, tile_cols, model_width = fields.shape
    head_dim = model_width // HEADS
    score_scale = 1.0 / math.sqrt(head_dim)
    cell_count = tile_rows * tile_cols
    blocks = cell_count // CELLB
    padded_cot = with_halo(cotangent, (("row", 1), ("col", 2)), 1)
    summed = jnp.zeros(fields.shape, jnp.float32)
    for row_off in range(3):
        for col_off in range(3):
            summed = summed + mix_kernel[row_off, col_off] * padded_cot[
                :, 2 - row_off : 2 - row_off + tile_rows, 2 - col_off : 2 - col_off + tile_cols, :
            ].astype(jnp.float32)
    grad_mixed_all = summed.astype(jnp.bfloat16)

    def to_blocks(values):
        return jnp.swapaxes(values.reshape(members, blocks, CELLB, model_width), 0, 1)

    def one_block(running, block_in):
        blk_fields, blk_grad_mixed, blk_cot = block_in
        flat_in = blk_fields.astype(jnp.float32)
        inv_rms = lax.rsqrt(jnp.mean(flat_in * flat_in, axis=-1, keepdims=True) + epsilon)
        normed = flat_in * inv_rms
        inputs = (normed * norm_gain).astype(jnp.bfloat16)
        queries = project(inputs, w_query).astype(jnp.bfloat16)
        key_proj = project(inputs, w_key).astype(jnp.bfloat16)
        value_proj = project(inputs, w_value).astype(jnp.bfloat16)
        every_key, every_value = (
            lax.all_gather(key_proj, "mem", axis=0, tiled=True),
            lax.all_gather(value_proj, "mem", axis=0, tiled=True),
        )
        members_all = every_key.shape[0]
        local_shape = (members, CELLB, HEADS, head_dim)
        all_shape = (members_all, CELLB, HEADS, head_dim)
        query_heads = queries.reshape(local_shape)
        key_heads = every_key.reshape(all_shape)
        value_heads = every_value.reshape(all_shape)
        scores = (
            jnp.einsum(
                "mche,nche->chmn", query_heads, key_heads, preferred_element_type=jnp.float32
            )
            * score_scale
        )
        row_max = jnp.max(scores, axis=-1, keepdims=True)
        lifted = jnp.exp(scores - row_max)
        totals = jnp.sum(lifted, axis=-1, keepdims=True)
        attn_prob = lifted / totals
        prob_b = attn_prob.astype(jnp.bfloat16)
        attended = jnp.einsum(
            "chmn,nche->mche", prob_b, value_heads, preferred_element_type=jnp.float32
        ).astype(jnp.bfloat16)
        attended = attended.reshape(members, CELLB, model_width)
        mixed_blk = project(attended, w_out).astype(jnp.bfloat16)
        grad_att = project(blk_grad_mixed, w_out.T).astype(jnp.bfloat16)
        grad_heads = grad_att.reshape(local_shape)
        grad_prob = jnp.einsum(
            "mche,nche->chmn", grad_heads, value_heads, preferred_element_type=jnp.float32
        )
        inner = jnp.sum(attn_prob * grad_prob, axis=-1, keepdims=True)
        grad_score = (attn_prob * (grad_prob - inner) * score_scale).astype(jnp.bfloat16)
        grad_q = jnp.einsum(
            "chmn,nche->mche", grad_score, key_heads, preferred_element_type=jnp.float32
        ).astype(jnp.bfloat16)
        part_k = jnp.einsum(
            "chmn,mche->nche", grad_score, query_heads, preferred_element_type=jnp.float32
        ).reshape(members_all, CELLB, model_width)
        part_v = jnp.einsum(
            "chmn,mche->nche", prob_b, grad_heads, preferred_element_type=jnp.float32
        ).reshape(members_all, CELLB, model_width)
        sum_k, sum_v = (
            lax.psum_scatter(
                part_k.astype(jnp.bfloat16), "mem", scatter_dimension=0, tiled=True
            ).astype(jnp.float32),
            lax.psum_scatter(
                part_v.astype(jnp.bfloat16), "mem", scatter_dimension=0, tiled=True
            ).astype(jnp.float32),
        )
        flat_shape = (members * CELLB, model_width)
        grad_q2 = grad_q.reshape(flat_shape)
        grad_k2 = sum_k.astype(jnp.bfloat16).reshape(flat_shape)
        grad_v2 = sum_v.astype(jnp.bfloat16).reshape(flat_shape)
        inputs2 = inputs.reshape(flat_shape)
        grad_in = (
            jnp.dot(grad_q2, w_query.T, preferred_element_type=jnp.float32)
            + jnp.dot(grad_k2, w_key.T, preferred_element_type=jnp.float32)
            + jnp.dot(grad_v2, w_value.T, preferred_element_type=jnp.float32)
        )
        normed2 = normed.reshape(flat_shape)
        grad_normed = grad_in * norm_gain
        inv2 = inv_rms.reshape(-1, 1)
        grad_blk = blk_cot.reshape(flat_shape).astype(jnp.float32) + inv2 * (
            grad_normed - normed2 * jnp.mean(grad_normed * normed2, axis=-1, keepdims=True)
        )
        acc_q, acc_k, acc_v, acc_out, acc_gain = running
        acc_q = acc_q + jnp.einsum(
            "rd,re->de", inputs2, grad_q2, preferred_element_type=jnp.float32
        )
        acc_k = acc_k + jnp.einsum(
            "rd,re->de", inputs2, grad_k2, preferred_element_type=jnp.float32
        )
        acc_v = acc_v + jnp.einsum(
            "rd,re->de", inputs2, grad_v2, preferred_element_type=jnp.float32
        )
        acc_out = acc_out + jnp.einsum(
            "rd,re->de",
            attended.reshape(flat_shape),
            blk_grad_mixed.reshape(flat_shape),
            preferred_element_type=jnp.float32,
        )
        acc_gain = acc_gain + jnp.sum(grad_in * normed2, axis=0)
        outputs = (mixed_blk, grad_blk.astype(jnp.bfloat16).reshape(members, CELLB, model_width))
        return ((acc_q, acc_k, acc_v, acc_out, acc_gain), outputs)

    square = jnp.zeros((model_width, model_width), jnp.float32)
    start = (square, square, square, square, jnp.zeros((model_width,), jnp.float32))
    block_inputs = (to_blocks(fields), to_blocks(grad_mixed_all), to_blocks(cotangent))
    running, outputs = lax.scan(one_block, start, block_inputs)
    mixed_all = jnp.swapaxes(outputs[0], 0, 1).reshape(members, tile_rows, tile_cols, model_width)
    grad_fields = jnp.swapaxes(outputs[1], 0, 1).reshape(members, tile_rows, tile_cols, model_width)
    kernel_terms = []
    padded_mixed = with_halo(mixed_all, (("row", 1), ("col", 2)), 1)
    cot_wide = cotangent.astype(jnp.float32)
    for row_off in range(3):
        for col_off in range(3):
            shifted = padded_mixed[
                :, row_off : row_off + tile_rows, col_off : col_off + tile_cols, :
            ].astype(jnp.float32)
            kernel_terms.append(jnp.sum(shifted * cot_wide, axis=(0, 1, 2)))
    local_kernel = jnp.stack(kernel_terms).reshape(3, 3, model_width)
    acc_q, acc_k, acc_v, acc_out, acc_gain = running
    tot_q, tot_k, tot_v, tot_out, tot_gain, tot_kernel = lax.psum(
        (acc_q, acc_k, acc_v, acc_out, acc_gain, local_kernel), ("mem", "row", "col")
    )
    token_total = (
        members
        * lax.axis_size("mem")
        * tile_rows
        * lax.axis_size("row")
        * tile_cols
        * lax.axis_size("col")
    )
    scale_all = 1.0 / math.sqrt(token_total)
    return (
        grad_fields,
        tot_gain * scale_all,
        tot_q * scale_all,
        tot_k * scale_all,
        tot_v * scale_all,
        tot_out * scale_all,
        tot_kernel * scale_all,
    )


def solution(mesh):
    in_specs = (
        P("mem", "row", "col", None),
        P(),
        P(),
        P(),
        P(),
        P(),
        P(),
        P("mem", "row", "col", None),
    )
    out_specs = (P("mem", "row", "col", None), P(), P(), P(), P(), P(), P())
    return jax.shard_map(local, mesh=mesh, in_specs=in_specs, out_specs=out_specs, check_vma=False)
```

profile of v0, /device:TPU:1, one launch (start us, length us, event | category | flops | bytes accessed | tf_op | source)
XLA Modules:
  0.0 691.0 jit_solution(8502054716683009661)
XLA Ops:
  8.9 4.4 collective-permute-start
  15.6 2.9 collective-permute-done.1
  18.5 7.7 %collective-permute-start.3 = (bf16[4,6,1,256]{3,2,1,0:T(2,128)(2,1)S(1)}, bf16[4,6,1,256]{3,2,1,0:T(2,128)(2,1)S(1)}, u32[]{:S(2)}, u32[]{:S(2)}) collective-permute-start(bf16[4,6,1,256]{3,2,1,0:T(2,128)(2,1)S(1)} %get-tuple-element.250), channel_id=1, source_target_pairs={{0,1},{1,2},{2,3},{3,4},{4,5},{5,6},{6,7},{8,9},{9,10},{10,11},{11... | collective-permute-start | bytes 36872 | tf_op jit(solution)/shard_map/ppermute | solution.py:22
  28.5 6.2 collective-permute-done.2
  34.7 2.5 fusion.56
  37.3 363.9 %while.23 = (s32[]{:T(128)}, f32[256,256]{1,0:T(8,128)}, f32[256,256]{1,0:T(8,128)}, f32[256,256]{1,0:T(8,128)}, f32[256,256]{1,0:T(8,128)}, /*index=5*/f32[256]...) while((s32[]{:T(128)}, f32[256,256]{1,0:T(8,128)}, ...), condition=%wide.region_9.10_spmd.clone, body=%wide.region_0.9_spmd.clone.sunk | while | flops 434180704 | bytes 60141380 | solution.py:152
  38.3 1.9 convolution_convert_fusion.15
  40.2 1.9 convolution_convert_fusion.17
  47.4 20.0 %all-gather.3.cloned.1.call-done = bf16[32,64,256]{2,1,0:T(8,128)(2,1)} async-done(((bf16[4,64,256]{2,1,0:T(8,128)(2,1)}), bf16[32,64,256]{2,1,0:T(8,128)(2,1)}) %all-gather.3.cloned.1.call-update) | async-done | bytes 1048592 | tf_op jit(solution)/shard_map/while/body/eval_jaxpr/all_gather | solution.py:64
  67.5 2.0 copy.91
  69.5 6.8 copy.92
  76.3 19.0 %all-gather.5.cloned.1.call-done = bf16[32,64,256]{2,1,0:T(8,128)(2,1)} async-done(((bf16[4,64,256]{2,1,0:T(8,128)(2,1)}), bf16[32,64,256]{2,1,0:T(8,128)(2,1)}) %all-gather.5.cloned.1.call-update) | async-done | bytes 1048592 | tf_op jit(solution)/shard_map/while/body/eval_jaxpr/all_gather | solution.py:65
  95.3 2.0 copy.95
  97.3 6.8 copy.96
  104.2 4.4 fusion.184
  108.6 5.8 fusion.185
  114.4 27.0 %convolution_convert_fusion.19 = bf16[64,8,32,32]{3,2,1,0:T(8,128)(2,1)} fusion(bf16[4,64,8,32]{3,0,2,1:T(4,128)(2,1)S(1)} %copy.98, f32[64,8,4,32]{3,2,1,0:T(4,128)S(1)} %fusion.184, f32[64,8,4,32]{3,2,1,0:T(4,128)S(1)} %get-tuple-element.373, f32[64,8,4]{2,1,0:T(8,128)} %get-tuple-element.374), kind=kOutput, calls=%fused_computation.3.clone.1 | convolution fusion | flops 5179423 | bytes 1712128 | tf_op jit(solution)/shard_map/while/body/eval_jaxpr/chmn,mche->nche/dot_general | solution.py:99
  141.4 4.9 copy.100
  147.2 3.6 convolution_convert_fusion.20
  150.8 4.9 copy.101
  155.7 3.9 fusion.189
  160.9 25.1 %fusion.186 = bf16[4,64,8,32]{3,0,2,1:T(4,128)(2,1)S(1)} fusion(bf16[32,64,8,32]{3,0,2,1:T(8,128)(2,1)} %copy.92, f32[64,8,4,32]{3,2,1,0:T(4,128)S(1)} %copy-done.2, f32[64,8,4,32]{3,2,1,0:T(4,128)} %copy-done.3, f32[64,8,4]{2,1,0:T(8,128)} %get-tuple-element.374), kind=kOutput, calls=%fused_computation.13.clone.1 | convolution fusion | flops 4720671 | bytes 1712128 | tf_op jit(solution)/shard_map/while/body/eval_jaxpr/chmn,nche->mche/dot_general | solution.py:96
  192.2 22.0 %reduce-scatter.5.cloned.1.call-done = bf16[4,64,256]{2,1,0:T(8,128)(2,1)} async-done(((bf16[32,64,256]{2,1,0:T(8,128)(2,1)}), bf16[4,64,256]{2,1,0:T(8,128)(2,1)}) %reduce-scatter.5.cloned.1.call-update) | async-done | bytes 131088 | tf_op jit(solution)/shard_map/while/body/eval_jaxpr/reduce_scatter | solution.py:109
  220.1 1.9 convolution_convert_fusion.15
  222.0 1.9 convolution_convert_fusion.17
  229.2 20.5 %all-gather.3.cloned.1.call-done = bf16[32,64,256]{2,1,0:T(8,128)(2,1)} async-done(((bf16[4,64,256]{2,1,0:T(8,128)(2,1)}), bf16[32,64,256]{2,1,0:T(8,128)(2,1)}) %all-gather.3.cloned.1.call-update) | async-done | bytes 1048592 | tf_op jit(solution)/shard_map/while/body/eval_jaxpr/all_gather | solution.py:64
  249.7 2.0 copy.91
  251.7 6.8 copy.92
  258.5 18.9 %all-gather.5.cloned.1.call-done = bf16[32,64,256]{2,1,0:T(8,128)(2,1)} async-done(((bf16[4,64,256]{2,1,0:T(8,128)(2,1)}), bf16[32,64,256]{2,1,0:T(8,128)(2,1)}) %all-gather.5.cloned.1.call-update) | async-done | bytes 1048592 | tf_op jit(solution)/shard_map/while/body/eval_jaxpr/all_gather | solution.py:65
  277.4 2.0 copy.95
  279.4 6.8 copy.96
  286.2 4.4 fusion.184
  290.7 5.8 fusion.185
  296.4 27.0 %convolution_convert_fusion.19 = bf16[64,8,32,32]{3,2,1,0:T(8,128)(2,1)} fusion(bf16[4,64,8,32]{3,0,2,1:T(4,128)(2,1)S(1)} %copy.98, f32[64,8,4,32]{3,2,1,0:T(4,128)S(1)} %fusion.184, f32[64,8,4,32]{3,2,1,0:T(4,128)S(1)} %get-tuple-element.373, f32[64,8,4]{2,1,0:T(8,128)} %get-tuple-element.374), kind=kOutput, calls=%fused_computation.3.clone.1 | convolution fusion | flops 5179423 | bytes 1712128 | tf_op jit(solution)/shard_map/while/body/eval_jaxpr/chmn,mche->nche/dot_general | solution.py:99
  323.4 4.9 copy.100
  329.3 3.6 convolution_convert_fusion.20
  332.9 4.9 copy.101
  337.8 3.9 fusion.189
  343.0 25.1 %fusion.186 = bf16[4,64,8,32]{3,0,2,1:T(4,128)(2,1)S(1)} fusion(bf16[32,64,8,32]{3,0,2,1:T(8,128)(2,1)} %copy.92, f32[64,8,4,32]{3,2,1,0:T(4,128)S(1)} %copy-done.2, f32[64,8,4,32]{3,2,1,0:T(4,128)} %copy-done.3, f32[64,8,4]{2,1,0:T(8,128)} %get-tuple-element.374), kind=kOutput, calls=%fused_computation.13.clone.1 | convolution fusion | flops 4720671 | bytes 1712128 | tf_op jit(solution)/shard_map/while/body/eval_jaxpr/chmn,nche->mche/dot_general | solution.py:96
  370.4 2.0 convolution_add_fusion.7
  375.3 20.9 %reduce-scatter.5.cloned.1.call-done = bf16[4,64,256]{2,1,0:T(8,128)(2,1)} async-done(((bf16[32,64,256]{2,1,0:T(8,128)(2,1)}), bf16[4,64,256]{2,1,0:T(8,128)(2,1)}) %reduce-scatter.5.cloned.1.call-update) | async-done | bytes 131088 | tf_op jit(solution)/shard_map/while/body/eval_jaxpr/reduce_scatter | solution.py:109
  403.3 4.0 collective-permute-start.4
  409.6 7.1 %collective-permute-start.6 = (bf16[4,6,1,256]{3,2,1,0:T(2,128)(2,1)S(1)}, bf16[4,6,1,256]{3,2,1,0:T(2,128)(2,1)S(1)}, u32[]{:S(2)}, u32[]{:S(2)}) collective-permute-start(bf16[4,6,1,256]{3,2,1,0:T(2,128)(2,1)S(1)} %get-tuple-element.247), channel_id=1, source_target_pairs={{0,1},{1,2},{2,3},{3,4},{4,5},{5,6},{6,7},{8,9},{9,10},{10,11},{11... | collective-permute-start | bytes 36872 | tf_op jit(solution)/shard_map/ppermute | solution.py:22
  419.7 5.5 collective-permute-done.7
  428.3 80.8 %all-reduce = (f32[256]{0:T(256)S(1)}, f32[3,3,256]{2,1,0:T(4,128)S(1)}) all-reduce(f32[256]{0:T(256)S(1)} %get-tuple-element.96, f32[3,3,256]{2,1,0:T(4,128)S(1)} %reshape.187), channel_id=1, replica_groups=mesh['mem'=8,'row'=4,'col'=8] {'mem','row','col'}, use_global_device_ids=true, to_apply=%region_10.11 | all-reduce | flops 2560 | bytes 20480 | tf_op jit(solution)/shard_map/psum | solution.py:166
  510.3 169.5 %all-reduce.4.cloned.1.call-done = (f32[256,256]{1,0:T(8,128)}, f32[256,256]{1,0:T(8,128)}, f32[256,256]{1,0:T(8,128)}, f32[256,256]{1,0:T(8,128)}) async-done(((f32[256,256]{1,0:T(8,128)}, f32[256,256]{1,0:T(8,128)}, f32[256,256]{1,0:T(8,128)}, f32[256,256]{1,0:T(8,128)}), (f32[256,256]{1,0:T(8,128)}, f32[256,256]{1,0:T(8,128)}, f32[256,256]{1,0:T(8,128)}, ...) | async-done | bytes 1048592 | tf_op jit(solution)/shard_map/psum | solution.py:166
  679.8 1.9 broadcast_multiply_fusion.3
  681.7 1.9 broadcast_multiply_fusion.1
  (170 shorter events, 54.8 us)
Async XLA Ops:
  8.9 5.7 collective-permute-start
  13.3 5.2 collective-permute-start.1
  18.5 10.0 %collective-permute-start.3 = (bf16[4,6,1,256]{3,2,1,0:T(2,128)(2,1)S(1)}, bf16[4,6,1,256]{3,2,1,0:T(2,128)(2,1)S(1)}, u32[]{:S(2)}, u32[]{:S(2)}) collective-permute-start(bf16[4,6,1,256]{3,2,1,0:T(2,128)(2,1)S(1)} %get-tuple-element.250), channel_id=1, source_target_pairs={{0,1},{1,2},{2,3},{3,4},{4,5},{5,6},{6,7},{8,9},{9,10},{10,11},{11... | collective-permute-start | bytes 36872 | tf_op jit(solution)/shard_map/ppermute | solution.py:22
  26.3 8.5 %collective-permute-start.2 = (bf16[4,6,1,256]{3,2,1,0:T(2,128)(2,1)S(1)}, bf16[4,6,1,256]{3,2,1,0:T(2,128)(2,1)S(1)}, u32[]{:S(2)}, u32[]{:S(2)}) collective-permute-start(bf16[4,6,1,256]{3,2,1,0:T(2,128)(2,1)S(1)} %get-tuple-element.249), channel_id=1, source_target_pairs={{1,0},{2,1},{3,2},{4,3},{5,4},{6,5},{7,6},{9,8},{10,9},{11,10},{12... | collective-permute-start | bytes 36872 | tf_op jit(solution)/shard_map/ppermute | solution.py:23
  37.3 30.2 %all-gather.3.cloned.1.call-start = ((), (), s32[]{:S(2)}) async-start(), calls=%async_computation.3 | async-start | bytes 1179648 | tf_op jit(solution)/shard_map/while/body/eval_jaxpr/all_gather | solution.py:64
  40.2 55.1 %all-gather.5.cloned.1.call-start = ((), (), s32[]{:S(2)}) async-start(), calls=%async_computation.4 | async-start | bytes 1179648 | tf_op jit(solution)/shard_map/while/body/eval_jaxpr/all_gather | solution.py:65
  42.1 148.9 %reduce-scatter.3.cloned.1.call-start = ((), (), s32[]{:S(2)}) async-start(), calls=%async_computation.5 | async-start | bytes 1179648 | tf_op jit(solution)/shard_map/while/body/eval_jaxpr/reduce_scatter | solution.py:106
  108.6 5.8 copy-start.1
  114.3 32.9 %copy-start.3 = (f32[64,8,4,32]{3,2,1,0:T(4,128)}, f32[64,8,4,32]{3,2,1,0:T(4,128)S(1)}, u32[]{:S(2)}) copy-start(f32[64,8,4,32]{3,2,1,0:T(4,128)S(1)} %get-tuple-element.373) | copy-start | bytes 786436 | tf_op jit(solution)/shard_map/while
  141.4 5.1 copy-start
  141.4 5.1 copy-start.13
  141.4 5.9 copy-start.12
  146.3 67.8 %reduce-scatter.5.cloned.1.call-start = ((), (), s32[]{:S(2)}) async-start(), calls=%async_computation.6 | async-start | bytes 1179648 | tf_op jit(solution)/shard_map/while/body/eval_jaxpr/reduce_scatter | solution.py:109
  155.7 5.1 copy-start.2
  160.9 26.3 %copy-start.7 = (bf16[256,256]{1,0:T(8,128)(2,1)S(1)}, bf16[256,256]{1,0:T(8,128)(2,1)}, u32[]{:S(2)}) copy-start(bf16[256,256]{1,0:T(8,128)(2,1)} %get-tuple-element.426) | copy-start | bytes 393220 | tf_op jit(solution)/shard_map/while
  160.9 26.5 %copy-start.4 = (bf16[256,256]{1,0:T(8,128)(2,1)S(1)}, bf16[256,256]{1,0:T(8,128)(2,1)}, u32[]{:S(2)}) copy-start(bf16[256,256]{1,0:T(8,128)(2,1)} %get-tuple-element.428) | copy-start | bytes 393220 | tf_op jit(solution)/shard_map/while
  186.1 5.0 copy-start.6
  186.1 28.0 %copy-start.5 = (bf16[256,256]{1,0:T(8,128)(2,1)S(1)}, bf16[256,256]{1,0:T(8,128)(2,1)}, u32[]{:S(2)}) copy-start(bf16[256,256]{1,0:T(8,128)(2,1)} %get-tuple-element.429) | copy-start | bytes 393220 | tf_op jit(solution)/shard_map/while
  186.1 29.5 %copy-start.14 = (bf16[2,4,64,256]{3,2,1,0:T(8,128)(2,1)S(1)}, bf16[2,4,64,256]{3,2,1,0:T(8,128)(2,1)}, u32[]{:S(2)}) copy-start(bf16[2,4,64,256]{3,2,1,0:T(8,128)(2,1)} %get-tuple-element.404) | copy-start | bytes 786436 | tf_op jit(solution)/shard_map/while
  186.1 29.5 %copy-start.8 = (f32[256,256]{1,0:T(8,128)S(1)}, f32[256,256]{1,0:T(8,128)}, u32[]{:S(2)}) copy-start(f32[256,256]{1,0:T(8,128)} %get-tuple-element.399) | copy-start | bytes 786436 | tf_op jit(solution)/shard_map/while
  186.1 30.8 %copy-start.10 = (f32[256,256]{1,0:T(8,128)S(1)}, f32[256,256]{1,0:T(8,128)}, u32[]{:S(2)}) copy-start(f32[256,256]{1,0:T(8,128)} %get-tuple-element.400) | copy-start | bytes 786436 | tf_op jit(solution)/shard_map/while
  215.6 2.8 copy-start.15
  216.9 1.4 copy-start.9
  219.0 30.7 %all-gather.3.cloned.1.call-start = ((), (), s32[]{:S(2)}) async-start(), calls=%async_computation.3 | async-start | bytes 1179648 | tf_op jit(solution)/shard_map/while/body/eval_jaxpr/all_gather | solution.py:64
  221.9 55.4 %all-gather.5.cloned.1.call-start = ((), (), s32[]{:S(2)}) async-start(), calls=%async_computation.4 | async-start | bytes 1179648 | tf_op jit(solution)/shard_map/while/body/eval_jaxpr/all_gather | solution.py:65
  223.9 150.3 %reduce-scatter.3.cloned.1.call-start = ((), (), s32[]{:S(2)}) async-start(), calls=%async_computation.5 | async-start | bytes 1179648 | tf_op jit(solution)/shard_map/while/body/eval_jaxpr/reduce_scatter | solution.py:106
  290.7 5.8 copy-start.1
  296.4 32.9 %copy-start.3 = (f32[64,8,4,32]{3,2,1,0:T(4,128)}, f32[64,8,4,32]{3,2,1,0:T(4,128)S(1)}, u32[]{:S(2)}) copy-start(f32[64,8,4,32]{3,2,1,0:T(4,128)S(1)} %get-tuple-element.373) | copy-start | bytes 786436 | tf_op jit(solution)/shard_map/while
  323.4 5.1 copy-start
  323.4 5.1 copy-start.13
  323.4 5.9 copy-start.12
  328.4 67.8 %reduce-scatter.5.cloned.1.call-start = ((), (), s32[]{:S(2)}) async-start(), calls=%async_computation.6 | async-start | bytes 1179648 | tf_op jit(solution)/shard_map/while/body/eval_jaxpr/reduce_scatter | solution.py:109
  337.8 5.1 copy-start.2
  343.0 26.3 %copy-start.7 = (bf16[256,256]{1,0:T(8,128)(2,1)S(1)}, bf16[256,256]{1,0:T(8,128)(2,1)}, u32[]{:S(2)}) copy-start(bf16[256,256]{1,0:T(8,128)(2,1)} %get-tuple-element.426) | copy-start | bytes 393220 | tf_op jit(solution)/shard_map/while
  343.0 26.5 %copy-start.4 = (bf16[256,256]{1,0:T(8,128)(2,1)S(1)}, bf16[256,256]{1,0:T(8,128)(2,1)}, u32[]{:S(2)}) copy-start(bf16[256,256]{1,0:T(8,128)(2,1)} %get-tuple-element.428) | copy-start | bytes 393220 | tf_op jit(solution)/shard_map/while
  368.1 6.0 copy-start.6
  368.1 28.1 %copy-start.5 = (bf16[256,256]{1,0:T(8,128)(2,1)S(1)}, bf16[256,256]{1,0:T(8,128)(2,1)}, u32[]{:S(2)}) copy-start(bf16[256,256]{1,0:T(8,128)(2,1)} %get-tuple-element.429) | copy-start | bytes 393220 | tf_op jit(solution)/shard_map/while
  368.2 29.5 %copy-start.14 = (bf16[2,4,64,256]{3,2,1,0:T(8,128)(2,1)S(1)}, bf16[2,4,64,256]{3,2,1,0:T(8,128)(2,1)}, u32[]{:S(2)}) copy-start(bf16[2,4,64,256]{3,2,1,0:T(8,128)(2,1)} %get-tuple-element.404) | copy-start | bytes 786436 | tf_op jit(solution)/shard_map/while
  368.2 29.6 %copy-start.8 = (f32[256,256]{1,0:T(8,128)S(1)}, f32[256,256]{1,0:T(8,128)}, u32[]{:S(2)}) copy-start(f32[256,256]{1,0:T(8,128)} %get-tuple-element.399) | copy-start | bytes 786436 | tf_op jit(solution)/shard_map/while
  368.2 30.9 %copy-start.10 = (f32[256,256]{1,0:T(8,128)S(1)}, f32[256,256]{1,0:T(8,128)}, u32[]{:S(2)}) copy-start(f32[256,256]{1,0:T(8,128)} %get-tuple-element.400) | copy-start | bytes 786436 | tf_op jit(solution)/shard_map/while
  397.7 2.8 copy-start.15
  399.1 1.4 copy-start.9
  400.4 0.7 copy-start.11
  401.2 278.7 %all-reduce.4.cloned.1.call-start = ((), (), s32[]{:S(2)}) async-start(), calls=%async_computation.2 | async-start | bytes 2097152 | tf_op jit(solution)/shard_map/psum | solution.py:166
  402.0 5.3 collective-permute-start.5
  403.3 5.3 collective-permute-start.4
  409.6 10.1 %collective-permute-start.6 = (bf16[4,6,1,256]{3,2,1,0:T(2,128)(2,1)S(1)}, bf16[4,6,1,256]{3,2,1,0:T(2,128)(2,1)S(1)}, u32[]{:S(2)}, u32[]{:S(2)}) collective-permute-start(bf16[4,6,1,256]{3,2,1,0:T(2,128)(2,1)S(1)} %get-tuple-element.247), channel_id=1, source_target_pairs={{0,1},{1,2},{2,3},{3,4},{4,5},{5,6},{6,7},{8,9},{9,10},{10,11},{11... | collective-permute-start | bytes 36872 | tf_op jit(solution)/shard_map/ppermute | solution.py:22
  416.7 8.5 %collective-permute-start.7 = (bf16[4,6,1,256]{3,2,1,0:T(2,128)(2,1)S(1)}, bf16[4,6,1,256]{3,2,1,0:T(2,128)(2,1)S(1)}, u32[]{:S(2)}, u32[]{:S(2)}) collective-permute-start(bf16[4,6,1,256]{3,2,1,0:T(2,128)(2,1)S(1)} %get-tuple-element.248), channel_id=1, source_target_pairs={{1,0},{2,1},{3,2},{4,3},{5,4},{6,5},{7,6},{9,8},{10,9},{11,10},{12... | collective-permute-start | bytes 36872 | tf_op jit(solution)/shard_map/ppermute | solution.py:23
  (1 other events, 0.7 us)
Sparse Core Ops, SparseCore 0:
  40.3 27.1 all-gather.2
  69.5 25.7 all-gather.4
  146.4 31.6 reduce-scatter.2
  180.7 33.4 reduce-scatter.4
  222.1 27.5 all-gather.2
  251.6 25.7 all-gather.4
  328.5 31.6 reduce-scatter.2
  362.9 33.2 reduce-scatter.4
Sparse Core Ops, SparseCore 1:
  419.8 260.0 all-reduce.3
where the time goes:
time: 693 us; the launch traced here: 691 us
  waiting for transfers between devices  307 us (44%)
  matrix products  171 us (25%)
  blocking collectives  80.8 us (12%)
  local copies, waits for them, and re-layouts  72.3 us (10%)
  starting transfers between devices  28.7 us (4%)
  between operations  15.6 us (2%)
  other arithmetic  15.3 us (2%)
    psum x1, waiting for transfers between devices, local(): lax.psum((acc_q, acc_k, acc_v, acc_out, acc_gain, local_kernel), ('mem',...  169 us
    psum x1, blocking collectives, local(): lax.psum((acc_q, acc_k, acc_v, acc_out, acc_gain, local_kernel), ('mem',...  80.8 us
    dot_general x2, matrix products, one_block(): jnp.einsum('chmn,mche->nche', grad_score, query_heads, preferred_element_...  54 us
    dot_general x2, matrix products, one_block(): jnp.einsum('chmn,nche->mche', grad_score, key_heads, preferred_element_ty...  50.3 us
    reduce_scatter x2, waiting for transfers between devices, one_block(): lax.psum_scatter(part_v.astype(jnp.bfloat16), 'mem', scatter_dimension=0,...  42.9 us
    all_gather x2, waiting for transfers between devices, one_block(): lax.all_gather(key_proj, 'mem', axis=0, tiled=True)  40.5 us
    all_gather x2, waiting for transfers between devices, one_block(): lax.all_gather(value_proj, 'mem', axis=0, tiled=True)  37.9 us
    ppermute x4, starting transfers between devices, with_halo(): before = lax.ppermute(last, axis, up)  23.2 us
  transfers between devices with their start and end apart: 17, of which 11 were waited for; matrix products, arithmetic and copies ran while one was open for 19% of the time, Pallas kernels for 0%

commit v1 on v0

v1 whole, which is shorter than its diff:
```python
import functools
import math

import jax
import jax.numpy as jnp
import numpy as np
from jax import lax
from jax.experimental import pallas as pl
from jax.experimental.pallas import tpu as pltpu
from jax.sharding import PartitionSpec as P

HEADS = 8
EPS = 1e-06
BF = jnp.bfloat16
F32 = jnp.float32
NT = (((1,), (1,)), ((), ()))
TN = (((0,), (0,)), ((), ()))


def dot(a, b, dims=None):
    if dims is None:
        return jnp.dot(a, b, preferred_element_type=F32)
    return lax.dot_general(a, b, dims, preferred_element_type=F32)


def split_matrix(parts, members, cols):
    per = cols // parts
    out = np.zeros((parts, per, members, members, cols), np.float32)
    for j in range(parts):
        for c in range(per):
            for m in range(members):
                out[j, c, m, m, j * per + c] = 1
    return out.reshape(parts * per * members, members * cols)


def halo_matrices(parts, members, rows, cols, side):
    per = cols // parts
    mats = []
    for pair in range((rows + 2) // 2):
        out = np.zeros((parts, 2, per + 2, members, 2 * members * cols + 2 * side), np.float32)
        for j in range(parts):
            for q in range(2):
                for c in range(per + 2):
                    for m in range(members):
                        col = j * per + c - 1
                        edge = (2 * pair + q) * members + m
                        if col < 0:
                            src = 2 * members * cols + edge
                        elif col >= cols:
                            src = 2 * members * cols + side + edge
                        else:
                            src = (q * members + m) * cols + col
                        out[j, q, c, m, src] = 1
        mats.append(out.reshape(-1, out.shape[-1]))
    return np.stack(mats)


def gather_matrix(parts, cells, members):
    out = np.zeros((cells, parts, members, parts, cells, members), np.float32)
    for s in range(parts):
        for c in range(cells):
            for m in range(members):
                out[c, s, m, s, c, m] = 1
    return out.reshape(cells * parts * members, -1)


def pack_kernel(fields, cot, before, after, left, right, split, halo, send):
    members, rows, cols, width = fields.shape
    parts = send.shape[0]
    per = cols // parts * members
    for r in range(rows):
        tokens = fields[:, r].reshape(members * cols, width)
        moved = dot(split[...], tokens).astype(BF).reshape(parts, per, width)
        send[:, r * per : (r + 1) * per, :] = moved
    base = rows * per
    lines = [before[...]] + [cot[:, r] for r in range(rows)] + [after[...]]
    lines = [x.reshape(members * cols, width) for x in lines]
    step = 2 * (per + 2 * members)
    for pair in range(halo.shape[0]):
        tokens = jnp.concatenate([lines[2 * pair], lines[2 * pair + 1], left[...], right[...]], axis=0)
        moved = dot(halo[pair], tokens).astype(BF).reshape(parts, step, width)
        send[:, base + pair * step : base + (pair + 1) * step, :] = moved


def main_kernel(
    tile_rows,
    tile_cols,
    recv,
    gain,
    mix,
    wq,
    wk,
    wv,
    wo,
    gather8,
    gather4,
    headsum,
    send,
    padded,
    lhs_a,
    lhs_b,
    mat_k,
    mat_v,
):
    parts, _, width = recv.shape
    head_dim = width // HEADS
    scale = 1.0 / math.sqrt(head_dim)
    cells = tile_rows * tile_cols
    mem_dev = 4
    all_members = parts * mem_dev
    tokens = cells * all_members
    pad_cols = tile_cols + 2
    pad_cells = (tile_rows + 2) * pad_cols
    base = cells * mem_dev

    def regroup(start, count, matrix):
        rows = count * mem_dev
        part = recv[:, start : start + rows, :].reshape(parts * rows, width)
        return dot(matrix[...], part)

    x = jnp.concatenate([regroup(g * 32, 8, gather8) for g in range(cells // 8)], axis=0)
    done = 0
    while done < pad_cells:
        count = 8 if pad_cells - done >= 8 else 4
        block = regroup(base + done * mem_dev, count, gather8 if count == 8 else gather4)
        padded[done : done + count] = block.reshape(count, all_members, width)
        done += count

    def shifted(i, j):
        picked = [
            padded[(r + 2 - i) * pad_cols + 2 - j : (r + 2 - i) * pad_cols + 2 - j + tile_cols]
            for r in range(tile_rows)
        ]
        return jnp.concatenate(picked, axis=0).reshape(tokens, width)

    inv = lax.rsqrt(jnp.mean(x * x, axis=-1, keepdims=True) + EPS)
    normed = x * inv
    inputs = (normed * gain[...]).astype(BF)
    queries = dot(inputs, wq[...]).astype(BF)
    keys = dot(inputs, wk[...]).astype(BF)
    values = dot(inputs, wv[...]).astype(BF)

    conv = jnp.zeros((tokens, width), F32)
    for i in range(3):
        for j in range(3):
            conv = conv + mix[3 * i + j : 3 * i + j + 1, :] * shifted(i, j)
    grad_mixed = conv.astype(BF)
    grad_att = dot(grad_mixed, wo[...], NT).astype(BF)

    row_head = lax.broadcasted_iota(jnp.int32, (width, width), 0) // head_dim
    col_head = lax.broadcasted_iota(jnp.int32, (width, width), 1) // head_dim
    same = row_head == col_head
    lane_head = lax.broadcasted_iota(jnp.int32, (all_members, width), 1) // head_dim

    def expand(block):
        tiled = jnp.concatenate([block] * HEADS, axis=0)
        return jnp.where(same, tiled, jnp.zeros_like(tiled))

    for c in range(cells):
        rows = slice(c * all_members, (c + 1) * all_members)
        mat_k[c] = expand(keys[rows])
        mat_v[c] = expand(values[rows])
    for c in range(cells):
        rows = slice(c * all_members, (c + 1) * all_members)
        lhs_a[rows, :] = dot(queries[rows], mat_k[c], NT)
        lhs_b[rows, :] = dot(grad_att[rows], mat_v[c], NT)

    scores = lhs_a[...] * scale
    lane = lax.broadcasted_iota(jnp.int32, (tokens, 128), 1)
    halves = []
    for h in range(width // 128):
        top = scores[:, h * 128 : (h + 1) * 128]
        step = 1
        while step < all_members:
            up = pltpu.roll(top, step, 1)
            down = pltpu.roll(top, 128 - step, 1)
            top = jnp.maximum(top, jnp.where((lane & step) != 0, up, down))
            step *= 2
        halves.append(top)
    lifted = jnp.exp(scores - jnp.concatenate(halves, axis=1))

    def head_sums(v):
        hi = v.astype(BF)
        lo = (v - hi.astype(F32)).astype(BF)
        return dot(hi, headsum[...]) + dot(lo, headsum[...])

    prob = lifted / head_sums(lifted)
    prob_b = prob.astype(BF)
    grad_prob = lhs_b[...]
    inner = head_sums(prob * grad_prob)
    grad_score = (prob * (grad_prob - inner) * scale).astype(BF)

    att_l, gq_l, gk_l, gv_l = [], [], [], []

    def diagonal(full):
        out = jnp.zeros((all_members, width), F32)
        for h in range(HEADS):
            out = jnp.where(lane_head == h, full[h * all_members : (h + 1) * all_members], out)
        return out

    for c in range(cells):
        rows = slice(c * all_members, (c + 1) * all_members)
        att_l.append(dot(prob_b[rows], mat_v[c]).astype(BF))
        gq_l.append(dot(grad_score[rows], mat_k[c]).astype(BF))
        gk_l.append(diagonal(dot(grad_score[rows], queries[rows], TN)).astype(BF))
        gv_l.append(diagonal(dot(prob_b[rows], grad_att[rows], TN)).astype(BF))
    attended = jnp.concatenate(att_l, axis=0)
    grad_q = jnp.concatenate(gq_l, axis=0)
    grad_k = jnp.concatenate(gk_l, axis=0)
    grad_v = jnp.concatenate(gv_l, axis=0)

    mixed = dot(attended, wo[...]).astype(BF).astype(F32)
    extra = []
    for i in range(3):
        for j in range(3):
            extra.append(jnp.sum(mixed * shifted(i, j), axis=0, keepdims=True))

    grad_in = dot(grad_q, wq[...], NT) + dot(grad_k, wk[...], NT) + dot(grad_v, wv[...], NT)
    extra.append(jnp.sum(grad_in * normed, axis=0, keepdims=True))
    grad_normed = grad_in * gain[...]
    mean = jnp.mean(grad_normed * normed, axis=-1, keepdims=True)
    grad = (shifted(1, 1) + inv * (grad_normed - normed * mean)).astype(BF)
    for g in range(cells // 8):
        back = dot(gather8[...], grad[g * 256 : (g + 1) * 256], TN).astype(BF)
        send[:, g * 32 : (g + 1) * 32, :] = back.reshape(parts, 32, width)

    weights = [
        dot(inputs, grad_q, TN),
        dot(inputs, grad_k, TN),
        dot(inputs, grad_v, TN),
        dot(attended, grad_mixed, TN),
    ]
    shard = 4 * width // parts
    for j in range(parts):
        which, start = divmod(j * shard, width)
        send[j, base : base + shard, :] = weights[which][start : start + shard].astype(BF)
    extras = jnp.concatenate(extra + [jnp.zeros((16 - len(extra), width), F32)], axis=0).astype(BF)
    for j in range(parts):
        send[j, base + shard : base + shard + 16, :] = extras


def unpack_kernel(base, shard, recv, split, out, total):
    members, rows, cols, width = out.shape
    parts = recv.shape[0]
    per = cols // parts * members
    for r in range(rows):
        tokens = recv[:, r * per : (r + 1) * per, :].reshape(parts * per, width)
        out[:, r] = dot(split[...], tokens, TN).astype(BF).reshape(members, cols, width)
    acc = recv[0, base:, :].astype(F32)
    for j in range(1, parts):
        acc = acc + recv[j, base:, :].astype(F32)
    total[...] = acc


def ring(axis, step):
    size = lax.axis_size(axis)
    return [(i, (i + step) % size) for i in range(size)]


def edges(first, last, axis):
    before = lax.ppermute(last, axis, ring(axis, 1))
    after = lax.ppermute(first, axis, ring(axis, -1))
    place, size = lax.axis_index(axis), lax.axis_size(axis)
    zero = jnp.zeros_like(before)
    return jnp.where(place > 0, before, zero), jnp.where(place < size - 1, after, zero)


def local(fields, norm_gain, w_query, w_key, w_value, w_out, mix_kernel, cotangent):
    members, rows, cols, width = fields.shape
    parts = lax.axis_size("mem")
    per = cols // parts
    cells = rows * per
    pad_cells = (rows + 2) * (per + 2)
    params = pltpu.CompilerParams(vmem_limit_bytes=60 * 1024 * 1024)

    with jax.named_scope("halo"):
        before, after = edges(cotangent[:, 0], cotangent[:, rows - 1], "row")

        def column(c):
            parts_c = [before[None, :, c], jnp.swapaxes(cotangent[:, :, c], 0, 1), after[None, :, c]]
            flat = jnp.concatenate(parts_c, axis=0).reshape((rows + 2) * members, width)
            return jnp.pad(flat, ((0, 32 - flat.shape[0]), (0, 0)))

        left, right = edges(column(0), column(cols - 1), "col")

    split = jnp.asarray(split_matrix(parts, members, cols), BF)
    halo = jnp.asarray(halo_matrices(parts, members, rows, cols, 32), BF)
    with jax.named_scope("pack"):
        send = pl.pallas_call(
            pack_kernel,
            out_shape=jax.ShapeDtypeStruct((parts, (cells + pad_cells) * members, width), BF),
            compiler_params=params,
        )(fields, cotangent, before, after, left, right, split, halo)
    with jax.named_scope("to_cells"):
        recv = lax.all_to_all(send, "mem", 0, 0)

    tokens = cells * members * parts
    base = cells * members
    shard = 4 * width // parts
    headsum = np.kron(np.eye(HEADS), np.ones((width // HEADS, width // HEADS)))
    with jax.named_scope("attention"):
        back = pl.pallas_call(
            functools.partial(main_kernel, rows, per),
            out_shape=jax.ShapeDtypeStruct((parts, base + shard + 16, width), BF),
            scratch_shapes=[
                pltpu.VMEM((pad_cells, members * parts, width), F32),
                pltpu.VMEM((tokens, width), F32),
                pltpu.VMEM((tokens, width), F32),
                pltpu.VMEM((cells, width, width), BF),
                pltpu.VMEM((cells, width, width), BF),
            ],
            compiler_params=params,
        )(
            recv,
            norm_gain.reshape(1, width),
            mix_kernel.reshape(9, width),
            w_query,
            w_key,
            w_value,
            w_out,
            jnp.asarray(gather_matrix(parts, 8, members), BF),
            jnp.asarray(gather_matrix(parts, 4, members), BF),
            jnp.asarray(headsum, BF),
        )
    with jax.named_scope("to_members"):
        landed = lax.all_to_all(back, "mem", 0, 0)
    with jax.named_scope("unpack"):
        grad_fields, total = pl.pallas_call(
            functools.partial(unpack_kernel, base, shard),
            out_shape=(
                jax.ShapeDtypeStruct(fields.shape, BF),
                jax.ShapeDtypeStruct((shard + 16, width), F32),
            ),
            compiler_params=params,
        )(landed, split)

    with jax.named_scope("reduce"):
        grid = lax.axis_size("row") * lax.axis_size("col")
        deep = shard // grid
        extras = jnp.pad(total[shard:], ((0, grid - 16), (0, 0))).reshape(grid, 1, width)
        chunk = jnp.concatenate([total[:shard].reshape(grid, deep, width), extras], axis=1)
        chunk = jnp.pad(chunk.astype(BF), ((0, 0), (0, -(deep + 1) % 8), (0, 0)))
        got = lax.all_to_all(chunk, ("row", "col"), 0, 0)
        mine = jnp.sum(got.astype(F32), axis=0, keepdims=True).astype(BF)
        all_got = lax.all_to_all(jnp.broadcast_to(mine, chunk.shape), ("row", "col"), 0, 0)
        piece = all_got[:, :deep].reshape(shard, width)
        extras = all_got[:10, deep].astype(F32)
        pieces = lax.all_gather(piece, "mem", axis=0, tiled=True)

    token_total = parts * members * rows * cols * grid
    scale_all = 1.0 / math.sqrt(token_total)
    grads = pieces.astype(F32) * scale_all
    extras = extras * scale_all
    return (
        grad_fields,
        extras[9],
        grads[:width],
        grads[width : 2 * width],
        grads[2 * width : 3 * width],
        grads[3 * width :],
        extras[:9].reshape(3, 3, width),
    )


def solution(mesh):
    tile = P("mem", "row", "col", None)
    in_specs = (tile, P(), P(), P(), P(), P(), P(), tile)
    out_specs = (tile, P(), P(), P(), P(), P(), P())
    return jax.shard_map(local, mesh=mesh, in_specs=in_specs, out_specs=out_specs, check_vma=False)
```

time: 693 us -> 125 us (0.18)
  waiting for transfers between devices: 307 us -> 16.4 us
  matrix products: 171 us -> 0 us
  local copies, waits for them, and re-layouts: 72.3 us -> 6.6 us
  blocking collectives: 80.8 us -> 63.6 us
  between operations: 15.6 us -> 0.8 us
  Pallas kernels: 0 us -> 13.1 us
  other arithmetic: 15.3 us -> 2.43 us
    psum x1 -> x0, waiting for transfers between devices: 169 us -> none  [local(): lax.psum((acc_q, acc_k, acc_v, acc_out, acc_gain, local_kernel), ('mem',...]
    dot_general x34 -> x0, matrix products: 159 us -> none  [the longest x2 54 us: one_block(): jnp.einsum('chmn,mche->nche', grad_score, query_heads, preferred_element_...]
    psum x1 -> x0, blocking collectives: 80.8 us -> none  [local(): lax.psum((acc_q, acc_k, acc_v, acc_out, acc_gain, local_kernel), ('mem',...]
    all_gather x4 -> x0, waiting for transfers between devices: 78.3 us -> none  [the longest x2 40.5 us: one_block(): lax.all_gather(key_proj, 'mem', axis=0, tiled=True)]
    all_to_all x0 -> x3, blocking collectives: none -> 47.3 us  [the longest x1 18.3 us: local(): landed = lax.all_to_all(back, 'mem', 0, 0)]
    reduce_scatter x4 -> x0, waiting for transfers between devices: 42.9 us -> none  [the longest x2 42.9 us: one_block(): lax.psum_scatter(part_v.astype(jnp.bfloat16), 'mem', scatter_dimension=0,...]
    reshape x13 -> x8, local copies, waits for them, and re-layouts: 31.3 us -> 1.32 us  [the longest x1 0.61 us: local(): mix_kernel.reshape(9, width)]
    convert_element_type x14 -> x0, local copies, waits for them, and re-layouts: 23.9 us -> none  [the longest x2 9.87 us: one_block(): part_k.astype(jnp.bfloat16)]
  transfers between devices with their start and end apart: 17 -> 5, of which waited for: 11 -> 5; matrix products, arithmetic and copies ran while one was open for 19% -> 2% of each run, Pallas kernels for 0% -> 0%
where the time goes in v1:
time: 125 us
  blocking collectives  63.6 us (51%)
  starting transfers between devices  22 us (18%)
  waiting for transfers between devices  16.4 us (13%)
  Pallas kernels  13.1 us (10%)
  local copies, waits for them, and re-layouts  6.6 us (5%)
  other arithmetic  2.43 us (2%)
    all_to_all x1, blocking collectives, local(): landed = lax.all_to_all(back, 'mem', 0, 0)  18.3 us
    all_to_all x1, blocking collectives, local(): got = lax.all_to_all(chunk, ('row', 'col'), 0, 0)  16.3 us
    all_gather x1, blocking collectives, local(): pieces = lax.all_gather(piece, 'mem', axis=0, tiled=True)  16.3 us
    all_to_all x1, blocking collectives, local(): lax.all_to_all(jnp.broadcast_to(mine, chunk.shape), ('row', 'col'), 0, 0)  12.7 us
    all_to_all x1, waiting for transfers between devices, local(): recv = lax.all_to_all(send, 'mem', 0, 0)  12.4 us
    all_to_all x1, starting transfers between devices, local(): recv = lax.all_to_all(send, 'mem', 0, 0)  8.35 us
    ppermute x2, starting transfers between devices, edges(): before = lax.ppermute(last, axis, ring(axis, 1))  8.28 us
    pallas_call x1, Pallas kernels, local(): pl.pallas_call(functools.partial(main_kernel, rows, per), out_shape=jax.S...  8.02 us
  transfers between devices with their start and end apart: 5, of which 5 were waited for; matrix products, arithmetic and copies ran while one was open for 2% of the time, Pallas kernels for 0%

profile of v1, /device:TPU:1, one launch (start us, length us, event | category | flops | bytes accessed | tf_op | source)
XLA Modules:
  0.0 124.9 jit_solution(2364539722458518620)
XLA Ops:
  0.6 0.9 slice_bitcast_fusion
  1.5 2.5 %collective-permute-start = (bf16[4,32,256]{2,1,0:T(8,128)(2,1)S(1)}, bf16[4,32,256]{2,1,0:T(8,128)(2,1)S(1)}, u32[]{:S(2)}, u32[]{:S(2)}) collective-permute-start(bf16[4,32,256]{2,1,0:T(8,128)(2,1)S(1)} %get-tuple-element.18), channel_id=1, source_target_pairs={{0,8},{8,16},{16,24},{24,0},{1,9},{9,17},{17,25},{25,1},{2,10},{10... | collective-permute-start | bytes 196616 | tf_op jit(solution)/shard_map/halo/ppermute | solution.py:261
  4.1 2.8 %collective-permute-start.1 = (bf16[4,32,256]{2,1,0:T(8,128)(2,1)S(1)}, bf16[4,32,256]{2,1,0:T(8,128)(2,1)S(1)}, u32[]{:S(2)}, u32[]{:S(2)}) collective-permute-start(bf16[4,32,256]{2,1,0:T(8,128)(2,1)S(1)} %get-tuple-element.17), channel_id=1, source_target_pairs={{0,24},{8,0},{16,8},{24,16},{1,25},{9,1},{17,9},{25,17},{2,26},{10... | collective-permute-start | bytes 196616 | tf_op jit(solution)/shard_map/halo/ppermute | solution.py:262
  6.9 0.9 fusion.5
  7.8 0.4 collective-permute-done.1
  8.2 0.0 copy-start.1
  8.2 0.2 collective-permute-done
  8.5 0.3 copy-done.1
  8.8 0.0 copy-start.2
  8.9 0.5 copy-done.2
  9.5 5.7 %collective-permute-start.2 = (bf16[32,256]{1,0:T(8,128)(2,1)S(1)}, bf16[32,256]{1,0:T(8,128)(2,1)S(1)}, u32[]{:S(2)}, u32[]{:S(2)}) collective-permute-start(bf16[32,256]{1,0:T(8,128)(2,1)S(1)} %pad.16), channel_id=1, source_target_pairs={{0,1},{1,2},{2,3},{3,4},{4,5},{5,6},{6,7},{7,0},{8,9},{9,10},{10,1... | collective-permute-start | bytes 49160 | tf_op jit(solution)/shard_map/halo/ppermute | solution.py:261
  15.2 2.5 %collective-permute-start.3 = (bf16[32,256]{1,0:T(8,128)(2,1)S(1)}, bf16[32,256]{1,0:T(8,128)(2,1)S(1)}, u32[]{:S(2)}, u32[]{:S(2)}) collective-permute-start(bf16[32,256]{1,0:T(8,128)(2,1)S(1)} %pad.17), channel_id=1, source_target_pairs={{0,7},{1,0},{2,1},{3,2},{4,3},{5,4},{6,5},{7,6},{8,15},{9,8},{10,9... | collective-permute-start | bytes 49160 | tf_op jit(solution)/shard_map/halo/ppermute | solution.py:262
  17.8 1.0 collective-permute-done.2
  18.8 0.6 broadcast_select_fusion.3.left
  19.4 2.4 %collective-permute-done.3 = bf16[32,256]{1,0:T(8,128)(2,1)S(1)} collective-permute-done((bf16[32,256]{1,0:T(8,128)(2,1)S(1)}, bf16[32,256]{1,0:T(8,128)(2,1)S(1)}, u32[]{:S(2)}, u32[]{:S(2)}) %collective-permute-start.3) | collective-permute-done | bytes 16416 | tf_op jit(solution)/shard_map/halo/ppermute | solution.py:262
  21.8 0.6 broadcast_select_fusion.2.right
  22.4 2.9 %pack.1 = bf16[8,208,256]{2,1,0:T(8,128)(2,1)} custom-call(bf16[4,4,32,256]{3,2,1,0:T(8,128)(2,1)} %fields.1, bf16[4,4,32,256]{3,2,1,0:T(8,128)(2,1)} %cot.1, bf16[4,32,256]{2,1,0:T(8,128)(2,1)} %copy-done.2, bf16[4,32,256]{2,1,0:T(8,128)(2,1)} %copy-done.1, bf16[32,256]{1,0:T(8,128)(2,1)} %broadcast_select_fusion.3.left, ...), custom_call_target="tpu_custom_call" | custom-call | tf_op jit(solution)/shard_map/pack/pallas_call | solution.py:289
  25.3 0.0 copy-start.3
  25.3 8.4 %all-to-all-start = ((bf16[8,208,256]{2,1,0:T(8,128)(2,1)}), bf16[8,208,256]{2,1,0:T(8,128)(2,1)S(1)}, u32[]{:S(2)}, u32[]{:S(2)}) async-start(bf16[8,208,256]{2,1,0:T(8,128)(2,1)} %pack.1), calls=%async_computation | async-start | bytes 1703936 | tf_op jit(solution)/shard_map/to_cells/all_to_all | solution.py:295
  33.7 0.0 copy-done.3
  33.7 0.6 reshape.54.mix
  34.3 12.4 %all-to-all-done.recv = bf16[8,208,256]{2,1,0:T(8,128)(2,1)S(1)} async-done(((bf16[8,208,256]{2,1,0:T(8,128)(2,1)}), bf16[8,208,256]{2,1,0:T(8,128)(2,1)S(1)}, u32[]{:S(2)}, u32[]{:S(2)}) %all-to-all-start) | async-done | bytes 852000 | tf_op jit(solution)/shard_map/to_cells/all_to_all | solution.py:295
  46.7 0.0 copy-start
  46.7 0.9 copy-done
  47.6 8.0 %attention.1 = bf16[8,208,256]{2,1,0:T(8,128)(2,1)} custom-call(bf16[8,208,256]{2,1,0:T(8,128)(2,1)} %copy-done, f32[1,256]{1,0:T(1,128)} %bitcast.32, f32[9,256]{1,0:T(8,128)} %reshape.54.mix, bf16[256,256]{1,0:T(8,128)(2,1)} %wq.1, bf16[256,256]{1,0:T(8,128)(2,1)} %wk.1, bf16[256,256]{1,0:T(8,128)(2,1)} %wv.1, bf16[256,256]{1,0:T(8,128)(2,1)} %wo.1, ...), custom_call_target="tpu_custom_call" | custom-call | tf_op jit(solution)/shard_map/attention/pallas_call | solution.py:302
  55.6 18.3 %all_to_all.20.recv = bf16[8,208,256]{2,1,0:T(8,128)(2,1)} all-to-all(bf16[8,208,256]{2,1,0:T(8,128)(2,1)} %attention.1), channel_id=1, replica_groups=mesh['mem'=8,'row'=4,'col'=8] {'mem'}, dimensions={0} | all-to-all | bytes 1703936 | tf_op jit(solution)/shard_map/to_members/all_to_all | solution.py:326
  73.9 2.2 %unpack.1 = (bf16[4,4,32,256]{3,2,1,0:T(8,128)(2,1)}, f32[144,256]{1,0:T(8,128)}) custom-call(bf16[8,208,256]{2,1,0:T(8,128)(2,1)} %all_to_all.20.recv, bf16[128,128]{1,0:T(8,128)(2,1)} %constant.35.clone.split), custom_call_target="tpu_custom_call" | custom-call | tf_op jit(solution)/shard_map/unpack/pallas_call | solution.py:328
  76.1 0.9 convert.11
  77.1 0.1 fusion.2
  77.2 16.3 %all_to_all.21 = bf16[32,8,256]{2,1,0:T(8,128)(2,1)S(1)} all-to-all(bf16[32,8,256]{2,1,0:T(8,128)(2,1)S(1)} %fusion.2), channel_id=1, replica_groups=mesh['mem'=8,'row'=4,'col'=8] {'row','col'}, dimensions={0} | all-to-all | bytes 262144 | tf_op jit(solution)/shard_map/reduce/all_to_all | solution.py:343
  93.6 12.7 %all_to_all.22 = bf16[32,8,256]{2,1,0:T(8,128)(2,1)S(1)} all-to-all(bf16[32,8,256]{2,1,0:T(8,128)(2,1)S(1)} %broadcast_in_dim.14), channel_id=1, replica_groups=mesh['mem'=8,'row'=4,'col'=8] {'row','col'}, dimensions={0} | all-to-all | bytes 262144 | tf_op jit(solution)/shard_map/reduce/all_to_all | solution.py:345
  106.3 0.6 slice.83
  106.9 16.3 %all_gather.3 = bf16[1024,256]{1,0:T(8,128)(2,1)S(1)} all-gather(bf16[128,256]{1,0:T(8,128)(2,1)S(1)} %reshape.57), channel_id=1, replica_groups=mesh['mem'=8,'row'=4,'col'=8] {'mem'}, dimensions={0}, use_global_device_ids=true | all-gather | bytes 589824 | tf_op jit(solution)/shard_map/reduce/all_gather | solution.py:348
  123.2 0.1 convert_multiply_fusion
  123.3 1.0 fusion.4
  124.3 0.6 reshape.58
  (24 shorter events, 0.3 us)
Async XLA Ops:
  1.5 7.0 %collective-permute-start = (bf16[4,32,256]{2,1,0:T(8,128)(2,1)S(1)}, bf16[4,32,256]{2,1,0:T(8,128)(2,1)S(1)}, u32[]{:S(2)}, u32[]{:S(2)}) collective-permute-start(bf16[4,32,256]{2,1,0:T(8,128)(2,1)S(1)} %get-tuple-element.18), channel_id=1, source_target_pairs={{0,8},{8,16},{16,24},{24,0},{1,9},{9,17},{17,25},{25,1},{2,10},{10... | collective-permute-start | bytes 196616 | tf_op jit(solution)/shard_map/halo/ppermute | solution.py:261
  4.1 4.1 %collective-permute-start.1 = (bf16[4,32,256]{2,1,0:T(8,128)(2,1)S(1)}, bf16[4,32,256]{2,1,0:T(8,128)(2,1)S(1)}, u32[]{:S(2)}, u32[]{:S(2)}) collective-permute-start(bf16[4,32,256]{2,1,0:T(8,128)(2,1)S(1)} %get-tuple-element.17), channel_id=1, source_target_pairs={{0,24},{8,0},{16,8},{24,16},{1,25},{9,1},{17,9},{25,17},{2,26},{10... | collective-permute-start | bytes 196616 | tf_op jit(solution)/shard_map/halo/ppermute | solution.py:262
  8.2 0.6 copy-start.1
  8.8 0.6 copy-start.2
  9.5 9.3 %collective-permute-start.2 = (bf16[32,256]{1,0:T(8,128)(2,1)S(1)}, bf16[32,256]{1,0:T(8,128)(2,1)S(1)}, u32[]{:S(2)}, u32[]{:S(2)}) collective-permute-start(bf16[32,256]{1,0:T(8,128)(2,1)S(1)} %pad.16), channel_id=1, source_target_pairs={{0,1},{1,2},{2,3},{3,4},{4,5},{5,6},{6,7},{7,0},{8,9},{9,10},{10,1... | collective-permute-start | bytes 49160 | tf_op jit(solution)/shard_map/halo/ppermute | solution.py:261
  15.2 6.6 %collective-permute-start.3 = (bf16[32,256]{1,0:T(8,128)(2,1)S(1)}, bf16[32,256]{1,0:T(8,128)(2,1)S(1)}, u32[]{:S(2)}, u32[]{:S(2)}) collective-permute-start(bf16[32,256]{1,0:T(8,128)(2,1)S(1)} %pad.17), channel_id=1, source_target_pairs={{0,7},{1,0},{2,1},{3,2},{4,3},{5,4},{6,5},{7,6},{8,15},{9,8},{10,9... | collective-permute-start | bytes 49160 | tf_op jit(solution)/shard_map/halo/ppermute | solution.py:262
  25.3 8.4 %copy-start.3 = (f32[3,3,256]{2,1,0:T(4,128)S(1)}, f32[3,3,256]{2,1,0:T(4,128)}, u32[]{:S(2)}) copy-start(f32[3,3,256]{2,1,0:T(4,128)} %param.19) | copy-start | bytes 27652
  25.3 21.3 %all-to-all-start = ((bf16[8,208,256]{2,1,0:T(8,128)(2,1)}), bf16[8,208,256]{2,1,0:T(8,128)(2,1)S(1)}, u32[]{:S(2)}, u32[]{:S(2)}) async-start(bf16[8,208,256]{2,1,0:T(8,128)(2,1)} %pack.1), calls=%async_computation | async-start | bytes 1703936 | tf_op jit(solution)/shard_map/to_cells/all_to_all | solution.py:295
  46.7 0.9 copy-start

commit v2 on v1

--- a/solution.py
+++ b/solution.py
@@ -143,7 +143,7 @@
     conv = jnp.zeros((tokens, width), F32)
     for i in range(3):
         for j in range(3):
-            conv = conv + mix[3 * i + j : 3 * i + j + 1, :] * shifted(i, j)
+            conv = conv + mix[i, j : j + 1, :] * shifted(i, j)
     grad_mixed = conv.astype(BF)
     grad_att = dot(grad_mixed, wo[...], NT).astype(BF)
 
@@ -249,7 +249,34 @@
     acc = recv[0, base:, :].astype(F32)
     for j in range(1, parts):
         acc = acc + recv[j, base:, :].astype(F32)
-    total[...] = acc
+    total[...] = acc.astype(BF)
+
+
+def finish_kernel(scale, place, same_core, other_core, extras, g_q, g_k, g_v, g_o, g_mix, g_gain):
+    count, shard, width = same_core.shape
+    per = width // shard
+    outs = (g_q, g_k, g_v, g_o)
+    for p in range(2 * count):
+        code = lax.bitwise_xor(place[0], p)
+        spot = lax.shift_right_logical(code, 1)
+        got = jnp.where(code == 2 * spot, same_core[spot], other_core[spot]).astype(F32)
+        outs[p // per][p % per * shard : (p % per + 1) * shard, :] = got * scale
+    rest = extras[...].astype(F32) * scale
+    for i in range(3):
+        g_mix[i] = rest[3 * i : 3 * i + 3]
+    g_gain[...] = rest[9:10]
+
+
+def partner(axis, code):
+    return [(i, i ^ code) for i in range(lax.axis_size(axis))]
+
+
+def meet(values, axis, codes):
+    got = [values] + [lax.ppermute(values, axis, partner(axis, k)) for k in codes]
+    got = [x.astype(F32) for x in got]
+    while len(got) > 1:
+        got = [a + b for a, b in zip(got[::2], got[1::2])]
+    return lax.optimization_barrier(got[0].astype(BF))
 
 
 def ring(axis, step):
@@ -313,7 +340,7 @@
         )(
             recv,
             norm_gain.reshape(1, width),
-            mix_kernel.reshape(9, width),
+            mix_kernel,
             w_query,
             w_key,
             w_value,
@@ -329,37 +356,32 @@
             functools.partial(unpack_kernel, base, shard),
             out_shape=(
                 jax.ShapeDtypeStruct(fields.shape, BF),
-                jax.ShapeDtypeStruct((shard + 16, width), F32),
+                jax.ShapeDtypeStruct((shard + 16, width), BF),
             ),
             compiler_params=params,
         )(landed, split)
 
     with jax.named_scope("reduce"):
-        grid = lax.axis_size("row") * lax.axis_size("col")
-        deep = shard // grid
-        extras = jnp.pad(total[shard:], ((0, grid - 16), (0, 0))).reshape(grid, 1, width)
-        chunk = jnp.concatenate([total[:shard].reshape(grid, deep, width), extras], axis=1)
-        chunk = jnp.pad(chunk.astype(BF), ((0, 0), (0, -(deep + 1) % 8), (0, 0)))
-        got = lax.all_to_all(chunk, ("row", "col"), 0, 0)
-        mine = jnp.sum(got.astype(F32), axis=0, keepdims=True).astype(BF)
-        all_got = lax.all_to_all(jnp.broadcast_to(mine, chunk.shape), ("row", "col"), 0, 0)
-        piece = all_got[:, :deep].reshape(shard, width)
-        extras = all_got[:10, deep].astype(F32)
-        pieces = lax.all_gather(piece, "mem", axis=0, tiled=True)
-
-    token_total = parts * members * rows * cols * grid
-    scale_all = 1.0 / math.sqrt(token_total)
-    grads = pieces.astype(F32) * scale_all
-    extras = extras * scale_all
-    return (
-        grad_fields,
-        extras[9],
-        grads[:width],
-        grads[width : 2 * width],
-        grads[2 * width : 3 * width],
-        grads[3 * width :],
-        extras[:9].reshape(3, 3, width),
-    )
+        total = meet(total, "row", (1, 2, 3))
+        total = meet(total, "col", (2, 4, 6))
+        total = meet(total, "col", (1,))
+        piece = total[:shard]
+        same_core = jnp.stack([piece] + [lax.ppermute(piece, "mem", partner("mem", k)) for k in (2, 4, 6)])
+        same_core = lax.optimization_barrier(same_core)
+        other_core = lax.ppermute(same_core, "mem", partner("mem", 1))
+
+    grid = lax.axis_size("row") * lax.axis_size("col")
+    scale_all = 1.0 / math.sqrt(tokens * grid * parts)
+    with jax.named_scope("finish"):
+        square = jax.ShapeDtypeStruct((width, width), F32)
+        place = lax.axis_index("mem").astype(jnp.int32).reshape(1)
+        grads = pl.pallas_call(
+            functools.partial(finish_kernel, scale_all),
+            in_specs=[pl.BlockSpec(memory_space=pltpu.SMEM)] + [pl.BlockSpec(memory_space=pltpu.VMEM)] * 3,
+            out_shape=(square,) * 4 + (jax.ShapeDtypeStruct((3, 3, width), F32), jax.ShapeDtypeStruct((1, width), F32)),
+            compiler_params=params,
+        )(place, same_core, other_core, total[shard:])
+    return (grad_fields, grads[5].reshape(width)) + tuple(grads[:5])
 
 
 def solution(mesh):

time: 125 us -> 119 us (0.952)
  blocking collectives: 63.6 us -> 39.2 us
  waiting for transfers between devices: 16.4 us -> 31.3 us
  starting transfers between devices: 22 us -> 26.3 us
  local copies, waits for them, and re-layouts: 6.6 us -> 3.71 us
  Pallas kernels: 13.1 us -> 15.2 us
    ppermute x0 -> x11, waiting for transfers between devices: none -> 19.3 us  [the longest x7 16.2 us: meet(): lax.ppermute(values, axis, partner(axis, k))]
    all_gather x1 -> x0, blocking collectives: 16.3 us -> none  [local(): pieces = lax.all_gather(piece, 'mem', axis=0, tiled=True)]
    ppermute x0 -> x11, starting transfers between devices: none -> 14.3 us  [the longest x7 6.97 us: meet(): lax.ppermute(values, axis, partner(axis, k))]
    all_to_all x1 -> x0, waiting for transfers between devices: 12.4 us -> none  [local(): recv = lax.all_to_all(send, 'mem', 0, 0)]
    ppermute x2, waiting for transfers between devices: 1.25 us -> 10.9 us  [edges(): before = lax.ppermute(last, axis, ring(axis, 1))]
    all_to_all x1 -> x0, starting transfers between devices: 8.35 us -> none  [local(): recv = lax.all_to_all(send, 'mem', 0, 0)]
    ppermute x2, starting transfers between devices: 8.28 us -> 0.09 us  [edges(): before = lax.ppermute(last, axis, ring(axis, 1))]
    all_to_all x2 -> x1, blocking collectives: 29 us -> 21 us  [local(): recv = lax.all_to_all(send, 'mem', 0, 0)]
  transfers between devices with their start and end apart: 5 -> 15, of which waited for: 5 -> 12; matrix products, arithmetic and copies ran while one was open for 2% -> 2% of each run, Pallas kernels for 0% -> 0%
where the time goes in v2:
time: 119 us
  blocking collectives  39.2 us (33%)
  waiting for transfers between devices  31.3 us (26%)
  starting transfers between devices  26.3 us (22%)
  Pallas kernels  15.2 us (13%)
  local copies, waits for them, and re-layouts  3.71 us (3%)
  other arithmetic  2.3 us (2%)
    all_to_all x1, blocking collectives, local(): recv = lax.all_to_all(send, 'mem', 0, 0)  21 us
    all_to_all x1, blocking collectives, local(): landed = lax.all_to_all(back, 'mem', 0, 0)  18.1 us
    ppermute x7, waiting for transfers between devices, meet(): lax.ppermute(values, axis, partner(axis, k))  16.2 us
    ppermute x2, starting transfers between devices, edges(): after = lax.ppermute(first, axis, ring(axis, -1))  11.9 us
    ppermute x2, waiting for transfers between devices, edges(): before = lax.ppermute(last, axis, ring(axis, 1))  10.9 us
    pallas_call x1, Pallas kernels, local(): pl.pallas_call(functools.partial(main_kernel, rows, per), out_shape=jax.S...  8.04 us
    ppermute x7, starting transfers between devices, meet(): lax.ppermute(values, axis, partner(axis, k))  6.97 us
    ppermute x1, starting transfers between devices, local(): other_core = lax.ppermute(same_core, 'mem', partner('mem', 1))  3.97 us
  transfers between devices with their start and end apart: 15, of which 12 were waited for; matrix products, arithmetic and copies ran while one was open for 2% of the time, Pallas kernels for 0%

profile of v2, /device:TPU:1, one launch (start us, length us, event | category | flops | bytes accessed | tf_op | source)
XLA Modules:
  0.0 118.8 jit_solution(15580750515220355961)
XLA Ops:
  0.6 0.9 slice_bitcast_fusion
  1.5 5.3 %collective-permute-start.1 = (bf16[4,32,256]{2,1,0:T(8,128)(2,1)S(1)}, bf16[4,32,256]{2,1,0:T(8,128)(2,1)S(1)}, u32[]{:S(2)}, u32[]{:S(2)}) collective-permute-start(bf16[4,32,256]{2,1,0:T(8,128)(2,1)S(1)} %get-tuple-element.25), channel_id=1, source_target_pairs={{0,24},{8,0},{16,8},{24,16},{1,25},{9,1},{17,9},{25,17},{2,26},{10... | collective-permute-start | bytes 196616 | tf_op jit(solution)/shard_map/halo/ppermute | solution.py:289
  6.8 0.0 collective-permute-start
  6.8 0.9 fusion
  7.7 0.4 collective-permute-done.1
  8.1 0.0 copy-start.1
  8.1 3.5 %collective-permute-done = bf16[4,32,256]{2,1,0:T(8,128)(2,1)S(1)} collective-permute-done((bf16[4,32,256]{2,1,0:T(8,128)(2,1)S(1)}, bf16[4,32,256]{2,1,0:T(8,128)(2,1)S(1)}, u32[]{:S(2)}, u32[]{:S(2)}) %collective-permute-start) | collective-permute-done | bytes 65568 | tf_op jit(solution)/shard_map/halo/ppermute | solution.py:288
  11.7 0.0 copy-done.1
  11.7 0.0 copy-start.2
  11.8 0.5 copy-done.2
  12.3 6.7 %collective-permute-start.3 = (bf16[32,256]{1,0:T(8,128)(2,1)S(1)}, bf16[32,256]{1,0:T(8,128)(2,1)S(1)}, u32[]{:S(2)}, u32[]{:S(2)}) collective-permute-start(bf16[32,256]{1,0:T(8,128)(2,1)S(1)} %pad.8), channel_id=1, source_target_pairs={{0,7},{1,0},{2,1},{3,2},{4,3},{5,4},{6,5},{7,6},{8,15},{9,8},{10,9... | collective-permute-start | bytes 49160 | tf_op jit(solution)/shard_map/halo/ppermute | solution.py:289
  19.0 0.1 collective-permute-start.2
  19.1 0.7 collective-permute-done.3
  19.9 0.6 broadcast_select_fusion.2.right
  20.5 7.3 %collective-permute-done.2 = bf16[32,256]{1,0:T(8,128)(2,1)S(1)} collective-permute-done((bf16[32,256]{1,0:T(8,128)(2,1)S(1)}, bf16[32,256]{1,0:T(8,128)(2,1)S(1)}, u32[]{:S(2)}, u32[]{:S(2)}) %collective-permute-start.2) | collective-permute-done | bytes 16416 | tf_op jit(solution)/shard_map/halo/ppermute | solution.py:288
  27.8 0.6 broadcast_select_fusion.3.left
  28.4 2.9 %pack.1 = bf16[8,208,256]{2,1,0:T(8,128)(2,1)} custom-call(bf16[4,4,32,256]{3,2,1,0:T(8,128)(2,1)} %fields.1, bf16[4,4,32,256]{3,2,1,0:T(8,128)(2,1)} %cot.1, bf16[4,32,256]{2,1,0:T(8,128)(2,1)} %copy-done.2, bf16[4,32,256]{2,1,0:T(8,128)(2,1)} %copy-done.1, bf16[32,256]{1,0:T(8,128)(2,1)} %broadcast_select_fusion.3.left, ...), custom_call_target="tpu_custom_call" | custom-call | tf_op jit(solution)/shard_map/pack/pallas_call | solution.py:316
  31.3 21.0 %all_to_all.10.recv = bf16[8,208,256]{2,1,0:T(8,128)(2,1)} all-to-all(bf16[8,208,256]{2,1,0:T(8,128)(2,1)} %pack.1), channel_id=1, replica_groups=mesh['mem'=8,'row'=4,'col'=8] {'mem'}, dimensions={0} | all-to-all | bytes 1703936 | tf_op jit(solution)/shard_map/to_cells/all_to_all | solution.py:322
  52.4 8.0 %attention.1 = bf16[8,208,256]{2,1,0:T(8,128)(2,1)} custom-call(bf16[8,208,256]{2,1,0:T(8,128)(2,1)} %all_to_all.10.recv, f32[1,256]{1,0:T(1,128)} %bitcast.39, f32[3,3,256]{2,1,0:T(4,128)} %mix.1, bf16[256,256]{1,0:T(8,128)(2,1)} %wq.1, bf16[256,256]{1,0:T(8,128)(2,1)} %wk.1, bf16[256,256]{1,0:T(8,128)(2,1)} %wv.1, bf16[256,256]{1,0:T(8,128)(2,1)} %wo.1, ...), custom_call_target="tpu_custom_call" | custom-call | tf_op jit(solution)/shard_map/attention/pallas_call | solution.py:329
  60.4 18.1 %all_to_all.11.recv = bf16[8,208,256]{2,1,0:T(8,128)(2,1)} all-to-all(bf16[8,208,256]{2,1,0:T(8,128)(2,1)} %attention.1), channel_id=1, replica_groups=mesh['mem'=8,'row'=4,'col'=8] {'mem'}, dimensions={0} | all-to-all | bytes 1703936 | tf_op jit(solution)/shard_map/to_members/all_to_all | solution.py:353
  78.6 2.1 %unpack.1 = (bf16[4,4,32,256]{3,2,1,0:T(8,128)(2,1)}, bf16[144,256]{1,0:T(8,128)(2,1)}) custom-call(bf16[8,208,256]{2,1,0:T(8,128)(2,1)} %all_to_all.11.recv, bf16[128,128]{1,0:T(8,128)(2,1)} %constant.32.clone.split), custom_call_target="tpu_custom_call" | custom-call | tf_op jit(solution)/shard_map/unpack/pallas_call | solution.py:355
  80.7 0.7 collective-permute-start.6
  81.4 0.0 collective-permute-start.5
  81.4 2.9 %collective-permute-start.4 = (bf16[144,256]{1,0:T(8,128)(2,1)}, bf16[144,256]{1,0:T(8,128)(2,1)S(1)}, u32[]{:S(2)}, u32[]{:S(2)}) collective-permute-start(bf16[144,256]{1,0:T(8,128)(2,1)} %get-tuple-element.16), channel_id=1, source_target_pairs={{0,8},{8,0},{16,24},{24,16},{1,9},{9,1},{17,25},{25,17},{2,10},{10... | collective-permute-start | bytes 221192 | tf_op jit(solution)/shard_map/reduce/ppermute | solution.py:275
  84.2 1.8 %collective-permute-done.6 = bf16[144,256]{1,0:T(8,128)(2,1)S(1)} collective-permute-done((bf16[144,256]{1,0:T(8,128)(2,1)}, bf16[144,256]{1,0:T(8,128)(2,1)S(1)}, u32[]{:S(2)}, u32[]{:S(2)}) %collective-permute-start.6) | collective-permute-done | bytes 73760 | tf_op jit(solution)/shard_map/reduce/ppermute | solution.py:275
  86.1 3.5 %collective-permute-done.5 = bf16[144,256]{1,0:T(8,128)(2,1)S(1)} collective-permute-done((bf16[144,256]{1,0:T(8,128)(2,1)}, bf16[144,256]{1,0:T(8,128)(2,1)S(1)}, u32[]{:S(2)}, u32[]{:S(2)}) %collective-permute-start.5) | collective-permute-done | bytes 73760 | tf_op jit(solution)/shard_map/reduce/ppermute | solution.py:275
  89.6 0.0 collective-permute-done.4
  89.6 0.9 add_convert_fusion.2
  90.5 0.1 collective-permute-start.9
  90.6 0.3 collective-permute-start.8
  90.9 3.0 %collective-permute-start.7 = (bf16[144,256]{1,0:T(8,128)(2,1)S(1)}, bf16[144,256]{1,0:T(8,128)(2,1)S(1)}, u32[]{:S(2)}, u32[]{:S(2)}) collective-permute-start(bf16[144,256]{1,0:T(8,128)(2,1)S(1)} %add_convert_fusion.2), channel_id=1, source_target_pairs={{0,2},{1,3},{2,0},{3,1},{4,6},{5,7},{6,4},{7,5},{8,10},{9,11},{10,... | collective-permute-start | bytes 221192 | tf_op jit(solution)/shard_map/reduce/ppermute | solution.py:275
  93.9 2.3 %collective-permute-done.9 = bf16[144,256]{1,0:T(8,128)(2,1)S(1)} collective-permute-done((bf16[144,256]{1,0:T(8,128)(2,1)S(1)}, bf16[144,256]{1,0:T(8,128)(2,1)S(1)}, u32[]{:S(2)}, u32[]{:S(2)}) %collective-permute-start.9) | collective-permute-done | bytes 73760 | tf_op jit(solution)/shard_map/reduce/ppermute | solution.py:275
  96.2 0.0 collective-permute-done.8
  96.2 0.5 collective-permute-done.7
  96.8 0.1 collective-permute-start.10
  96.9 8.0 %collective-permute-done.10 = bf16[144,256]{1,0:T(8,128)(2,1)S(1)} collective-permute-done((bf16[144,256]{1,0:T(8,128)(2,1)S(1)}, bf16[144,256]{1,0:T(8,128)(2,1)S(1)}, u32[]{:S(2)}, u32[]{:S(2)}) %collective-permute-start.10) | collective-permute-done | bytes 73760 | tf_op jit(solution)/shard_map/reduce/ppermute | solution.py:275
  104.9 0.8 collective-permute-start.12
  105.7 0.8 collective-permute-start.11
  106.5 1.8 %collective-permute-start.13 = (bf16[128,256]{1,0:T(8,128)(2,1)S(1)}, bf16[128,256]{1,0:T(8,128)(2,1)S(1)}, u32[]{:S(2)}, u32[]{:S(2)}) collective-permute-start(bf16[128,256]{1,0:T(8,128)(2,1)S(1)} %get-tuple-element.28), channel_id=1, source_target_pairs={{0,192},{32,224},{64,128},{96,160},{128,64},{160,96},{192,0},{224,... | collective-permute-start | bytes 196616 | tf_op jit(solution)/shard_map/reduce/ppermute | solution.py:369
  108.3 1.4 %collective-permute-done.12 = bf16[128,256]{1,0:T(8,128)(2,1)S(1)} collective-permute-done((bf16[128,256]{1,0:T(8,128)(2,1)S(1)}, bf16[128,256]{1,0:T(8,128)(2,1)S(1)}, u32[]{:S(2)}, u32[]{:S(2)}) %collective-permute-start.12) | collective-permute-done | bytes 65568 | tf_op jit(solution)/shard_map/reduce/ppermute | solution.py:369
  109.6 0.0 collective-permute-done.11
  109.6 1.2 collective-permute-done.13
  110.8 0.0 copy-start
  110.9 4.0 %collective-permute-start.14 = (bf16[4,128,256]{2,1,0:T(8,128)(2,1)S(1)}, bf16[4,128,256]{2,1,0:T(8,128)(2,1)S(1)}, u32[]{:S(2)}, u32[]{:S(2)}) collective-permute-start(bf16[4,128,256]{2,1,0:T(8,128)(2,1)S(1)} %pad_maximum_fusion.same_core), channel_id=1, source_target_pairs={{0,32},{32,0},{64,96},{96,64},{128,160},{160,128},{192,224},{224,1... | collective-permute-start | bytes 786440 | tf_op jit(solution)/shard_map/reduce/ppermute | solution.py:371
  114.8 0.6 slice.45.extras
  115.4 0.6 collective-permute-done.14.other_core
  116.0 0.7 copy-done.3
  116.7 2.1 %finish.1 = (f32[256,256]{1,0:T(8,128)}, f32[256,256]{1,0:T(8,128)}, f32[256,256]{1,0:T(8,128)}, f32[256,256]{1,0:T(8,128)}, f32[3,3,256]{2,1,0:T(4,128)}, /*index=5*/f32[1,256]{1,0:T(1,128)}) custom-call(s32[1]{0:T(128)} %bitcast.9.place, bf16[4,128,256]{2,1,0:T(8,128)(2,1)} %copy-done, bf16[4,128,256]{2,1,0:T(8,128)(2,1)} %copy-done.3, ...), custom_call_target="tpu_custom_call" | custom-call | tf_op jit(solution)/shard_map/finish/pallas_call | solution.py:378
  (19 shorter events, 0.2 us)
Async XLA Ops:
  1.5 6.6 %collective-permute-start.1 = (bf16[4,32,256]{2,1,0:T(8,128)(2,1)S(1)}, bf16[4,32,256]{2,1,0:T(8,128)(2,1)S(1)}, u32[]{:S(2)}, u32[]{:S(2)}) collective-permute-start(bf16[4,32,256]{2,1,0:T(8,128)(2,1)S(1)} %get-tuple-element.25), channel_id=1, source_target_pairs={{0,24},{8,0},{16,8},{24,16},{1,25},{9,1},{17,9},{25,17},{2,26},{10... | collective-permute-start | bytes 196616 | tf_op jit(solution)/shard_map/halo/ppermute | solution.py:289
  6.8 4.9 %collective-permute-start = (bf16[4,32,256]{2,1,0:T(8,128)(2,1)S(1)}, bf16[4,32,256]{2,1,0:T(8,128)(2,1)S(1)}, u32[]{:S(2)}, u32[]{:S(2)}) collective-permute-start(bf16[4,32,256]{2,1,0:T(8,128)(2,1)S(1)} %get-tuple-element.26), channel_id=1, source_target_pairs={{0,8},{8,16},{16,24},{24,0},{1,9},{9,17},{17,25},{25,1},{2,10},{10... | collective-permute-start | bytes 196616 | tf_op jit(solution)/shard_map/halo/ppermute | solution.py:288
  8.1 3.6 %copy-start.1 = (bf16[4,32,256]{2,1,0:T(8,128)(2,1)}, bf16[4,32,256]{2,1,0:T(8,128)(2,1)S(1)}, u32[]{:S(2)}) copy-start(bf16[4,32,256]{2,1,0:T(8,128)(2,1)S(1)} %broadcast_select_fusion.after) | copy-start | bytes 196612
  11.7 0.6 copy-start.2
  12.3 7.5 %collective-permute-start.3 = (bf16[32,256]{1,0:T(8,128)(2,1)S(1)}, bf16[32,256]{1,0:T(8,128)(2,1)S(1)}, u32[]{:S(2)}, u32[]{:S(2)}) collective-permute-start(bf16[32,256]{1,0:T(8,128)(2,1)S(1)} %pad.8), channel_id=1, source_target_pairs={{0,7},{1,0},{2,1},{3,2},{4,3},{5,4},{6,5},{7,6},{8,15},{9,8},{10,9... | collective-permute-start | bytes 49160 | tf_op jit(solution)/shard_map/halo/ppermute | solution.py:289
  19.0 8.8 %collective-permute-start.2 = (bf16[32,256]{1,0:T(8,128)(2,1)S(1)}, bf16[32,256]{1,0:T(8,128)(2,1)S(1)}, u32[]{:S(2)}, u32[]{:S(2)}) collective-permute-start(bf16[32,256]{1,0:T(8,128)(2,1)S(1)} %pad.7), channel_id=1, source_target_pairs={{0,1},{1,2},{2,3},{3,4},{4,5},{5,6},{6,7},{7,0},{8,9},{9,10},{10,1... | collective-permute-start | bytes 49160 | tf_op jit(solution)/shard_map/halo/ppermute | solution.py:288
  80.7 5.4 %collective-permute-start.6 = (bf16[144,256]{1,0:T(8,128)(2,1)}, bf16[144,256]{1,0:T(8,128)(2,1)S(1)}, u32[]{:S(2)}, u32[]{:S(2)}) collective-permute-start(bf16[144,256]{1,0:T(8,128)(2,1)} %get-tuple-element.16), channel_id=1, source_target_pairs={{0,24},{8,16},{16,8},{24,0},{1,25},{9,17},{17,9},{25,1},{2,26},{10... | collective-permute-start | bytes 221192 | tf_op jit(solution)/shard_map/reduce/ppermute | solution.py:275
  81.4 8.2 %collective-permute-start.5 = (bf16[144,256]{1,0:T(8,128)(2,1)}, bf16[144,256]{1,0:T(8,128)(2,1)S(1)}, u32[]{:S(2)}, u32[]{:S(2)}) collective-permute-start(bf16[144,256]{1,0:T(8,128)(2,1)} %get-tuple-element.16), channel_id=1, source_target_pairs={{0,16},{8,24},{16,0},{24,8},{1,17},{9,25},{17,1},{25,9},{2,18},{10... | collective-permute-start | bytes 221192 | tf_op jit(solution)/shard_map/reduce/ppermute | solution.py:275
  81.4 8.2 %collective-permute-start.4 = (bf16[144,256]{1,0:T(8,128)(2,1)}, bf16[144,256]{1,0:T(8,128)(2,1)S(1)}, u32[]{:S(2)}, u32[]{:S(2)}) collective-permute-start(bf16[144,256]{1,0:T(8,128)(2,1)} %get-tuple-element.16), channel_id=1, source_target_pairs={{0,8},{8,0},{16,24},{24,16},{1,9},{9,1},{17,25},{25,17},{2,10},{10... | collective-permute-start | bytes 221192 | tf_op jit(solution)/shard_map/reduce/ppermute | solution.py:275
  90.5 5.7 %collective-permute-start.9 = (bf16[144,256]{1,0:T(8,128)(2,1)S(1)}, bf16[144,256]{1,0:T(8,128)(2,1)S(1)}, u32[]{:S(2)}, u32[]{:S(2)}) collective-permute-start(bf16[144,256]{1,0:T(8,128)(2,1)S(1)} %add_convert_fusion.2), channel_id=1, source_target_pairs={{0,6},{1,7},{2,4},{3,5},{4,2},{5,3},{6,0},{7,1},{8,14},{9,15},{10,... | collective-permute-start | bytes 221192 | tf_op jit(solution)/shard_map/reduce/ppermute | solution.py:275
  90.6 5.6 %collective-permute-start.8 = (bf16[144,256]{1,0:T(8,128)(2,1)S(1)}, bf16[144,256]{1,0:T(8,128)(2,1)S(1)}, u32[]{:S(2)}, u32[]{:S(2)}) collective-permute-start(bf16[144,256]{1,0:T(8,128)(2,1)S(1)} %add_convert_fusion.2), channel_id=1, source_target_pairs={{0,4},{1,5},{2,6},{3,7},{4,0},{5,1},{6,2},{7,3},{8,12},{9,13},{10,... | collective-permute-start | bytes 221192 | tf_op jit(solution)/shard_map/reduce/ppermute | solution.py:275
  90.9 5.8 %collective-permute-start.7 = (bf16[144,256]{1,0:T(8,128)(2,1)S(1)}, bf16[144,256]{1,0:T(8,128)(2,1)S(1)}, u32[]{:S(2)}, u32[]{:S(2)}) collective-permute-start(bf16[144,256]{1,0:T(8,128)(2,1)S(1)} %add_convert_fusion.2), channel_id=1, source_target_pairs={{0,2},{1,3},{2,0},{3,1},{4,6},{5,7},{6,4},{7,5},{8,10},{9,11},{10,... | collective-permute-start | bytes 221192 | tf_op jit(solution)/shard_map/reduce/ppermute | solution.py:275
  96.8 8.1 %collective-permute-start.10 = (bf16[144,256]{1,0:T(8,128)(2,1)S(1)}, bf16[144,256]{1,0:T(8,128)(2,1)S(1)}, u32[]{:S(2)}, u32[]{:S(2)}) collective-permute-start(bf16[144,256]{1,0:T(8,128)(2,1)S(1)} %add_convert_fusion.1), channel_id=1, source_target_pairs={{0,1},{1,0},{2,3},{3,2},{4,5},{5,4},{6,7},{7,6},{8,9},{9,8},{10,11... | collective-permute-start | bytes 221192 | tf_op jit(solution)/shard_map/reduce/ppermute | solution.py:275
  104.9 4.7 %collective-permute-start.12 = (bf16[128,256]{1,0:T(8,128)(2,1)S(1)}, bf16[128,256]{1,0:T(8,128)(2,1)S(1)}, u32[]{:S(2)}, u32[]{:S(2)}) collective-permute-start(bf16[128,256]{1,0:T(8,128)(2,1)S(1)} %get-tuple-element.28), channel_id=1, source_target_pairs={{0,128},{32,160},{64,192},{96,224},{128,0},{160,32},{192,64},{224,... | collective-permute-start | bytes 196616 | tf_op jit(solution)/shard_map/reduce/ppermute | solution.py:369
  105.7 3.9 %collective-permute-start.11 = (bf16[128,256]{1,0:T(8,128)(2,1)S(1)}, bf16[128,256]{1,0:T(8,128)(2,1)S(1)}, u32[]{:S(2)}, u32[]{:S(2)}) collective-permute-start(bf16[128,256]{1,0:T(8,128)(2,1)S(1)} %get-tuple-element.28), channel_id=1, source_target_pairs={{0,64},{32,96},{64,0},{96,32},{128,192},{160,224},{192,128},{224,1... | collective-permute-start | bytes 196616 | tf_op jit(solution)/shard_map/reduce/ppermute | solution.py:369
  106.5 4.3 %collective-permute-start.13 = (bf16[128,256]{1,0:T(8,128)(2,1)S(1)}, bf16[128,256]{1,0:T(8,128)(2,1)S(1)}, u32[]{:S(2)}, u32[]{:S(2)}) collective-permute-start(bf16[128,256]{1,0:T(8,128)(2,1)S(1)} %get-tuple-element.28), channel_id=1, source_target_pairs={{0,192},{32,224},{64,128},{96,160},{128,64},{160,96},{192,0},{224,... | collective-permute-start | bytes 196616 | tf_op jit(solution)/shard_map/reduce/ppermute | solution.py:369
  110.8 5.1 %copy-start = (bf16[4,128,256]{2,1,0:T(8,128)(2,1)}, bf16[4,128,256]{2,1,0:T(8,128)(2,1)S(1)}, u32[]{:S(2)}) copy-start(bf16[4,128,256]{2,1,0:T(8,128)(2,1)S(1)} %pad_maximum_fusion.same_core) | copy-start | bytes 786436
  110.9 5.1 %collective-permute-start.14 = (bf16[4,128,256]{2,1,0:T(8,128)(2,1)S(1)}, bf16[4,128,256]{2,1,0:T(8,128)(2,1)S(1)}, u32[]{:S(2)}, u32[]{:S(2)}) collective-permute-start(bf16[4,128,256]{2,1,0:T(8,128)(2,1)S(1)} %pad_maximum_fusion.same_core), channel_id=1, source_target_pairs={{0,32},{32,0},{64,96},{96,64},{128,160},{160,128},{192,224},{224,1... | collective-permute-start | bytes 786440 | tf_op jit(solution)/shard_map/reduce/ppermute | solution.py:371
  116.0 0.7 copy-start.3

commit v3 on v2

v3 whole, which is shorter than its diff:
```python
import functools
import math

import jax
import jax.numpy as jnp
import numpy as np
from jax import lax
from jax.experimental import pallas as pl
from jax.experimental.pallas import tpu as pltpu
from jax.sharding import PartitionSpec as P

HEADS = 8
EPS = 1e-06
BF = jnp.bfloat16
F32 = jnp.float32
NT = (((1,), (1,)), ((), ()))
TN = (((0,), (0,)), ((), ()))


def dot(a, b, dims=None):
    if dims is None:
        return jnp.dot(a, b, preferred_element_type=F32)
    return lax.dot_general(a, b, dims, preferred_element_type=F32)


def split_matrix(parts, members, cols):
    per = cols // parts
    out = np.zeros((parts, per, members, members, cols), np.float32)
    for j in range(parts):
        for c in range(per):
            for m in range(members):
                out[j, c, m, m, j * per + c] = 1
    return out.reshape(parts * per * members, members * cols)


def halo_matrices(parts, members, rows, cols, side):
    per = cols // parts
    mats = []
    for pair in range((rows + 2) // 2):
        out = np.zeros((parts, 2, per + 2, members, 2 * members * cols + 2 * side), np.float32)
        for j in range(parts):
            for q in range(2):
                for c in range(per + 2):
                    for m in range(members):
                        col = j * per + c - 1
                        edge = (2 * pair + q) * members + m
                        if col < 0:
                            src = 2 * members * cols + edge
                        elif col >= cols:
                            src = 2 * members * cols + side + edge
                        else:
                            src = (q * members + m) * cols + col
                        out[j, q, c, m, src] = 1
        mats.append(out.reshape(-1, out.shape[-1]))
    return np.stack(mats)


def gather_matrix(parts, cells, members):
    out = np.zeros((cells, parts, members, parts, cells, members), np.float32)
    for s in range(parts):
        for c in range(cells):
            for m in range(members):
                out[c, s, m, s, c, m] = 1
    return out.reshape(cells * parts * members, -1)


def pack_fields_kernel(fields, split, send):
    members, rows, cols, width = fields.shape
    parts = send.shape[0]
    per = cols // parts * members
    for r in range(rows):
        tokens = fields[:, r].reshape(members * cols, width)
        moved = dot(split[...], tokens).astype(BF).reshape(parts, per, width)
        send[:, r * per : (r + 1) * per, :] = moved


def pack_cot_kernel(inside, cot, before, after, left, right, halo, send):
    members, rows, cols, width = cot.shape
    parts = send.shape[0]
    per = cols // parts * members
    lines = [before[...]] + [cot[:, r] for r in range(rows)] + [after[...]]
    lines = [x.reshape(members * cols, width) for x in lines]
    sides = [jnp.where(inside[i] > 0, x[...], jnp.zeros_like(x[...])) for i, x in enumerate((left, right))]
    step = 2 * (per + 2 * members)
    for pair in range(halo.shape[0]):
        tokens = jnp.concatenate([lines[2 * pair], lines[2 * pair + 1]] + sides, axis=0)
        moved = dot(halo[pair], tokens).astype(BF).reshape(parts, step, width)
        send[:, pair * step : (pair + 1) * step, :] = moved


def regroup(recv, start, count, members, matrix):
    parts, _, width = recv.shape
    rows = count * members
    return dot(matrix[...], recv[:, start : start + rows, :].reshape(parts * rows, width))


def norm(x):
    inv = lax.rsqrt(jnp.mean(x * x, axis=-1, keepdims=True) + EPS)
    return inv, x * inv


def head_sums(v, headsum):
    hi = v.astype(BF)
    lo = (v - hi.astype(F32)).astype(BF)
    return dot(hi, headsum[...]) + dot(lo, headsum[...])


def expand_all(blocks, mats):
    cells, width, _ = mats.shape
    size = blocks.shape[0] // cells
    head_dim = width // HEADS
    row_head = lax.broadcasted_iota(jnp.int32, (width, width), 0) // head_dim
    col_head = lax.broadcasted_iota(jnp.int32, (width, width), 1) // head_dim
    same = row_head == col_head
    for c in range(cells):
        tiled = jnp.concatenate([blocks[c * size : (c + 1) * size]] * HEADS, axis=0)
        mats[c] = jnp.where(same, tiled, jnp.zeros_like(tiled))


def forward_kernel(
    members,
    recv,
    gain,
    wq,
    wk,
    wv,
    wo,
    gather8,
    headsum,
    x_out,
    q_out,
    k_out,
    v_out,
    prob_out,
    att_out,
    mixed_out,
    sums,
    mat_k,
    mat_v,
):
    parts, _, width = recv.shape
    scale = 1.0 / math.sqrt(width // HEADS)
    all_members = parts * members
    tokens = x_out.shape[0]
    cells = tokens // all_members
    x = jnp.concatenate([regroup(recv, g * 32, 8, members, gather8) for g in range(cells // 8)], axis=0)
    x_out[...] = x.astype(BF)
    _, normed = norm(x)
    inputs = (normed * gain[...]).astype(BF)
    queries = dot(inputs, wq[...]).astype(BF)
    keys = dot(inputs, wk[...]).astype(BF)
    values = dot(inputs, wv[...]).astype(BF)
    q_out[...] = queries
    k_out[...] = keys
    v_out[...] = values
    expand_all(keys, mat_k)
    expand_all(values, mat_v)
    for c in range(cells):
        rows = slice(c * all_members, (c + 1) * all_members)
        sums[rows, :] = dot(queries[rows], mat_k[c], NT)
    scores = sums[...] * scale
    lane = lax.broadcasted_iota(jnp.int32, (tokens, 128), 1)
    halves = []
    for h in range(width // 128):
        top = scores[:, h * 128 : (h + 1) * 128]
        step = 1
        while step < all_members:
            up = pltpu.roll(top, step, 1)
            down = pltpu.roll(top, 128 - step, 1)
            top = jnp.maximum(top, jnp.where((lane & step) != 0, up, down))
            step *= 2
        halves.append(top)
    lifted = jnp.exp(scores - jnp.concatenate(halves, axis=1))
    prob = lifted / head_sums(lifted, headsum)
    prob_out[...] = prob
    prob_b = prob.astype(BF)
    for c in range(cells):
        rows = slice(c * all_members, (c + 1) * all_members)
        att_out[rows, :] = dot(prob_b[rows], mat_v[c]).astype(BF)
    mixed_out[...] = dot(att_out[...], wo[...]).astype(BF)


def backward_kernel(
    tile_rows,
    tile_cols,
    members,
    recv,
    x_in,
    q_in,
    k_in,
    v_in,
    prob_in,
    att_in,
    mixed_in,
    gain,
    mix,
    wq,
    wk,
    wv,
    wo,
    gather8,
    gather4,
    headsum,
    send,
    padded,
    sums,
    mat_k,
    mat_v,
):
    parts, _, width = recv.shape
    head_dim = width // HEADS
    scale = 1.0 / math.sqrt(head_dim)
    cells = tile_rows * tile_cols
    all_members = parts * members
    tokens = cells * all_members
    pad_cols = tile_cols + 2
    pad_cells = (tile_rows + 2) * pad_cols
    done = 0
    while done < pad_cells:
        count = 8 if pad_cells - done >= 8 else 4
        block = regroup(recv, done * members, count, members, gather8 if count == 8 else gather4)
        padded[done : done + count] = block.reshape(count, all_members, width)
        done += count

    def shifted(i, j):
        picked = [
            padded[(r + 2 - i) * pad_cols + 2 - j : (r + 2 - i) * pad_cols + 2 - j + tile_cols]
            for r in range(tile_rows)
        ]
        return jnp.concatenate(picked, axis=0).reshape(tokens, width)

    expand_all(k_in[...], mat_k)
    expand_all(v_in[...], mat_v)
    inv, normed = norm(x_in[...].astype(F32))
    inputs = (normed * gain[...]).astype(BF)
    mixed = mixed_in[...].astype(F32)
    extra = []
    conv = jnp.zeros((tokens, width), F32)
    for i in range(3):
        for j in range(3):
            moved = shifted(i, j)
            conv = conv + mix[i, j : j + 1, :] * moved
            extra.append(jnp.sum(mixed * moved, axis=0, keepdims=True))
    grad_mixed = conv.astype(BF)
    grad_att = dot(grad_mixed, wo[...], NT).astype(BF)
    for c in range(cells):
        rows = slice(c * all_members, (c + 1) * all_members)
        sums[rows, :] = dot(grad_att[rows], mat_v[c], NT)

    prob = prob_in[...]
    prob_b = prob.astype(BF)
    grad_prob = sums[...]
    inner = head_sums(prob * grad_prob, headsum)
    grad_score = (prob * (grad_prob - inner) * scale).astype(BF)
    lane_head = lax.broadcasted_iota(jnp.int32, (all_members, width), 1) // head_dim

    def diagonal(full):
        out = jnp.zeros((all_members, width), F32)
        for h in range(HEADS):
            out = jnp.where(lane_head == h, full[h * all_members : (h + 1) * all_members], out)
        return out

    gq_l, gk_l, gv_l = [], [], []
    for c in range(cells):
        rows = slice(c * all_members, (c + 1) * all_members)
        gq_l.append(dot(grad_score[rows], mat_k[c]).astype(BF))
        gk_l.append(diagonal(dot(grad_score[rows], q_in[rows, :], TN)).astype(BF))
        gv_l.append(diagonal(dot(prob_b[rows], grad_att[rows], TN)).astype(BF))
    grad_q = jnp.concatenate(gq_l, axis=0)
    grad_k = jnp.concatenate(gk_l, axis=0)
    grad_v = jnp.concatenate(gv_l, axis=0)

    grad_in = dot(grad_q, wq[...], NT) + dot(grad_k, wk[...], NT) + dot(grad_v, wv[...], NT)
    extra.append(jnp.sum(grad_in * normed, axis=0, keepdims=True))
    grad_normed = grad_in * gain[...]
    mean = jnp.mean(grad_normed * normed, axis=-1, keepdims=True)
    grad = (shifted(1, 1) + inv * (grad_normed - normed * mean)).astype(BF)
    for g in range(cells // 8):
        back = dot(gather8[...], grad[g * 256 : (g + 1) * 256], TN).astype(BF)
        send[:, g * 32 : (g + 1) * 32, :] = back.reshape(parts, 32, width)

    weights = [
        dot(inputs, grad_q, TN),
        dot(inputs, grad_k, TN),
        dot(inputs, grad_v, TN),
        dot(att_in[...], grad_mixed, TN),
    ]
    base = cells * members
    shard = 4 * width // parts
    for j in range(parts):
        which, start = divmod(j * shard, width)
        send[j, base : base + shard, :] = weights[which][start : start + shard].astype(BF)
    extras = jnp.concatenate(extra + [jnp.zeros((16 - len(extra), width), F32)], axis=0).astype(BF)
    for j in range(parts):
        send[j, base + shard : base + shard + 16, :] = extras


def unpack_kernel(recv, split, out):
    members, rows, cols, width = out.shape
    parts = recv.shape[0]
    per = cols // parts * members
    for r in range(rows):
        tokens = recv[:, r * per : (r + 1) * per, :].reshape(parts * per, width)
        out[:, r] = dot(split[...], tokens, TN).astype(BF).reshape(members, cols, width)


def total_kernel(base, recv, total):
    acc = recv[0, base:, :].astype(F32)
    for j in range(1, recv.shape[0]):
        acc = acc + recv[j, base:, :].astype(F32)
    total[...] = acc.astype(BF)


def finish_kernel(scale, place, same_core, other_core, extras, g_q, g_k, g_v, g_o, g_mix, g_gain):
    count, shard, width = same_core.shape
    per = width // shard
    outs = (g_q, g_k, g_v, g_o)
    for p in range(2 * count):
        code = lax.bitwise_xor(place[0], p)
        spot = lax.shift_right_logical(code, 1)
        got = jnp.where(code == 2 * spot, same_core[spot], other_core[spot]).astype(F32)
        outs[p // per][p % per * shard : (p % per + 1) * shard, :] = got * scale
    rest = extras[...].astype(F32) * scale
    for i in range(3):
        g_mix[i] = rest[3 * i : 3 * i + 3]
    g_gain[...] = rest[9:10]


def partner(axis, code):
    return [(i, i ^ code) for i in range(lax.axis_size(axis))]


def meet(values, axis, codes):
    got = [values] + [lax.ppermute(values, axis, partner(axis, k)) for k in codes]
    got = [x.astype(F32) for x in got]
    while len(got) > 1:
        got = [a + b for a, b in zip(got[::2], got[1::2])]
    return lax.optimization_barrier(got[0].astype(BF))


def ring(axis, step):
    size = lax.axis_size(axis)
    return [(i, (i + step) % size) for i in range(size)]


def local(fields, norm_gain, w_query, w_key, w_value, w_out, mix_kernel, cotangent):
    members, rows, cols, width = fields.shape
    parts = lax.axis_size("mem")
    per = cols // parts
    cells = rows * per
    pad_cells = (rows + 2) * (per + 2)
    tokens = cells * members * parts
    base = cells * members
    shard = 4 * width // parts
    params = pltpu.CompilerParams(vmem_limit_bytes=60 * 1024 * 1024)
    split = jnp.asarray(split_matrix(parts, members, cols), BF)
    halo = jnp.asarray(halo_matrices(parts, members, rows, cols, 32), BF)
    gather8 = jnp.asarray(gather_matrix(parts, 8, members), BF)
    gather4 = jnp.asarray(gather_matrix(parts, 4, members), BF)
    headsum = jnp.asarray(np.kron(np.eye(HEADS), np.ones((width // HEADS, width // HEADS))), BF)
    gain = norm_gain.reshape(1, width)

    with jax.named_scope("halo"):
        row, col = lax.axis_index("row"), lax.axis_index("col")
        before = lax.ppermute(cotangent[:, rows - 1], "row", ring("row", 1))
        after = lax.ppermute(cotangent[:, 0], "row", ring("row", -1))
        zero = jnp.zeros_like(before)
        before = jnp.where(row > 0, before, zero)
        after = jnp.where(row < lax.axis_size("row") - 1, after, zero)

    with jax.named_scope("pack_fields"):
        send_f = pl.pallas_call(
            pack_fields_kernel,
            out_shape=jax.ShapeDtypeStruct((parts, base, width), BF),
            compiler_params=params,
        )(fields, split)
    with jax.named_scope("fields_to_cells"):
        recv_f = lax.all_to_all(send_f, "mem", 0, 0)

    with jax.named_scope("halo_cols"):

        def column(c):
            pieces = [before[None, :, c], jnp.swapaxes(cotangent[:, :, c], 0, 1), after[None, :, c]]
            flat = jnp.concatenate(pieces, axis=0).reshape((rows + 2) * members, width)
            return jnp.pad(flat, ((0, 32 - flat.shape[0]), (0, 0)))

        left = lax.ppermute(column(cols - 1), "col", ring("col", 1))
        right = lax.ppermute(column(0), "col", ring("col", -1))
        inside = jnp.stack([col > 0, col < lax.axis_size("col") - 1]).astype(jnp.int32)

    with jax.named_scope("forward"):
        token = jax.ShapeDtypeStruct((tokens, width), BF)
        token_f = jax.ShapeDtypeStruct((tokens, width), F32)
        mats = [pltpu.VMEM((cells, width, width), BF), pltpu.VMEM((cells, width, width), BF)]
        kept = pl.pallas_call(
            functools.partial(forward_kernel, members),
            out_shape=(token, token, token, token, token_f, token, token),
            scratch_shapes=[pltpu.VMEM((tokens, width), F32)] + mats,
            compiler_params=params,
        )(recv_f, gain, w_query, w_key, w_value, w_out, gather8, headsum)

    with jax.named_scope("pack_cot"):
        smem = pl.BlockSpec(memory_space=pltpu.SMEM)
        vmem = pl.BlockSpec(memory_space=pltpu.VMEM)
        send_c = pl.pallas_call(
            pack_cot_kernel,
            in_specs=[smem] + [vmem] * 6,
            out_shape=jax.ShapeDtypeStruct((parts, pad_cells * members, width), BF),
            compiler_params=params,
        )(inside, cotangent, before, after, left, right, halo)
    with jax.named_scope("cot_to_cells"):
        recv_c = lax.all_to_all(send_c, "mem", 0, 0)

    with jax.named_scope("backward"):
        back = pl.pallas_call(
            functools.partial(backward_kernel, rows, per, members),
            out_shape=jax.ShapeDtypeStruct((parts, base + shard + 16, width), BF),
            scratch_shapes=[
                pltpu.VMEM((pad_cells, members * parts, width), F32),
                pltpu.VMEM((tokens, width), F32),
            ]
            + mats,
            compiler_params=params,
        )(recv_c, *kept, gain, mix_kernel, w_query, w_key, w_value, w_out, gather8, gather4, headsum)
    with jax.named_scope("to_members"):
        landed = lax.all_to_all(back, "mem", 0, 0)
    with jax.named_scope("unpack"):
        total = pl.pallas_call(
            functools.partial(total_kernel, base),
            out_shape=jax.ShapeDtypeStruct((shard + 16, width), BF),
            compiler_params=params,
        )(landed)
        grad_fields = pl.pallas_call(
            unpack_kernel,
            out_shape=jax.ShapeDtypeStruct(fields.shape, BF),
            compiler_params=params,
        )(landed, split)

    with jax.named_scope("reduce"):
        total = meet(total, "row", (1, 2, 3))
        total = meet(total, "col", (2, 4, 6))
        total = meet(total, "col", (1,))
        piece = total[:shard]
        same_core = jnp.stack([piece] + [lax.ppermute(piece, "mem", partner("mem", k)) for k in (2, 4, 6)])
        same_core = lax.optimization_barrier(same_core)
        other_core = lax.ppermute(same_core, "mem", partner("mem", 1))

    grid = lax.axis_size("row") * lax.axis_size("col")
    scale_all = 1.0 / math.sqrt(tokens * grid * parts)
    with jax.named_scope("finish"):
        square = jax.ShapeDtypeStruct((width, width), F32)
        place = lax.axis_index("mem").astype(jnp.int32).reshape(1)
        grads = pl.pallas_call(
            functools.partial(finish_kernel, scale_all),
            in_specs=[pl.BlockSpec(memory_space=pltpu.SMEM)] + [pl.BlockSpec(memory_space=pltpu.VMEM)] * 3,
            out_shape=(square,) * 4 + (jax.ShapeDtypeStruct((3, 3, width), F32), jax.ShapeDtypeStruct((1, width), F32)),
            compiler_params=params,
        )(place, same_core, other_core, total[shard:])
    return (grad_fields, grads[5].reshape(width)) + tuple(grads[:5])


def solution(mesh):
    tile = P("mem", "row", "col", None)
    in_specs = (tile, P(), P(), P(), P(), P(), P(), tile)
    out_specs = (tile, P(), P(), P(), P(), P(), P())
    return jax.shard_map(local, mesh=mesh, in_specs=in_specs, out_specs=out_specs, check_vma=False)
```

time: 119 us -> 121 us (1.017)
  blocking collectives: 39.2 us -> 18.3 us
  starting transfers between devices: 26.3 us -> 38.9 us
  Pallas kernels: 15.2 us -> 22.6 us
  local copies, waits for them, and re-layouts: 3.71 us -> 6.45 us
    all_to_all x1 -> x0, blocking collectives: 21 us -> none  [local(): recv = lax.all_to_all(send, 'mem', 0, 0)]
    all_to_all x0 -> x2, starting transfers between devices: none -> 11.4 us  [the longest x1 6.2 us: local(): recv_c = lax.all_to_all(send_c, 'mem', 0, 0)]
    pallas_call x3 -> x6, Pallas kernels: 13.1 us -> 20.5 us  [the longest x1 7.09 us: local(): pl.pallas_call(functools.partial(backward_kernel, rows, per, members), ou...]
    all_to_all x0 -> x2, waiting for transfers between devices: none -> 5.21 us  [the longest x1 5.21 us: local(): recv_c = lax.all_to_all(send_c, 'mem', 0, 0)]
    ppermute x4, waiting for transfers between devices: 12 us -> 8.03 us  [the longest x1 7.77 us: local(): left = lax.ppermute(column(cols - 1), 'col', ring('col', 1))]
    unnamed x10 -> x18, local copies, waits for them, and re-layouts: 1.25 us -> 3.99 us
    select_n x4 -> x2, other arithmetic: 1.24 us -> 0.02 us  [the longest x1 0.01 us: local(): after = jnp.where(row < lax.axis_size('row') - 1, after, zero)]
  transfers between devices with their start and end apart: 15 -> 17, of which waited for: 12 -> 9; matrix products, arithmetic and copies ran while one was open for 2% -> 2% of each run, Pallas kernels for 0% -> 10%
where the time goes in v3:
time: 121 us
  starting transfers between devices  38.9 us (32%)
  waiting for transfers between devices  31.8 us (26%)
  Pallas kernels  22.6 us (19%)
  blocking collectives  18.3 us (15%)
  local copies, waits for them, and re-layouts  6.45 us (5%)
  other arithmetic  1.69 us (1%)
    all_to_all x1, blocking collectives, local(): landed = lax.all_to_all(back, 'mem', 0, 0)  18.3 us
    ppermute x7, waiting for transfers between devices, meet(): lax.ppermute(values, axis, partner(axis, k))  16.1 us
    ppermute x1, waiting for transfers between devices, local(): left = lax.ppermute(column(cols - 1), 'col', ring('col', 1))  7.77 us
    ppermute x7, starting transfers between devices, meet(): lax.ppermute(values, axis, partner(axis, k))  7.16 us
    pallas_call x1, Pallas kernels, local(): pl.pallas_call(functools.partial(backward_kernel, rows, per, members), ou...  7.09 us
    ppermute x1, starting transfers between devices, local(): right = lax.ppermute(column(0), 'col', ring('col', -1))  6.83 us
    all_to_all x1, starting transfers between devices, local(): recv_c = lax.all_to_all(send_c, 'mem', 0, 0)  6.2 us
    all_to_all x1, starting transfers between devices, local(): recv_f = lax.all_to_all(send_f, 'mem', 0, 0)  5.25 us
  transfers between devices with their start and end apart: 17, of which 9 were waited for; matrix products, arithmetic and copies ran while one was open for 2% of the time, Pallas kernels for 10%

profile of v3, /device:TPU:1, one launch (start us, length us, event | category | flops | bytes accessed | tf_op | source)
XLA Modules:
  0.0 120.6 jit_solution(6983264535596589301)
XLA Ops:
  0.6 0.9 slice_bitcast_fusion
  1.5 5.3 %collective-permute-start.1 = (bf16[4,32,256]{2,1,0:T(8,128)(2,1)S(1)}, bf16[4,32,256]{2,1,0:T(8,128)(2,1)S(1)}, u32[]{:S(2)}, u32[]{:S(2)}) collective-permute-start(bf16[4,32,256]{2,1,0:T(8,128)(2,1)S(1)} %get-tuple-element.35), channel_id=1, source_target_pairs={{0,24},{8,0},{16,8},{24,16},{1,25},{9,1},{17,9},{25,17},{2,26},{10... | collective-permute-start | bytes 196616 | tf_op jit(solution)/shard_map/halo/ppermute | solution.py:366
  6.8 0.0 collective-permute-start
  6.8 1.9 %pack_fields.1 = bf16[8,64,256]{2,1,0:T(8,128)(2,1)} custom-call(bf16[4,4,32,256]{3,2,1,0:T(8,128)(2,1)} %fields.1, bf16[128,128]{1,0:T(8,128)(2,1)} %constant.31.clone.split), custom_call_target="tpu_custom_call" | custom-call | tf_op jit(solution)/shard_map/pack_fields/pallas_call | solution.py:372
  8.6 5.3 %all-to-all-start.1 = ((bf16[8,64,256]{2,1,0:T(8,128)(2,1)}), bf16[8,64,256]{2,1,0:T(8,128)(2,1)S(1)}, u32[]{:S(2)}, u32[]{:S(2)}) async-start(bf16[8,64,256]{2,1,0:T(8,128)(2,1)} %pack_fields.1), calls=%async_computation.1 | async-start | bytes 524288 | tf_op jit(solution)/shard_map/fields_to_cells/all_to_all | solution.py:378
  13.9 0.9 fusion
  14.8 0.0 collective-permute-done.1
  14.9 0.0 copy-start.3
  14.9 0.0 collective-permute-done
  14.9 0.6 copy-done.3
  15.6 0.5 copy-done.4
  16.2 6.8 %collective-permute-start.3 = (bf16[32,256]{1,0:T(8,128)(2,1)S(1)}, bf16[32,256]{1,0:T(8,128)(2,1)S(1)}, u32[]{:S(2)}, u32[]{:S(2)}) collective-permute-start(bf16[32,256]{1,0:T(8,128)(2,1)S(1)} %pad.8), channel_id=1, source_target_pairs={{0,7},{1,0},{2,1},{3,2},{4,3},{5,4},{6,5},{7,6},{8,15},{9,8},{10,9... | collective-permute-start | bytes 49160 | tf_op jit(solution)/shard_map/halo_cols/ppermute | solution.py:388
  23.0 0.6 add_convert_fusion.3.inside
  23.6 0.3 collective-permute-done.3.right
  23.9 7.8 %collective-permute-done.2.left = bf16[32,256]{1,0:T(8,128)(2,1)S(1)} collective-permute-done((bf16[32,256]{1,0:T(8,128)(2,1)S(1)}, bf16[32,256]{1,0:T(8,128)(2,1)S(1)}, u32[]{:S(2)}, u32[]{:S(2)}) %collective-permute-start.2) | collective-permute-done | bytes 16416 | tf_op jit(solution)/shard_map/halo_cols/ppermute | solution.py:387
  31.7 0.6 copy-done.7
  32.3 2.6 %pack_cot.1 = bf16[8,144,256]{2,1,0:T(8,128)(2,1)} custom-call(s32[2]{0:T(128)} %add_convert_fusion.3.inside, bf16[4,4,32,256]{3,2,1,0:T(8,128)(2,1)} %cot.1, bf16[4,32,256]{2,1,0:T(8,128)(2,1)} %copy-done.4, bf16[4,32,256]{2,1,0:T(8,128)(2,1)} %copy-done.3, bf16[32,256]{1,0:T(8,128)(2,1)} %copy-done.7, bf16[32,256]{1,0:T(8,128)(2,1)} %copy-done.6, ...), custom_call_target="tpu_custom_call" | custom-call | tf_op jit(solution)/shard_map/pack_cot/pallas_call | solution.py:405
  34.9 0.0 all-to-all-done.1.recv
  34.9 0.7 copy-done.1
  35.6 6.2 %all-to-all-start = ((bf16[8,144,256]{2,1,0:T(8,128)(2,1)}), bf16[8,144,256]{2,1,0:T(8,128)(2,1)S(1)}, u32[]{:S(2)}, u32[]{:S(2)}) async-start(bf16[8,144,256]{2,1,0:T(8,128)(2,1)} %pack_cot.1), calls=%async_computation | async-start | bytes 1179648 | tf_op jit(solution)/shard_map/cot_to_cells/all_to_all | solution.py:412
  41.8 5.0 %forward.1 = (bf16[512,256]{1,0:T(8,128)(2,1)}, bf16[512,256]{1,0:T(8,128)(2,1)}, bf16[512,256]{1,0:T(8,128)(2,1)}, bf16[512,256]{1,0:T(8,128)(2,1)}, f32[512,25...) custom-call(bf16[8,64,256]{2,1,0:T(8,128)(2,1)} %copy-done.1, f32[1,256]{1,0:T(1,128)} %bitcast.41, ...), custom_call_target="tpu_custom_call" | custom-call | tf_op jit(solution)/shard_map/forward/pallas_call | solution.py:395
  46.8 5.2 %all-to-all-done.recv = bf16[8,144,256]{2,1,0:T(8,128)(2,1)S(1)} async-done(((bf16[8,144,256]{2,1,0:T(8,128)(2,1)}), bf16[8,144,256]{2,1,0:T(8,128)(2,1)S(1)}, u32[]{:S(2)}, u32[]{:S(2)}) %all-to-all-start) | async-done | bytes 589856 | tf_op jit(solution)/shard_map/cot_to_cells/all_to_all | solution.py:412
  52.0 0.8 copy-done
  52.8 7.1 %backward.1 = bf16[8,208,256]{2,1,0:T(8,128)(2,1)} custom-call(bf16[8,144,256]{2,1,0:T(8,128)(2,1)} %copy-done, bf16[512,256]{1,0:T(8,128)(2,1)} %get-tuple-element.20.x_in, bf16[512,256]{1,0:T(8,128)(2,1)} %get-tuple-element.21.q_in, bf16[512,256]{1,0:T(8,128)(2,1)} %get-tuple-element.22.k_in, bf16[512,256]{1,0:T(8,128)(2,1)} %get-tuple-element.23.v_in, ...), custom_call_target="tpu_custom_call" | custom-call | tf_op jit(solution)/shard_map/backward/pallas_call | solution.py:415
  59.9 18.3 %all_to_all.15.recv = bf16[8,208,256]{2,1,0:T(8,128)(2,1)} all-to-all(bf16[8,208,256]{2,1,0:T(8,128)(2,1)} %backward.1), channel_id=1, replica_groups=mesh['mem'=8,'row'=4,'col'=8] {'mem'}, dimensions={0} | all-to-all | bytes 1703936 | tf_op jit(solution)/shard_map/to_members/all_to_all | solution.py:426
  78.2 1.9 %unpack.3 = bf16[144,256]{1,0:T(8,128)(2,1)} custom-call(bf16[8,208,256]{2,1,0:T(8,128)(2,1)} %all_to_all.15.recv), custom_call_target="tpu_custom_call" | custom-call | tf_op jit(solution)/shard_map/unpack/pallas_call | solution.py:428
  80.1 3.5 %collective-permute-start.6 = (bf16[144,256]{1,0:T(8,128)(2,1)}, bf16[144,256]{1,0:T(8,128)(2,1)S(1)}, u32[]{:S(2)}, u32[]{:S(2)}) collective-permute-start(bf16[144,256]{1,0:T(8,128)(2,1)} %unpack.3), channel_id=1, source_target_pairs={{0,24},{8,16},{16,8},{24,0},{1,25},{9,17},{17,9},{25,1},{2,26},{10... | collective-permute-start | bytes 221192 | tf_op jit(solution)/shard_map/reduce/ppermute | solution.py:334
  83.5 0.3 collective-permute-start.4
  83.8 1.8 %collective-permute-done.6 = bf16[144,256]{1,0:T(8,128)(2,1)S(1)} collective-permute-done((bf16[144,256]{1,0:T(8,128)(2,1)}, bf16[144,256]{1,0:T(8,128)(2,1)S(1)}, u32[]{:S(2)}, u32[]{:S(2)}) %collective-permute-start.6) | collective-permute-done | bytes 73760 | tf_op jit(solution)/shard_map/reduce/ppermute | solution.py:334
  85.6 4.3 %collective-permute-done.5 = bf16[144,256]{1,0:T(8,128)(2,1)S(1)} collective-permute-done((bf16[144,256]{1,0:T(8,128)(2,1)}, bf16[144,256]{1,0:T(8,128)(2,1)S(1)}, u32[]{:S(2)}, u32[]{:S(2)}) %collective-permute-start.5) | collective-permute-done | bytes 73760 | tf_op jit(solution)/shard_map/reduce/ppermute | solution.py:334
  89.9 0.9 add_convert_fusion.2
  90.8 0.1 collective-permute-start.9
  90.9 0.1 collective-permute-start.8
  91.0 3.1 %collective-permute-start.7 = (bf16[144,256]{1,0:T(8,128)(2,1)S(1)}, bf16[144,256]{1,0:T(8,128)(2,1)S(1)}, u32[]{:S(2)}, u32[]{:S(2)}) collective-permute-start(bf16[144,256]{1,0:T(8,128)(2,1)S(1)} %add_convert_fusion.2), channel_id=1, source_target_pairs={{0,2},{1,3},{2,0},{3,1},{4,6},{5,7},{6,4},{7,5},{8,10},{9,11},{10,... | collective-permute-start | bytes 221192 | tf_op jit(solution)/shard_map/reduce/ppermute | solution.py:334
  94.2 2.8 %collective-permute-done.9 = bf16[144,256]{1,0:T(8,128)(2,1)S(1)} collective-permute-done((bf16[144,256]{1,0:T(8,128)(2,1)S(1)}, bf16[144,256]{1,0:T(8,128)(2,1)S(1)}, u32[]{:S(2)}, u32[]{:S(2)}) %collective-permute-start.9) | collective-permute-done | bytes 73760 | tf_op jit(solution)/shard_map/reduce/ppermute | solution.py:334
  97.0 0.0 collective-permute-done.7
  97.1 0.1 collective-permute-start.10
  97.2 7.1 %collective-permute-done.10 = bf16[144,256]{1,0:T(8,128)(2,1)S(1)} collective-permute-done((bf16[144,256]{1,0:T(8,128)(2,1)S(1)}, bf16[144,256]{1,0:T(8,128)(2,1)S(1)}, u32[]{:S(2)}, u32[]{:S(2)}) %collective-permute-start.10) | collective-permute-done | bytes 73760 | tf_op jit(solution)/shard_map/reduce/ppermute | solution.py:334
  104.3 0.7 collective-permute-start.12
  105.0 0.8 collective-permute-start.11
  105.9 1.8 %collective-permute-start.13 = (bf16[128,256]{1,0:T(8,128)(2,1)S(1)}, bf16[128,256]{1,0:T(8,128)(2,1)S(1)}, u32[]{:S(2)}, u32[]{:S(2)}) collective-permute-start(bf16[128,256]{1,0:T(8,128)(2,1)S(1)} %get-tuple-element.38), channel_id=1, source_target_pairs={{0,192},{32,224},{64,128},{96,160},{128,64},{160,96},{192,0},{224,... | collective-permute-start | bytes 196616 | tf_op jit(solution)/shard_map/reduce/ppermute | solution.py:444
  107.7 1.4 %collective-permute-done.12 = bf16[128,256]{1,0:T(8,128)(2,1)S(1)} collective-permute-done((bf16[128,256]{1,0:T(8,128)(2,1)S(1)}, bf16[128,256]{1,0:T(8,128)(2,1)S(1)}, u32[]{:S(2)}, u32[]{:S(2)}) %collective-permute-start.12) | collective-permute-done | bytes 65568 | tf_op jit(solution)/shard_map/reduce/ppermute | solution.py:444
  109.0 1.2 collective-permute-done.13
  110.2 4.9 %collective-permute-start.14 = (bf16[4,128,256]{2,1,0:T(8,128)(2,1)S(1)}, bf16[4,128,256]{2,1,0:T(8,128)(2,1)S(1)}, u32[]{:S(2)}, u32[]{:S(2)}) collective-permute-start(bf16[4,128,256]{2,1,0:T(8,128)(2,1)S(1)} %pad_maximum_fusion.same_core), channel_id=1, source_target_pairs={{0,32},{32,0},{64,96},{96,64},{128,160},{160,128},{192,224},{224,1... | collective-permute-start | bytes 786440 | tf_op jit(solution)/shard_map/reduce/ppermute | solution.py:446
  115.1 2.1 %unpack.2 = bf16[4,4,32,256]{3,2,1,0:T(8,128)(2,1)} custom-call(bf16[8,208,256]{2,1,0:T(8,128)(2,1)} %all_to_all.15.recv, bf16[128,128]{1,0:T(8,128)(2,1)} %constant.31.clone.split), custom_call_target="tpu_custom_call" | custom-call | tf_op jit(solution)/shard_map/unpack/pallas_call | solution.py:433
  117.3 0.6 slice.45.extras
  117.9 0.7 copy-done.5
  118.6 2.1 %finish.1 = (f32[256,256]{1,0:T(8,128)}, f32[256,256]{1,0:T(8,128)}, f32[256,256]{1,0:T(8,128)}, f32[256,256]{1,0:T(8,128)}, f32[3,3,256]{2,1,0:T(4,128)}, /*index=5*/f32[1,256]{1,0:T(1,128)}) custom-call(s32[1]{0:T(128)} %bitcast.11.place, bf16[4,128,256]{2,1,0:T(8,128)(2,1)} %copy-done.2, bf16[4,128,256]{2,1,0:T(8,128)(2,1)} %copy-done.5, ...), custom_call_target="tpu_custom_call" | custom-call | tf_op jit(solution)/shard_map/finish/pallas_call | solution.py:453
  (32 shorter events, 0.3 us)
Async XLA Ops:
  1.5 13.3 %collective-permute-start.1 = (bf16[4,32,256]{2,1,0:T(8,128)(2,1)S(1)}, bf16[4,32,256]{2,1,0:T(8,128)(2,1)S(1)}, u32[]{:S(2)}, u32[]{:S(2)}) collective-permute-start(bf16[4,32,256]{2,1,0:T(8,128)(2,1)S(1)} %get-tuple-element.35), channel_id=1, source_target_pairs={{0,24},{8,0},{16,8},{24,16},{1,25},{9,1},{17,9},{25,17},{2,26},{10... | collective-permute-start | bytes 196616 | tf_op jit(solution)/shard_map/halo/ppermute | solution.py:366
  6.8 8.1 %collective-permute-start = (bf16[4,32,256]{2,1,0:T(8,128)(2,1)S(1)}, bf16[4,32,256]{2,1,0:T(8,128)(2,1)S(1)}, u32[]{:S(2)}, u32[]{:S(2)}) collective-permute-start(bf16[4,32,256]{2,1,0:T(8,128)(2,1)S(1)} %get-tuple-element.36), channel_id=1, source_target_pairs={{0,8},{8,16},{16,24},{24,0},{1,9},{9,17},{17,25},{25,1},{2,10},{10... | collective-permute-start | bytes 196616 | tf_op jit(solution)/shard_map/halo/ppermute | solution.py:365
  8.6 26.3 %all-to-all-start.1 = ((bf16[8,64,256]{2,1,0:T(8,128)(2,1)}), bf16[8,64,256]{2,1,0:T(8,128)(2,1)S(1)}, u32[]{:S(2)}, u32[]{:S(2)}) async-start(bf16[8,64,256]{2,1,0:T(8,128)(2,1)} %pack_fields.1), calls=%async_computation.1 | async-start | bytes 524288 | tf_op jit(solution)/shard_map/fields_to_cells/all_to_all | solution.py:378
  14.9 0.6 copy-start.3
  15.5 0.6 copy-start.4
  16.2 7.7 %collective-permute-start.3 = (bf16[32,256]{1,0:T(8,128)(2,1)S(1)}, bf16[32,256]{1,0:T(8,128)(2,1)S(1)}, u32[]{:S(2)}, u32[]{:S(2)}) collective-permute-start(bf16[32,256]{1,0:T(8,128)(2,1)S(1)} %pad.8), channel_id=1, source_target_pairs={{0,7},{1,0},{2,1},{3,2},{4,3},{5,4},{6,5},{7,6},{8,15},{9,8},{10,9... | collective-permute-start | bytes 49160 | tf_op jit(solution)/shard_map/halo_cols/ppermute | solution.py:388
  23.0 8.6 %collective-permute-start.2 = (bf16[32,256]{1,0:T(8,128)(2,1)S(1)}, bf16[32,256]{1,0:T(8,128)(2,1)S(1)}, u32[]{:S(2)}, u32[]{:S(2)}) collective-permute-start(bf16[32,256]{1,0:T(8,128)(2,1)S(1)} %pad.7), channel_id=1, source_target_pairs={{0,1},{1,2},{2,3},{3,4},{4,5},{5,6},{6,7},{7,0},{8,9},{9,10},{10,1... | collective-permute-start | bytes 49160 | tf_op jit(solution)/shard_map/halo_cols/ppermute | solution.py:387
  23.9 7.8 %copy-start.6 = (bf16[32,256]{1,0:T(8,128)(2,1)}, bf16[32,256]{1,0:T(8,128)(2,1)S(1)}, u32[]{:S(2)}) copy-start(bf16[32,256]{1,0:T(8,128)(2,1)S(1)} %collective-permute-done.3.right) | copy-start | bytes 49156
  31.6 0.6 copy-start.7
  34.9 0.7 copy-start.1
  35.6 16.4 %all-to-all-start = ((bf16[8,144,256]{2,1,0:T(8,128)(2,1)}), bf16[8,144,256]{2,1,0:T(8,128)(2,1)S(1)}, u32[]{:S(2)}, u32[]{:S(2)}) async-start(bf16[8,144,256]{2,1,0:T(8,128)(2,1)} %pack_cot.1), calls=%async_computation | async-start | bytes 1179648 | tf_op jit(solution)/shard_map/cot_to_cells/all_to_all | solution.py:412
  52.0 0.8 copy-start
  80.1 5.5 %collective-permute-start.6 = (bf16[144,256]{1,0:T(8,128)(2,1)}, bf16[144,256]{1,0:T(8,128)(2,1)S(1)}, u32[]{:S(2)}, u32[]{:S(2)}) collective-permute-start(bf16[144,256]{1,0:T(8,128)(2,1)} %unpack.3), channel_id=1, source_target_pairs={{0,24},{8,16},{16,8},{24,0},{1,25},{9,17},{17,9},{25,1},{2,26},{10... | collective-permute-start | bytes 221192 | tf_op jit(solution)/shard_map/reduce/ppermute | solution.py:334
  83.5 6.4 %collective-permute-start.5 = (bf16[144,256]{1,0:T(8,128)(2,1)}, bf16[144,256]{1,0:T(8,128)(2,1)S(1)}, u32[]{:S(2)}, u32[]{:S(2)}) collective-permute-start(bf16[144,256]{1,0:T(8,128)(2,1)} %unpack.3), channel_id=1, source_target_pairs={{0,16},{8,24},{16,0},{24,8},{1,17},{9,25},{17,1},{25,9},{2,18},{10... | collective-permute-start | bytes 221192 | tf_op jit(solution)/shard_map/reduce/ppermute | solution.py:334
  83.5 6.4 %collective-permute-start.4 = (bf16[144,256]{1,0:T(8,128)(2,1)}, bf16[144,256]{1,0:T(8,128)(2,1)S(1)}, u32[]{:S(2)}, u32[]{:S(2)}) collective-permute-start(bf16[144,256]{1,0:T(8,128)(2,1)} %unpack.3), channel_id=1, source_target_pairs={{0,8},{8,0},{16,24},{24,16},{1,9},{9,1},{17,25},{25,17},{2,10},{10... | collective-permute-start | bytes 221192 | tf_op jit(solution)/shard_map/reduce/ppermute | solution.py:334
  90.8 6.2 %collective-permute-start.9 = (bf16[144,256]{1,0:T(8,128)(2,1)S(1)}, bf16[144,256]{1,0:T(8,128)(2,1)S(1)}, u32[]{:S(2)}, u32[]{:S(2)}) collective-permute-start(bf16[144,256]{1,0:T(8,128)(2,1)S(1)} %add_convert_fusion.2), channel_id=1, source_target_pairs={{0,6},{1,7},{2,4},{3,5},{4,2},{5,3},{6,0},{7,1},{8,14},{9,15},{10,... | collective-permute-start | bytes 221192 | tf_op jit(solution)/shard_map/reduce/ppermute | solution.py:334
  90.9 6.1 %collective-permute-start.8 = (bf16[144,256]{1,0:T(8,128)(2,1)S(1)}, bf16[144,256]{1,0:T(8,128)(2,1)S(1)}, u32[]{:S(2)}, u32[]{:S(2)}) collective-permute-start(bf16[144,256]{1,0:T(8,128)(2,1)S(1)} %add_convert_fusion.2), channel_id=1, source_target_pairs={{0,4},{1,5},{2,6},{3,7},{4,0},{5,1},{6,2},{7,3},{8,12},{9,13},{10,... | collective-permute-start | bytes 221192 | tf_op jit(solution)/shard_map/reduce/ppermute | solution.py:334
  91.0 6.0 %collective-permute-start.7 = (bf16[144,256]{1,0:T(8,128)(2,1)S(1)}, bf16[144,256]{1,0:T(8,128)(2,1)S(1)}, u32[]{:S(2)}, u32[]{:S(2)}) collective-permute-start(bf16[144,256]{1,0:T(8,128)(2,1)S(1)} %add_convert_fusion.2), channel_id=1, source_target_pairs={{0,2},{1,3},{2,0},{3,1},{4,6},{5,7},{6,4},{7,5},{8,10},{9,11},{10,... | collective-permute-start | bytes 221192 | tf_op jit(solution)/shard_map/reduce/ppermute | solution.py:334
  97.1 7.2 %collective-permute-start.10 = (bf16[144,256]{1,0:T(8,128)(2,1)S(1)}, bf16[144,256]{1,0:T(8,128)(2,1)S(1)}, u32[]{:S(2)}, u32[]{:S(2)}) collective-permute-start(bf16[144,256]{1,0:T(8,128)(2,1)S(1)} %add_convert_fusion.1), channel_id=1, source_target_pairs={{0,1},{1,0},{2,3},{3,2},{4,5},{5,4},{6,7},{7,6},{8,9},{9,8},{10,11... | collective-permute-start | bytes 221192 | tf_op jit(solution)/shard_map/reduce/ppermute | solution.py:334
  104.3 4.7 %collective-permute-start.12 = (bf16[128,256]{1,0:T(8,128)(2,1)S(1)}, bf16[128,256]{1,0:T(8,128)(2,1)S(1)}, u32[]{:S(2)}, u32[]{:S(2)}) collective-permute-start(bf16[128,256]{1,0:T(8,128)(2,1)S(1)} %get-tuple-element.38), channel_id=1, source_target_pairs={{0,128},{32,160},{64,192},{96,224},{128,0},{160,32},{192,64},{224,... | collective-permute-start | bytes 196616 | tf_op jit(solution)/shard_map/reduce/ppermute | solution.py:444
  105.0 4.0 %collective-permute-start.11 = (bf16[128,256]{1,0:T(8,128)(2,1)S(1)}, bf16[128,256]{1,0:T(8,128)(2,1)S(1)}, u32[]{:S(2)}, u32[]{:S(2)}) collective-permute-start(bf16[128,256]{1,0:T(8,128)(2,1)S(1)} %get-tuple-element.38), channel_id=1, source_target_pairs={{0,64},{32,96},{64,0},{96,32},{128,192},{160,224},{192,128},{224,1... | collective-permute-start | bytes 196616 | tf_op jit(solution)/shard_map/reduce/ppermute | solution.py:444
  105.9 4.3 %collective-permute-start.13 = (bf16[128,256]{1,0:T(8,128)(2,1)S(1)}, bf16[128,256]{1,0:T(8,128)(2,1)S(1)}, u32[]{:S(2)}, u32[]{:S(2)}) collective-permute-start(bf16[128,256]{1,0:T(8,128)(2,1)S(1)} %get-tuple-element.38), channel_id=1, source_target_pairs={{0,192},{32,224},{64,128},{96,160},{128,64},{160,96},{192,0},{224,... | collective-permute-start | bytes 196616 | tf_op jit(solution)/shard_map/reduce/ppermute | solution.py:444
  110.2 7.0 %copy-start.2 = (bf16[4,128,256]{2,1,0:T(8,128)(2,1)}, bf16[4,128,256]{2,1,0:T(8,128)(2,1)S(1)}, u32[]{:S(2)}) copy-start(bf16[4,128,256]{2,1,0:T(8,128)(2,1)S(1)} %pad_maximum_fusion.same_core) | copy-start | bytes 786436
  110.2 7.6 %collective-permute-start.14 = (bf16[4,128,256]{2,1,0:T(8,128)(2,1)S(1)}, bf16[4,128,256]{2,1,0:T(8,128)(2,1)S(1)}, u32[]{:S(2)}, u32[]{:S(2)}) collective-permute-start(bf16[4,128,256]{2,1,0:T(8,128)(2,1)S(1)} %pad_maximum_fusion.same_core), channel_id=1, source_target_pairs={{0,32},{32,0},{64,96},{96,64},{128,160},{160,128},{192,224},{224,1... | collective-permute-start | bytes 786440 | tf_op jit(solution)/shard_map/reduce/ppermute | solution.py:446
  117.9 0.7 copy-start.5

commit v4 on v2

--- a/solution.py
+++ b/solution.py
@@ -33,23 +33,24 @@
     return out.reshape(parts * per * members, members * cols)
 
 
-def halo_matrices(parts, members, rows, cols, side):
+def halo_matrices(parts, members, rows, cols):
     per = cols // parts
+    edge = members * rows
     mats = []
     for pair in range((rows + 2) // 2):
-        out = np.zeros((parts, 2, per + 2, members, 2 * members * cols + 2 * side), np.float32)
+        out = np.zeros((parts, 2, per + 2, members, 2 * members * cols + 6 * edge), np.float32)
         for j in range(parts):
             for q in range(2):
+                row = 2 * pair + q - 1
+                level = 0 if row < 0 else (2 if row >= rows else 1)
                 for c in range(per + 2):
                     for m in range(members):
                         col = j * per + c - 1
-                        edge = (2 * pair + q) * members + m
-                        if col < 0:
-                            src = 2 * members * cols + edge
-                        elif col >= cols:
-                            src = 2 * members * cols + side + edge
+                        if 0 <= col < cols:
+                            src = (q * members + m) * cols + col
                         else:
-                            src = (q * members + m) * cols + col
+                            side = level if col < 0 else 3 + level
+                            src = 2 * members * cols + side * edge + m * rows + row % rows
                         out[j, q, c, m, src] = 1
         mats.append(out.reshape(-1, out.shape[-1]))
     return np.stack(mats)
@@ -64,7 +65,7 @@
     return out.reshape(cells * parts * members, -1)
 
 
-def pack_kernel(fields, cot, before, after, left, right, split, halo, send):
+def pack_kernel(grid, place, fields, cot, before, after, got, split, halo, send):
     members, rows, cols, width = fields.shape
     parts = send.shape[0]
     per = cols // parts * members
@@ -73,11 +74,23 @@
         moved = dot(split[...], tokens).astype(BF).reshape(parts, per, width)
         send[:, r * per : (r + 1) * per, :] = moved
     base = rows * per
-    lines = [before[...]] + [cot[:, r] for r in range(rows)] + [after[...]]
-    lines = [x.reshape(members * cols, width) for x in lines]
+
+    def masked(inside, x):
+        return jnp.where(inside, x, jnp.zeros_like(x))
+
+    row, col = place[0], place[1]
+    sides = []
+    for dc in (-1, 1):
+        for dr in (-1, 0, 1):
+            r, c = row + dr, col + dc
+            inside = (r >= 0) & (r < grid[0]) & (c >= 0) & (c < grid[1])
+            spot = jnp.clip(r, 0, grid[0] - 1) * grid[1] + jnp.clip(c, 0, grid[1] - 1)
+            sides.append(masked(inside, got[spot]))
+    lines = [masked(row > 0, before[...])] + [cot[:, r] for r in range(rows)]
+    lines = [x.reshape(members * cols, width) for x in lines + [masked(row < grid[0] - 1, after[...])]]
     step = 2 * (per + 2 * members)
     for pair in range(halo.shape[0]):
-        tokens = jnp.concatenate([lines[2 * pair], lines[2 * pair + 1], left[...], right[...]], axis=0)
+        tokens = jnp.concatenate([lines[2 * pair], lines[2 * pair + 1]] + sides, axis=0)
         moved = dot(halo[pair], tokens).astype(BF).reshape(parts, step, width)
         send[:, base + pair * step : base + (pair + 1) * step, :] = moved
 
@@ -239,20 +252,16 @@
         send[j, base + shard : base + shard + 16, :] = extras
 
 
-def unpack_kernel(base, shard, recv, split, out, total):
+def unpack_kernel(recv, split, out):
     members, rows, cols, width = out.shape
     parts = recv.shape[0]
     per = cols // parts * members
     for r in range(rows):
         tokens = recv[:, r * per : (r + 1) * per, :].reshape(parts * per, width)
         out[:, r] = dot(split[...], tokens, TN).astype(BF).reshape(members, cols, width)
-    acc = recv[0, base:, :].astype(F32)
-    for j in range(1, parts):
-        acc = acc + recv[j, base:, :].astype(F32)
-    total[...] = acc.astype(BF)
-
-
-def finish_kernel(scale, place, same_core, other_core, extras, g_q, g_k, g_v, g_o, g_mix, g_gain):
+
+
+def finish_kernel(scale, place, same_core, other_core, total, g_q, g_k, g_v, g_o, g_mix, g_gain):
     count, shard, width = same_core.shape
     per = width // shard
     outs = (g_q, g_k, g_v, g_o)
@@ -261,7 +270,7 @@
         spot = lax.shift_right_logical(code, 1)
         got = jnp.where(code == 2 * spot, same_core[spot], other_core[spot]).astype(F32)
         outs[p // per][p % per * shard : (p % per + 1) * shard, :] = got * scale
-    rest = extras[...].astype(F32) * scale
+    rest = total[shard:, :].astype(F32) * scale
     for i in range(3):
         g_mix[i] = rest[3 * i : 3 * i + 3]
     g_gain[...] = rest[9:10]
@@ -282,14 +291,6 @@
 def ring(axis, step):
     size = lax.axis_size(axis)
     return [(i, (i + step) % size) for i in range(size)]
-
-
-def edges(first, last, axis):
-    before = lax.ppermute(last, axis, ring(axis, 1))
-    after = lax.ppermute(first, axis, ring(axis, -1))
-    place, size = lax.axis_index(axis), lax.axis_size(axis)
-    zero = jnp.zeros_like(before)
-    return jnp.where(place > 0, before, zero), jnp.where(place < size - 1, after, zero)
 
 
 def local(fields, norm_gain, w_query, w_key, w_value, w_out, mix_kernel, cotangent):
@@ -300,24 +301,30 @@
     pad_cells = (rows + 2) * (per + 2)
     params = pltpu.CompilerParams(vmem_limit_bytes=60 * 1024 * 1024)
 
+    split = jnp.asarray(split_matrix(parts, members, cols), BF)
+    halo = jnp.asarray(halo_matrices(parts, members, rows, cols), BF)
+    grid = (lax.axis_size("row"), lax.axis_size("col"))
+    smem = pl.BlockSpec(memory_space=pltpu.SMEM)
+    vmem = pl.BlockSpec(memory_space=pltpu.VMEM)
     with jax.named_scope("halo"):
-        before, after = edges(cotangent[:, 0], cotangent[:, rows - 1], "row")
-
-        def column(c):
-            parts_c = [before[None, :, c], jnp.swapaxes(cotangent[:, :, c], 0, 1), after[None, :, c]]
-            flat = jnp.concatenate(parts_c, axis=0).reshape((rows + 2) * members, width)
-            return jnp.pad(flat, ((0, 32 - flat.shape[0]), (0, 0)))
-
-        left, right = edges(column(0), column(cols - 1), "col")
-
-    split = jnp.asarray(split_matrix(parts, members, cols), BF)
-    halo = jnp.asarray(halo_matrices(parts, members, rows, cols, 32), BF)
+        row, col = lax.axis_index("row"), lax.axis_index("col")
+        place = jnp.stack([row, col]).astype(jnp.int32)
+        before = lax.ppermute(cotangent[:, rows - 1], "row", ring("row", 1))
+        after = lax.ppermute(cotangent[:, 0], "row", ring("row", -1))
+        first = cotangent[:, :, 0].reshape(1, 1, members * rows, width)
+        last = cotangent[:, :, cols - 1].reshape(1, 1, members * rows, width)
+        to_right = (lax.iota(jnp.int32, grid[1]) == col + 1).reshape(1, grid[1], 1, 1)
+        columns = jnp.broadcast_to(jnp.where(to_right, last, first), grid + (members * rows, width))
+        columns = columns.reshape(grid[0] * grid[1], members * rows, width)
+        got = lax.all_to_all(columns, ("row", "col"), 0, 0)
+
     with jax.named_scope("pack"):
         send = pl.pallas_call(
-            pack_kernel,
+            functools.partial(pack_kernel, grid),
+            in_specs=[smem] + [vmem] * 7,
             out_shape=jax.ShapeDtypeStruct((parts, (cells + pad_cells) * members, width), BF),
             compiler_params=params,
-        )(fields, cotangent, before, after, left, right, split, halo)
+        )(place, fields, cotangent, before, after, got, split, halo)
     with jax.named_scope("to_cells"):
         recv = lax.all_to_all(send, "mem", 0, 0)
 
@@ -352,12 +359,11 @@
     with jax.named_scope("to_members"):
         landed = lax.all_to_all(back, "mem", 0, 0)
     with jax.named_scope("unpack"):
-        grad_fields, total = pl.pallas_call(
-            functools.partial(unpack_kernel, base, shard),
-            out_shape=(
-                jax.ShapeDtypeStruct(fields.shape, BF),
-                jax.ShapeDtypeStruct((shard + 16, width), BF),
-            ),
+        total = jnp.sum(landed[:, base:, :].astype(F32), axis=0)
+        total = lax.optimization_barrier(total.astype(BF))
+        grad_fields = pl.pallas_call(
+            unpack_kernel,
+            out_shape=jax.ShapeDtypeStruct(fields.shape, BF),
             compiler_params=params,
         )(landed, split)
 
@@ -370,17 +376,16 @@
         same_core = lax.optimization_barrier(same_core)
         other_core = lax.ppermute(same_core, "mem", partner("mem", 1))
 
-    grid = lax.axis_size("row") * lax.axis_size("col")
-    scale_all = 1.0 / math.sqrt(tokens * grid * parts)
+    scale_all = 1.0 / math.sqrt(tokens * grid[0] * grid[1] * parts)
     with jax.named_scope("finish"):
         square = jax.ShapeDtypeStruct((width, width), F32)
-        place = lax.axis_index("mem").astype(jnp.int32).reshape(1)
+        own = lax.axis_index("mem").astype(jnp.int32).reshape(1)
         grads = pl.pallas_call(
             functools.partial(finish_kernel, scale_all),
-            in_specs=[pl.BlockSpec(memory_space=pltpu.SMEM)] + [pl.BlockSpec(memory_space=pltpu.VMEM)] * 3,
+            in_specs=[smem] + [vmem] * 3,
             out_shape=(square,) * 4 + (jax.ShapeDtypeStruct((3, 3, width), F32), jax.ShapeDtypeStruct((1, width), F32)),
             compiler_params=params,
-        )(place, same_core, other_core, total[shard:])
+        )(own, same_core, other_core, total)
     return (grad_fields, grads[5].reshape(width)) + tuple(grads[:5])
 
 

time: 119 us -> 116 us (0.975)
  waiting for transfers between devices: 31.3 us -> 22.4 us
  starting transfers between devices: 26.3 us -> 34.6 us
  blocking collectives: 39.2 us -> 37.4 us
  other arithmetic: 2.3 us -> 0.88 us
    all_to_all x0 -> x1, starting transfers between devices: none -> 12.2 us  [local(): got = lax.all_to_all(columns, ('row', 'col'), 0, 0)]
    ppermute x4 -> x2, starting transfers between devices: 12 us -> 3.15 us  [the longest x1 3.15 us: local(): after = lax.ppermute(cotangent[:, 0], 'row', ring('row', -1))]
    ppermute x4 -> x2, waiting for transfers between devices: 12 us -> 6.98 us  [the longest x1 4.28 us: local(): after = lax.ppermute(cotangent[:, 0], 'row', ring('row', -1))]
    ppermute x7, starting transfers between devices: 6.97 us -> 10.9 us  [meet(): lax.ppermute(values, axis, partner(axis, k))]
    ppermute x7, waiting for transfers between devices: 16.2 us -> 12.9 us  [meet(): lax.ppermute(values, axis, partner(axis, k))]
    unnamed x10 -> x16, local copies, waits for them, and re-layouts: 1.25 us -> 2.63 us
    ppermute x1, starting transfers between devices: 3.97 us -> 5.17 us  [local(): other_core = lax.ppermute(same_core, 'mem', partner('mem', 1))]
  transfers between devices with their start and end apart: 15 -> 14, of which waited for: 12 -> 10; matrix products, arithmetic and copies ran while one was open for 2% -> 1% of each run, Pallas kernels for 0% -> 2%
where the time goes in v4:
time: 116 us
  blocking collectives  37.4 us (32%)
  starting transfers between devices  34.6 us (30%)
  waiting for transfers between devices  22.4 us (19%)
  Pallas kernels  15.2 us (13%)
  local copies, waits for them, and re-layouts  4.36 us (4%)
    all_to_all x1, blocking collectives, local(): recv = lax.all_to_all(send, 'mem', 0, 0)  20 us
    all_to_all x1, blocking collectives, local(): landed = lax.all_to_all(back, 'mem', 0, 0)  17.4 us
    ppermute x7, waiting for transfers between devices, meet(): lax.ppermute(values, axis, partner(axis, k))  12.9 us
    all_to_all x1, starting transfers between devices, local(): got = lax.all_to_all(columns, ('row', 'col'), 0, 0)  12.2 us
    ppermute x7, starting transfers between devices, meet(): lax.ppermute(values, axis, partner(axis, k))  10.9 us
    pallas_call x1, Pallas kernels, local(): pl.pallas_call(functools.partial(main_kernel, rows, per), out_shape=jax.S...  8.06 us
    ppermute x1, starting transfers between devices, local(): other_core = lax.ppermute(same_core, 'mem', partner('mem', 1))  5.17 us
    ppermute x1, waiting for transfers between devices, local(): after = lax.ppermute(cotangent[:, 0], 'row', ring('row', -1))  4.28 us
  transfers between devices with their start and end apart: 14, of which 10 were waited for; matrix products, arithmetic and copies ran while one was open for 1% of the time, Pallas kernels for 2%

profile of v4, /device:TPU:1, one launch (start us, length us, event | category | flops | bytes accessed | tf_op | source)
XLA Modules:
  0.0 115.7 jit_solution(14233714545801615495)
XLA Ops:
  0.6 1.0 slice_reduce_fusion.2
  1.6 0.1 broadcast_select_fusion
  1.7 0.7 broadcast_in_dim.38
  2.4 12.2 %all-to-all-start = ((bf16[32,16,256]{2,1,0:T(8,128)(2,1)}), bf16[32,16,256]{2,1,0:T(8,128)(2,1)S(1)}, u32[]{:S(2)}, u32[]{:S(2)}) async-start(bf16[32,16,256]{2,1,0:T(8,128)(2,1)} %bitcast.4), calls=%async_computation | async-start | bytes 524288 | tf_op jit(solution)/shard_map/halo/all_to_all | solution.py:319
  14.6 0.0 copy-done.3
  14.7 3.1 %collective-permute-start.1 = (bf16[4,32,256]{2,1,0:T(8,128)(2,1)S(1)}, bf16[4,32,256]{2,1,0:T(8,128)(2,1)S(1)}, u32[]{:S(2)}, u32[]{:S(2)}) collective-permute-start(bf16[4,32,256]{2,1,0:T(8,128)(2,1)S(1)} %get-tuple-element.21), channel_id=1, source_target_pairs={{0,24},{8,0},{16,8},{24,16},{1,25},{9,1},{17,9},{25,17},{2,26},{10... | collective-permute-start | bytes 196616 | tf_op jit(solution)/shard_map/halo/ppermute | solution.py:313
  17.8 0.0 collective-permute-start
  17.8 0.6 pad_add_fusion.place
  18.4 4.3 %collective-permute-done.1.after = bf16[4,32,256]{2,1,0:T(8,128)(2,1)S(1)} collective-permute-done((bf16[4,32,256]{2,1,0:T(8,128)(2,1)S(1)}, bf16[4,32,256]{2,1,0:T(8,128)(2,1)S(1)}, u32[]{:S(2)}, u32[]{:S(2)}) %collective-permute-start.1) | collective-permute-done | bytes 65568 | tf_op jit(solution)/shard_map/halo/ppermute | solution.py:313
  22.7 2.7 %collective-permute-done.before = bf16[4,32,256]{2,1,0:T(8,128)(2,1)S(1)} collective-permute-done((bf16[4,32,256]{2,1,0:T(8,128)(2,1)S(1)}, bf16[4,32,256]{2,1,0:T(8,128)(2,1)S(1)}, u32[]{:S(2)}, u32[]{:S(2)}) %collective-permute-start) | collective-permute-done | bytes 65568 | tf_op jit(solution)/shard_map/halo/ppermute | solution.py:312
  25.4 0.0 all-to-all-done.got
  25.4 0.0 copy-done.6
  25.4 0.6 copy-done.7
  26.0 0.7 copy-done.1
  26.7 3.0 %pack.1 = bf16[8,208,256]{2,1,0:T(8,128)(2,1)} custom-call(s32[2]{0:T(128)} %pad_add_fusion.place, bf16[4,4,32,256]{3,2,1,0:T(8,128)(2,1)} %fields.1, bf16[4,4,32,256]{3,2,1,0:T(8,128)(2,1)} %cot.1, bf16[4,32,256]{2,1,0:T(8,128)(2,1)} %copy-done.7, bf16[4,32,256]{2,1,0:T(8,128)(2,1)} %copy-done.6, bf16[32,16,256]{2,1,0:T(8,128)(2,1)} %copy-done.1, ...), custom_call_target="tpu_custom_call" | custom-call | tf_op jit(solution)/shard_map/pack/pallas_call | solution.py:322
  29.7 20.0 %all_to_all.15.recv = bf16[8,208,256]{2,1,0:T(8,128)(2,1)} all-to-all(bf16[8,208,256]{2,1,0:T(8,128)(2,1)} %pack.1), channel_id=1, replica_groups=mesh['mem'=8,'row'=4,'col'=8] {'mem'}, dimensions={0} | all-to-all | bytes 1703936 | tf_op jit(solution)/shard_map/to_cells/all_to_all | solution.py:329
  49.7 8.1 %attention.1 = bf16[8,208,256]{2,1,0:T(8,128)(2,1)} custom-call(bf16[8,208,256]{2,1,0:T(8,128)(2,1)} %all_to_all.15.recv, f32[1,256]{1,0:T(1,128)} %bitcast.22, f32[3,3,256]{2,1,0:T(4,128)} %mix.1, bf16[256,256]{1,0:T(8,128)(2,1)} %wq.1, bf16[256,256]{1,0:T(8,128)(2,1)} %wk.1, bf16[256,256]{1,0:T(8,128)(2,1)} %wv.1, bf16[256,256]{1,0:T(8,128)(2,1)} %wo.1, ...), custom_call_target="tpu_custom_call" | custom-call | tf_op jit(solution)/shard_map/attention/pallas_call | solution.py:336
  57.8 17.4 %all_to_all.16.recv = bf16[8,208,256]{2,1,0:T(8,128)(2,1)S(1)} all-to-all(bf16[8,208,256]{2,1,0:T(8,128)(2,1)} %attention.1), channel_id=1, replica_groups=mesh['mem'=8,'row'=4,'col'=8] {'mem'}, dimensions={0} | all-to-all | bytes 1703936 | tf_op jit(solution)/shard_map/to_members/all_to_all | solution.py:360
  75.2 0.1 slice_reduce_fusion
  75.2 1.8 %collective-permute-start.4 = (bf16[144,256]{1,0:T(8,128)(2,1)S(1)}, bf16[144,256]{1,0:T(8,128)(2,1)S(1)}, u32[]{:S(2)}, u32[]{:S(2)}) collective-permute-start(bf16[144,256]{1,0:T(8,128)(2,1)S(1)} %slice_reduce_fusion), channel_id=1, source_target_pairs={{0,24},{8,16},{16,8},{24,0},{1,25},{9,17},{17,9},{25,1},{2,26},{10... | collective-permute-start | bytes 221192 | tf_op jit(solution)/shard_map/reduce/ppermute | solution.py:284
  77.0 0.5 collective-permute-start.3
  77.6 1.3 %collective-permute-start.2 = (bf16[144,256]{1,0:T(8,128)(2,1)S(1)}, bf16[144,256]{1,0:T(8,128)(2,1)S(1)}, u32[]{:S(2)}, u32[]{:S(2)}) collective-permute-start(bf16[144,256]{1,0:T(8,128)(2,1)S(1)} %slice_reduce_fusion), channel_id=1, source_target_pairs={{0,8},{8,0},{16,24},{24,16},{1,9},{9,1},{17,25},{25,17},{2,10},{10... | collective-permute-start | bytes 221192 | tf_op jit(solution)/shard_map/reduce/ppermute | solution.py:284
  78.9 1.6 %collective-permute-done.4 = bf16[144,256]{1,0:T(8,128)(2,1)S(1)} collective-permute-done((bf16[144,256]{1,0:T(8,128)(2,1)S(1)}, bf16[144,256]{1,0:T(8,128)(2,1)S(1)}, u32[]{:S(2)}, u32[]{:S(2)}) %collective-permute-start.4) | collective-permute-done | bytes 73760 | tf_op jit(solution)/shard_map/reduce/ppermute | solution.py:284
  80.5 4.2 %collective-permute-done.3 = bf16[144,256]{1,0:T(8,128)(2,1)S(1)} collective-permute-done((bf16[144,256]{1,0:T(8,128)(2,1)S(1)}, bf16[144,256]{1,0:T(8,128)(2,1)S(1)}, u32[]{:S(2)}, u32[]{:S(2)}) %collective-permute-start.3) | collective-permute-done | bytes 73760 | tf_op jit(solution)/shard_map/reduce/ppermute | solution.py:284
  84.7 0.0 collective-permute-done.2
  84.7 0.6 collective-permute-start.7
  85.4 2.0 %collective-permute-start.6 = (bf16[144,256]{1,0:T(8,128)(2,1)S(1)}, bf16[144,256]{1,0:T(8,128)(2,1)S(1)}, u32[]{:S(2)}, u32[]{:S(2)}) collective-permute-start(bf16[144,256]{1,0:T(8,128)(2,1)S(1)} %add_convert_fusion.2), channel_id=1, source_target_pairs={{0,4},{1,5},{2,6},{3,7},{4,0},{5,1},{6,2},{7,3},{8,12},{9,13},{10,... | collective-permute-start | bytes 221192 | tf_op jit(solution)/shard_map/reduce/ppermute | solution.py:284
  87.3 0.7 collective-permute-start.5
  88.1 1.2 %collective-permute-done.7 = bf16[144,256]{1,0:T(8,128)(2,1)S(1)} collective-permute-done((bf16[144,256]{1,0:T(8,128)(2,1)S(1)}, bf16[144,256]{1,0:T(8,128)(2,1)S(1)}, u32[]{:S(2)}, u32[]{:S(2)}) %collective-permute-start.7) | collective-permute-done | bytes 73760 | tf_op jit(solution)/shard_map/reduce/ppermute | solution.py:284
  89.2 0.9 collective-permute-done.6
  90.1 0.8 collective-permute-done.5
  90.9 3.9 %collective-permute-start.8 = (bf16[144,256]{1,0:T(8,128)(2,1)S(1)}, bf16[144,256]{1,0:T(8,128)(2,1)S(1)}, u32[]{:S(2)}, u32[]{:S(2)}) collective-permute-start(bf16[144,256]{1,0:T(8,128)(2,1)S(1)} %add_convert_fusion.1), channel_id=1, source_target_pairs={{0,1},{1,0},{2,3},{3,2},{4,5},{5,4},{6,7},{7,6},{8,9},{9,8},{10,11... | collective-permute-start | bytes 221192 | tf_op jit(solution)/shard_map/reduce/ppermute | solution.py:284
  94.8 4.3 %collective-permute-done.8 = bf16[144,256]{1,0:T(8,128)(2,1)S(1)} collective-permute-done((bf16[144,256]{1,0:T(8,128)(2,1)S(1)}, bf16[144,256]{1,0:T(8,128)(2,1)S(1)}, u32[]{:S(2)}, u32[]{:S(2)}) %collective-permute-start.8) | collective-permute-done | bytes 73760 | tf_op jit(solution)/shard_map/reduce/ppermute | solution.py:284
  99.1 0.0 copy-start.4
  99.1 0.0 copy-done
  99.2 0.6 copy-done.4
  99.7 0.7 collective-permute-start.10
  100.4 0.8 collective-permute-start.9
  101.2 1.8 %collective-permute-start.11 = (bf16[128,256]{1,0:T(8,128)(2,1)S(1)}, bf16[128,256]{1,0:T(8,128)(2,1)S(1)}, u32[]{:S(2)}, u32[]{:S(2)}) collective-permute-start(bf16[128,256]{1,0:T(8,128)(2,1)S(1)} %get-tuple-element.24), channel_id=1, source_target_pairs={{0,192},{32,224},{64,128},{96,160},{128,64},{160,96},{192,0},{224,... | collective-permute-start | bytes 196616 | tf_op jit(solution)/shard_map/reduce/ppermute | solution.py:375
  103.0 1.4 %collective-permute-done.10 = bf16[128,256]{1,0:T(8,128)(2,1)S(1)} collective-permute-done((bf16[128,256]{1,0:T(8,128)(2,1)S(1)}, bf16[128,256]{1,0:T(8,128)(2,1)S(1)}, u32[]{:S(2)}, u32[]{:S(2)}) %collective-permute-start.10) | collective-permute-done | bytes 65568 | tf_op jit(solution)/shard_map/reduce/ppermute | solution.py:375
  104.4 0.0 collective-permute-done.9
  104.4 1.2 %collective-permute-done.11 = bf16[128,256]{1,0:T(8,128)(2,1)S(1)} collective-permute-done((bf16[128,256]{1,0:T(8,128)(2,1)S(1)}, bf16[128,256]{1,0:T(8,128)(2,1)S(1)}, u32[]{:S(2)}, u32[]{:S(2)}) %collective-permute-start.11) | collective-permute-done | bytes 65568 | tf_op jit(solution)/shard_map/reduce/ppermute | solution.py:375
  105.6 0.0 copy-start.2
  105.6 5.2 %collective-permute-start.12 = (bf16[4,128,256]{2,1,0:T(8,128)(2,1)S(1)}, bf16[4,128,256]{2,1,0:T(8,128)(2,1)S(1)}, u32[]{:S(2)}, u32[]{:S(2)}) collective-permute-start(bf16[4,128,256]{2,1,0:T(8,128)(2,1)S(1)} %pad_maximum_fusion.same_core), channel_id=1, source_target_pairs={{0,32},{32,0},{64,96},{96,64},{128,160},{160,128},{192,224},{224,1... | collective-permute-start | bytes 786440 | tf_op jit(solution)/shard_map/reduce/ppermute | solution.py:377
  110.8 2.1 %unpack.1 = bf16[4,4,32,256]{3,2,1,0:T(8,128)(2,1)} custom-call(bf16[8,208,256]{2,1,0:T(8,128)(2,1)} %copy-done, bf16[128,128]{1,0:T(8,128)(2,1)} %constant.27.clone.split), custom_call_target="tpu_custom_call" | custom-call | tf_op jit(solution)/shard_map/unpack/pallas_call | solution.py:364
  112.9 0.0 collective-permute-done.12.other_core
  112.9 0.7 copy-done.5
  113.6 2.1 %finish.1 = (f32[256,256]{1,0:T(8,128)}, f32[256,256]{1,0:T(8,128)}, f32[256,256]{1,0:T(8,128)}, f32[256,256]{1,0:T(8,128)}, f32[3,3,256]{2,1,0:T(4,128)}, /*index=5*/f32[1,256]{1,0:T(1,128)}) custom-call(s32[1]{0:T(128)} %bitcast.6.place, bf16[4,128,256]{2,1,0:T(8,128)(2,1)} %copy-done.2, bf16[4,128,256]{2,1,0:T(8,128)(2,1)} %copy-done.5, ...), custom_call_target="tpu_custom_call" | custom-call | tf_op jit(solution)/shard_map/finish/pallas_call | solution.py:383
  (16 shorter events, 0.2 us)
Async XLA Ops:
  2.4 12.2 %copy-start.3 = (bf16[4,4,32,256]{3,2,1,0:T(8,128)(2,1)S(1)}, bf16[4,4,32,256]{3,2,1,0:T(8,128)(2,1)}, u32[]{:S(2)}) copy-start(bf16[4,4,32,256]{3,2,1,0:T(8,128)(2,1)} %cot.1) | copy-start | bytes 786436
  2.4 22.9 %all-to-all-start = ((bf16[32,16,256]{2,1,0:T(8,128)(2,1)}), bf16[32,16,256]{2,1,0:T(8,128)(2,1)S(1)}, u32[]{:S(2)}, u32[]{:S(2)}) async-start(bf16[32,16,256]{2,1,0:T(8,128)(2,1)} %bitcast.4), calls=%async_computation | async-start | bytes 524288 | tf_op jit(solution)/shard_map/halo/all_to_all | solution.py:319
  14.7 8.0 %collective-permute-start.1 = (bf16[4,32,256]{2,1,0:T(8,128)(2,1)S(1)}, bf16[4,32,256]{2,1,0:T(8,128)(2,1)S(1)}, u32[]{:S(2)}, u32[]{:S(2)}) collective-permute-start(bf16[4,32,256]{2,1,0:T(8,128)(2,1)S(1)} %get-tuple-element.21), channel_id=1, source_target_pairs={{0,24},{8,0},{16,8},{24,16},{1,25},{9,1},{17,9},{25,17},{2,26},{10... | collective-permute-start | bytes 196616 | tf_op jit(solution)/shard_map/halo/ppermute | solution.py:313
  17.8 7.6 %collective-permute-start = (bf16[4,32,256]{2,1,0:T(8,128)(2,1)S(1)}, bf16[4,32,256]{2,1,0:T(8,128)(2,1)S(1)}, u32[]{:S(2)}, u32[]{:S(2)}) collective-permute-start(bf16[4,32,256]{2,1,0:T(8,128)(2,1)S(1)} %get-tuple-element.22), channel_id=1, source_target_pairs={{0,8},{8,16},{16,24},{24,0},{1,9},{9,17},{17,25},{25,1},{2,10},{10... | collective-permute-start | bytes 196616 | tf_op jit(solution)/shard_map/halo/ppermute | solution.py:312
  22.7 2.7 %copy-start.6 = (bf16[4,32,256]{2,1,0:T(8,128)(2,1)}, bf16[4,32,256]{2,1,0:T(8,128)(2,1)S(1)}, u32[]{:S(2)}) copy-start(bf16[4,32,256]{2,1,0:T(8,128)(2,1)S(1)} %collective-permute-done.1.after) | copy-start | bytes 196612
  25.4 0.6 copy-start.7
  26.0 0.7 copy-start.1
  75.2 24.0 %copy-start = (bf16[8,208,256]{2,1,0:T(8,128)(2,1)}, bf16[8,208,256]{2,1,0:T(8,128)(2,1)S(1)}, u32[]{:S(2)}) copy-start(bf16[8,208,256]{2,1,0:T(8,128)(2,1)S(1)} %all_to_all.16.recv) | copy-start | bytes 2555908
  75.2 5.2 %collective-permute-start.4 = (bf16[144,256]{1,0:T(8,128)(2,1)S(1)}, bf16[144,256]{1,0:T(8,128)(2,1)S(1)}, u32[]{:S(2)}, u32[]{:S(2)}) collective-permute-start(bf16[144,256]{1,0:T(8,128)(2,1)S(1)} %slice_reduce_fusion), channel_id=1, source_target_pairs={{0,24},{8,16},{16,8},{24,0},{1,25},{9,17},{17,9},{25,1},{2,26},{10... | collective-permute-start | bytes 221192 | tf_op jit(solution)/shard_map/reduce/ppermute | solution.py:284
  77.0 7.6 %collective-permute-start.3 = (bf16[144,256]{1,0:T(8,128)(2,1)S(1)}, bf16[144,256]{1,0:T(8,128)(2,1)S(1)}, u32[]{:S(2)}, u32[]{:S(2)}) collective-permute-start(bf16[144,256]{1,0:T(8,128)(2,1)S(1)} %slice_reduce_fusion), channel_id=1, source_target_pairs={{0,16},{8,24},{16,0},{24,8},{1,17},{9,25},{17,1},{25,9},{2,18},{10... | collective-permute-start | bytes 221192 | tf_op jit(solution)/shard_map/reduce/ppermute | solution.py:284
  77.6 7.1 %collective-permute-start.2 = (bf16[144,256]{1,0:T(8,128)(2,1)S(1)}, bf16[144,256]{1,0:T(8,128)(2,1)S(1)}, u32[]{:S(2)}, u32[]{:S(2)}) collective-permute-start(bf16[144,256]{1,0:T(8,128)(2,1)S(1)} %slice_reduce_fusion), channel_id=1, source_target_pairs={{0,8},{8,0},{16,24},{24,16},{1,9},{9,1},{17,25},{25,17},{2,10},{10... | collective-permute-start | bytes 221192 | tf_op jit(solution)/shard_map/reduce/ppermute | solution.py:284
  84.7 4.5 %collective-permute-start.7 = (bf16[144,256]{1,0:T(8,128)(2,1)S(1)}, bf16[144,256]{1,0:T(8,128)(2,1)S(1)}, u32[]{:S(2)}, u32[]{:S(2)}) collective-permute-start(bf16[144,256]{1,0:T(8,128)(2,1)S(1)} %add_convert_fusion.2), channel_id=1, source_target_pairs={{0,6},{1,7},{2,4},{3,5},{4,2},{5,3},{6,0},{7,1},{8,14},{9,15},{10,... | collective-permute-start | bytes 221192 | tf_op jit(solution)/shard_map/reduce/ppermute | solution.py:284
  85.4 4.7 %collective-permute-start.6 = (bf16[144,256]{1,0:T(8,128)(2,1)S(1)}, bf16[144,256]{1,0:T(8,128)(2,1)S(1)}, u32[]{:S(2)}, u32[]{:S(2)}) collective-permute-start(bf16[144,256]{1,0:T(8,128)(2,1)S(1)} %add_convert_fusion.2), channel_id=1, source_target_pairs={{0,4},{1,5},{2,6},{3,7},{4,0},{5,1},{6,2},{7,3},{8,12},{9,13},{10,... | collective-permute-start | bytes 221192 | tf_op jit(solution)/shard_map/reduce/ppermute | solution.py:284
  87.3 3.6 %collective-permute-start.5 = (bf16[144,256]{1,0:T(8,128)(2,1)S(1)}, bf16[144,256]{1,0:T(8,128)(2,1)S(1)}, u32[]{:S(2)}, u32[]{:S(2)}) collective-permute-start(bf16[144,256]{1,0:T(8,128)(2,1)S(1)} %add_convert_fusion.2), channel_id=1, source_target_pairs={{0,2},{1,3},{2,0},{3,1},{4,6},{5,7},{6,4},{7,5},{8,10},{9,11},{10,... | collective-permute-start | bytes 221192 | tf_op jit(solution)/shard_map/reduce/ppermute | solution.py:284
  90.9 8.2 %collective-permute-start.8 = (bf16[144,256]{1,0:T(8,128)(2,1)S(1)}, bf16[144,256]{1,0:T(8,128)(2,1)S(1)}, u32[]{:S(2)}, u32[]{:S(2)}) collective-permute-start(bf16[144,256]{1,0:T(8,128)(2,1)S(1)} %add_convert_fusion.1), channel_id=1, source_target_pairs={{0,1},{1,0},{2,3},{3,2},{4,5},{5,4},{6,7},{7,6},{8,9},{9,8},{10,11... | collective-permute-start | bytes 221192 | tf_op jit(solution)/shard_map/reduce/ppermute | solution.py:284
  99.1 0.6 copy-start.4
  99.7 4.6 %collective-permute-start.10 = (bf16[128,256]{1,0:T(8,128)(2,1)S(1)}, bf16[128,256]{1,0:T(8,128)(2,1)S(1)}, u32[]{:S(2)}, u32[]{:S(2)}) collective-permute-start(bf16[128,256]{1,0:T(8,128)(2,1)S(1)} %get-tuple-element.24), channel_id=1, source_target_pairs={{0,128},{32,160},{64,192},{96,224},{128,0},{160,32},{192,64},{224,... | collective-permute-start | bytes 196616 | tf_op jit(solution)/shard_map/reduce/ppermute | solution.py:375
  100.4 3.9 %collective-permute-start.9 = (bf16[128,256]{1,0:T(8,128)(2,1)S(1)}, bf16[128,256]{1,0:T(8,128)(2,1)S(1)}, u32[]{:S(2)}, u32[]{:S(2)}) collective-permute-start(bf16[128,256]{1,0:T(8,128)(2,1)S(1)} %get-tuple-element.24), channel_id=1, source_target_pairs={{0,64},{32,96},{64,0},{96,32},{128,192},{160,224},{192,128},{224,1... | collective-permute-start | bytes 196616 | tf_op jit(solution)/shard_map/reduce/ppermute | solution.py:375
  101.2 4.3 %collective-permute-start.11 = (bf16[128,256]{1,0:T(8,128)(2,1)S(1)}, bf16[128,256]{1,0:T(8,128)(2,1)S(1)}, u32[]{:S(2)}, u32[]{:S(2)}) collective-permute-start(bf16[128,256]{1,0:T(8,128)(2,1)S(1)} %get-tuple-element.24), channel_id=1, source_target_pairs={{0,192},{32,224},{64,128},{96,160},{128,64},{160,96},{192,0},{224,... | collective-permute-start | bytes 196616 | tf_op jit(solution)/shard_map/reduce/ppermute | solution.py:375
  105.6 7.3 %copy-start.2 = (bf16[4,128,256]{2,1,0:T(8,128)(2,1)}, bf16[4,128,256]{2,1,0:T(8,128)(2,1)S(1)}, u32[]{:S(2)}) copy-start(bf16[4,128,256]{2,1,0:T(8,128)(2,1)S(1)} %pad_maximum_fusion.same_core) | copy-start | bytes 786436
  105.6 7.3 %collective-permute-start.12 = (bf16[4,128,256]{2,1,0:T(8,128)(2,1)S(1)}, bf16[4,128,256]{2,1,0:T(8,128)(2,1)S(1)}, u32[]{:S(2)}, u32[]{:S(2)}) collective-permute-start(bf16[4,128,256]{2,1,0:T(8,128)(2,1)S(1)} %pad_maximum_fusion.same_core), channel_id=1, source_target_pairs={{0,32},{32,0},{64,96},{96,64},{128,160},{160,128},{192,224},{224,1... | collective-permute-start | bytes 786440 | tf_op jit(solution)/shard_map/reduce/ppermute | solution.py:377
  112.9 0.7 copy-start.5

commit v5 on v3

--- a/solution.py
+++ b/solution.py
@@ -33,23 +33,22 @@
     return out.reshape(parts * per * members, members * cols)
 
 
-def halo_matrices(parts, members, rows, cols, side):
+def halo_matrices(parts, members, rows, cols):
     per = cols // parts
+    edge = members * rows
     mats = []
-    for pair in range((rows + 2) // 2):
-        out = np.zeros((parts, 2, per + 2, members, 2 * members * cols + 2 * side), np.float32)
+    for pair in range(rows // 2):
+        out = np.zeros((parts, 2, per + 2, members, 2 * members * cols + 2 * edge), np.float32)
         for j in range(parts):
             for q in range(2):
                 for c in range(per + 2):
                     for m in range(members):
                         col = j * per + c - 1
-                        edge = (2 * pair + q) * members + m
-                        if col < 0:
-                            src = 2 * members * cols + edge
-                        elif col >= cols:
-                            src = 2 * members * cols + side + edge
+                        if 0 <= col < cols:
+                            src = (q * members + m) * cols + col
                         else:
-                            src = (q * members + m) * cols + col
+                            side = 0 if col < 0 else 1
+                            src = 2 * members * cols + side * edge + m * rows + 2 * pair + q
                         out[j, q, c, m, src] = 1
         mats.append(out.reshape(-1, out.shape[-1]))
     return np.stack(mats)
@@ -64,7 +63,11 @@
     return out.reshape(cells * parts * members, -1)
 
 
-def pack_fields_kernel(fields, split, send):
+def masked(inside, x):
+    return jnp.where(inside, x, jnp.zeros_like(x))
+
+
+def pack_kernel(col_size, place, fields, cot, got, split, halo, send):
     members, rows, cols, width = fields.shape
     parts = send.shape[0]
     per = cols // parts * members
@@ -72,20 +75,17 @@
         tokens = fields[:, r].reshape(members * cols, width)
         moved = dot(split[...], tokens).astype(BF).reshape(parts, per, width)
         send[:, r * per : (r + 1) * per, :] = moved
-
-
-def pack_cot_kernel(inside, cot, before, after, left, right, halo, send):
-    members, rows, cols, width = cot.shape
-    parts = send.shape[0]
-    per = cols // parts * members
-    lines = [before[...]] + [cot[:, r] for r in range(rows)] + [after[...]]
-    lines = [x.reshape(members * cols, width) for x in lines]
-    sides = [jnp.where(inside[i] > 0, x[...], jnp.zeros_like(x[...])) for i, x in enumerate((left, right))]
+    base = rows * per
+    col = place[1]
+    sides = [
+        masked(col > 0, got[jnp.maximum(col - 1, 0)]),
+        masked(col < col_size - 1, got[jnp.minimum(col + 1, col_size - 1)]),
+    ]
     step = 2 * (per + 2 * members)
-    for pair in range(halo.shape[0]):
-        tokens = jnp.concatenate([lines[2 * pair], lines[2 * pair + 1]] + sides, axis=0)
-        moved = dot(halo[pair], tokens).astype(BF).reshape(parts, step, width)
-        send[:, pair * step : (pair + 1) * step, :] = moved
+    for pair in range(rows // 2):
+        lines = [cot[:, 2 * pair + q].reshape(members * cols, width) for q in range(2)]
+        moved = dot(halo[pair], jnp.concatenate(lines + sides, axis=0)).astype(BF)
+        send[:, base + pair * step : base + (pair + 1) * step, :] = moved.reshape(parts, step, width)
 
 
 def regroup(recv, start, count, members, matrix):
@@ -184,7 +184,11 @@
     tile_rows,
     tile_cols,
     members,
+    row_size,
+    place,
     recv,
+    above,
+    below,
     x_in,
     q_in,
     k_in,
@@ -199,7 +203,7 @@
     wv,
     wo,
     gather8,
-    gather4,
+    gather6,
     headsum,
     send,
     padded,
@@ -215,12 +219,15 @@
     tokens = cells * all_members
     pad_cols = tile_cols + 2
     pad_cells = (tile_rows + 2) * pad_cols
-    done = 0
-    while done < pad_cells:
-        count = 8 if pad_cells - done >= 8 else 4
-        block = regroup(recv, done * members, count, members, gather8 if count == 8 else gather4)
-        padded[done : done + count] = block.reshape(count, all_members, width)
-        done += count
+    base = cells * members
+    row = place[0]
+    top = dot(gather6[...], masked(row > 0, above[...]))
+    padded[:pad_cols] = top.reshape(pad_cols, all_members, width)
+    for g in range(tile_rows * pad_cols // 8):
+        block = regroup(recv, base + g * 8 * members, 8, members, gather8)
+        padded[pad_cols + g * 8 : pad_cols + (g + 1) * 8] = block.reshape(8, all_members, width)
+    bottom = dot(gather6[...], masked(row < row_size - 1, below[...]))
+    padded[pad_cells - pad_cols :] = bottom.reshape(pad_cols, all_members, width)
 
     def shifted(i, j):
         picked = [
@@ -285,7 +292,6 @@
         dot(inputs, grad_v, TN),
         dot(att_in[...], grad_mixed, TN),
     ]
-    base = cells * members
     shard = 4 * width // parts
     for j in range(parts):
         which, start = divmod(j * shard, width)
@@ -304,14 +310,7 @@
         out[:, r] = dot(split[...], tokens, TN).astype(BF).reshape(members, cols, width)
 
 
-def total_kernel(base, recv, total):
-    acc = recv[0, base:, :].astype(F32)
-    for j in range(1, recv.shape[0]):
-        acc = acc + recv[j, base:, :].astype(F32)
-    total[...] = acc.astype(BF)
-
-
-def finish_kernel(scale, place, same_core, other_core, extras, g_q, g_k, g_v, g_o, g_mix, g_gain):
+def finish_kernel(scale, place, same_core, other_core, total, g_q, g_k, g_v, g_o, g_mix, g_gain):
     count, shard, width = same_core.shape
     per = width // shard
     outs = (g_q, g_k, g_v, g_o)
@@ -320,7 +319,7 @@
         spot = lax.shift_right_logical(code, 1)
         got = jnp.where(code == 2 * spot, same_core[spot], other_core[spot]).astype(F32)
         outs[p // per][p % per * shard : (p % per + 1) * shard, :] = got * scale
-    rest = extras[...].astype(F32) * scale
+    rest = total[shard:, :].astype(F32) * scale
     for i in range(3):
         g_mix[i] = rest[3 * i : 3 * i + 3]
     g_gain[...] = rest[9:10]
@@ -348,45 +347,42 @@
     parts = lax.axis_size("mem")
     per = cols // parts
     cells = rows * per
-    pad_cells = (rows + 2) * (per + 2)
+    line = (per + 2) * members
     tokens = cells * members * parts
     base = cells * members
     shard = 4 * width // parts
+    grid = (lax.axis_size("row"), lax.axis_size("col"))
     params = pltpu.CompilerParams(vmem_limit_bytes=60 * 1024 * 1024)
+    smem = pl.BlockSpec(memory_space=pltpu.SMEM)
+    vmem = pl.BlockSpec(memory_space=pltpu.VMEM)
     split = jnp.asarray(split_matrix(parts, members, cols), BF)
-    halo = jnp.asarray(halo_matrices(parts, members, rows, cols, 32), BF)
+    halo = jnp.asarray(halo_matrices(parts, members, rows, cols), BF)
     gather8 = jnp.asarray(gather_matrix(parts, 8, members), BF)
-    gather4 = jnp.asarray(gather_matrix(parts, 4, members), BF)
+    gather6 = jnp.asarray(gather_matrix(parts, per + 2, members), BF)
     headsum = jnp.asarray(np.kron(np.eye(HEADS), np.ones((width // HEADS, width // HEADS))), BF)
     gain = norm_gain.reshape(1, width)
-
-    with jax.named_scope("halo"):
-        row, col = lax.axis_index("row"), lax.axis_index("col")
-        before = lax.ppermute(cotangent[:, rows - 1], "row", ring("row", 1))
-        after = lax.ppermute(cotangent[:, 0], "row", ring("row", -1))
-        zero = jnp.zeros_like(before)
-        before = jnp.where(row > 0, before, zero)
-        after = jnp.where(row < lax.axis_size("row") - 1, after, zero)
-
-    with jax.named_scope("pack_fields"):
-        send_f = pl.pallas_call(
-            pack_fields_kernel,
-            out_shape=jax.ShapeDtypeStruct((parts, base, width), BF),
+    row, col = lax.axis_index("row"), lax.axis_index("col")
+    place = jnp.stack([row, col]).astype(jnp.int32)
+
+    with jax.named_scope("halo_cols"):
+        first = cotangent[:, :, 0].reshape(1, members * rows, width)
+        last = cotangent[:, :, cols - 1].reshape(1, members * rows, width)
+        to_right = (lax.iota(jnp.int32, grid[1]) == col + 1).reshape(grid[1], 1, 1)
+        got = lax.all_to_all(jnp.where(to_right, last, first), "col", 0, 0)
+    with jax.named_scope("pack"):
+        send = pl.pallas_call(
+            functools.partial(pack_kernel, grid[1]),
+            in_specs=[smem] + [vmem] * 5,
+            out_shape=jax.ShapeDtypeStruct((parts, base + rows * line, width), BF),
             compiler_params=params,
-        )(fields, split)
-    with jax.named_scope("fields_to_cells"):
-        recv_f = lax.all_to_all(send_f, "mem", 0, 0)
-
-    with jax.named_scope("halo_cols"):
-
-        def column(c):
-            pieces = [before[None, :, c], jnp.swapaxes(cotangent[:, :, c], 0, 1), after[None, :, c]]
-            flat = jnp.concatenate(pieces, axis=0).reshape((rows + 2) * members, width)
-            return jnp.pad(flat, ((0, 32 - flat.shape[0]), (0, 0)))
-
-        left = lax.ppermute(column(cols - 1), "col", ring("col", 1))
-        right = lax.ppermute(column(0), "col", ring("col", -1))
-        inside = jnp.stack([col > 0, col < lax.axis_size("col") - 1]).astype(jnp.int32)
+        )(place, fields, cotangent, got, split, halo)
+    with jax.named_scope("to_cells"):
+        recv = lax.all_to_all(send, "mem", 0, 0)
+    with jax.named_scope("halo_rows"):
+        top = recv[:, base : base + line].reshape(parts * line, width)
+        bottom = recv[:, base + (rows - 1) * line :].reshape(parts * line, width)
+        above = lax.ppermute(bottom, "row", ring("row", 1))
+        below = lax.ppermute(top, "row", ring("row", -1))
 
     with jax.named_scope("forward"):
         token = jax.ShapeDtypeStruct((tokens, width), BF)
@@ -397,39 +393,39 @@
             out_shape=(token, token, token, token, token_f, token, token),
             scratch_shapes=[pltpu.VMEM((tokens, width), F32)] + mats,
             compiler_params=params,
-        )(recv_f, gain, w_query, w_key, w_value, w_out, gather8, headsum)
-
-    with jax.named_scope("pack_cot"):
-        smem = pl.BlockSpec(memory_space=pltpu.SMEM)
-        vmem = pl.BlockSpec(memory_space=pltpu.VMEM)
-        send_c = pl.pallas_call(
-            pack_cot_kernel,
-            in_specs=[smem] + [vmem] * 6,
-            out_shape=jax.ShapeDtypeStruct((parts, pad_cells * members, width), BF),
-            compiler_params=params,
-        )(inside, cotangent, before, after, left, right, halo)
-    with jax.named_scope("cot_to_cells"):
-        recv_c = lax.all_to_all(send_c, "mem", 0, 0)
-
+        )(recv, gain, w_query, w_key, w_value, w_out, gather8, headsum)
     with jax.named_scope("backward"):
         back = pl.pallas_call(
-            functools.partial(backward_kernel, rows, per, members),
+            functools.partial(backward_kernel, rows, per, members, grid[0]),
+            in_specs=[smem] + [vmem] * 19,
             out_shape=jax.ShapeDtypeStruct((parts, base + shard + 16, width), BF),
             scratch_shapes=[
-                pltpu.VMEM((pad_cells, members * parts, width), F32),
+                pltpu.VMEM(((rows + 2) * (per + 2), members * parts, width), F32),
                 pltpu.VMEM((tokens, width), F32),
             ]
             + mats,
             compiler_params=params,
-        )(recv_c, *kept, gain, mix_kernel, w_query, w_key, w_value, w_out, gather8, gather4, headsum)
+        )(
+            place,
+            recv,
+            above,
+            below,
+            *kept,
+            gain,
+            mix_kernel,
+            w_query,
+            w_key,
+            w_value,
+            w_out,
+            gather8,
+            gather6,
+            headsum,
+        )
     with jax.named_scope("to_members"):
         landed = lax.all_to_all(back, "mem", 0, 0)
     with jax.named_scope("unpack"):
-        total = pl.pallas_call(
-            functools.partial(total_kernel, base),
-            out_shape=jax.ShapeDtypeStruct((shard + 16, width), BF),
-            compiler_params=params,
-        )(landed)
+        total = jnp.sum(landed[:, base:, :].astype(F32), axis=0)
+        total = lax.optimization_barrier(total.astype(BF))
         grad_fields = pl.pallas_call(
             unpack_kernel,
             out_shape=jax.ShapeDtypeStruct(fields.shape, BF),
@@ -445,17 +441,16 @@
         same_core = lax.optimization_barrier(same_core)
         other_core = lax.ppermute(same_core, "mem", partner("mem", 1))
 
-    grid = lax.axis_size("row") * lax.axis_size("col")
-    scale_all = 1.0 / math.sqrt(tokens * grid * parts)
+    scale_all = 1.0 / math.sqrt(tokens * grid[0] * grid[1] * parts)
     with jax.named_scope("finish"):
         square = jax.ShapeDtypeStruct((width, width), F32)
-        place = lax.axis_index("mem").astype(jnp.int32).reshape(1)
+        own = lax.axis_index("mem").astype(jnp.int32).reshape(1)
         grads = pl.pallas_call(
             functools.partial(finish_kernel, scale_all),
-            in_specs=[pl.BlockSpec(memory_space=pltpu.SMEM)] + [pl.BlockSpec(memory_space=pltpu.VMEM)] * 3,
+            in_specs=[smem] + [vmem] * 3,
             out_shape=(square,) * 4 + (jax.ShapeDtypeStruct((3, 3, width), F32), jax.ShapeDtypeStruct((1, width), F32)),
             compiler_params=params,
-        )(place, same_core, other_core, total[shard:])
+        )(own, same_core, other_core, total)
     return (grad_fields, grads[5].reshape(width)) + tuple(grads[:5])
 
 

time: 121 us -> 118 us (0.975)
  blocking collectives: 18.3 us -> 35.4 us
  starting transfers between devices: 38.9 us -> 30.3 us
  waiting for transfers between devices: 31.8 us -> 26.5 us
  Pallas kernels: 22.6 us -> 19 us
  local copies, waits for them, and re-layouts: 6.45 us -> 3.58 us
    all_to_all x0 -> x1, blocking collectives: none -> 17.3 us  [local(): recv = lax.all_to_all(send, 'mem', 0, 0)]
    ppermute x4 -> x2, starting transfers between devices: 12.1 us -> 3.34 us  [the longest x1 2.52 us: local(): below = lax.ppermute(top, 'row', ring('row', -1))]
    ppermute x4 -> x2, waiting for transfers between devices: 8.03 us -> 0.01 us  [the longest x1 0.01 us: local(): above = lax.ppermute(bottom, 'row', ring('row', 1))]
    pallas_call x5 -> x3, Pallas kernels: 15.5 us -> 11.8 us  [the longest x1 7.13 us: local(): pl.pallas_call(functools.partial(backward_kernel, rows, per, members, gri...]
    all_to_all x2 -> x1, waiting for transfers between devices: 5.21 us -> 8.49 us  [local(): got = lax.all_to_all(jnp.where(to_right, last, first), 'col', 0, 0)]
    unnamed x18 -> x16, local copies, waits for them, and re-layouts: 3.99 us -> 2.57 us
    all_to_all x2 -> x1, starting transfers between devices: 11.4 us -> 11.6 us  [local(): got = lax.all_to_all(jnp.where(to_right, last, first), 'col', 0, 0)]
  transfers between devices with their start and end apart: 17 -> 14, of which waited for: 9 -> 9; matrix products, arithmetic and copies ran while one was open for 2% -> 1% of each run, Pallas kernels for 10% -> 6%
where the time goes in v5:
time: 118 us; the launch traced here: 117 us
  blocking collectives  35.4 us (30%)
  starting transfers between devices  30.3 us (26%)
  waiting for transfers between devices  26.5 us (22%)
  Pallas kernels  19 us (16%)
  local copies, waits for them, and re-layouts  3.58 us (3%)
  other arithmetic  1.55 us (1%)
    all_to_all x1, blocking collectives, local(): landed = lax.all_to_all(back, 'mem', 0, 0)  18.1 us
    all_to_all x1, blocking collectives, local(): recv = lax.all_to_all(send, 'mem', 0, 0)  17.3 us
    ppermute x7, waiting for transfers between devices, meet(): lax.ppermute(values, axis, partner(axis, k))  15.5 us
    all_to_all x1, starting transfers between devices, local(): got = lax.all_to_all(jnp.where(to_right, last, first), 'col', 0, 0)  11.6 us
    all_to_all x1, waiting for transfers between devices, local(): got = lax.all_to_all(jnp.where(to_right, last, first), 'col', 0, 0)  8.49 us
    ppermute x7, starting transfers between devices, meet(): lax.ppermute(values, axis, partner(axis, k))  7.53 us
    pallas_call x1, Pallas kernels, local(): pl.pallas_call(functools.partial(backward_kernel, rows, per, members, gri...  7.13 us
    pallas_call x1, Pallas kernels, local(): pl.pallas_call(functools.partial(forward_kernel, members), out_shape=(tok...  5.1 us
  transfers between devices with their start and end apart: 14, of which 9 were waited for; matrix products, arithmetic and copies ran while one was open for 1% of the time, Pallas kernels for 6%

profile of v5, /device:TPU:1, one launch (start us, length us, event | category | flops | bytes accessed | tf_op | source)
XLA Modules:
  0.0 117.0 jit_solution(12549685283469445362)
XLA Ops:
  0.6 1.0 slice_reduce_fusion.2
  1.6 0.7 broadcast_select_fusion
  2.3 11.6 %all-to-all-start = ((bf16[8,16,256]{2,1,0:T(8,128)(2,1)}), bf16[8,16,256]{2,1,0:T(8,128)(2,1)S(1)}, u32[]{:S(2)}, u32[]{:S(2)}) async-start(bf16[8,16,256]{2,1,0:T(8,128)(2,1)} %broadcast_select_fusion), calls=%async_computation | async-start | bytes 131072 | tf_op jit(solution)/shard_map/halo_cols/all_to_all | solution.py:371
  14.0 0.6 pad_add_fusion.place
  14.6 8.5 %all-to-all-done.got = bf16[8,16,256]{2,1,0:T(8,128)(2,1)S(1)} async-done(((bf16[8,16,256]{2,1,0:T(8,128)(2,1)}), bf16[8,16,256]{2,1,0:T(8,128)(2,1)S(1)}, u32[]{:S(2)}, u32[]{:S(2)}) %all-to-all-start) | async-done | bytes 65568 | tf_op jit(solution)/shard_map/halo_cols/all_to_all | solution.py:371
  23.1 0.6 copy-done.4
  23.7 2.6 %pack.1 = bf16[8,160,256]{2,1,0:T(8,128)(2,1)} custom-call(s32[2]{0:T(128)} %pad_add_fusion.place, bf16[4,4,32,256]{3,2,1,0:T(8,128)(2,1)} %fields.1, bf16[4,4,32,256]{3,2,1,0:T(8,128)(2,1)} %cot.1, bf16[8,16,256]{2,1,0:T(8,128)(2,1)} %copy-done.4, bf16[128,128]{1,0:T(8,128)(2,1)} %constant.27.clone.split, bf16[2,384,288]{2,1,0:T(8,128)(2,1)} %constant.28.clone.halo), custom_call_target="tpu_custom_call" | custom-call | tf_op jit(solution)/shard_map/pack/pallas_call | solution.py:373
  26.3 17.3 %all_to_all.15.recv = bf16[8,160,256]{2,1,0:T(8,128)(2,1)S(1)} all-to-all(bf16[8,160,256]{2,1,0:T(8,128)(2,1)} %pack.1), channel_id=1, replica_groups=mesh['mem'=8,'row'=4,'col'=8] {'mem'}, dimensions={0} | all-to-all | bytes 1310720 | tf_op jit(solution)/shard_map/to_cells/all_to_all | solution.py:380
  43.6 0.8 collective-permute-start
  44.5 2.5 %collective-permute-start.1 = (bf16[192,256]{1,0:T(8,128)(2,1)S(1)}, bf16[192,256]{1,0:T(8,128)(2,1)S(1)}, u32[]{:S(2)}, u32[]{:S(2)}) collective-permute-start(bf16[192,256]{1,0:T(8,128)(2,1)S(1)} %bitcast.12), channel_id=1, source_target_pairs={{0,24},{8,0},{16,8},{24,16},{1,25},{9,1},{17,9},{25,17},{2,26},{10... | collective-permute-start | bytes 294920 | tf_op jit(solution)/shard_map/halo_rows/ppermute | solution.py:385
  47.0 0.0 copy-done
  47.0 5.1 %forward.1 = (bf16[512,256]{1,0:T(8,128)(2,1)}, bf16[512,256]{1,0:T(8,128)(2,1)}, bf16[512,256]{1,0:T(8,128)(2,1)}, bf16[512,256]{1,0:T(8,128)(2,1)}, f32[512,25...) custom-call(bf16[8,160,256]{2,1,0:T(8,128)(2,1)} %copy-done, f32[1,256]{1,0:T(1,128)} %bitcast.17, ...), custom_call_target="tpu_custom_call" | custom-call | tf_op jit(solution)/shard_map/forward/pallas_call | solution.py:391
  52.1 0.0 collective-permute-done.above
  52.1 0.0 collective-permute-done.1.below
  52.1 0.0 copy-start.7
  52.1 0.6 copy-done.6
  52.7 0.0 copy-done.7
  52.8 7.1 %backward.1 = bf16[8,208,256]{2,1,0:T(8,128)(2,1)} custom-call(s32[2]{0:T(128)} %pad_add_fusion.place, bf16[8,160,256]{2,1,0:T(8,128)(2,1)} %copy-done, bf16[192,256]{1,0:T(8,128)(2,1)} %copy-done.6, bf16[192,256]{1,0:T(8,128)(2,1)} %copy-done.7, bf16[512,256]{1,0:T(8,128)(2,1)} %get-tuple-element.20.x_in, bf16[512,256]{1,0:T(8,128)(2,1)} %get-tuple-element.21.q_in, ...), custom_call_target="tpu_custom_call" | custom-call | tf_op jit(solution)/shard_map/backward/pallas_call | solution.py:398
  59.9 18.1 %all_to_all.16.recv = bf16[8,208,256]{2,1,0:T(8,128)(2,1)S(1)} all-to-all(bf16[8,208,256]{2,1,0:T(8,128)(2,1)} %backward.1), channel_id=1, replica_groups=mesh['mem'=8,'row'=4,'col'=8] {'mem'}, dimensions={0} | all-to-all | bytes 1703936 | tf_op jit(solution)/shard_map/to_members/all_to_all | solution.py:425
  78.0 0.1 slice_reduce_fusion
  78.0 1.1 collective-permute-start.4
  79.1 0.0 collective-permute-start.3
  79.1 2.6 %collective-permute-start.2 = (bf16[144,256]{1,0:T(8,128)(2,1)S(1)}, bf16[144,256]{1,0:T(8,128)(2,1)S(1)}, u32[]{:S(2)}, u32[]{:S(2)}) collective-permute-start(bf16[144,256]{1,0:T(8,128)(2,1)S(1)} %slice_reduce_fusion), channel_id=1, source_target_pairs={{0,8},{8,0},{16,24},{24,16},{1,9},{9,1},{17,25},{25,17},{2,10},{10... | collective-permute-start | bytes 221192 | tf_op jit(solution)/shard_map/reduce/ppermute | solution.py:333
  81.7 1.6 %collective-permute-done.4 = bf16[144,256]{1,0:T(8,128)(2,1)S(1)} collective-permute-done((bf16[144,256]{1,0:T(8,128)(2,1)S(1)}, bf16[144,256]{1,0:T(8,128)(2,1)S(1)}, u32[]{:S(2)}, u32[]{:S(2)}) %collective-permute-start.4) | collective-permute-done | bytes 73760 | tf_op jit(solution)/shard_map/reduce/ppermute | solution.py:333
  83.3 4.0 %collective-permute-done.3 = bf16[144,256]{1,0:T(8,128)(2,1)S(1)} collective-permute-done((bf16[144,256]{1,0:T(8,128)(2,1)S(1)}, bf16[144,256]{1,0:T(8,128)(2,1)S(1)}, u32[]{:S(2)}, u32[]{:S(2)}) %collective-permute-start.3) | collective-permute-done | bytes 73760 | tf_op jit(solution)/shard_map/reduce/ppermute | solution.py:333
  87.3 0.0 collective-permute-done.2
  87.3 1.0 collective-permute-start.7
  88.3 1.2 %collective-permute-start.6 = (bf16[144,256]{1,0:T(8,128)(2,1)S(1)}, bf16[144,256]{1,0:T(8,128)(2,1)S(1)}, u32[]{:S(2)}, u32[]{:S(2)}) collective-permute-start(bf16[144,256]{1,0:T(8,128)(2,1)S(1)} %add_convert_fusion.2), channel_id=1, source_target_pairs={{0,4},{1,5},{2,6},{3,7},{4,0},{5,1},{6,2},{7,3},{8,12},{9,13},{10,... | collective-permute-start | bytes 221192 | tf_op jit(solution)/shard_map/reduce/ppermute | solution.py:333
  89.5 1.2 %collective-permute-start.5 = (bf16[144,256]{1,0:T(8,128)(2,1)S(1)}, bf16[144,256]{1,0:T(8,128)(2,1)S(1)}, u32[]{:S(2)}, u32[]{:S(2)}) collective-permute-start(bf16[144,256]{1,0:T(8,128)(2,1)S(1)} %add_convert_fusion.2), channel_id=1, source_target_pairs={{0,2},{1,3},{2,0},{3,1},{4,6},{5,7},{6,4},{7,5},{8,10},{9,11},{10,... | collective-permute-start | bytes 221192 | tf_op jit(solution)/shard_map/reduce/ppermute | solution.py:333
  90.7 1.2 collective-permute-done.7
  91.8 1.3 %collective-permute-done.6 = bf16[144,256]{1,0:T(8,128)(2,1)S(1)} collective-permute-done((bf16[144,256]{1,0:T(8,128)(2,1)S(1)}, bf16[144,256]{1,0:T(8,128)(2,1)S(1)}, u32[]{:S(2)}, u32[]{:S(2)}) %collective-permute-start.6) | collective-permute-done | bytes 73760 | tf_op jit(solution)/shard_map/reduce/ppermute | solution.py:333
  93.1 0.7 collective-permute-done.5
  93.8 0.6 collective-permute-start.8
  94.4 6.7 %collective-permute-done.8 = bf16[144,256]{1,0:T(8,128)(2,1)S(1)} collective-permute-done((bf16[144,256]{1,0:T(8,128)(2,1)S(1)}, bf16[144,256]{1,0:T(8,128)(2,1)S(1)}, u32[]{:S(2)}, u32[]{:S(2)}) %collective-permute-start.8) | collective-permute-done | bytes 73760 | tf_op jit(solution)/shard_map/reduce/ppermute | solution.py:333
  101.2 0.0 copy-start.3
  101.2 0.0 copy-done.1
  101.2 0.6 copy-done.3
  101.8 0.7 collective-permute-start.10
  102.5 0.8 collective-permute-start.9
  103.3 1.8 %collective-permute-start.11 = (bf16[128,256]{1,0:T(8,128)(2,1)S(1)}, bf16[128,256]{1,0:T(8,128)(2,1)S(1)}, u32[]{:S(2)}, u32[]{:S(2)}) collective-permute-start(bf16[128,256]{1,0:T(8,128)(2,1)S(1)} %get-tuple-element.38), channel_id=1, source_target_pairs={{0,192},{32,224},{64,128},{96,160},{128,64},{160,96},{192,0},{224,... | collective-permute-start | bytes 196616 | tf_op jit(solution)/shard_map/reduce/ppermute | solution.py:440
  105.0 1.4 %collective-permute-done.10 = bf16[128,256]{1,0:T(8,128)(2,1)S(1)} collective-permute-done((bf16[128,256]{1,0:T(8,128)(2,1)S(1)}, bf16[128,256]{1,0:T(8,128)(2,1)S(1)}, u32[]{:S(2)}, u32[]{:S(2)}) %collective-permute-start.10) | collective-permute-done | bytes 65568 | tf_op jit(solution)/shard_map/reduce/ppermute | solution.py:440
  106.4 0.0 collective-permute-done.9
  106.4 1.2 collective-permute-done.11
  107.6 4.5 %collective-permute-start.12 = (bf16[4,128,256]{2,1,0:T(8,128)(2,1)S(1)}, bf16[4,128,256]{2,1,0:T(8,128)(2,1)S(1)}, u32[]{:S(2)}, u32[]{:S(2)}) collective-permute-start(bf16[4,128,256]{2,1,0:T(8,128)(2,1)S(1)} %pad_maximum_fusion.same_core), channel_id=1, source_target_pairs={{0,32},{32,0},{64,96},{96,64},{128,160},{160,128},{192,224},{224,1... | collective-permute-start | bytes 786440 | tf_op jit(solution)/shard_map/reduce/ppermute | solution.py:442
  112.2 2.1 %unpack.1 = bf16[4,4,32,256]{3,2,1,0:T(8,128)(2,1)} custom-call(bf16[8,208,256]{2,1,0:T(8,128)(2,1)} %copy-done.1, bf16[128,128]{1,0:T(8,128)(2,1)} %constant.27.clone.split), custom_call_target="tpu_custom_call" | custom-call | tf_op jit(solution)/shard_map/unpack/pallas_call | solution.py:429
  114.3 0.0 collective-permute-done.12.other_core
  114.3 0.7 copy-done.5
  115.0 2.1 %finish.1 = (f32[256,256]{1,0:T(8,128)}, f32[256,256]{1,0:T(8,128)}, f32[256,256]{1,0:T(8,128)}, f32[256,256]{1,0:T(8,128)}, f32[3,3,256]{2,1,0:T(4,128)}, /*index=5*/f32[1,256]{1,0:T(1,128)}) custom-call(s32[1]{0:T(128)} %bitcast.5.place, bf16[4,128,256]{2,1,0:T(8,128)(2,1)} %copy-done.2, bf16[4,128,256]{2,1,0:T(8,128)(2,1)} %copy-done.5, ...), custom_call_target="tpu_custom_call" | custom-call | tf_op jit(solution)/shard_map/finish/pallas_call | solution.py:448
  (16 shorter events, 0.2 us)
Async XLA Ops:
  2.3 20.8 %all-to-all-start = ((bf16[8,16,256]{2,1,0:T(8,128)(2,1)}), bf16[8,16,256]{2,1,0:T(8,128)(2,1)S(1)}, u32[]{:S(2)}, u32[]{:S(2)}) async-start(bf16[8,16,256]{2,1,0:T(8,128)(2,1)} %broadcast_select_fusion), calls=%async_computation | async-start | bytes 131072 | tf_op jit(solution)/shard_map/halo_cols/all_to_all | solution.py:371
  23.1 0.6 copy-start.4
  43.6 3.4 %copy-start = (bf16[8,160,256]{2,1,0:T(8,128)(2,1)}, bf16[8,160,256]{2,1,0:T(8,128)(2,1)S(1)}, u32[]{:S(2)}) copy-start(bf16[8,160,256]{2,1,0:T(8,128)(2,1)S(1)} %all_to_all.15.recv) | copy-start | bytes 1966084
  43.6 8.4 %collective-permute-start = (bf16[192,256]{1,0:T(8,128)(2,1)S(1)}, bf16[192,256]{1,0:T(8,128)(2,1)S(1)}, u32[]{:S(2)}, u32[]{:S(2)}) collective-permute-start(bf16[192,256]{1,0:T(8,128)(2,1)S(1)} %bitcast.13), channel_id=1, source_target_pairs={{0,8},{8,16},{16,24},{24,0},{1,9},{9,17},{17,25},{25,1},{2,10},{10... | collective-permute-start | bytes 294920 | tf_op jit(solution)/shard_map/halo_rows/ppermute | solution.py:384
  44.5 7.6 %collective-permute-start.1 = (bf16[192,256]{1,0:T(8,128)(2,1)S(1)}, bf16[192,256]{1,0:T(8,128)(2,1)S(1)}, u32[]{:S(2)}, u32[]{:S(2)}) collective-permute-start(bf16[192,256]{1,0:T(8,128)(2,1)S(1)} %bitcast.12), channel_id=1, source_target_pairs={{0,24},{8,0},{16,8},{24,16},{1,25},{9,1},{17,9},{25,17},{2,26},{10... | collective-permute-start | bytes 294920 | tf_op jit(solution)/shard_map/halo_rows/ppermute | solution.py:385
  52.1 0.6 copy-start.6
  52.1 0.7 copy-start.7
  78.0 23.2 %copy-start.1 = (bf16[8,208,256]{2,1,0:T(8,128)(2,1)}, bf16[8,208,256]{2,1,0:T(8,128)(2,1)S(1)}, u32[]{:S(2)}) copy-start(bf16[8,208,256]{2,1,0:T(8,128)(2,1)S(1)} %all_to_all.16.recv) | copy-start | bytes 2555908
  78.0 5.2 %collective-permute-start.4 = (bf16[144,256]{1,0:T(8,128)(2,1)S(1)}, bf16[144,256]{1,0:T(8,128)(2,1)S(1)}, u32[]{:S(2)}, u32[]{:S(2)}) collective-permute-start(bf16[144,256]{1,0:T(8,128)(2,1)S(1)} %slice_reduce_fusion), channel_id=1, source_target_pairs={{0,24},{8,16},{16,8},{24,0},{1,25},{9,17},{17,9},{25,1},{2,26},{10... | collective-permute-start | bytes 221192 | tf_op jit(solution)/shard_map/reduce/ppermute | solution.py:333
  79.1 8.2 %collective-permute-start.3 = (bf16[144,256]{1,0:T(8,128)(2,1)S(1)}, bf16[144,256]{1,0:T(8,128)(2,1)S(1)}, u32[]{:S(2)}, u32[]{:S(2)}) collective-permute-start(bf16[144,256]{1,0:T(8,128)(2,1)S(1)} %slice_reduce_fusion), channel_id=1, source_target_pairs={{0,16},{8,24},{16,0},{24,8},{1,17},{9,25},{17,1},{25,9},{2,18},{10... | collective-permute-start | bytes 221192 | tf_op jit(solution)/shard_map/reduce/ppermute | solution.py:333
  79.1 8.2 %collective-permute-start.2 = (bf16[144,256]{1,0:T(8,128)(2,1)S(1)}, bf16[144,256]{1,0:T(8,128)(2,1)S(1)}, u32[]{:S(2)}, u32[]{:S(2)}) collective-permute-start(bf16[144,256]{1,0:T(8,128)(2,1)S(1)} %slice_reduce_fusion), channel_id=1, source_target_pairs={{0,8},{8,0},{16,24},{24,16},{1,9},{9,1},{17,25},{25,17},{2,10},{10... | collective-permute-start | bytes 221192 | tf_op jit(solution)/shard_map/reduce/ppermute | solution.py:333
  87.3 4.5 %collective-permute-start.7 = (bf16[144,256]{1,0:T(8,128)(2,1)S(1)}, bf16[144,256]{1,0:T(8,128)(2,1)S(1)}, u32[]{:S(2)}, u32[]{:S(2)}) collective-permute-start(bf16[144,256]{1,0:T(8,128)(2,1)S(1)} %add_convert_fusion.2), channel_id=1, source_target_pairs={{0,6},{1,7},{2,4},{3,5},{4,2},{5,3},{6,0},{7,1},{8,14},{9,15},{10,... | collective-permute-start | bytes 221192 | tf_op jit(solution)/shard_map/reduce/ppermute | solution.py:333
  88.3 4.8 %collective-permute-start.6 = (bf16[144,256]{1,0:T(8,128)(2,1)S(1)}, bf16[144,256]{1,0:T(8,128)(2,1)S(1)}, u32[]{:S(2)}, u32[]{:S(2)}) collective-permute-start(bf16[144,256]{1,0:T(8,128)(2,1)S(1)} %add_convert_fusion.2), channel_id=1, source_target_pairs={{0,4},{1,5},{2,6},{3,7},{4,0},{5,1},{6,2},{7,3},{8,12},{9,13},{10,... | collective-permute-start | bytes 221192 | tf_op jit(solution)/shard_map/reduce/ppermute | solution.py:333
  89.5 4.3 %collective-permute-start.5 = (bf16[144,256]{1,0:T(8,128)(2,1)S(1)}, bf16[144,256]{1,0:T(8,128)(2,1)S(1)}, u32[]{:S(2)}, u32[]{:S(2)}) collective-permute-start(bf16[144,256]{1,0:T(8,128)(2,1)S(1)} %add_convert_fusion.2), channel_id=1, source_target_pairs={{0,2},{1,3},{2,0},{3,1},{4,6},{5,7},{6,4},{7,5},{8,10},{9,11},{10,... | collective-permute-start | bytes 221192 | tf_op jit(solution)/shard_map/reduce/ppermute | solution.py:333
  93.8 7.3 %collective-permute-start.8 = (bf16[144,256]{1,0:T(8,128)(2,1)S(1)}, bf16[144,256]{1,0:T(8,128)(2,1)S(1)}, u32[]{:S(2)}, u32[]{:S(2)}) collective-permute-start(bf16[144,256]{1,0:T(8,128)(2,1)S(1)} %add_convert_fusion.1), channel_id=1, source_target_pairs={{0,1},{1,0},{2,3},{3,2},{4,5},{5,4},{6,7},{7,6},{8,9},{9,8},{10,11... | collective-permute-start | bytes 221192 | tf_op jit(solution)/shard_map/reduce/ppermute | solution.py:333
  101.2 0.6 copy-start.3
  101.8 4.6 %collective-permute-start.10 = (bf16[128,256]{1,0:T(8,128)(2,1)S(1)}, bf16[128,256]{1,0:T(8,128)(2,1)S(1)}, u32[]{:S(2)}, u32[]{:S(2)}) collective-permute-start(bf16[128,256]{1,0:T(8,128)(2,1)S(1)} %get-tuple-element.38), channel_id=1, source_target_pairs={{0,128},{32,160},{64,192},{96,224},{128,0},{160,32},{192,64},{224,... | collective-permute-start | bytes 196616 | tf_op jit(solution)/shard_map/reduce/ppermute | solution.py:440
  102.5 3.9 %collective-permute-start.9 = (bf16[128,256]{1,0:T(8,128)(2,1)S(1)}, bf16[128,256]{1,0:T(8,128)(2,1)S(1)}, u32[]{:S(2)}, u32[]{:S(2)}) collective-permute-start(bf16[128,256]{1,0:T(8,128)(2,1)S(1)} %get-tuple-element.38), channel_id=1, source_target_pairs={{0,64},{32,96},{64,0},{96,32},{128,192},{160,224},{192,128},{224,1... | collective-permute-start | bytes 196616 | tf_op jit(solution)/shard_map/reduce/ppermute | solution.py:440
  103.3 4.3 %collective-permute-start.11 = (bf16[128,256]{1,0:T(8,128)(2,1)S(1)}, bf16[128,256]{1,0:T(8,128)(2,1)S(1)}, u32[]{:S(2)}, u32[]{:S(2)}) collective-permute-start(bf16[128,256]{1,0:T(8,128)(2,1)S(1)} %get-tuple-element.38), channel_id=1, source_target_pairs={{0,192},{32,224},{64,128},{96,160},{128,64},{160,96},{192,0},{224,... | collective-permute-start | bytes 196616 | tf_op jit(solution)/shard_map/reduce/ppermute | solution.py:440
  107.6 6.6 %copy-start.2 = (bf16[4,128,256]{2,1,0:T(8,128)(2,1)}, bf16[4,128,256]{2,1,0:T(8,128)(2,1)S(1)}, u32[]{:S(2)}) copy-start(bf16[4,128,256]{2,1,0:T(8,128)(2,1)S(1)} %pad_maximum_fusion.same_core) | copy-start | bytes 786436
  107.6 6.6 %collective-permute-start.12 = (bf16[4,128,256]{2,1,0:T(8,128)(2,1)S(1)}, bf16[4,128,256]{2,1,0:T(8,128)(2,1)S(1)}, u32[]{:S(2)}, u32[]{:S(2)}) collective-permute-start(bf16[4,128,256]{2,1,0:T(8,128)(2,1)S(1)} %pad_maximum_fusion.same_core), channel_id=1, source_target_pairs={{0,32},{32,0},{64,96},{96,64},{128,160},{160,128},{192,224},{224,1... | collective-permute-start | bytes 786440 | tf_op jit(solution)/shard_map/reduce/ppermute | solution.py:442
  114.3 0.7 copy-start.5

commit v6 on v4

--- a/solution.py
+++ b/solution.py
@@ -288,6 +288,10 @@
     return lax.optimization_barrier(got[0].astype(BF))
 
 
+def near(x):
+    return pltpu.with_memory_space_constraint(x, pltpu.VMEM)
+
+
 def ring(axis, step):
     size = lax.axis_size(axis)
     return [(i, (i + step) % size) for i in range(size)]
@@ -299,7 +303,7 @@
     per = cols // parts
     cells = rows * per
     pad_cells = (rows + 2) * (per + 2)
-    params = pltpu.CompilerParams(vmem_limit_bytes=60 * 1024 * 1024)
+    params = pltpu.CompilerParams(vmem_limit_bytes=40 * 1024 * 1024)
 
     split = jnp.asarray(split_matrix(parts, members, cols), BF)
     halo = jnp.asarray(halo_matrices(parts, members, rows, cols), BF)
@@ -322,9 +326,9 @@
         send = pl.pallas_call(
             functools.partial(pack_kernel, grid),
             in_specs=[smem] + [vmem] * 7,
-            out_shape=jax.ShapeDtypeStruct((parts, (cells + pad_cells) * members, width), BF),
+            out_shape=pltpu.VMEM((parts, (cells + pad_cells) * members, width), BF),
             compiler_params=params,
-        )(place, fields, cotangent, before, after, got, split, halo)
+        )(place, fields, cotangent, near(before), near(after), near(got), split, halo)
     with jax.named_scope("to_cells"):
         recv = lax.all_to_all(send, "mem", 0, 0)
 
@@ -335,7 +339,7 @@
     with jax.named_scope("attention"):
         back = pl.pallas_call(
             functools.partial(main_kernel, rows, per),
-            out_shape=jax.ShapeDtypeStruct((parts, base + shard + 16, width), BF),
+            out_shape=pltpu.VMEM((parts, base + shard + 16, width), BF),
             scratch_shapes=[
                 pltpu.VMEM((pad_cells, members * parts, width), F32),
                 pltpu.VMEM((tokens, width), F32),
@@ -345,7 +349,7 @@
             ],
             compiler_params=params,
         )(
-            recv,
+            near(recv),
             norm_gain.reshape(1, width),
             mix_kernel,
             w_query,
@@ -365,12 +369,13 @@
             unpack_kernel,
             out_shape=jax.ShapeDtypeStruct(fields.shape, BF),
             compiler_params=params,
-        )(landed, split)
+        )(near(landed), split)
 
     with jax.named_scope("reduce"):
         total = meet(total, "row", (1, 2, 3))
         total = meet(total, "col", (2, 4, 6))
         total = meet(total, "col", (1,))
+        total, grad_fields = lax.optimization_barrier((total, grad_fields))
         piece = total[:shard]
         same_core = jnp.stack([piece] + [lax.ppermute(piece, "mem", partner("mem", k)) for k in (2, 4, 6)])
         same_core = lax.optimization_barrier(same_core)
@@ -385,7 +390,7 @@
             in_specs=[smem] + [vmem] * 3,
             out_shape=(square,) * 4 + (jax.ShapeDtypeStruct((3, 3, width), F32), jax.ShapeDtypeStruct((1, width), F32)),
             compiler_params=params,
-        )(own, same_core, other_core, total)
+        )(own, near(same_core), near(other_core), near(total))
     return (grad_fields, grads[5].reshape(width)) + tuple(grads[:5])
 
 

time: 116 us -> 109 us (0.940)
  Pallas kernels: 15.2 us -> 8.69 us
  blocking collectives: 37.4 us -> 35.6 us
  starting transfers between devices: 34.6 us -> 36 us
    pallas_call x1, Pallas kernels: 8.06 us -> 5.63 us  [local(): pl.pallas_call(functools.partial(main_kernel, rows, per), out_shape=pltpu...]
    pallas_call x1, Pallas kernels: 2.99 us -> 1.07 us  [local(): pl.pallas_call(functools.partial(pack_kernel, grid), in_specs=[smem] + [v...]
    ppermute x7, waiting for transfers between devices: 12.9 us -> 11.1 us  [meet(): lax.ppermute(values, axis, partner(axis, k))]
    ppermute x1, starting transfers between devices: 5.17 us -> 6.36 us  [local(): other_core = lax.ppermute(same_core, 'mem', partner('mem', 1))]
    unnamed x16 -> x26, local copies, waits for them, and re-layouts: 2.63 us -> 1.63 us
  transfers between devices with their start and end apart: 14 -> 14, of which waited for: 10 -> 11; matrix products, arithmetic and copies ran while one was open for 1% -> 1% of each run, Pallas kernels for 2% -> 1%
where the time goes in v6:
time: 109 us; the launch traced here: 108 us
  starting transfers between devices  36 us (33%)
  blocking collectives  35.6 us (33%)
  waiting for transfers between devices  22.4 us (21%)
  Pallas kernels  8.69 us (8%)
  local copies, waits for them, and re-layouts  4.35 us (4%)
    all_to_all x1, blocking collectives, local(): recv = lax.all_to_all(send, 'mem', 0, 0)  19.3 us
    all_to_all x1, blocking collectives, local(): landed = lax.all_to_all(back, 'mem', 0, 0)  16.3 us
    all_to_all x1, starting transfers between devices, local(): got = lax.all_to_all(columns, ('row', 'col'), 0, 0)  12.2 us
    ppermute x7, waiting for transfers between devices, meet(): lax.ppermute(values, axis, partner(axis, k))  11.1 us
    ppermute x7, starting transfers between devices, meet(): lax.ppermute(values, axis, partner(axis, k))  11 us
    ppermute x1, starting transfers between devices, local(): other_core = lax.ppermute(same_core, 'mem', partner('mem', 1))  6.36 us
    pallas_call x1, Pallas kernels, local(): pl.pallas_call(functools.partial(main_kernel, rows, per), out_shape=pltpu...  5.63 us
    ppermute x1, waiting for transfers between devices, local(): after = lax.ppermute(cotangent[:, 0], 'row', ring('row', -1))  3.85 us
  transfers between devices with their start and end apart: 14, of which 11 were waited for; matrix products, arithmetic and copies ran while one was open for 1% of the time, Pallas kernels for 1%

profile of v6, /device:TPU:1, one launch (start us, length us, event | category | flops | bytes accessed | tf_op | source)
XLA Modules:
  0.0 108.3 jit_solution(9205348291057618221)
XLA Ops:
  0.6 0.0 copy-start
  0.7 1.0 slice_reduce_fusion.2
  1.7 0.1 broadcast_select_fusion
  1.8 0.7 broadcast_in_dim.38
  2.5 12.2 %all-to-all-start = ((bf16[32,16,256]{2,1,0:T(8,128)(2,1)}), bf16[32,16,256]{2,1,0:T(8,128)(2,1)S(1)}, u32[]{:S(2)}, u32[]{:S(2)}) async-start(bf16[32,16,256]{2,1,0:T(8,128)(2,1)} %bitcast.4), calls=%async_computation | async-start | bytes 524288 | tf_op jit(solution)/shard_map/halo/all_to_all | solution.py:323
  14.7 0.0 copy-start.1
  14.7 0.9 slice_bitcast_fusion
  15.7 3.1 %collective-permute-start.1 = (bf16[4,32,256]{2,1,0:T(8,128)(2,1)S(1)}, bf16[4,32,256]{2,1,0:T(8,128)(2,1)S(1)}, u32[]{:S(2)}, u32[]{:S(2)}) collective-permute-start(bf16[4,32,256]{2,1,0:T(8,128)(2,1)S(1)} %get-tuple-element.25), channel_id=1, source_target_pairs={{0,24},{8,0},{16,8},{24,16},{1,25},{9,1},{17,9},{25,17},{2,26},{10... | collective-permute-start | bytes 196616 | tf_op jit(solution)/shard_map/halo/ppermute | solution.py:317
  18.8 0.1 pad_add_fusion.place
  18.9 3.8 %collective-permute-done.1.after = bf16[4,32,256]{2,1,0:T(8,128)(2,1)S(1)} collective-permute-done((bf16[4,32,256]{2,1,0:T(8,128)(2,1)S(1)}, bf16[4,32,256]{2,1,0:T(8,128)(2,1)S(1)}, u32[]{:S(2)}, u32[]{:S(2)}) %collective-permute-start.1) | collective-permute-done | bytes 65568 | tf_op jit(solution)/shard_map/halo/ppermute | solution.py:317
  22.7 3.7 %collective-permute-done.before = bf16[4,32,256]{2,1,0:T(8,128)(2,1)S(1)} collective-permute-done((bf16[4,32,256]{2,1,0:T(8,128)(2,1)S(1)}, bf16[4,32,256]{2,1,0:T(8,128)(2,1)S(1)}, u32[]{:S(2)}, u32[]{:S(2)}) %collective-permute-start) | collective-permute-done | bytes 65568 | tf_op jit(solution)/shard_map/halo/ppermute | solution.py:316
  26.4 0.0 copy-start.2
  26.5 0.9 copy-done.2
  27.4 1.1 pack.1
  28.5 0.0 copy-start.4
  28.5 0.0 copy-start.5
  28.5 0.0 copy-start.6
  28.5 0.0 copy-start.7
  28.5 0.0 copy-start.8
  28.5 0.0 copy-start.9
  28.5 0.0 copy-start.10
  28.6 0.0 copy-start.11
  28.6 19.3 %all_to_all.15.recv = bf16[8,208,256]{2,1,0:T(8,128)(2,1)S(1)} all-to-all(bf16[8,208,256]{2,1,0:T(8,128)(2,1)S(1)} %pack.1), channel_id=1, replica_groups=mesh['mem'=8,'row'=4,'col'=8] {'mem'}, dimensions={0} | all-to-all | bytes 1703936 | tf_op jit(solution)/shard_map/to_cells/all_to_all | solution.py:333
  47.9 0.6 copy-done.12
  48.6 5.6 %attention.1 = bf16[8,208,256]{2,1,0:T(8,128)(2,1)S(1)} custom-call(bf16[8,208,256]{2,1,0:T(8,128)(2,1)S(1)} %all_to_all.15.recv, f32[1,256]{1,0:T(1,128)S(1)} %bitcast.19, f32[3,3,256]{2,1,0:T(4,128)S(1)} %copy-done.11, bf16[256,256]{1,0:T(8,128)(2,1)S(1)} %copy-done.4, bf16[256,256]{1,0:T(8,128)(2,1)S(1)} %copy-done.5, bf16[256,256]{1,0:T(8,128)(2,1)S(1)} %copy-done.6, ...), custom_call_target="tpu_custom_call" | custom-call | tf_op jit(solution)/shard_map/attention/pallas_call | solution.py:340
  54.2 16.3 %all_to_all.16.recv = bf16[8,208,256]{2,1,0:T(8,128)(2,1)S(1)} all-to-all(bf16[8,208,256]{2,1,0:T(8,128)(2,1)S(1)} %attention.1), channel_id=1, replica_groups=mesh['mem'=8,'row'=4,'col'=8] {'mem'}, dimensions={0} | all-to-all | bytes 1703936 | tf_op jit(solution)/shard_map/to_members/all_to_all | solution.py:364
  70.5 0.1 slice_reduce_fusion
  70.6 2.0 %collective-permute-start.4 = (bf16[144,256]{1,0:T(8,128)(2,1)S(1)}, bf16[144,256]{1,0:T(8,128)(2,1)S(1)}, u32[]{:S(2)}, u32[]{:S(2)}) collective-permute-start(bf16[144,256]{1,0:T(8,128)(2,1)S(1)} %slice_reduce_fusion), channel_id=1, source_target_pairs={{0,24},{8,16},{16,8},{24,0},{1,25},{9,17},{17,9},{25,1},{2,26},{10... | collective-permute-start | bytes 221192 | tf_op jit(solution)/shard_map/reduce/ppermute | solution.py:284
  72.6 0.5 collective-permute-start.3
  73.1 1.1 %collective-permute-start.2 = (bf16[144,256]{1,0:T(8,128)(2,1)S(1)}, bf16[144,256]{1,0:T(8,128)(2,1)S(1)}, u32[]{:S(2)}, u32[]{:S(2)}) collective-permute-start(bf16[144,256]{1,0:T(8,128)(2,1)S(1)} %slice_reduce_fusion), channel_id=1, source_target_pairs={{0,8},{8,0},{16,24},{24,16},{1,9},{9,1},{17,25},{25,17},{2,10},{10... | collective-permute-start | bytes 221192 | tf_op jit(solution)/shard_map/reduce/ppermute | solution.py:284
  74.2 1.6 %collective-permute-done.4 = bf16[144,256]{1,0:T(8,128)(2,1)S(1)} collective-permute-done((bf16[144,256]{1,0:T(8,128)(2,1)S(1)}, bf16[144,256]{1,0:T(8,128)(2,1)S(1)}, u32[]{:S(2)}, u32[]{:S(2)}) %collective-permute-start.4) | collective-permute-done | bytes 73760 | tf_op jit(solution)/shard_map/reduce/ppermute | solution.py:284
  75.9 4.3 %collective-permute-done.3 = bf16[144,256]{1,0:T(8,128)(2,1)S(1)} collective-permute-done((bf16[144,256]{1,0:T(8,128)(2,1)S(1)}, bf16[144,256]{1,0:T(8,128)(2,1)S(1)}, u32[]{:S(2)}, u32[]{:S(2)}) %collective-permute-start.3) | collective-permute-done | bytes 73760 | tf_op jit(solution)/shard_map/reduce/ppermute | solution.py:284
  80.2 0.8 collective-permute-start.7
  81.0 1.8 %collective-permute-start.6 = (bf16[144,256]{1,0:T(8,128)(2,1)S(1)}, bf16[144,256]{1,0:T(8,128)(2,1)S(1)}, u32[]{:S(2)}, u32[]{:S(2)}) collective-permute-start(bf16[144,256]{1,0:T(8,128)(2,1)S(1)} %add_convert_fusion.2), channel_id=1, source_target_pairs={{0,4},{1,5},{2,6},{3,7},{4,0},{5,1},{6,2},{7,3},{8,12},{9,13},{10,... | collective-permute-start | bytes 221192 | tf_op jit(solution)/shard_map/reduce/ppermute | solution.py:284
  82.8 0.7 collective-permute-start.5
  83.6 1.2 %collective-permute-done.7 = bf16[144,256]{1,0:T(8,128)(2,1)S(1)} collective-permute-done((bf16[144,256]{1,0:T(8,128)(2,1)S(1)}, bf16[144,256]{1,0:T(8,128)(2,1)S(1)}, u32[]{:S(2)}, u32[]{:S(2)}) %collective-permute-start.7) | collective-permute-done | bytes 73760 | tf_op jit(solution)/shard_map/reduce/ppermute | solution.py:284
  84.7 1.0 collective-permute-done.6
  85.7 0.7 collective-permute-done.5
  86.4 4.1 %collective-permute-start.8 = (bf16[144,256]{1,0:T(8,128)(2,1)S(1)}, bf16[144,256]{1,0:T(8,128)(2,1)S(1)}, u32[]{:S(2)}, u32[]{:S(2)}) collective-permute-start(bf16[144,256]{1,0:T(8,128)(2,1)S(1)} %add_convert_fusion.1), channel_id=1, source_target_pairs={{0,1},{1,0},{2,3},{3,2},{4,5},{5,4},{6,7},{7,6},{8,9},{9,8},{10,11... | collective-permute-start | bytes 221192 | tf_op jit(solution)/shard_map/reduce/ppermute | solution.py:284
  90.5 1.0 unpack.1
  91.4 2.4 %collective-permute-done.8 = bf16[144,256]{1,0:T(8,128)(2,1)S(1)} collective-permute-done((bf16[144,256]{1,0:T(8,128)(2,1)S(1)}, bf16[144,256]{1,0:T(8,128)(2,1)S(1)}, u32[]{:S(2)}, u32[]{:S(2)}) %collective-permute-start.8) | collective-permute-done | bytes 73760 | tf_op jit(solution)/shard_map/reduce/ppermute | solution.py:284
  93.9 1.6 %collective-permute-start.10 = (bf16[128,256]{1,0:T(8,128)(2,1)S(1)}, bf16[128,256]{1,0:T(8,128)(2,1)S(1)}, u32[]{:S(2)}, u32[]{:S(2)}) collective-permute-start(bf16[128,256]{1,0:T(8,128)(2,1)S(1)} %get-tuple-element.28), channel_id=1, source_target_pairs={{0,128},{32,160},{64,192},{96,224},{128,0},{160,32},{192,64},{224,... | collective-permute-start | bytes 196616 | tf_op jit(solution)/shard_map/reduce/ppermute | solution.py:380
  95.4 1.8 %collective-permute-start.11 = (bf16[128,256]{1,0:T(8,128)(2,1)S(1)}, bf16[128,256]{1,0:T(8,128)(2,1)S(1)}, u32[]{:S(2)}, u32[]{:S(2)}) collective-permute-start(bf16[128,256]{1,0:T(8,128)(2,1)S(1)} %get-tuple-element.28), channel_id=1, source_target_pairs={{0,192},{32,224},{64,128},{96,160},{128,64},{160,96},{192,0},{224,... | collective-permute-start | bytes 196616 | tf_op jit(solution)/shard_map/reduce/ppermute | solution.py:380
  97.2 1.4 %collective-permute-done.10 = bf16[128,256]{1,0:T(8,128)(2,1)S(1)} collective-permute-done((bf16[128,256]{1,0:T(8,128)(2,1)S(1)}, bf16[128,256]{1,0:T(8,128)(2,1)S(1)}, u32[]{:S(2)}, u32[]{:S(2)}) %collective-permute-start.10) | collective-permute-done | bytes 65568 | tf_op jit(solution)/shard_map/reduce/ppermute | solution.py:380
  98.6 1.2 %collective-permute-done.11 = bf16[128,256]{1,0:T(8,128)(2,1)S(1)} collective-permute-done((bf16[128,256]{1,0:T(8,128)(2,1)S(1)}, bf16[128,256]{1,0:T(8,128)(2,1)S(1)}, u32[]{:S(2)}, u32[]{:S(2)}) %collective-permute-start.11) | collective-permute-done | bytes 65568 | tf_op jit(solution)/shard_map/reduce/ppermute | solution.py:380
  99.8 6.4 %collective-permute-start.12 = (bf16[4,128,256]{2,1,0:T(8,128)(2,1)S(1)}, bf16[4,128,256]{2,1,0:T(8,128)(2,1)S(1)}, u32[]{:S(2)}, u32[]{:S(2)}) collective-permute-start(bf16[4,128,256]{2,1,0:T(8,128)(2,1)S(1)} %pad_maximum_fusion.same_core), channel_id=1, source_target_pairs={{0,32},{32,0},{64,96},{96,64},{128,160},{160,128},{192,224},{224,1... | collective-permute-start | bytes 786440 | tf_op jit(solution)/shard_map/reduce/ppermute | solution.py:382
  106.1 1.2 %collective-permute-done.12.other_core = bf16[4,128,256]{2,1,0:T(8,128)(2,1)S(1)} collective-permute-done((bf16[4,128,256]{2,1,0:T(8,128)(2,1)S(1)}, bf16[4,128,256]{2,1,0:T(8,128)(2,1)S(1)}, u32[]{:S(2)}, u32[]{:S(2)}) %collective-permute-start.12) | collective-permute-done | bytes 262176 | tf_op jit(solution)/shard_map/reduce/ppermute | solution.py:382
  107.3 1.0 finish.1
  (26 shorter events, 0.2 us)
Async XLA Ops:
  0.6 25.8 %copy-start = (bf16[3,384,352]{2,1,0:T(8,128)(2,1)S(1)}, bf16[3,384,352]{2,1,0:T(8,128)(2,1)}, u32[]{:S(2)}) copy-start(bf16[3,384,352]{2,1,0:T(8,128)(2,1)} %constant.28.clone.halo) | copy-start | bytes 2433028
  2.5 23.9 %copy-start.3 = (bf16[128,128]{1,0:T(8,128)(2,1)S(1)}, bf16[128,128]{1,0:T(8,128)(2,1)}, u32[]{:S(2)}) copy-start(bf16[128,128]{1,0:T(8,128)(2,1)} %constant.27.clone.split) | copy-start | bytes 98308
  2.5 23.9 %all-to-all-start = ((bf16[32,16,256]{2,1,0:T(8,128)(2,1)}), bf16[32,16,256]{2,1,0:T(8,128)(2,1)S(1)}, u32[]{:S(2)}, u32[]{:S(2)}) async-start(bf16[32,16,256]{2,1,0:T(8,128)(2,1)} %bitcast.4), calls=%async_computation | async-start | bytes 524288 | tf_op jit(solution)/shard_map/halo/all_to_all | solution.py:323
  14.7 11.7 %copy-start.1 = (bf16[4,4,32,256]{3,2,1,0:T(8,128)(2,1)S(1)}, bf16[4,4,32,256]{3,2,1,0:T(8,128)(2,1)}, u32[]{:S(2)}) copy-start(bf16[4,4,32,256]{3,2,1,0:T(8,128)(2,1)} %cot.1) | copy-start | bytes 786436
  15.7 7.1 %collective-permute-start.1 = (bf16[4,32,256]{2,1,0:T(8,128)(2,1)S(1)}, bf16[4,32,256]{2,1,0:T(8,128)(2,1)S(1)}, u32[]{:S(2)}, u32[]{:S(2)}) collective-permute-start(bf16[4,32,256]{2,1,0:T(8,128)(2,1)S(1)} %get-tuple-element.25), channel_id=1, source_target_pairs={{0,24},{8,0},{16,8},{24,16},{1,25},{9,1},{17,9},{25,17},{2,26},{10... | collective-permute-start | bytes 196616 | tf_op jit(solution)/shard_map/halo/ppermute | solution.py:317
  18.8 7.6 %collective-permute-start = (bf16[4,32,256]{2,1,0:T(8,128)(2,1)S(1)}, bf16[4,32,256]{2,1,0:T(8,128)(2,1)S(1)}, u32[]{:S(2)}, u32[]{:S(2)}) collective-permute-start(bf16[4,32,256]{2,1,0:T(8,128)(2,1)S(1)} %get-tuple-element.26), channel_id=1, source_target_pairs={{0,8},{8,16},{16,24},{24,0},{1,9},{9,17},{17,25},{25,1},{2,10},{10... | collective-permute-start | bytes 196616 | tf_op jit(solution)/shard_map/halo/ppermute | solution.py:316
  26.4 1.0 copy-start.2
  28.5 19.4 %copy-start.4 = (bf16[256,256]{1,0:T(8,128)(2,1)S(1)}, bf16[256,256]{1,0:T(8,128)(2,1)}, u32[]{:S(2)}) copy-start(bf16[256,256]{1,0:T(8,128)(2,1)} %wq.1) | copy-start | bytes 393220
  28.5 19.4 %copy-start.5 = (bf16[256,256]{1,0:T(8,128)(2,1)S(1)}, bf16[256,256]{1,0:T(8,128)(2,1)}, u32[]{:S(2)}) copy-start(bf16[256,256]{1,0:T(8,128)(2,1)} %wk.1) | copy-start | bytes 393220
  28.5 19.4 %copy-start.6 = (bf16[256,256]{1,0:T(8,128)(2,1)S(1)}, bf16[256,256]{1,0:T(8,128)(2,1)}, u32[]{:S(2)}) copy-start(bf16[256,256]{1,0:T(8,128)(2,1)} %wv.1) | copy-start | bytes 393220
  28.5 19.4 %copy-start.7 = (bf16[256,256]{1,0:T(8,128)(2,1)S(1)}, bf16[256,256]{1,0:T(8,128)(2,1)}, u32[]{:S(2)}) copy-start(bf16[256,256]{1,0:T(8,128)(2,1)} %wo.1) | copy-start | bytes 393220
  28.5 19.4 %copy-start.8 = (bf16[256,256]{1,0:T(8,128)(2,1)S(1)}, bf16[256,256]{1,0:T(8,128)(2,1)}, u32[]{:S(2)}) copy-start(bf16[256,256]{1,0:T(8,128)(2,1)} %constant.31.clone.headsum) | copy-start | bytes 393220
  28.5 19.4 %copy-start.9 = (bf16[256,256]{1,0:T(8,128)(2,1)S(1)}, bf16[256,256]{1,0:T(8,128)(2,1)}, u32[]{:S(2)}) copy-start(bf16[256,256]{1,0:T(8,128)(2,1)} %constant.29.clone.gather8) | copy-start | bytes 393220
  28.5 19.4 %copy-start.10 = (bf16[128,128]{1,0:T(8,128)(2,1)S(1)}, bf16[128,128]{1,0:T(8,128)(2,1)}, u32[]{:S(2)}) copy-start(bf16[128,128]{1,0:T(8,128)(2,1)} %constant.30.clone.gather4) | copy-start | bytes 98308
  28.6 19.4 %copy-start.11 = (f32[3,3,256]{2,1,0:T(4,128)S(1)}, f32[3,3,256]{2,1,0:T(4,128)}, u32[]{:S(2)}) copy-start(f32[3,3,256]{2,1,0:T(4,128)} %mix.1) | copy-start | bytes 27652
  47.9 0.7 copy-start.12
  70.6 5.3 %collective-permute-start.4 = (bf16[144,256]{1,0:T(8,128)(2,1)S(1)}, bf16[144,256]{1,0:T(8,128)(2,1)S(1)}, u32[]{:S(2)}, u32[]{:S(2)}) collective-permute-start(bf16[144,256]{1,0:T(8,128)(2,1)S(1)} %slice_reduce_fusion), channel_id=1, source_target_pairs={{0,24},{8,16},{16,8},{24,0},{1,25},{9,17},{17,9},{25,1},{2,26},{10... | collective-permute-start | bytes 221192 | tf_op jit(solution)/shard_map/reduce/ppermute | solution.py:284
  72.6 7.6 %collective-permute-start.3 = (bf16[144,256]{1,0:T(8,128)(2,1)S(1)}, bf16[144,256]{1,0:T(8,128)(2,1)S(1)}, u32[]{:S(2)}, u32[]{:S(2)}) collective-permute-start(bf16[144,256]{1,0:T(8,128)(2,1)S(1)} %slice_reduce_fusion), channel_id=1, source_target_pairs={{0,16},{8,24},{16,0},{24,8},{1,17},{9,25},{17,1},{25,9},{2,18},{10... | collective-permute-start | bytes 221192 | tf_op jit(solution)/shard_map/reduce/ppermute | solution.py:284
  73.1 7.0 %collective-permute-start.2 = (bf16[144,256]{1,0:T(8,128)(2,1)S(1)}, bf16[144,256]{1,0:T(8,128)(2,1)S(1)}, u32[]{:S(2)}, u32[]{:S(2)}) collective-permute-start(bf16[144,256]{1,0:T(8,128)(2,1)S(1)} %slice_reduce_fusion), channel_id=1, source_target_pairs={{0,8},{8,0},{16,24},{24,16},{1,9},{9,1},{17,25},{25,17},{2,10},{10... | collective-permute-start | bytes 221192 | tf_op jit(solution)/shard_map/reduce/ppermute | solution.py:284
  80.2 4.5 %collective-permute-start.7 = (bf16[144,256]{1,0:T(8,128)(2,1)S(1)}, bf16[144,256]{1,0:T(8,128)(2,1)S(1)}, u32[]{:S(2)}, u32[]{:S(2)}) collective-permute-start(bf16[144,256]{1,0:T(8,128)(2,1)S(1)} %add_convert_fusion.2), channel_id=1, source_target_pairs={{0,6},{1,7},{2,4},{3,5},{4,2},{5,3},{6,0},{7,1},{8,14},{9,15},{10,... | collective-permute-start | bytes 221192 | tf_op jit(solution)/shard_map/reduce/ppermute | solution.py:284
  81.0 4.7 %collective-permute-start.6 = (bf16[144,256]{1,0:T(8,128)(2,1)S(1)}, bf16[144,256]{1,0:T(8,128)(2,1)S(1)}, u32[]{:S(2)}, u32[]{:S(2)}) collective-permute-start(bf16[144,256]{1,0:T(8,128)(2,1)S(1)} %add_convert_fusion.2), channel_id=1, source_target_pairs={{0,4},{1,5},{2,6},{3,7},{4,0},{5,1},{6,2},{7,3},{8,12},{9,13},{10,... | collective-permute-start | bytes 221192 | tf_op jit(solution)/shard_map/reduce/ppermute | solution.py:284
  82.8 3.6 %collective-permute-start.5 = (bf16[144,256]{1,0:T(8,128)(2,1)S(1)}, bf16[144,256]{1,0:T(8,128)(2,1)S(1)}, u32[]{:S(2)}, u32[]{:S(2)}) collective-permute-start(bf16[144,256]{1,0:T(8,128)(2,1)S(1)} %add_convert_fusion.2), channel_id=1, source_target_pairs={{0,2},{1,3},{2,0},{3,1},{4,6},{5,7},{6,4},{7,5},{8,10},{9,11},{10,... | collective-permute-start | bytes 221192 | tf_op jit(solution)/shard_map/reduce/ppermute | solution.py:284
  86.4 7.4 %collective-permute-start.8 = (bf16[144,256]{1,0:T(8,128)(2,1)S(1)}, bf16[144,256]{1,0:T(8,128)(2,1)S(1)}, u32[]{:S(2)}, u32[]{:S(2)}) collective-permute-start(bf16[144,256]{1,0:T(8,128)(2,1)S(1)} %add_convert_fusion.1), channel_id=1, source_target_pairs={{0,1},{1,0},{2,3},{3,2},{4,5},{5,4},{6,7},{7,6},{8,9},{9,8},{10,11... | collective-permute-start | bytes 221192 | tf_op jit(solution)/shard_map/reduce/ppermute | solution.py:284
  93.9 4.7 %collective-permute-start.10 = (bf16[128,256]{1,0:T(8,128)(2,1)S(1)}, bf16[128,256]{1,0:T(8,128)(2,1)S(1)}, u32[]{:S(2)}, u32[]{:S(2)}) collective-permute-start(bf16[128,256]{1,0:T(8,128)(2,1)S(1)} %get-tuple-element.28), channel_id=1, source_target_pairs={{0,128},{32,160},{64,192},{96,224},{128,0},{160,32},{192,64},{224,... | collective-permute-start | bytes 196616 | tf_op jit(solution)/shard_map/reduce/ppermute | solution.py:380
  95.4 3.2 %collective-permute-start.9 = (bf16[128,256]{1,0:T(8,128)(2,1)S(1)}, bf16[128,256]{1,0:T(8,128)(2,1)S(1)}, u32[]{:S(2)}, u32[]{:S(2)}) collective-permute-start(bf16[128,256]{1,0:T(8,128)(2,1)S(1)} %get-tuple-element.28), channel_id=1, source_target_pairs={{0,64},{32,96},{64,0},{96,32},{128,192},{160,224},{192,128},{224,1... | collective-permute-start | bytes 196616 | tf_op jit(solution)/shard_map/reduce/ppermute | solution.py:380
  95.4 4.3 %collective-permute-start.11 = (bf16[128,256]{1,0:T(8,128)(2,1)S(1)}, bf16[128,256]{1,0:T(8,128)(2,1)S(1)}, u32[]{:S(2)}, u32[]{:S(2)}) collective-permute-start(bf16[128,256]{1,0:T(8,128)(2,1)S(1)} %get-tuple-element.28), channel_id=1, source_target_pairs={{0,192},{32,224},{64,128},{96,160},{128,64},{160,96},{192,0},{224,... | collective-permute-start | bytes 196616 | tf_op jit(solution)/shard_map/reduce/ppermute | solution.py:380
  99.8 7.5 %collective-permute-start.12 = (bf16[4,128,256]{2,1,0:T(8,128)(2,1)S(1)}, bf16[4,128,256]{2,1,0:T(8,128)(2,1)S(1)}, u32[]{:S(2)}, u32[]{:S(2)}) collective-permute-start(bf16[4,128,256]{2,1,0:T(8,128)(2,1)S(1)} %pad_maximum_fusion.same_core), channel_id=1, source_target_pairs={{0,32},{32,0},{64,96},{96,64},{128,160},{160,128},{192,224},{224,1... | collective-permute-start | bytes 786440 | tf_op jit(solution)/shard_map/reduce/ppermute | solution.py:382

commit v7 on v5

--- a/solution.py
+++ b/solution.py
@@ -337,6 +337,10 @@
     return lax.optimization_barrier(got[0].astype(BF))
 
 
+def near(x):
+    return pltpu.with_memory_space_constraint(x, pltpu.VMEM)
+
+
 def ring(axis, step):
     size = lax.axis_size(axis)
     return [(i, (i + step) % size) for i in range(size)]
@@ -352,7 +356,7 @@
     base = cells * members
     shard = 4 * width // parts
     grid = (lax.axis_size("row"), lax.axis_size("col"))
-    params = pltpu.CompilerParams(vmem_limit_bytes=60 * 1024 * 1024)
+    params = pltpu.CompilerParams(vmem_limit_bytes=40 * 1024 * 1024)
     smem = pl.BlockSpec(memory_space=pltpu.SMEM)
     vmem = pl.BlockSpec(memory_space=pltpu.VMEM)
     split = jnp.asarray(split_matrix(parts, members, cols), BF)
@@ -373,9 +377,9 @@
         send = pl.pallas_call(
             functools.partial(pack_kernel, grid[1]),
             in_specs=[smem] + [vmem] * 5,
-            out_shape=jax.ShapeDtypeStruct((parts, base + rows * line, width), BF),
+            out_shape=pltpu.VMEM((parts, base + rows * line, width), BF),
             compiler_params=params,
-        )(place, fields, cotangent, got, split, halo)
+        )(place, fields, cotangent, near(got), split, halo)
     with jax.named_scope("to_cells"):
         recv = lax.all_to_all(send, "mem", 0, 0)
     with jax.named_scope("halo_rows"):
@@ -385,20 +389,20 @@
         below = lax.ppermute(top, "row", ring("row", -1))
 
     with jax.named_scope("forward"):
-        token = jax.ShapeDtypeStruct((tokens, width), BF)
-        token_f = jax.ShapeDtypeStruct((tokens, width), F32)
+        token = pltpu.VMEM((tokens, width), BF)
+        token_f = pltpu.VMEM((tokens, width), F32)
         mats = [pltpu.VMEM((cells, width, width), BF), pltpu.VMEM((cells, width, width), BF)]
         kept = pl.pallas_call(
             functools.partial(forward_kernel, members),
             out_shape=(token, token, token, token, token_f, token, token),
             scratch_shapes=[pltpu.VMEM((tokens, width), F32)] + mats,
             compiler_params=params,
-        )(recv, gain, w_query, w_key, w_value, w_out, gather8, headsum)
+        )(near(recv), gain, w_query, w_key, w_value, w_out, gather8, headsum)
     with jax.named_scope("backward"):
         back = pl.pallas_call(
             functools.partial(backward_kernel, rows, per, members, grid[0]),
             in_specs=[smem] + [vmem] * 19,
-            out_shape=jax.ShapeDtypeStruct((parts, base + shard + 16, width), BF),
+            out_shape=pltpu.VMEM((parts, base + shard + 16, width), BF),
             scratch_shapes=[
                 pltpu.VMEM(((rows + 2) * (per + 2), members * parts, width), F32),
                 pltpu.VMEM((tokens, width), F32),
@@ -407,10 +411,10 @@
             compiler_params=params,
         )(
             place,
-            recv,
-            above,
-            below,
-            *kept,
+            near(recv),
+            near(above),
+            near(below),
+            *[near(x) for x in kept],
             gain,
             mix_kernel,
             w_query,
@@ -430,12 +434,13 @@
             unpack_kernel,
             out_shape=jax.ShapeDtypeStruct(fields.shape, BF),
             compiler_params=params,
-        )(landed, split)
+        )(near(landed), split)
 
     with jax.named_scope("reduce"):
         total = meet(total, "row", (1, 2, 3))
         total = meet(total, "col", (2, 4, 6))
         total = meet(total, "col", (1,))
+        total, grad_fields = lax.optimization_barrier((total, grad_fields))
         piece = total[:shard]
         same_core = jnp.stack([piece] + [lax.ppermute(piece, "mem", partner("mem", k)) for k in (2, 4, 6)])
         same_core = lax.optimization_barrier(same_core)
@@ -450,7 +455,7 @@
             in_specs=[smem] + [vmem] * 3,
             out_shape=(square,) * 4 + (jax.ShapeDtypeStruct((3, 3, width), F32), jax.ShapeDtypeStruct((1, width), F32)),
             compiler_params=params,
-        )(own, same_core, other_core, total)
+        )(own, near(same_core), near(other_core), near(total))
     return (grad_fields, grads[5].reshape(width)) + tuple(grads[:5])
 
 

time: 118 us -> 109 us (0.924)
  Pallas kernels: 19 us -> 10.8 us
    pallas_call x1, Pallas kernels: 7.13 us -> 4.78 us  [local(): pl.pallas_call(functools.partial(backward_kernel, rows, per, members, gri...]
    pallas_call x1, Pallas kernels: 5.1 us -> 3.04 us  [local(): pl.pallas_call(functools.partial(forward_kernel, members), out_shape=(tok...]
    pallas_call x1, Pallas kernels: 2.55 us -> 0.96 us  [local(): pl.pallas_call(functools.partial(pack_kernel, grid[1]), in_specs=[smem] +...]
    unnamed x16 -> x26, local copies, waits for them, and re-layouts: 2.57 us -> 2.75 us
  transfers between devices with their start and end apart: 14 -> 14, of which waited for: 9 -> 10; matrix products, arithmetic and copies ran while one was open for 1% -> 0% of each run, Pallas kernels for 6% -> 4%
where the time goes in v7:
time: 109 us
  blocking collectives  34.3 us (31%)
  starting transfers between devices  30.5 us (28%)
  waiting for transfers between devices  27.5 us (25%)
  Pallas kernels  10.8 us (10%)
  local copies, waits for them, and re-layouts  3.79 us (3%)
    all_to_all x1, blocking collectives, local(): recv = lax.all_to_all(send, 'mem', 0, 0)  17.3 us
    all_to_all x1, blocking collectives, local(): landed = lax.all_to_all(back, 'mem', 0, 0)  17 us
    ppermute x7, waiting for transfers between devices, meet(): lax.ppermute(values, axis, partner(axis, k))  14.8 us
    all_to_all x1, starting transfers between devices, local(): got = lax.all_to_all(jnp.where(to_right, last, first), 'col', 0, 0)  11.8 us
    all_to_all x1, waiting for transfers between devices, local(): got = lax.all_to_all(jnp.where(to_right, last, first), 'col', 0, 0)  9.03 us
    ppermute x7, starting transfers between devices, meet(): lax.ppermute(values, axis, partner(axis, k))  7.54 us
    pallas_call x1, Pallas kernels, local(): pl.pallas_call(functools.partial(backward_kernel, rows, per, members, gri...  4.78 us
    ppermute x1, starting transfers between devices, local(): other_core = lax.ppermute(same_core, 'mem', partner('mem', 1))  4.48 us
  transfers between devices with their start and end apart: 14, of which 10 were waited for; matrix products, arithmetic and copies ran while one was open for 0% of the time, Pallas kernels for 4%

profile of v7, /device:TPU:1, one launch (start us, length us, event | category | flops | bytes accessed | tf_op | source)
XLA Modules:
  0.0 108.7 jit_solution(926053031083663798)
XLA Ops:
  0.6 0.0 copy-start.7
  0.7 1.0 slice_reduce_fusion.2
  1.7 0.7 broadcast_select_fusion
  2.4 11.8 %all-to-all-start = ((bf16[8,16,256]{2,1,0:T(8,128)(2,1)}), bf16[8,16,256]{2,1,0:T(8,128)(2,1)S(1)}, u32[]{:S(2)}, u32[]{:S(2)}) async-start(bf16[8,16,256]{2,1,0:T(8,128)(2,1)} %broadcast_select_fusion), calls=%async_computation | async-start | bytes 131072 | tf_op jit(solution)/shard_map/halo_cols/all_to_all | solution.py:375
  14.2 0.1 pad_add_fusion.place
  14.3 9.0 %all-to-all-done.got = bf16[8,16,256]{2,1,0:T(8,128)(2,1)S(1)} async-done(((bf16[8,16,256]{2,1,0:T(8,128)(2,1)}), bf16[8,16,256]{2,1,0:T(8,128)(2,1)S(1)}, u32[]{:S(2)}, u32[]{:S(2)}) %all-to-all-start) | async-done | bytes 65568 | tf_op jit(solution)/shard_map/halo_cols/all_to_all | solution.py:375
  23.3 0.0 copy-done.9
  23.3 1.1 copy-done
  24.4 0.9 copy-done.8
  25.3 1.0 pack.1
  26.3 0.0 copy-start.4
  26.3 0.0 copy-start.5
  26.3 0.0 copy-start.6
  26.3 17.3 %all_to_all.15.recv = bf16[8,160,256]{2,1,0:T(8,128)(2,1)S(1)} all-to-all(bf16[8,160,256]{2,1,0:T(8,128)(2,1)S(1)} %pack.1), channel_id=1, replica_groups=mesh['mem'=8,'row'=4,'col'=8] {'mem'}, dimensions={0} | all-to-all | bytes 1310720 | tf_op jit(solution)/shard_map/to_cells/all_to_all | solution.py:384
  43.6 0.8 collective-permute-start
  44.4 2.5 %collective-permute-start.1 = (bf16[192,256]{1,0:T(8,128)(2,1)S(1)}, bf16[192,256]{1,0:T(8,128)(2,1)S(1)}, u32[]{:S(2)}, u32[]{:S(2)}) collective-permute-start(bf16[192,256]{1,0:T(8,128)(2,1)S(1)} %bitcast.14), channel_id=1, source_target_pairs={{0,24},{8,0},{16,8},{24,16},{1,25},{9,1},{17,9},{25,17},{2,26},{10... | collective-permute-start | bytes 294920 | tf_op jit(solution)/shard_map/halo_rows/ppermute | solution.py:389
  47.0 0.0 copy-start.10
  47.0 3.0 %forward.1 = (bf16[512,256]{1,0:T(8,128)(2,1)S(1)}, bf16[512,256]{1,0:T(8,128)(2,1)S(1)}, bf16[512,256]{1,0:T(8,128)(2,1)S(1)}, bf16[512,256]{1,0:T(8,128)(2,1)S...) custom-call(bf16[8,160,256]{2,1,0:T(8,128)(2,1)S(1)} %all_to_all.15.recv, ...), custom_call_target="tpu_custom_call" | custom-call | tf_op jit(solution)/shard_map/forward/pallas_call | solution.py:395
  50.0 0.0 collective-permute-done.above
  50.1 0.0 collective-permute-done.1.below
  50.1 0.7 copy-done.11
  50.8 4.8 %backward.1 = bf16[8,208,256]{2,1,0:T(8,128)(2,1)S(1)} custom-call(s32[2]{0:T(128)S(1)} %pad_add_fusion.place, bf16[8,160,256]{2,1,0:T(8,128)(2,1)S(1)} %all_to_all.15.recv, bf16[192,256]{1,0:T(8,128)(2,1)S(1)} %collective-permute-done.above, bf16[192,256]{1,0:T(8,128)(2,1)S(1)} %collective-permute-done.1.below, ...), custom_call_target="tpu_custom_call" | custom-call | tf_op jit(solution)/shard_map/backward/pallas_call | solution.py:402
  55.5 17.0 %all_to_all.16.recv = bf16[8,208,256]{2,1,0:T(8,128)(2,1)S(1)} all-to-all(bf16[8,208,256]{2,1,0:T(8,128)(2,1)S(1)} %backward.1), channel_id=1, replica_groups=mesh['mem'=8,'row'=4,'col'=8] {'mem'}, dimensions={0} | all-to-all | bytes 1703936 | tf_op jit(solution)/shard_map/to_members/all_to_all | solution.py:429
  72.6 0.1 slice_reduce_fusion
  72.6 2.4 %collective-permute-start.4 = (bf16[144,256]{1,0:T(8,128)(2,1)S(1)}, bf16[144,256]{1,0:T(8,128)(2,1)S(1)}, u32[]{:S(2)}, u32[]{:S(2)}) collective-permute-start(bf16[144,256]{1,0:T(8,128)(2,1)S(1)} %slice_reduce_fusion), channel_id=1, source_target_pairs={{0,24},{8,16},{16,8},{24,0},{1,25},{9,17},{17,9},{25,1},{2,26},{10... | collective-permute-start | bytes 221192 | tf_op jit(solution)/shard_map/reduce/ppermute | solution.py:333
  75.1 0.0 collective-permute-start.3
  75.1 1.2 %collective-permute-start.2 = (bf16[144,256]{1,0:T(8,128)(2,1)S(1)}, bf16[144,256]{1,0:T(8,128)(2,1)S(1)}, u32[]{:S(2)}, u32[]{:S(2)}) collective-permute-start(bf16[144,256]{1,0:T(8,128)(2,1)S(1)} %slice_reduce_fusion), channel_id=1, source_target_pairs={{0,8},{8,0},{16,24},{24,16},{1,9},{9,1},{17,25},{25,17},{2,10},{10... | collective-permute-start | bytes 221192 | tf_op jit(solution)/shard_map/reduce/ppermute | solution.py:333
  76.3 1.6 %collective-permute-done.4 = bf16[144,256]{1,0:T(8,128)(2,1)S(1)} collective-permute-done((bf16[144,256]{1,0:T(8,128)(2,1)S(1)}, bf16[144,256]{1,0:T(8,128)(2,1)S(1)}, u32[]{:S(2)}, u32[]{:S(2)}) %collective-permute-start.4) | collective-permute-done | bytes 73760 | tf_op jit(solution)/shard_map/reduce/ppermute | solution.py:333
  77.9 4.3 %collective-permute-done.3 = bf16[144,256]{1,0:T(8,128)(2,1)S(1)} collective-permute-done((bf16[144,256]{1,0:T(8,128)(2,1)S(1)}, bf16[144,256]{1,0:T(8,128)(2,1)S(1)}, u32[]{:S(2)}, u32[]{:S(2)}) %collective-permute-start.3) | collective-permute-done | bytes 73760 | tf_op jit(solution)/shard_map/reduce/ppermute | solution.py:333
  82.1 0.0 collective-permute-done.2
  82.2 1.0 collective-permute-start.7
  83.2 1.2 %collective-permute-start.6 = (bf16[144,256]{1,0:T(8,128)(2,1)S(1)}, bf16[144,256]{1,0:T(8,128)(2,1)S(1)}, u32[]{:S(2)}, u32[]{:S(2)}) collective-permute-start(bf16[144,256]{1,0:T(8,128)(2,1)S(1)} %add_convert_fusion.2), channel_id=1, source_target_pairs={{0,4},{1,5},{2,6},{3,7},{4,0},{5,1},{6,2},{7,3},{8,12},{9,13},{10,... | collective-permute-start | bytes 221192 | tf_op jit(solution)/shard_map/reduce/ppermute | solution.py:333
  84.3 1.2 %collective-permute-start.5 = (bf16[144,256]{1,0:T(8,128)(2,1)S(1)}, bf16[144,256]{1,0:T(8,128)(2,1)S(1)}, u32[]{:S(2)}, u32[]{:S(2)}) collective-permute-start(bf16[144,256]{1,0:T(8,128)(2,1)S(1)} %add_convert_fusion.2), channel_id=1, source_target_pairs={{0,2},{1,3},{2,0},{3,1},{4,6},{5,7},{6,4},{7,5},{8,10},{9,11},{10,... | collective-permute-start | bytes 221192 | tf_op jit(solution)/shard_map/reduce/ppermute | solution.py:333
  85.5 1.2 %collective-permute-done.7 = bf16[144,256]{1,0:T(8,128)(2,1)S(1)} collective-permute-done((bf16[144,256]{1,0:T(8,128)(2,1)S(1)}, bf16[144,256]{1,0:T(8,128)(2,1)S(1)}, u32[]{:S(2)}, u32[]{:S(2)}) %collective-permute-start.7) | collective-permute-done | bytes 73760 | tf_op jit(solution)/shard_map/reduce/ppermute | solution.py:333
  86.7 1.3 %collective-permute-done.6 = bf16[144,256]{1,0:T(8,128)(2,1)S(1)} collective-permute-done((bf16[144,256]{1,0:T(8,128)(2,1)S(1)}, bf16[144,256]{1,0:T(8,128)(2,1)S(1)}, u32[]{:S(2)}, u32[]{:S(2)}) %collective-permute-start.6) | collective-permute-done | bytes 73760 | tf_op jit(solution)/shard_map/reduce/ppermute | solution.py:333
  88.0 0.7 collective-permute-done.5
  88.7 0.6 collective-permute-start.8
  89.3 1.0 unpack.1
  90.3 5.8 %collective-permute-done.8 = bf16[144,256]{1,0:T(8,128)(2,1)S(1)} collective-permute-done((bf16[144,256]{1,0:T(8,128)(2,1)S(1)}, bf16[144,256]{1,0:T(8,128)(2,1)S(1)}, u32[]{:S(2)}, u32[]{:S(2)}) %collective-permute-start.8) | collective-permute-done | bytes 73760 | tf_op jit(solution)/shard_map/reduce/ppermute | solution.py:333
  96.1 0.7 collective-permute-start.10
  96.8 0.8 collective-permute-start.9
  97.6 1.8 %collective-permute-start.11 = (bf16[128,256]{1,0:T(8,128)(2,1)S(1)}, bf16[128,256]{1,0:T(8,128)(2,1)S(1)}, u32[]{:S(2)}, u32[]{:S(2)}) collective-permute-start(bf16[128,256]{1,0:T(8,128)(2,1)S(1)} %get-tuple-element.42), channel_id=1, source_target_pairs={{0,192},{32,224},{64,128},{96,160},{128,64},{160,96},{192,0},{224,... | collective-permute-start | bytes 196616 | tf_op jit(solution)/shard_map/reduce/ppermute | solution.py:445
  99.4 1.4 %collective-permute-done.10 = bf16[128,256]{1,0:T(8,128)(2,1)S(1)} collective-permute-done((bf16[128,256]{1,0:T(8,128)(2,1)S(1)}, bf16[128,256]{1,0:T(8,128)(2,1)S(1)}, u32[]{:S(2)}, u32[]{:S(2)}) %collective-permute-start.10) | collective-permute-done | bytes 65568 | tf_op jit(solution)/shard_map/reduce/ppermute | solution.py:445
  100.8 0.0 collective-permute-done.9
  100.8 1.2 %collective-permute-done.11 = bf16[128,256]{1,0:T(8,128)(2,1)S(1)} collective-permute-done((bf16[128,256]{1,0:T(8,128)(2,1)S(1)}, bf16[128,256]{1,0:T(8,128)(2,1)S(1)}, u32[]{:S(2)}, u32[]{:S(2)}) %collective-permute-start.11) | collective-permute-done | bytes 65568 | tf_op jit(solution)/shard_map/reduce/ppermute | solution.py:445
  102.0 4.5 %collective-permute-start.12 = (bf16[4,128,256]{2,1,0:T(8,128)(2,1)S(1)}, bf16[4,128,256]{2,1,0:T(8,128)(2,1)S(1)}, u32[]{:S(2)}, u32[]{:S(2)}) collective-permute-start(bf16[4,128,256]{2,1,0:T(8,128)(2,1)S(1)} %pad_maximum_fusion.same_core), channel_id=1, source_target_pairs={{0,32},{32,0},{64,96},{96,64},{128,160},{160,128},{192,224},{224,1... | collective-permute-start | bytes 786440 | tf_op jit(solution)/shard_map/reduce/ppermute | solution.py:447
  106.5 1.2 %collective-permute-done.12.other_core = bf16[4,128,256]{2,1,0:T(8,128)(2,1)S(1)} collective-permute-done((bf16[4,128,256]{2,1,0:T(8,128)(2,1)S(1)}, bf16[4,128,256]{2,1,0:T(8,128)(2,1)S(1)}, u32[]{:S(2)}, u32[]{:S(2)}) %collective-permute-start.12) | collective-permute-done | bytes 262176 | tf_op jit(solution)/shard_map/reduce/ppermute | solution.py:447
  107.6 1.0 finish.1
  (26 shorter events, 0.2 us)
Async XLA Ops:
  0.6 22.7 %copy-start.7 = (bf16[4,4,32,256]{3,2,1,0:T(8,128)(2,1)S(1)}, bf16[4,4,32,256]{3,2,1,0:T(8,128)(2,1)}, u32[]{:S(2)}) copy-start(bf16[4,4,32,256]{3,2,1,0:T(8,128)(2,1)} %cot.1) | copy-start | bytes 786436
  2.4 20.9 %copy-start.9 = (bf16[128,128]{1,0:T(8,128)(2,1)S(1)}, bf16[128,128]{1,0:T(8,128)(2,1)}, u32[]{:S(2)}) copy-start(bf16[128,128]{1,0:T(8,128)(2,1)} %constant.27.clone.split) | copy-start | bytes 98308
  2.4 20.9 %all-to-all-start = ((bf16[8,16,256]{2,1,0:T(8,128)(2,1)}), bf16[8,16,256]{2,1,0:T(8,128)(2,1)S(1)}, u32[]{:S(2)}, u32[]{:S(2)}) async-start(bf16[8,16,256]{2,1,0:T(8,128)(2,1)} %broadcast_select_fusion), calls=%async_computation | async-start | bytes 131072 | tf_op jit(solution)/shard_map/halo_cols/all_to_all | solution.py:375
  23.3 1.1 copy-start
  24.4 0.9 copy-start.8
  26.3 20.7 %copy-start.4 = (bf16[256,256]{1,0:T(8,128)(2,1)S(1)}, bf16[256,256]{1,0:T(8,128)(2,1)}, u32[]{:S(2)}) copy-start(bf16[256,256]{1,0:T(8,128)(2,1)} %wo.3) | copy-start | bytes 393220
  26.3 20.7 %copy-start.5 = (bf16[256,256]{1,0:T(8,128)(2,1)S(1)}, bf16[256,256]{1,0:T(8,128)(2,1)}, u32[]{:S(2)}) copy-start(bf16[256,256]{1,0:T(8,128)(2,1)} %constant.31.clone.headsum) | copy-start | bytes 393220
  26.3 20.7 %copy-start.6 = (bf16[256,256]{1,0:T(8,128)(2,1)S(1)}, bf16[256,256]{1,0:T(8,128)(2,1)}, u32[]{:S(2)}) copy-start(bf16[256,256]{1,0:T(8,128)(2,1)} %constant.29.clone.gather8) | copy-start | bytes 393220
  43.6 3.4 %copy-start.1 = (bf16[256,256]{1,0:T(8,128)(2,1)S(1)}, bf16[256,256]{1,0:T(8,128)(2,1)}, u32[]{:S(2)}) copy-start(bf16[256,256]{1,0:T(8,128)(2,1)} %wq.3) | copy-start | bytes 393220
  43.6 3.4 %copy-start.2 = (bf16[256,256]{1,0:T(8,128)(2,1)S(1)}, bf16[256,256]{1,0:T(8,128)(2,1)}, u32[]{:S(2)}) copy-start(bf16[256,256]{1,0:T(8,128)(2,1)} %wk.3) | copy-start | bytes 393220
  43.6 3.4 %copy-start.3 = (bf16[256,256]{1,0:T(8,128)(2,1)S(1)}, bf16[256,256]{1,0:T(8,128)(2,1)}, u32[]{:S(2)}) copy-start(bf16[256,256]{1,0:T(8,128)(2,1)} %wv.3) | copy-start | bytes 393220
  43.6 6.4 %collective-permute-start = (bf16[192,256]{1,0:T(8,128)(2,1)S(1)}, bf16[192,256]{1,0:T(8,128)(2,1)S(1)}, u32[]{:S(2)}, u32[]{:S(2)}) collective-permute-start(bf16[192,256]{1,0:T(8,128)(2,1)S(1)} %bitcast.15), channel_id=1, source_target_pairs={{0,8},{8,16},{16,24},{24,0},{1,9},{9,17},{17,25},{25,1},{2,10},{10... | collective-permute-start | bytes 294920 | tf_op jit(solution)/shard_map/halo_rows/ppermute | solution.py:388
  44.4 2.6 %copy-start.12 = (f32[256]{0:T(256)S(1)}, f32[256]{0:T(256)}, u32[]{:S(2)}) copy-start(f32[256]{0:T(256)} %param.14) | copy-start | bytes 3076
  44.4 5.6 %collective-permute-start.1 = (bf16[192,256]{1,0:T(8,128)(2,1)S(1)}, bf16[192,256]{1,0:T(8,128)(2,1)S(1)}, u32[]{:S(2)}, u32[]{:S(2)}) collective-permute-start(bf16[192,256]{1,0:T(8,128)(2,1)S(1)} %bitcast.14), channel_id=1, source_target_pairs={{0,24},{8,0},{16,8},{24,16},{1,25},{9,1},{17,9},{25,17},{2,26},{10... | collective-permute-start | bytes 294920 | tf_op jit(solution)/shard_map/halo_rows/ppermute | solution.py:389
  47.0 3.1 %copy-start.10 = (bf16[192,192]{1,0:T(8,128)(2,1)S(1)}, bf16[192,192]{1,0:T(8,128)(2,1)}, u32[]{:S(2)}) copy-start(bf16[192,192]{1,0:T(8,128)(2,1)} %constant.30.clone.gather6) | copy-start | bytes 221188
  50.0 0.7 copy-start.11
  72.6 5.2 %collective-permute-start.4 = (bf16[144,256]{1,0:T(8,128)(2,1)S(1)}, bf16[144,256]{1,0:T(8,128)(2,1)S(1)}, u32[]{:S(2)}, u32[]{:S(2)}) collective-permute-start(bf16[144,256]{1,0:T(8,128)(2,1)S(1)} %slice_reduce_fusion), channel_id=1, source_target_pairs={{0,24},{8,16},{16,8},{24,0},{1,25},{9,17},{17,9},{25,1},{2,26},{10... | collective-permute-start | bytes 221192 | tf_op jit(solution)/shard_map/reduce/ppermute | solution.py:333
  75.1 7.1 %collective-permute-start.3 = (bf16[144,256]{1,0:T(8,128)(2,1)S(1)}, bf16[144,256]{1,0:T(8,128)(2,1)S(1)}, u32[]{:S(2)}, u32[]{:S(2)}) collective-permute-start(bf16[144,256]{1,0:T(8,128)(2,1)S(1)} %slice_reduce_fusion), channel_id=1, source_target_pairs={{0,16},{8,24},{16,0},{24,8},{1,17},{9,25},{17,1},{25,9},{2,18},{10... | collective-permute-start | bytes 221192 | tf_op jit(solution)/shard_map/reduce/ppermute | solution.py:333
  75.1 7.1 %collective-permute-start.2 = (bf16[144,256]{1,0:T(8,128)(2,1)S(1)}, bf16[144,256]{1,0:T(8,128)(2,1)S(1)}, u32[]{:S(2)}, u32[]{:S(2)}) collective-permute-start(bf16[144,256]{1,0:T(8,128)(2,1)S(1)} %slice_reduce_fusion), channel_id=1, source_target_pairs={{0,8},{8,0},{16,24},{24,16},{1,9},{9,1},{17,25},{25,17},{2,10},{10... | collective-permute-start | bytes 221192 | tf_op jit(solution)/shard_map/reduce/ppermute | solution.py:333
  82.2 4.5 %collective-permute-start.7 = (bf16[144,256]{1,0:T(8,128)(2,1)S(1)}, bf16[144,256]{1,0:T(8,128)(2,1)S(1)}, u32[]{:S(2)}, u32[]{:S(2)}) collective-permute-start(bf16[144,256]{1,0:T(8,128)(2,1)S(1)} %add_convert_fusion.2), channel_id=1, source_target_pairs={{0,6},{1,7},{2,4},{3,5},{4,2},{5,3},{6,0},{7,1},{8,14},{9,15},{10,... | collective-permute-start | bytes 221192 | tf_op jit(solution)/shard_map/reduce/ppermute | solution.py:333
  83.2 4.8 %collective-permute-start.6 = (bf16[144,256]{1,0:T(8,128)(2,1)S(1)}, bf16[144,256]{1,0:T(8,128)(2,1)S(1)}, u32[]{:S(2)}, u32[]{:S(2)}) collective-permute-start(bf16[144,256]{1,0:T(8,128)(2,1)S(1)} %add_convert_fusion.2), channel_id=1, source_target_pairs={{0,4},{1,5},{2,6},{3,7},{4,0},{5,1},{6,2},{7,3},{8,12},{9,13},{10,... | collective-permute-start | bytes 221192 | tf_op jit(solution)/shard_map/reduce/ppermute | solution.py:333
  84.3 4.4 %collective-permute-start.5 = (bf16[144,256]{1,0:T(8,128)(2,1)S(1)}, bf16[144,256]{1,0:T(8,128)(2,1)S(1)}, u32[]{:S(2)}, u32[]{:S(2)}) collective-permute-start(bf16[144,256]{1,0:T(8,128)(2,1)S(1)} %add_convert_fusion.2), channel_id=1, source_target_pairs={{0,2},{1,3},{2,0},{3,1},{4,6},{5,7},{6,4},{7,5},{8,10},{9,11},{10,... | collective-permute-start | bytes 221192 | tf_op jit(solution)/shard_map/reduce/ppermute | solution.py:333
  88.7 7.3 %collective-permute-start.8 = (bf16[144,256]{1,0:T(8,128)(2,1)S(1)}, bf16[144,256]{1,0:T(8,128)(2,1)S(1)}, u32[]{:S(2)}, u32[]{:S(2)}) collective-permute-start(bf16[144,256]{1,0:T(8,128)(2,1)S(1)} %add_convert_fusion.1), channel_id=1, source_target_pairs={{0,1},{1,0},{2,3},{3,2},{4,5},{5,4},{6,7},{7,6},{8,9},{9,8},{10,11... | collective-permute-start | bytes 221192 | tf_op jit(solution)/shard_map/reduce/ppermute | solution.py:333
  96.1 4.7 %collective-permute-start.10 = (bf16[128,256]{1,0:T(8,128)(2,1)S(1)}, bf16[128,256]{1,0:T(8,128)(2,1)S(1)}, u32[]{:S(2)}, u32[]{:S(2)}) collective-permute-start(bf16[128,256]{1,0:T(8,128)(2,1)S(1)} %get-tuple-element.42), channel_id=1, source_target_pairs={{0,128},{32,160},{64,192},{96,224},{128,0},{160,32},{192,64},{224,... | collective-permute-start | bytes 196616 | tf_op jit(solution)/shard_map/reduce/ppermute | solution.py:445
  96.8 4.0 %collective-permute-start.9 = (bf16[128,256]{1,0:T(8,128)(2,1)S(1)}, bf16[128,256]{1,0:T(8,128)(2,1)S(1)}, u32[]{:S(2)}, u32[]{:S(2)}) collective-permute-start(bf16[128,256]{1,0:T(8,128)(2,1)S(1)} %get-tuple-element.42), channel_id=1, source_target_pairs={{0,64},{32,96},{64,0},{96,32},{128,192},{160,224},{192,128},{224,1... | collective-permute-start | bytes 196616 | tf_op jit(solution)/shard_map/reduce/ppermute | solution.py:445
  97.6 4.3 %collective-permute-start.11 = (bf16[128,256]{1,0:T(8,128)(2,1)S(1)}, bf16[128,256]{1,0:T(8,128)(2,1)S(1)}, u32[]{:S(2)}, u32[]{:S(2)}) collective-permute-start(bf16[128,256]{1,0:T(8,128)(2,1)S(1)} %get-tuple-element.42), channel_id=1, source_target_pairs={{0,192},{32,224},{64,128},{96,160},{128,64},{160,96},{192,0},{224,... | collective-permute-start | bytes 196616 | tf_op jit(solution)/shard_map/reduce/ppermute | solution.py:445
  102.0 5.6 %collective-permute-start.12 = (bf16[4,128,256]{2,1,0:T(8,128)(2,1)S(1)}, bf16[4,128,256]{2,1,0:T(8,128)(2,1)S(1)}, u32[]{:S(2)}, u32[]{:S(2)}) collective-permute-start(bf16[4,128,256]{2,1,0:T(8,128)(2,1)S(1)} %pad_maximum_fusion.same_core), channel_id=1, source_target_pairs={{0,32},{32,0},{64,96},{96,64},{128,160},{160,128},{192,224},{224,1... | collective-permute-start | bytes 786440 | tf_op jit(solution)/shard_map/reduce/ppermute | solution.py:447

commit v8 on v7

--- a/solution.py
+++ b/solution.py
@@ -33,27 +33,6 @@
     return out.reshape(parts * per * members, members * cols)
 
 
-def halo_matrices(parts, members, rows, cols):
-    per = cols // parts
-    edge = members * rows
-    mats = []
-    for pair in range(rows // 2):
-        out = np.zeros((parts, 2, per + 2, members, 2 * members * cols + 2 * edge), np.float32)
-        for j in range(parts):
-            for q in range(2):
-                for c in range(per + 2):
-                    for m in range(members):
-                        col = j * per + c - 1
-                        if 0 <= col < cols:
-                            src = (q * members + m) * cols + col
-                        else:
-                            side = 0 if col < 0 else 1
-                            src = 2 * members * cols + side * edge + m * rows + 2 * pair + q
-                        out[j, q, c, m, src] = 1
-        mats.append(out.reshape(-1, out.shape[-1]))
-    return np.stack(mats)
-
-
 def gather_matrix(parts, cells, members):
     out = np.zeros((cells, parts, members, parts, cells, members), np.float32)
     for s in range(parts):
@@ -63,29 +42,25 @@
     return out.reshape(cells * parts * members, -1)
 
 
-def masked(inside, x):
-    return jnp.where(inside, x, jnp.zeros_like(x))
-
-
-def pack_kernel(col_size, place, fields, cot, got, split, halo, send):
+def pack_kernel(fields, cot, split, send):
     members, rows, cols, width = fields.shape
     parts = send.shape[0]
     per = cols // parts * members
-    for r in range(rows):
-        tokens = fields[:, r].reshape(members * cols, width)
-        moved = dot(split[...], tokens).astype(BF).reshape(parts, per, width)
-        send[:, r * per : (r + 1) * per, :] = moved
-    base = rows * per
-    col = place[1]
-    sides = [
-        masked(col > 0, got[jnp.maximum(col - 1, 0)]),
-        masked(col < col_size - 1, got[jnp.minimum(col + 1, col_size - 1)]),
-    ]
-    step = 2 * (per + 2 * members)
-    for pair in range(rows // 2):
-        lines = [cot[:, 2 * pair + q].reshape(members * cols, width) for q in range(2)]
-        moved = dot(halo[pair], jnp.concatenate(lines + sides, axis=0)).astype(BF)
-        send[:, base + pair * step : base + (pair + 1) * step, :] = moved.reshape(parts, step, width)
+    for k, source in enumerate((fields, cot)):
+        for r in range(rows):
+            tokens = source[:, r].reshape(members * cols, width)
+            moved = dot(split[...], tokens).astype(BF).reshape(parts, per, width)
+            start = (k * rows + r) * per
+            send[:, start : start + per, :] = moved
+
+
+def order_kernel(members, recv, gather8, x_out, cot_out):
+    rows, per, all_members, width = cot_out.shape
+    cells = rows * per
+    for g in range(cells // 8):
+        x_out[g * 8 * all_members : (g + 1) * 8 * all_members, :] = regroup(recv, g * 8 * members, 8, members, gather8).astype(BF)
+        block = regroup(recv, (cells + g * 8) * members, 8, members, gather8).astype(BF)
+        cot_out[g * 8 // per : (g + 1) * 8 // per] = block.reshape(8 // per, per, all_members, width)
 
 
 def regroup(recv, start, count, members, matrix):
@@ -118,41 +93,32 @@
 
 
 def forward_kernel(
-    members,
-    recv,
+    cells,
+    x_in,
     gain,
     wq,
     wk,
     wv,
     wo,
-    gather8,
     headsum,
-    x_out,
     q_out,
-    k_out,
-    v_out,
     prob_out,
     att_out,
     mixed_out,
-    sums,
     mat_k,
     mat_v,
+    sums,
 ):
-    parts, _, width = recv.shape
+    tokens, width = x_in.shape
     scale = 1.0 / math.sqrt(width // HEADS)
-    all_members = parts * members
-    tokens = x_out.shape[0]
-    cells = tokens // all_members
-    x = jnp.concatenate([regroup(recv, g * 32, 8, members, gather8) for g in range(cells // 8)], axis=0)
-    x_out[...] = x.astype(BF)
+    all_members = tokens // cells
+    x = x_in[...].astype(F32)
     _, normed = norm(x)
     inputs = (normed * gain[...]).astype(BF)
     queries = dot(inputs, wq[...]).astype(BF)
     keys = dot(inputs, wk[...]).astype(BF)
     values = dot(inputs, wv[...]).astype(BF)
     q_out[...] = queries
-    k_out[...] = keys
-    v_out[...] = values
     expand_all(keys, mat_k)
     expand_all(values, mat_v)
     for c in range(cells):
@@ -181,21 +147,20 @@
 
 
 def backward_kernel(
-    tile_rows,
-    tile_cols,
-    members,
-    row_size,
+    sizes,
     place,
-    recv,
+    cot,
+    left,
+    right,
     above,
     below,
     x_in,
     q_in,
-    k_in,
-    v_in,
     prob_in,
     att_in,
     mixed_in,
+    mat_k,
+    mat_v,
     gain,
     mix,
     wq,
@@ -203,31 +168,39 @@
     wv,
     wo,
     gather8,
-    gather6,
     headsum,
     send,
     padded,
     sums,
-    mat_k,
-    mat_v,
 ):
-    parts, _, width = recv.shape
+    parts = send.shape[0]
+    tile_rows, tile_cols, all_members, width = cot.shape
+    members = all_members // parts
     head_dim = width // HEADS
     scale = 1.0 / math.sqrt(head_dim)
     cells = tile_rows * tile_cols
-    all_members = parts * members
     tokens = cells * all_members
     pad_cols = tile_cols + 2
-    pad_cells = (tile_rows + 2) * pad_cols
     base = cells * members
-    row = place[0]
-    top = dot(gather6[...], masked(row > 0, above[...]))
-    padded[:pad_cols] = top.reshape(pad_cols, all_members, width)
-    for g in range(tile_rows * pad_cols // 8):
-        block = regroup(recv, base + g * 8 * members, 8, members, gather8)
-        padded[pad_cols + g * 8 : pad_cols + (g + 1) * 8] = block.reshape(8, all_members, width)
-    bottom = dot(gather6[...], masked(row < row_size - 1, below[...]))
-    padded[pad_cells - pad_cols :] = bottom.reshape(pad_cols, all_members, width)
+    row, block = place[0], place[1]
+
+    def side(inside, x):
+        x = x.astype(F32)
+        return jnp.where(inside, x, jnp.zeros_like(x))
+
+    in_left, in_right = block > 0, block < sizes[1] - 1
+    edges = {0: (above, row > 0), tile_rows + 1: (below, row < sizes[0] - 1)}
+    for r in range(tile_rows + 2):
+        start = r * pad_cols
+        if r in edges:
+            source, inside = edges[r]
+            padded[start] = side(inside & in_left, source[0])
+            padded[start + 1 : start + 1 + tile_cols] = side(inside, source[1 : 1 + tile_cols])
+            padded[start + 1 + tile_cols] = side(inside & in_right, source[1 + tile_cols])
+        else:
+            padded[start] = side(in_left, left[r - 1])
+            padded[start + 1 : start + 1 + tile_cols] = cot[r - 1].astype(F32)
+            padded[start + 1 + tile_cols] = side(in_right, right[r - 1])
 
     def shifted(i, j):
         picked = [
@@ -236,8 +209,6 @@
         ]
         return jnp.concatenate(picked, axis=0).reshape(tokens, width)
 
-    expand_all(k_in[...], mat_k)
-    expand_all(v_in[...], mat_v)
     inv, normed = norm(x_in[...].astype(F32))
     inputs = (normed * gain[...]).astype(BF)
     mixed = mixed_in[...].astype(F32)
@@ -351,7 +322,6 @@
     parts = lax.axis_size("mem")
     per = cols // parts
     cells = rows * per
-    line = (per + 2) * members
     tokens = cells * members * parts
     base = cells * members
     shard = 4 * width // parts
@@ -360,61 +330,59 @@
     smem = pl.BlockSpec(memory_space=pltpu.SMEM)
     vmem = pl.BlockSpec(memory_space=pltpu.VMEM)
     split = jnp.asarray(split_matrix(parts, members, cols), BF)
-    halo = jnp.asarray(halo_matrices(parts, members, rows, cols), BF)
     gather8 = jnp.asarray(gather_matrix(parts, 8, members), BF)
-    gather6 = jnp.asarray(gather_matrix(parts, per + 2, members), BF)
     headsum = jnp.asarray(np.kron(np.eye(HEADS), np.ones((width // HEADS, width // HEADS))), BF)
     gain = norm_gain.reshape(1, width)
-    row, col = lax.axis_index("row"), lax.axis_index("col")
-    place = jnp.stack([row, col]).astype(jnp.int32)
-
-    with jax.named_scope("halo_cols"):
-        first = cotangent[:, :, 0].reshape(1, members * rows, width)
-        last = cotangent[:, :, cols - 1].reshape(1, members * rows, width)
-        to_right = (lax.iota(jnp.int32, grid[1]) == col + 1).reshape(grid[1], 1, 1)
-        got = lax.all_to_all(jnp.where(to_right, last, first), "col", 0, 0)
+    blocks = parts * grid[1]
+    place = jnp.stack([lax.axis_index("row"), lax.axis_index("col") * parts + lax.axis_index("mem")]).astype(jnp.int32)
+
     with jax.named_scope("pack"):
         send = pl.pallas_call(
-            functools.partial(pack_kernel, grid[1]),
-            in_specs=[smem] + [vmem] * 5,
-            out_shape=pltpu.VMEM((parts, base + rows * line, width), BF),
-            compiler_params=params,
-        )(place, fields, cotangent, near(got), split, halo)
+            pack_kernel,
+            out_shape=pltpu.VMEM((parts, 2 * base, width), BF),
+            compiler_params=params,
+        )(fields, cotangent, split)
     with jax.named_scope("to_cells"):
         recv = lax.all_to_all(send, "mem", 0, 0)
-    with jax.named_scope("halo_rows"):
-        top = recv[:, base : base + line].reshape(parts * line, width)
-        bottom = recv[:, base + (rows - 1) * line :].reshape(parts * line, width)
-        above = lax.ppermute(bottom, "row", ring("row", 1))
-        below = lax.ppermute(top, "row", ring("row", -1))
-
+    with jax.named_scope("order"):
+        x, cot = pl.pallas_call(
+            functools.partial(order_kernel, members),
+            out_shape=(pltpu.VMEM((tokens, width), BF), pltpu.VMEM((rows, per, parts * members, width), BF)),
+            compiler_params=params,
+        )(near(recv), gather8)
+    with jax.named_scope("halo_cols"):
+        flat = [b % parts * grid[1] + b // parts for b in range(blocks)]
+        up = list(zip(flat, flat[1:] + flat[:1]))
+        down = [(j, i) for i, j in up]
+        left = lax.ppermute(cot[:, per - 1], ("mem", "col"), up)
+        right = lax.ppermute(cot[:, 0], ("mem", "col"), down)
     with jax.named_scope("forward"):
         token = pltpu.VMEM((tokens, width), BF)
         token_f = pltpu.VMEM((tokens, width), F32)
-        mats = [pltpu.VMEM((cells, width, width), BF), pltpu.VMEM((cells, width, width), BF)]
+        mat = pltpu.VMEM((cells, width, width), BF)
         kept = pl.pallas_call(
-            functools.partial(forward_kernel, members),
-            out_shape=(token, token, token, token, token_f, token, token),
-            scratch_shapes=[pltpu.VMEM((tokens, width), F32)] + mats,
-            compiler_params=params,
-        )(near(recv), gain, w_query, w_key, w_value, w_out, gather8, headsum)
+            functools.partial(forward_kernel, cells),
+            out_shape=(token, token_f, token, token, mat, mat),
+            scratch_shapes=[pltpu.VMEM((tokens, width), F32)],
+            compiler_params=params,
+        )(near(x), gain, w_query, w_key, w_value, w_out, headsum)
+    with jax.named_scope("halo_rows"):
+        top, bottom = [jnp.concatenate([left[r : r + 1], cot[r], right[r : r + 1]], axis=0) for r in (0, rows - 1)]
+        above = lax.ppermute(bottom, "row", ring("row", 1))
+        below = lax.ppermute(top, "row", ring("row", -1))
     with jax.named_scope("backward"):
         back = pl.pallas_call(
-            functools.partial(backward_kernel, rows, per, members, grid[0]),
-            in_specs=[smem] + [vmem] * 19,
+            functools.partial(backward_kernel, (grid[0], blocks)),
+            in_specs=[smem] + [vmem] * 20,
             out_shape=pltpu.VMEM((parts, base + shard + 16, width), BF),
             scratch_shapes=[
                 pltpu.VMEM(((rows + 2) * (per + 2), members * parts, width), F32),
                 pltpu.VMEM((tokens, width), F32),
-            ]
-            + mats,
+            ],
             compiler_params=params,
         )(
             place,
-            near(recv),
-            near(above),
-            near(below),
-            *[near(x) for x in kept],
+            *[near(a) for a in (cot, left, right, above, below, x, *kept)],
             gain,
             mix_kernel,
             w_query,
@@ -422,7 +390,6 @@
             w_value,
             w_out,
             gather8,
-            gather6,
             headsum,
         )
     with jax.named_scope("to_members"):

time: 109 us -> 107 us (0.982)
  waiting for transfers between devices: 27.5 us -> 37.3 us
  blocking collectives: 34.3 us -> 27.5 us
  starting transfers between devices: 30.5 us -> 26.6 us
    all_to_all x1 -> x0, blocking collectives: 17.3 us -> none  [local(): recv = lax.all_to_all(send, 'mem', 0, 0)]
    all_to_all x1, blocking collectives: 17 us -> 27.5 us  [local(): landed = lax.all_to_all(back, 'mem', 0, 0)]
    ppermute x0 -> x2, waiting for transfers between devices: none -> 8.5 us  [the longest x1 6.65 us: local(): left = lax.ppermute(cot[:, per - 1], ('mem', 'col'), up)]
    all_to_all x1, starting transfers between devices: 11.8 us -> 6.77 us  [local(): recv = lax.all_to_all(send, 'mem', 0, 0)]
    ppermute x0 -> x2, starting transfers between devices: none -> 1.9 us  [the longest x1 0.95 us: local(): left = lax.ppermute(cot[:, per - 1], ('mem', 'col'), up)]
    pallas_call x3 -> x4, Pallas kernels: 8.78 us -> 8.86 us  [the longest x1 4.51 us: local(): pl.pallas_call(functools.partial(backward_kernel, (grid[0], blocks)), in_...]
    unnamed x26 -> x24, local copies, waits for them, and re-layouts: 2.75 us -> 2.78 us
  transfers between devices with their start and end apart: 14 -> 16, of which waited for: 10 -> 11; matrix products, arithmetic and copies ran while one was open for 0% -> 0% of each run, Pallas kernels for 4% -> 4%
where the time goes in v8:
time: 107 us; the launch traced here: 106 us
  waiting for transfers between devices  37.3 us (35%)
  blocking collectives  27.5 us (26%)
  starting transfers between devices  26.6 us (25%)
  Pallas kernels  10.8 us (10%)
  local copies, waits for them, and re-layouts  2.82 us (3%)
    all_to_all x1, blocking collectives, local(): landed = lax.all_to_all(back, 'mem', 0, 0)  27.5 us
    ppermute x7, waiting for transfers between devices, meet(): lax.ppermute(values, axis, partner(axis, k))  15.6 us
    all_to_all x1, waiting for transfers between devices, local(): recv = lax.all_to_all(send, 'mem', 0, 0)  9.5 us
    ppermute x7, starting transfers between devices, meet(): lax.ppermute(values, axis, partner(axis, k))  7.05 us
    all_to_all x1, starting transfers between devices, local(): recv = lax.all_to_all(send, 'mem', 0, 0)  6.77 us
    ppermute x1, waiting for transfers between devices, local(): left = lax.ppermute(cot[:, per - 1], ('mem', 'col'), up)  6.65 us
    pallas_call x1, Pallas kernels, local(): pl.pallas_call(functools.partial(backward_kernel, (grid[0], blocks)), in_...  4.51 us
    ppermute x1, starting transfers between devices, local(): other_core = lax.ppermute(same_core, 'mem', partner('mem', 1))  4.08 us
  transfers between devices with their start and end apart: 16, of which 11 were waited for; matrix products, arithmetic and copies ran while one was open for 0% of the time, Pallas kernels for 4%

profile of v8, /device:TPU:1, one launch (start us, length us, event | category | flops | bytes accessed | tf_op | source)
XLA Modules:
  0.0 106.3 jit_solution(16565114380799031468)
XLA Ops:
  0.6 0.0 copy-start
  0.6 0.0 copy-start.5
  0.7 1.0 copy-done.6
  1.7 0.9 copy-done.7
  2.7 0.8 copy-done.8
  3.4 1.1 %pack.1 = bf16[8,128,256]{2,1,0:T(8,128)(2,1)} custom-call(bf16[4,4,32,256]{3,2,1,0:T(8,128)(2,1)S(1)} %copy-done.6, bf16[4,4,32,256]{3,2,1,0:T(8,128)(2,1)S(1)} %copy-done.7, bf16[128,128]{1,0:T(8,128)(2,1)S(1)} %copy-done.8), custom_call_target="tpu_custom_call" | custom-call | tf_op jit(solution)/shard_map/pack/pallas_call | solution.py:340
  4.5 6.8 %all-to-all-start = ((bf16[8,128,256]{2,1,0:T(8,128)(2,1)}), bf16[8,128,256]{2,1,0:T(8,128)(2,1)S(1)}, u32[]{:S(2)}, u32[]{:S(2)}) async-start(bf16[8,128,256]{2,1,0:T(8,128)(2,1)} %pack.1), calls=%async_computation | async-start | bytes 1048576 | tf_op jit(solution)/shard_map/to_cells/all_to_all | solution.py:346
  11.3 9.5 %all-to-all-done.recv = bf16[8,128,256]{2,1,0:T(8,128)(2,1)S(1)} async-done(((bf16[8,128,256]{2,1,0:T(8,128)(2,1)}), bf16[8,128,256]{2,1,0:T(8,128)(2,1)S(1)}, u32[]{:S(2)}, u32[]{:S(2)}) %all-to-all-start) | async-done | bytes 524320 | tf_op jit(solution)/shard_map/to_cells/all_to_all | solution.py:346
  20.8 0.3 order.1
  21.1 0.9 collective-permute-start.1
  22.1 1.0 collective-permute-start
  23.0 1.9 %collective-permute-done.1.right = bf16[4,32,256]{2,1,0:T(8,128)(2,1)S(1)} collective-permute-done((bf16[4,32,256]{2,1,0:T(8,128)(2,1)S(1)}, bf16[4,32,256]{2,1,0:T(8,128)(2,1)S(1)}, u32[]{:S(2)}, u32[]{:S(2)}) %collective-permute-start.1) | collective-permute-done | bytes 65568 | tf_op jit(solution)/shard_map/halo_cols/ppermute | solution.py:358
  24.9 6.6 %collective-permute-done.left = bf16[4,32,256]{2,1,0:T(8,128)(2,1)S(1)} collective-permute-done((bf16[4,32,256]{2,1,0:T(8,128)(2,1)S(1)}, bf16[4,32,256]{2,1,0:T(8,128)(2,1)S(1)}, u32[]{:S(2)}, u32[]{:S(2)}) %collective-permute-start) | collective-permute-done | bytes 65568 | tf_op jit(solution)/shard_map/halo_cols/ppermute | solution.py:357
  31.6 0.8 collective-permute-start.2
  32.4 2.6 %collective-permute-start.3 = (bf16[6,32,256]{2,1,0:T(8,128)(2,1)S(1)}, bf16[6,32,256]{2,1,0:T(8,128)(2,1)S(1)}, u32[]{:S(2)}, u32[]{:S(2)}) collective-permute-start(bf16[6,32,256]{2,1,0:T(8,128)(2,1)S(1)} %pad_maximum_fusion.2), channel_id=1, source_target_pairs={{0,24},{8,0},{16,8},{24,16},{1,25},{9,1},{17,9},{25,17},{2,26},{10... | collective-permute-start | bytes 294920 | tf_op jit(solution)/shard_map/halo_rows/ppermute | solution.py:372
  35.0 0.1 pad_add_fusion.place
  35.1 0.0 copy-done.2
  35.1 3.0 %forward.1 = (bf16[512,256]{1,0:T(8,128)(2,1)S(1)}, f32[512,256]{1,0:T(8,128)S(1)}, bf16[512,256]{1,0:T(8,128)(2,1)S(1)}, bf16[512,256]{1,0:T(8,128)(2,1)S(1)}, ...) custom-call(bf16[512,256]{1,0:T(8,128)(2,1)S(1)} %get-tuple-element.24.x_in, f32[1,256]{1,0:T(1,128)S(1)} %bitcast.18, ...), custom_call_target="tpu_custom_call" | custom-call | tf_op jit(solution)/shard_map/forward/pallas_call | solution.py:363
  38.1 0.0 collective-permute-done.2.above
  38.1 0.0 collective-permute-done.3.below
  38.1 4.5 %backward.1 = bf16[8,208,256]{2,1,0:T(8,128)(2,1)S(1)} custom-call(s32[2]{0:T(128)S(1)} %pad_add_fusion.place, bf16[4,4,32,256]{3,2,1,0:T(8,128)(2,1)S(1)} %get-tuple-element.23.cot, bf16[4,32,256]{2,1,0:T(8,128)(2,1)S(1)} %collective-permute-done.left, bf16[4,32,256]{2,1,0:T(8,128)(2,1)S(1)} %collective-permute-done.1.right, ...), custom_call_target="tpu_custom_call" | custom-call | tf_op jit(solution)/shard_map/backward/pallas_call | solution.py:374
  42.6 0.0 copy-start.9
  42.6 27.5 %all_to_all.10.recv = bf16[8,208,256]{2,1,0:T(8,128)(2,1)S(1)} all-to-all(bf16[8,208,256]{2,1,0:T(8,128)(2,1)S(1)} %backward.1), channel_id=1, replica_groups=mesh['mem'=8,'row'=4,'col'=8] {'mem'}, dimensions={0} | all-to-all | bytes 1703936 | tf_op jit(solution)/shard_map/to_members/all_to_all | solution.py:396
  70.2 0.1 slice_reduce_fusion
  70.3 2.9 %collective-permute-start.6 = (bf16[144,256]{1,0:T(8,128)(2,1)S(1)}, bf16[144,256]{1,0:T(8,128)(2,1)S(1)}, u32[]{:S(2)}, u32[]{:S(2)}) collective-permute-start(bf16[144,256]{1,0:T(8,128)(2,1)S(1)} %slice_reduce_fusion), channel_id=1, source_target_pairs={{0,24},{8,16},{16,8},{24,0},{1,25},{9,17},{17,9},{25,1},{2,26},{10... | collective-permute-start | bytes 221192 | tf_op jit(solution)/shard_map/reduce/ppermute | solution.py:304
  73.2 0.0 collective-permute-start.5
  73.2 0.7 collective-permute-start.4
  73.9 1.6 %collective-permute-done.6 = bf16[144,256]{1,0:T(8,128)(2,1)S(1)} collective-permute-done((bf16[144,256]{1,0:T(8,128)(2,1)S(1)}, bf16[144,256]{1,0:T(8,128)(2,1)S(1)}, u32[]{:S(2)}, u32[]{:S(2)}) %collective-permute-start.6) | collective-permute-done | bytes 73760 | tf_op jit(solution)/shard_map/reduce/ppermute | solution.py:304
  75.5 4.2 %collective-permute-done.5 = bf16[144,256]{1,0:T(8,128)(2,1)S(1)} collective-permute-done((bf16[144,256]{1,0:T(8,128)(2,1)S(1)}, bf16[144,256]{1,0:T(8,128)(2,1)S(1)}, u32[]{:S(2)}, u32[]{:S(2)}) %collective-permute-start.5) | collective-permute-done | bytes 73760 | tf_op jit(solution)/shard_map/reduce/ppermute | solution.py:304
  79.7 0.0 collective-permute-done.4
  79.7 0.1 collective-permute-start.9
  79.8 0.1 collective-permute-start.8
  79.9 3.1 %collective-permute-start.7 = (bf16[144,256]{1,0:T(8,128)(2,1)S(1)}, bf16[144,256]{1,0:T(8,128)(2,1)S(1)}, u32[]{:S(2)}, u32[]{:S(2)}) collective-permute-start(bf16[144,256]{1,0:T(8,128)(2,1)S(1)} %add_convert_fusion.2), channel_id=1, source_target_pairs={{0,2},{1,3},{2,0},{3,1},{4,6},{5,7},{6,4},{7,5},{8,10},{9,11},{10,... | collective-permute-start | bytes 221192 | tf_op jit(solution)/shard_map/reduce/ppermute | solution.py:304
  83.1 2.4 %collective-permute-done.9 = bf16[144,256]{1,0:T(8,128)(2,1)S(1)} collective-permute-done((bf16[144,256]{1,0:T(8,128)(2,1)S(1)}, bf16[144,256]{1,0:T(8,128)(2,1)S(1)}, u32[]{:S(2)}, u32[]{:S(2)}) %collective-permute-start.9) | collective-permute-done | bytes 73760 | tf_op jit(solution)/shard_map/reduce/ppermute | solution.py:304
  85.5 0.0 collective-permute-done.8
  85.5 0.4 collective-permute-done.7
  85.9 0.1 collective-permute-start.10
  86.1 1.0 unpack.1
  87.0 7.0 %collective-permute-done.10 = bf16[144,256]{1,0:T(8,128)(2,1)S(1)} collective-permute-done((bf16[144,256]{1,0:T(8,128)(2,1)S(1)}, bf16[144,256]{1,0:T(8,128)(2,1)S(1)}, u32[]{:S(2)}, u32[]{:S(2)}) %collective-permute-start.10) | collective-permute-done | bytes 73760 | tf_op jit(solution)/shard_map/reduce/ppermute | solution.py:304
  94.1 0.8 collective-permute-start.12
  94.9 0.8 collective-permute-start.11
  95.6 1.8 %collective-permute-start.13 = (bf16[128,256]{1,0:T(8,128)(2,1)S(1)}, bf16[128,256]{1,0:T(8,128)(2,1)S(1)}, u32[]{:S(2)}, u32[]{:S(2)}) collective-permute-start(bf16[128,256]{1,0:T(8,128)(2,1)S(1)} %get-tuple-element.44), channel_id=1, source_target_pairs={{0,192},{32,224},{64,128},{96,160},{128,64},{160,96},{192,0},{224,... | collective-permute-start | bytes 196616 | tf_op jit(solution)/shard_map/reduce/ppermute | solution.py:412
  97.4 1.4 %collective-permute-done.12 = bf16[128,256]{1,0:T(8,128)(2,1)S(1)} collective-permute-done((bf16[128,256]{1,0:T(8,128)(2,1)S(1)}, bf16[128,256]{1,0:T(8,128)(2,1)S(1)}, u32[]{:S(2)}, u32[]{:S(2)}) %collective-permute-start.12) | collective-permute-done | bytes 65568 | tf_op jit(solution)/shard_map/reduce/ppermute | solution.py:412
  98.8 0.0 collective-permute-done.11
  98.8 1.2 %collective-permute-done.13 = bf16[128,256]{1,0:T(8,128)(2,1)S(1)} collective-permute-done((bf16[128,256]{1,0:T(8,128)(2,1)S(1)}, bf16[128,256]{1,0:T(8,128)(2,1)S(1)}, u32[]{:S(2)}, u32[]{:S(2)}) %collective-permute-start.13) | collective-permute-done | bytes 65568 | tf_op jit(solution)/shard_map/reduce/ppermute | solution.py:412
  100.0 4.1 %collective-permute-start.14 = (bf16[4,128,256]{2,1,0:T(8,128)(2,1)S(1)}, bf16[4,128,256]{2,1,0:T(8,128)(2,1)S(1)}, u32[]{:S(2)}, u32[]{:S(2)}) collective-permute-start(bf16[4,128,256]{2,1,0:T(8,128)(2,1)S(1)} %pad_maximum_fusion.same_core), channel_id=1, source_target_pairs={{0,32},{32,0},{64,96},{96,64},{128,160},{160,128},{192,224},{224,1... | collective-permute-start | bytes 786440 | tf_op jit(solution)/shard_map/reduce/ppermute | solution.py:414
  104.1 1.2 %collective-permute-done.14.other_core = bf16[4,128,256]{2,1,0:T(8,128)(2,1)S(1)} collective-permute-done((bf16[4,128,256]{2,1,0:T(8,128)(2,1)S(1)}, bf16[4,128,256]{2,1,0:T(8,128)(2,1)S(1)}, u32[]{:S(2)}, u32[]{:S(2)}) %collective-permute-start.14) | collective-permute-done | bytes 262176 | tf_op jit(solution)/shard_map/reduce/ppermute | solution.py:414
  105.2 1.0 finish.1
  (28 shorter events, 0.2 us)
Async XLA Ops:
  0.6 20.2 %copy-start = (bf16[256,256]{1,0:T(8,128)(2,1)S(1)}, bf16[256,256]{1,0:T(8,128)(2,1)}, u32[]{:S(2)}) copy-start(bf16[256,256]{1,0:T(8,128)(2,1)} %constant.24.clone.gather8) | copy-start | bytes 393220
  0.6 34.4 %copy-start.5 = (bf16[256,256]{1,0:T(8,128)(2,1)S(1)}, bf16[256,256]{1,0:T(8,128)(2,1)}, u32[]{:S(2)}) copy-start(bf16[256,256]{1,0:T(8,128)(2,1)} %constant.25.clone.headsum) | copy-start | bytes 393220
  0.7 34.4 %copy-start.4 = (bf16[256,256]{1,0:T(8,128)(2,1)S(1)}, bf16[256,256]{1,0:T(8,128)(2,1)}, u32[]{:S(2)}) copy-start(bf16[256,256]{1,0:T(8,128)(2,1)} %wo.3) | copy-start | bytes 393220
  0.7 34.4 %copy-start.3 = (bf16[256,256]{1,0:T(8,128)(2,1)S(1)}, bf16[256,256]{1,0:T(8,128)(2,1)}, u32[]{:S(2)}) copy-start(bf16[256,256]{1,0:T(8,128)(2,1)} %wv.3) | copy-start | bytes 393220
  0.7 34.4 %copy-start.2 = (bf16[256,256]{1,0:T(8,128)(2,1)S(1)}, bf16[256,256]{1,0:T(8,128)(2,1)}, u32[]{:S(2)}) copy-start(bf16[256,256]{1,0:T(8,128)(2,1)} %wk.3) | copy-start | bytes 393220
  0.7 34.4 %copy-start.1 = (bf16[256,256]{1,0:T(8,128)(2,1)S(1)}, bf16[256,256]{1,0:T(8,128)(2,1)}, u32[]{:S(2)}) copy-start(bf16[256,256]{1,0:T(8,128)(2,1)} %wq.3) | copy-start | bytes 393220
  0.7 1.0 copy-start.6
  1.7 0.9 copy-start.7
  2.7 0.8 copy-start.8
  3.4 31.7 %copy-start.11 = (f32[256]{0:T(256)S(1)}, f32[256]{0:T(256)}, u32[]{:S(2)}) copy-start(f32[256]{0:T(256)} %param.12) | copy-start | bytes 3076
  4.5 33.6 %copy-start.10 = (f32[3,3,256]{2,1,0:T(4,128)S(1)}, f32[3,3,256]{2,1,0:T(4,128)}, u32[]{:S(2)}) copy-start(f32[3,3,256]{2,1,0:T(4,128)} %mix.1) | copy-start | bytes 27652
  4.5 16.3 %all-to-all-start = ((bf16[8,128,256]{2,1,0:T(8,128)(2,1)}), bf16[8,128,256]{2,1,0:T(8,128)(2,1)S(1)}, u32[]{:S(2)}, u32[]{:S(2)}) async-start(bf16[8,128,256]{2,1,0:T(8,128)(2,1)} %pack.1), calls=%async_computation | async-start | bytes 1048576 | tf_op jit(solution)/shard_map/to_cells/all_to_all | solution.py:346
  21.1 3.8 %collective-permute-start.1 = (bf16[4,32,256]{2,1,0:T(8,128)(2,1)S(1)}, bf16[4,32,256]{2,1,0:T(8,128)(2,1)S(1)}, u32[]{:S(2)}, u32[]{:S(2)}) collective-permute-start(bf16[4,32,256]{2,1,0:T(8,128)(2,1)S(1)} %get-tuple-element.41), channel_id=1, source_target_pairs={{32,0},{64,32},{96,64},{128,96},{160,128},{192,160},{224,192},{1,2... | collective-permute-start | bytes 196616 | tf_op jit(solution)/shard_map/halo_cols/ppermute | solution.py:358
  22.1 9.5 %collective-permute-start = (bf16[4,32,256]{2,1,0:T(8,128)(2,1)S(1)}, bf16[4,32,256]{2,1,0:T(8,128)(2,1)S(1)}, u32[]{:S(2)}, u32[]{:S(2)}) collective-permute-start(bf16[4,32,256]{2,1,0:T(8,128)(2,1)S(1)} %get-tuple-element.42), channel_id=1, source_target_pairs={{0,32},{32,64},{64,96},{96,128},{128,160},{160,192},{192,224},{224... | collective-permute-start | bytes 196616 | tf_op jit(solution)/shard_map/halo_cols/ppermute | solution.py:357
  31.6 6.5 %collective-permute-start.2 = (bf16[6,32,256]{2,1,0:T(8,128)(2,1)S(1)}, bf16[6,32,256]{2,1,0:T(8,128)(2,1)S(1)}, u32[]{:S(2)}, u32[]{:S(2)}) collective-permute-start(bf16[6,32,256]{2,1,0:T(8,128)(2,1)S(1)} %pad_maximum_fusion.1), channel_id=1, source_target_pairs={{0,8},{8,16},{16,24},{24,0},{1,9},{9,17},{17,25},{25,1},{2,10},{10... | collective-permute-start | bytes 294920 | tf_op jit(solution)/shard_map/halo_rows/ppermute | solution.py:371
  32.4 5.7 %collective-permute-start.3 = (bf16[6,32,256]{2,1,0:T(8,128)(2,1)S(1)}, bf16[6,32,256]{2,1,0:T(8,128)(2,1)S(1)}, u32[]{:S(2)}, u32[]{:S(2)}) collective-permute-start(bf16[6,32,256]{2,1,0:T(8,128)(2,1)S(1)} %pad_maximum_fusion.2), channel_id=1, source_target_pairs={{0,24},{8,0},{16,8},{24,16},{1,25},{9,1},{17,9},{25,17},{2,26},{10... | collective-permute-start | bytes 294920 | tf_op jit(solution)/shard_map/halo_rows/ppermute | solution.py:372
  42.6 43.4 %copy-start.9 = (bf16[128,128]{1,0:T(8,128)(2,1)S(1)}, bf16[128,128]{1,0:T(8,128)(2,1)}, u32[]{:S(2)}) copy-start(bf16[128,128]{1,0:T(8,128)(2,1)} %constant.23.clone.split) | copy-start | bytes 98308
  70.3 5.2 %collective-permute-start.6 = (bf16[144,256]{1,0:T(8,128)(2,1)S(1)}, bf16[144,256]{1,0:T(8,128)(2,1)S(1)}, u32[]{:S(2)}, u32[]{:S(2)}) collective-permute-start(bf16[144,256]{1,0:T(8,128)(2,1)S(1)} %slice_reduce_fusion), channel_id=1, source_target_pairs={{0,24},{8,16},{16,8},{24,0},{1,25},{9,17},{17,9},{25,1},{2,26},{10... | collective-permute-start | bytes 221192 | tf_op jit(solution)/shard_map/reduce/ppermute | solution.py:304
  73.2 6.5 %collective-permute-start.5 = (bf16[144,256]{1,0:T(8,128)(2,1)S(1)}, bf16[144,256]{1,0:T(8,128)(2,1)S(1)}, u32[]{:S(2)}, u32[]{:S(2)}) collective-permute-start(bf16[144,256]{1,0:T(8,128)(2,1)S(1)} %slice_reduce_fusion), channel_id=1, source_target_pairs={{0,16},{8,24},{16,0},{24,8},{1,17},{9,25},{17,1},{25,9},{2,18},{10... | collective-permute-start | bytes 221192 | tf_op jit(solution)/shard_map/reduce/ppermute | solution.py:304
  73.2 6.5 %collective-permute-start.4 = (bf16[144,256]{1,0:T(8,128)(2,1)S(1)}, bf16[144,256]{1,0:T(8,128)(2,1)S(1)}, u32[]{:S(2)}, u32[]{:S(2)}) collective-permute-start(bf16[144,256]{1,0:T(8,128)(2,1)S(1)} %slice_reduce_fusion), channel_id=1, source_target_pairs={{0,8},{8,0},{16,24},{24,16},{1,9},{9,1},{17,25},{25,17},{2,10},{10... | collective-permute-start | bytes 221192 | tf_op jit(solution)/shard_map/reduce/ppermute | solution.py:304
  79.7 5.8 %collective-permute-start.9 = (bf16[144,256]{1,0:T(8,128)(2,1)S(1)}, bf16[144,256]{1,0:T(8,128)(2,1)S(1)}, u32[]{:S(2)}, u32[]{:S(2)}) collective-permute-start(bf16[144,256]{1,0:T(8,128)(2,1)S(1)} %add_convert_fusion.2), channel_id=1, source_target_pairs={{0,6},{1,7},{2,4},{3,5},{4,2},{5,3},{6,0},{7,1},{8,14},{9,15},{10,... | collective-permute-start | bytes 221192 | tf_op jit(solution)/shard_map/reduce/ppermute | solution.py:304
  79.8 5.7 %collective-permute-start.8 = (bf16[144,256]{1,0:T(8,128)(2,1)S(1)}, bf16[144,256]{1,0:T(8,128)(2,1)S(1)}, u32[]{:S(2)}, u32[]{:S(2)}) collective-permute-start(bf16[144,256]{1,0:T(8,128)(2,1)S(1)} %add_convert_fusion.2), channel_id=1, source_target_pairs={{0,4},{1,5},{2,6},{3,7},{4,0},{5,1},{6,2},{7,3},{8,12},{9,13},{10,... | collective-permute-start | bytes 221192 | tf_op jit(solution)/shard_map/reduce/ppermute | solution.py:304
  79.9 6.0 %collective-permute-start.7 = (bf16[144,256]{1,0:T(8,128)(2,1)S(1)}, bf16[144,256]{1,0:T(8,128)(2,1)S(1)}, u32[]{:S(2)}, u32[]{:S(2)}) collective-permute-start(bf16[144,256]{1,0:T(8,128)(2,1)S(1)} %add_convert_fusion.2), channel_id=1, source_target_pairs={{0,2},{1,3},{2,0},{3,1},{4,6},{5,7},{6,4},{7,5},{8,10},{9,11},{10,... | collective-permute-start | bytes 221192 | tf_op jit(solution)/shard_map/reduce/ppermute | solution.py:304
  85.9 8.1 %collective-permute-start.10 = (bf16[144,256]{1,0:T(8,128)(2,1)S(1)}, bf16[144,256]{1,0:T(8,128)(2,1)S(1)}, u32[]{:S(2)}, u32[]{:S(2)}) collective-permute-start(bf16[144,256]{1,0:T(8,128)(2,1)S(1)} %add_convert_fusion.1), channel_id=1, source_target_pairs={{0,1},{1,0},{2,3},{3,2},{4,5},{5,4},{6,7},{7,6},{8,9},{9,8},{10,11... | collective-permute-start | bytes 221192 | tf_op jit(solution)/shard_map/reduce/ppermute | solution.py:304
  94.1 4.7 %collective-permute-start.12 = (bf16[128,256]{1,0:T(8,128)(2,1)S(1)}, bf16[128,256]{1,0:T(8,128)(2,1)S(1)}, u32[]{:S(2)}, u32[]{:S(2)}) collective-permute-start(bf16[128,256]{1,0:T(8,128)(2,1)S(1)} %get-tuple-element.44), channel_id=1, source_target_pairs={{0,128},{32,160},{64,192},{96,224},{128,0},{160,32},{192,64},{224,... | collective-permute-start | bytes 196616 | tf_op jit(solution)/shard_map/reduce/ppermute | solution.py:412
  94.9 3.9 %collective-permute-start.11 = (bf16[128,256]{1,0:T(8,128)(2,1)S(1)}, bf16[128,256]{1,0:T(8,128)(2,1)S(1)}, u32[]{:S(2)}, u32[]{:S(2)}) collective-permute-start(bf16[128,256]{1,0:T(8,128)(2,1)S(1)} %get-tuple-element.44), channel_id=1, source_target_pairs={{0,64},{32,96},{64,0},{96,32},{128,192},{160,224},{192,128},{224,1... | collective-permute-start | bytes 196616 | tf_op jit(solution)/shard_map/reduce/ppermute | solution.py:412
  95.6 4.3 %collective-permute-start.13 = (bf16[128,256]{1,0:T(8,128)(2,1)S(1)}, bf16[128,256]{1,0:T(8,128)(2,1)S(1)}, u32[]{:S(2)}, u32[]{:S(2)}) collective-permute-start(bf16[128,256]{1,0:T(8,128)(2,1)S(1)} %get-tuple-element.44), channel_id=1, source_target_pairs={{0,192},{32,224},{64,128},{96,160},{128,64},{160,96},{192,0},{224,... | collective-permute-start | bytes 196616 | tf_op jit(solution)/shard_map/reduce/ppermute | solution.py:412
  100.0 5.2 %collective-permute-start.14 = (bf16[4,128,256]{2,1,0:T(8,128)(2,1)S(1)}, bf16[4,128,256]{2,1,0:T(8,128)(2,1)S(1)}, u32[]{:S(2)}, u32[]{:S(2)}) collective-permute-start(bf16[4,128,256]{2,1,0:T(8,128)(2,1)S(1)} %pad_maximum_fusion.same_core), channel_id=1, source_target_pairs={{0,32},{32,0},{64,96},{96,64},{128,160},{160,128},{192,224},{224,1... | collective-permute-start | bytes 786440 | tf_op jit(solution)/shard_map/reduce/ppermute | solution.py:414

commit v9 on v8

--- a/solution.py
+++ b/solution.py
@@ -23,14 +23,18 @@
     return lax.dot_general(a, b, dims, preferred_element_type=F32)
 
 
+def snake(place, parts):
+    return jnp.where(place % 2 == 0, place // 2, parts - 1 - place // 2)
+
+
 def split_matrix(parts, members, cols):
+    size = members * cols
     per = cols // parts
-    out = np.zeros((parts, per, members, members, cols), np.float32)
-    for j in range(parts):
-        for c in range(per):
-            for m in range(members):
-                out[j, c, m, m, j * per + c] = 1
-    return out.reshape(parts * per * members, members * cols)
+    out = lax.broadcasted_iota(jnp.int32, (size, size), 0)
+    src = lax.broadcasted_iota(jnp.int32, (size, size), 1)
+    part, col, member = out // (per * members), out // members % per, out % members
+    hit = (src // cols == member) & (src % cols == snake(part, parts) * per + col)
+    return jnp.where(hit, 1.0, 0.0).astype(BF)
 
 
 def gather_matrix(parts, cells, members):
@@ -42,14 +46,15 @@
     return out.reshape(cells * parts * members, -1)
 
 
-def pack_kernel(fields, cot, split, send):
+def pack_kernel(fields, cot, send):
     members, rows, cols, width = fields.shape
     parts = send.shape[0]
     per = cols // parts * members
+    split = split_matrix(parts, members, cols)
     for k, source in enumerate((fields, cot)):
         for r in range(rows):
             tokens = source[:, r].reshape(members * cols, width)
-            moved = dot(split[...], tokens).astype(BF).reshape(parts, per, width)
+            moved = dot(split, tokens).astype(BF).reshape(parts, per, width)
             start = (k * rows + r) * per
             send[:, start : start + per, :] = moved
 
@@ -272,13 +277,14 @@
         send[j, base + shard : base + shard + 16, :] = extras
 
 
-def unpack_kernel(recv, split, out):
+def unpack_kernel(recv, out):
     members, rows, cols, width = out.shape
     parts = recv.shape[0]
     per = cols // parts * members
+    split = split_matrix(parts, members, cols)
     for r in range(rows):
         tokens = recv[:, r * per : (r + 1) * per, :].reshape(parts * per, width)
-        out[:, r] = dot(split[...], tokens, TN).astype(BF).reshape(members, cols, width)
+        out[:, r] = dot(split, tokens, TN).astype(BF).reshape(members, cols, width)
 
 
 def finish_kernel(scale, place, same_core, other_core, total, g_q, g_k, g_v, g_o, g_mix, g_gain):
@@ -312,9 +318,17 @@
     return pltpu.with_memory_space_constraint(x, pltpu.VMEM)
 
 
-def ring(axis, step):
-    size = lax.axis_size(axis)
-    return [(i, (i + step) % size) for i in range(size)]
+def swap(last, first, spot, axis, where, wrap):
+    size = len(where)
+    got = []
+    for odd in (0, 1):
+        pairs = []
+        for a in range(odd, size if wrap else size - 1, 2):
+            b = (a + 1) % size
+            pairs += [(where[a], where[b]), (where[b], where[a])]
+        got.append(lax.ppermute(jnp.where(spot % 2 == odd, last, first), axis, pairs))
+    even = spot % 2 == 0
+    return jnp.where(even, got[0], got[1]), jnp.where(even, got[1], got[0])
 
 
 def local(fields, norm_gain, w_query, w_key, w_value, w_out, mix_kernel, cotangent):
@@ -329,19 +343,19 @@
     params = pltpu.CompilerParams(vmem_limit_bytes=40 * 1024 * 1024)
     smem = pl.BlockSpec(memory_space=pltpu.SMEM)
     vmem = pl.BlockSpec(memory_space=pltpu.VMEM)
-    split = jnp.asarray(split_matrix(parts, members, cols), BF)
     gather8 = jnp.asarray(gather_matrix(parts, 8, members), BF)
     headsum = jnp.asarray(np.kron(np.eye(HEADS), np.ones((width // HEADS, width // HEADS))), BF)
     gain = norm_gain.reshape(1, width)
     blocks = parts * grid[1]
-    place = jnp.stack([lax.axis_index("row"), lax.axis_index("col") * parts + lax.axis_index("mem")]).astype(jnp.int32)
+    block = lax.axis_index("col") * parts + snake(lax.axis_index("mem"), parts)
+    place = jnp.stack([lax.axis_index("row"), block]).astype(jnp.int32)
 
     with jax.named_scope("pack"):
         send = pl.pallas_call(
             pack_kernel,
             out_shape=pltpu.VMEM((parts, 2 * base, width), BF),
             compiler_params=params,
-        )(fields, cotangent, split)
+        )(fields, cotangent)
     with jax.named_scope("to_cells"):
         recv = lax.all_to_all(send, "mem", 0, 0)
     with jax.named_scope("order"):
@@ -350,12 +364,14 @@
             out_shape=(pltpu.VMEM((tokens, width), BF), pltpu.VMEM((rows, per, parts * members, width), BF)),
             compiler_params=params,
         )(near(recv), gather8)
+        x, w_query, w_key, w_value, w_out = lax.optimization_barrier((x, w_query, w_key, w_value, w_out))
     with jax.named_scope("halo_cols"):
-        flat = [b % parts * grid[1] + b // parts for b in range(blocks)]
-        up = list(zip(flat, flat[1:] + flat[:1]))
-        down = [(j, i) for i, j in up]
-        left = lax.ppermute(cot[:, per - 1], ("mem", "col"), up)
-        right = lax.ppermute(cot[:, 0], ("mem", "col"), down)
+        where = {}
+        for mem in range(parts):
+            inner = mem // 2 if mem % 2 == 0 else parts - 1 - mem // 2
+            for c in range(grid[1]):
+                where[c * parts + inner] = mem * grid[1] + c
+        right, left = swap(cot[:, per - 1], cot[:, 0], block, ("mem", "col"), where, True)
     with jax.named_scope("forward"):
         token = pltpu.VMEM((tokens, width), BF)
         token_f = pltpu.VMEM((tokens, width), F32)
@@ -368,8 +384,8 @@
         )(near(x), gain, w_query, w_key, w_value, w_out, headsum)
     with jax.named_scope("halo_rows"):
         top, bottom = [jnp.concatenate([left[r : r + 1], cot[r], right[r : r + 1]], axis=0) for r in (0, rows - 1)]
-        above = lax.ppermute(bottom, "row", ring("row", 1))
-        below = lax.ppermute(top, "row", ring("row", -1))
+        rows_at = {r: r for r in range(grid[0])}
+        below, above = swap(bottom, top, lax.axis_index("row"), "row", rows_at, False)
     with jax.named_scope("backward"):
         back = pl.pallas_call(
             functools.partial(backward_kernel, (grid[0], blocks)),
@@ -401,7 +417,7 @@
             unpack_kernel,
             out_shape=jax.ShapeDtypeStruct(fields.shape, BF),
             compiler_params=params,
-        )(near(landed), split)
+        )(near(landed))
 
     with jax.named_scope("reduce"):
         total = meet(total, "row", (1, 2, 3))

time: 107 us -> 96.8 us (0.905)
  starting transfers between devices: 26.6 us -> 43.7 us
  waiting for transfers between devices: 37.3 us -> 21.8 us
  blocking collectives: 27.5 us -> 16.8 us
    ppermute x7, starting transfers between devices: 7.05 us -> 18.2 us  [meet(): lax.ppermute(values, axis, partner(axis, k))]
    all_to_all x1, blocking collectives: 27.5 us -> 16.8 us  [local(): landed = lax.all_to_all(back, 'mem', 0, 0)]
    ppermute x7, waiting for transfers between devices: 15.6 us -> 6.68 us  [meet(): lax.ppermute(values, axis, partner(axis, k))]
    ppermute x4, waiting for transfers between devices: 8.51 us -> 1.93 us  [swap(): lax.ppermute(jnp.where(spot % 2 == odd, last, first), axis, pairs)]
    ppermute x4, starting transfers between devices: 5.32 us -> 9.87 us  [swap(): lax.ppermute(jnp.where(spot % 2 == odd, last, first), axis, pairs)]
    ppermute x1, starting transfers between devices: 4.08 us -> 5.54 us  [local(): other_core = lax.ppermute(same_core, 'mem', partner('mem', 1))]
    unnamed x24 -> x20, local copies, waits for them, and re-layouts: 2.78 us -> 2.02 us
where the time goes in v9:
time: 96.8 us; the launch traced here: 96.5 us
  starting transfers between devices  43.7 us (45%)
  waiting for transfers between devices  21.8 us (23%)
  blocking collectives  16.8 us (17%)
  Pallas kernels  10.9 us (11%)
  local copies, waits for them, and re-layouts  2.04 us (2%)
    ppermute x7, starting transfers between devices, meet(): lax.ppermute(values, axis, partner(axis, k))  18.2 us
    all_to_all x1, blocking collectives, local(): landed = lax.all_to_all(back, 'mem', 0, 0)  16.8 us
    ppermute x4, starting transfers between devices, swap(): lax.ppermute(jnp.where(spot % 2 == odd, last, first), axis, pairs)  9.87 us
    all_to_all x1, waiting for transfers between devices, local(): recv = lax.all_to_all(send, 'mem', 0, 0)  9.5 us
    all_to_all x1, starting transfers between devices, local(): recv = lax.all_to_all(send, 'mem', 0, 0)  6.77 us
    ppermute x7, waiting for transfers between devices, meet(): lax.ppermute(values, axis, partner(axis, k))  6.68 us
    ppermute x1, starting transfers between devices, local(): other_core = lax.ppermute(same_core, 'mem', partner('mem', 1))  5.54 us
    pallas_call x1, Pallas kernels, local(): pl.pallas_call(functools.partial(backward_kernel, (grid[0], blocks)), in_...  4.51 us
  transfers between devices with their start and end apart: 16, of which 11 were waited for; matrix products, arithmetic and copies ran while one was open for 0% of the time, Pallas kernels for 4%

profile of v9, /device:TPU:1, one launch (start us, length us, event | category | flops | bytes accessed | tf_op | source)
XLA Modules:
  0.0 96.5 jit_solution(17685571396270657189)
XLA Ops:
  0.6 0.0 copy-start
  0.6 0.0 copy-start.5
  0.7 0.0 copy-start.4
  0.7 1.0 %copy-done.6 = bf16[4,4,32,256]{3,2,1,0:T(8,128)(2,1)S(1)} copy-done((bf16[4,4,32,256]{3,2,1,0:T(8,128)(2,1)S(1)}, bf16[4,4,32,256]{3,2,1,0:T(8,128)(2,1)}, u32[]{:S(2)}) %copy-start.6) | copy-done | bytes 262168
  1.7 0.9 copy-done.7
  2.7 1.1 %pack.1 = bf16[8,128,256]{2,1,0:T(8,128)(2,1)} custom-call(bf16[4,4,32,256]{3,2,1,0:T(8,128)(2,1)S(1)} %copy-done.6, bf16[4,4,32,256]{3,2,1,0:T(8,128)(2,1)S(1)} %copy-done.7), custom_call_target="tpu_custom_call" | custom-call | tf_op jit(solution)/shard_map/pack/pallas_call | solution.py:354
  3.8 6.8 %all-to-all-start = ((bf16[8,128,256]{2,1,0:T(8,128)(2,1)}), bf16[8,128,256]{2,1,0:T(8,128)(2,1)S(1)}, u32[]{:S(2)}, u32[]{:S(2)}) async-start(bf16[8,128,256]{2,1,0:T(8,128)(2,1)} %pack.1), calls=%async_computation | async-start | bytes 1048576 | tf_op jit(solution)/shard_map/to_cells/all_to_all | solution.py:360
  10.5 9.5 %all-to-all-done.recv = bf16[8,128,256]{2,1,0:T(8,128)(2,1)S(1)} async-done(((bf16[8,128,256]{2,1,0:T(8,128)(2,1)}), bf16[8,128,256]{2,1,0:T(8,128)(2,1)S(1)}, u32[]{:S(2)}, u32[]{:S(2)}) %all-to-all-start) | async-done | bytes 524320 | tf_op jit(solution)/shard_map/to_cells/all_to_all | solution.py:360
  20.0 0.0 copy-done
  20.0 0.3 order.1
  20.4 0.4 collective-permute-start.1
  20.8 7.1 %collective-permute-start = (bf16[4,32,256]{2,1,0:T(8,128)(2,1)S(1)}, bf16[4,32,256]{2,1,0:T(8,128)(2,1)S(1)}, u32[]{:S(2)}, u32[]{:S(2)}) collective-permute-start(bf16[4,32,256]{2,1,0:T(8,128)(2,1)S(1)} %get-tuple-element.52), channel_id=1, source_target_pairs={{64,128},{128,64},{192,224},{224,192},{160,96},{96,160},{32,1},{1,... | collective-permute-start | bytes 196616 | tf_op jit(solution)/shard_map/halo_cols/ppermute | solution.py:329
  27.9 0.0 collective-permute-done.1
  27.9 1.9 %collective-permute-done = bf16[4,32,256]{2,1,0:T(8,128)(2,1)S(1)} collective-permute-done((bf16[4,32,256]{2,1,0:T(8,128)(2,1)S(1)}, bf16[4,32,256]{2,1,0:T(8,128)(2,1)S(1)}, u32[]{:S(2)}, u32[]{:S(2)}) %collective-permute-start) | collective-permute-done | bytes 65568 | tf_op jit(solution)/shard_map/halo_cols/ppermute | solution.py:329
  29.9 1.8 %collective-permute-start.3 = (bf16[6,32,256]{2,1,0:T(8,128)(2,1)S(1)}, bf16[6,32,256]{2,1,0:T(8,128)(2,1)S(1)}, u32[]{:S(2)}, u32[]{:S(2)}) collective-permute-start(bf16[6,32,256]{2,1,0:T(8,128)(2,1)S(1)} %get-tuple-element.55), channel_id=1, source_target_pairs={{0,8},{8,0},{16,24},{24,16},{1,9},{9,1},{17,25},{25,17},{2,10},{10... | collective-permute-start | bytes 294920 | tf_op jit(solution)/shard_map/halo_rows/ppermute | solution.py:329
  31.6 0.7 collective-permute-start.2
  32.3 0.1 pad_add_fusion.place
  32.4 0.0 copy-done.5
  32.4 3.0 %forward.1 = (bf16[512,256]{1,0:T(8,128)(2,1)S(1)}, f32[512,256]{1,0:T(8,128)S(1)}, bf16[512,256]{1,0:T(8,128)(2,1)S(1)}, bf16[512,256]{1,0:T(8,128)(2,1)S(1)}, ...) custom-call(bf16[512,256]{1,0:T(8,128)(2,1)S(1)} %get-tuple-element.30.x_in, f32[1,256]{1,0:T(1,128)S(1)} %bitcast.18, ...), custom_call_target="tpu_custom_call" | custom-call | tf_op jit(solution)/shard_map/forward/pallas_call | solution.py:379
  35.4 0.0 collective-permute-done.3
  35.4 0.0 collective-permute-done.2
  35.4 4.5 %backward.1 = bf16[8,208,256]{2,1,0:T(8,128)(2,1)S(1)} custom-call(s32[2]{0:T(128)S(1)} %pad_add_fusion.place, bf16[4,4,32,256]{3,2,1,0:T(8,128)(2,1)S(1)} %get-tuple-element.28.cot, bf16[4,32,256]{2,1,0:T(8,128)(2,1)S(1)} %get-tuple-element.58.left, bf16[4,32,256]{2,1,0:T(8,128)(2,1)S(1)} %get-tuple-element.57.right, ...), custom_call_target="tpu_custom_call" | custom-call | tf_op jit(solution)/shard_map/backward/pallas_call | solution.py:390
  39.9 16.8 %all_to_all.10.recv = bf16[8,208,256]{2,1,0:T(8,128)(2,1)S(1)} all-to-all(bf16[8,208,256]{2,1,0:T(8,128)(2,1)S(1)} %backward.1), channel_id=1, replica_groups=mesh['mem'=8,'row'=4,'col'=8] {'mem'}, dimensions={0} | all-to-all | bytes 1703936 | tf_op jit(solution)/shard_map/to_members/all_to_all | solution.py:412
  56.8 0.1 slice_reduce_fusion
  56.8 4.8 %collective-permute-start.6 = (bf16[144,256]{1,0:T(8,128)(2,1)S(1)}, bf16[144,256]{1,0:T(8,128)(2,1)S(1)}, u32[]{:S(2)}, u32[]{:S(2)}) collective-permute-start(bf16[144,256]{1,0:T(8,128)(2,1)S(1)} %slice_reduce_fusion), channel_id=1, source_target_pairs={{0,24},{8,16},{16,8},{24,0},{1,25},{9,17},{17,9},{25,1},{2,26},{10... | collective-permute-start | bytes 221192 | tf_op jit(solution)/shard_map/reduce/ppermute | solution.py:310
  61.6 1.9 %collective-permute-start.5 = (bf16[144,256]{1,0:T(8,128)(2,1)S(1)}, bf16[144,256]{1,0:T(8,128)(2,1)S(1)}, u32[]{:S(2)}, u32[]{:S(2)}) collective-permute-start(bf16[144,256]{1,0:T(8,128)(2,1)S(1)} %slice_reduce_fusion), channel_id=1, source_target_pairs={{0,16},{8,24},{16,0},{24,8},{1,17},{9,25},{17,1},{25,9},{2,18},{10... | collective-permute-start | bytes 221192 | tf_op jit(solution)/shard_map/reduce/ppermute | solution.py:310
  63.5 0.0 collective-permute-start.4
  63.5 0.0 collective-permute-done.6
  63.5 2.8 %collective-permute-done.5 = bf16[144,256]{1,0:T(8,128)(2,1)S(1)} collective-permute-done((bf16[144,256]{1,0:T(8,128)(2,1)S(1)}, bf16[144,256]{1,0:T(8,128)(2,1)S(1)}, u32[]{:S(2)}, u32[]{:S(2)}) %collective-permute-start.5) | collective-permute-done | bytes 73760 | tf_op jit(solution)/shard_map/reduce/ppermute | solution.py:310
  66.3 0.6 collective-permute-done.4
  67.0 1.0 %collective-permute-start.9 = (bf16[144,256]{1,0:T(8,128)(2,1)S(1)}, bf16[144,256]{1,0:T(8,128)(2,1)S(1)}, u32[]{:S(2)}, u32[]{:S(2)}) collective-permute-start(bf16[144,256]{1,0:T(8,128)(2,1)S(1)} %add_convert_fusion.2), channel_id=1, source_target_pairs={{0,6},{1,7},{2,4},{3,5},{4,2},{5,3},{6,0},{7,1},{8,14},{9,15},{10,... | collective-permute-start | bytes 221192 | tf_op jit(solution)/shard_map/reduce/ppermute | solution.py:310
  68.0 0.3 collective-permute-start.8
  68.3 2.0 %collective-permute-start.7 = (bf16[144,256]{1,0:T(8,128)(2,1)S(1)}, bf16[144,256]{1,0:T(8,128)(2,1)S(1)}, u32[]{:S(2)}, u32[]{:S(2)}) collective-permute-start(bf16[144,256]{1,0:T(8,128)(2,1)S(1)} %add_convert_fusion.2), channel_id=1, source_target_pairs={{0,2},{1,3},{2,0},{3,1},{4,6},{5,7},{6,4},{7,5},{8,10},{9,11},{10,... | collective-permute-start | bytes 221192 | tf_op jit(solution)/shard_map/reduce/ppermute | solution.py:310
  70.3 1.2 %collective-permute-done.9 = bf16[144,256]{1,0:T(8,128)(2,1)S(1)} collective-permute-done((bf16[144,256]{1,0:T(8,128)(2,1)S(1)}, bf16[144,256]{1,0:T(8,128)(2,1)S(1)}, u32[]{:S(2)}, u32[]{:S(2)}) %collective-permute-start.9) | collective-permute-done | bytes 73760 | tf_op jit(solution)/shard_map/reduce/ppermute | solution.py:310
  71.5 1.2 %collective-permute-done.8 = bf16[144,256]{1,0:T(8,128)(2,1)S(1)} collective-permute-done((bf16[144,256]{1,0:T(8,128)(2,1)S(1)}, bf16[144,256]{1,0:T(8,128)(2,1)S(1)}, u32[]{:S(2)}, u32[]{:S(2)}) %collective-permute-start.8) | collective-permute-done | bytes 73760 | tf_op jit(solution)/shard_map/reduce/ppermute | solution.py:310
  72.7 0.1 collective-permute-done.7
  72.9 8.2 %collective-permute-start.10 = (bf16[144,256]{1,0:T(8,128)(2,1)S(1)}, bf16[144,256]{1,0:T(8,128)(2,1)S(1)}, u32[]{:S(2)}, u32[]{:S(2)}) collective-permute-start(bf16[144,256]{1,0:T(8,128)(2,1)S(1)} %add_convert_fusion.1), channel_id=1, source_target_pairs={{0,1},{1,0},{2,3},{3,2},{4,5},{5,4},{6,7},{7,6},{8,9},{9,8},{10,11... | collective-permute-start | bytes 221192 | tf_op jit(solution)/shard_map/reduce/ppermute | solution.py:310
  81.0 1.0 %unpack.1 = bf16[4,4,32,256]{3,2,1,0:T(8,128)(2,1)} custom-call(bf16[8,208,256]{2,1,0:T(8,128)(2,1)S(1)} %all_to_all.10.recv), custom_call_target="tpu_custom_call" | custom-call | tf_op jit(solution)/shard_map/unpack/pallas_call | solution.py:416
  82.0 0.8 collective-permute-done.10
  82.8 0.7 collective-permute-start.12
  83.5 0.8 collective-permute-start.11
  84.4 1.8 %collective-permute-start.13 = (bf16[128,256]{1,0:T(8,128)(2,1)S(1)}, bf16[128,256]{1,0:T(8,128)(2,1)S(1)}, u32[]{:S(2)}, u32[]{:S(2)}) collective-permute-start(bf16[128,256]{1,0:T(8,128)(2,1)S(1)} %get-tuple-element.60), channel_id=1, source_target_pairs={{0,192},{32,224},{64,128},{96,160},{128,64},{160,96},{192,0},{224,... | collective-permute-start | bytes 196616 | tf_op jit(solution)/shard_map/reduce/ppermute | solution.py:428
  86.1 1.4 %collective-permute-done.12 = bf16[128,256]{1,0:T(8,128)(2,1)S(1)} collective-permute-done((bf16[128,256]{1,0:T(8,128)(2,1)S(1)}, bf16[128,256]{1,0:T(8,128)(2,1)S(1)}, u32[]{:S(2)}, u32[]{:S(2)}) %collective-permute-start.12) | collective-permute-done | bytes 65568 | tf_op jit(solution)/shard_map/reduce/ppermute | solution.py:428
  87.5 0.0 collective-permute-done.11
  87.5 1.2 %collective-permute-done.13 = bf16[128,256]{1,0:T(8,128)(2,1)S(1)} collective-permute-done((bf16[128,256]{1,0:T(8,128)(2,1)S(1)}, bf16[128,256]{1,0:T(8,128)(2,1)S(1)}, u32[]{:S(2)}, u32[]{:S(2)}) %collective-permute-start.13) | collective-permute-done | bytes 65568 | tf_op jit(solution)/shard_map/reduce/ppermute | solution.py:428
  88.7 5.5 %collective-permute-start.14 = (bf16[4,128,256]{2,1,0:T(8,128)(2,1)S(1)}, bf16[4,128,256]{2,1,0:T(8,128)(2,1)S(1)}, u32[]{:S(2)}, u32[]{:S(2)}) collective-permute-start(bf16[4,128,256]{2,1,0:T(8,128)(2,1)S(1)} %pad_maximum_fusion.same_core), channel_id=1, source_target_pairs={{0,32},{32,0},{64,96},{96,64},{128,160},{160,128},{192,224},{224,1... | collective-permute-start | bytes 786440 | tf_op jit(solution)/shard_map/reduce/ppermute | solution.py:430
  94.3 1.2 %collective-permute-done.14.other_core = bf16[4,128,256]{2,1,0:T(8,128)(2,1)S(1)} collective-permute-done((bf16[4,128,256]{2,1,0:T(8,128)(2,1)S(1)}, bf16[4,128,256]{2,1,0:T(8,128)(2,1)S(1)}, u32[]{:S(2)}, u32[]{:S(2)}) %collective-permute-start.14) | collective-permute-done | bytes 262176 | tf_op jit(solution)/shard_map/reduce/ppermute | solution.py:430
  95.4 1.0 %finish.1 = (f32[256,256]{1,0:T(8,128)}, f32[256,256]{1,0:T(8,128)}, f32[256,256]{1,0:T(8,128)}, f32[256,256]{1,0:T(8,128)}, f32[3,3,256]{2,1,0:T(4,128)}, /*index=5*/f32[1,256]{1,0:T(1,128)}) custom-call(s32[1]{0:T(128)} %bitcast.7.place, bf16[4,128,256]{2,1,0:T(8,128)(2,1)S(1)} %pad_maximum_fusion.same_core, ...), custom_call_target="tpu_custom_call" | custom-call | tf_op jit(solution)/shard_map/finish/pallas_call | solution.py:436
  (24 shorter events, 0.3 us)
Async XLA Ops:
  0.6 19.4 %copy-start = (bf16[256,256]{1,0:T(8,128)(2,1)S(1)}, bf16[256,256]{1,0:T(8,128)(2,1)}, u32[]{:S(2)}) copy-start(bf16[256,256]{1,0:T(8,128)(2,1)} %constant.67.clone.gather8) | copy-start | bytes 393220
  0.6 31.7 %copy-start.5 = (bf16[256,256]{1,0:T(8,128)(2,1)S(1)}, bf16[256,256]{1,0:T(8,128)(2,1)}, u32[]{:S(2)}) copy-start(bf16[256,256]{1,0:T(8,128)(2,1)} %constant.68.clone.headsum) | copy-start | bytes 393220
  0.7 31.7 %copy-start.4 = (bf16[256,256]{1,0:T(8,128)(2,1)S(1)}, bf16[256,256]{1,0:T(8,128)(2,1)}, u32[]{:S(2)}) copy-start(bf16[256,256]{1,0:T(8,128)(2,1)} %wo.1) | copy-start | bytes 393220
  0.7 31.7 %copy-start.3 = (bf16[256,256]{1,0:T(8,128)(2,1)S(1)}, bf16[256,256]{1,0:T(8,128)(2,1)}, u32[]{:S(2)}) copy-start(bf16[256,256]{1,0:T(8,128)(2,1)} %wv.1) | copy-start | bytes 393220
  0.7 31.7 %copy-start.2 = (bf16[256,256]{1,0:T(8,128)(2,1)S(1)}, bf16[256,256]{1,0:T(8,128)(2,1)}, u32[]{:S(2)}) copy-start(bf16[256,256]{1,0:T(8,128)(2,1)} %wk.1) | copy-start | bytes 393220
  0.7 31.7 %copy-start.1 = (bf16[256,256]{1,0:T(8,128)(2,1)S(1)}, bf16[256,256]{1,0:T(8,128)(2,1)}, u32[]{:S(2)}) copy-start(bf16[256,256]{1,0:T(8,128)(2,1)} %wq.1) | copy-start | bytes 393220
  0.7 1.0 %copy-start.6 = (bf16[4,4,32,256]{3,2,1,0:T(8,128)(2,1)S(1)}, bf16[4,4,32,256]{3,2,1,0:T(8,128)(2,1)}, u32[]{:S(2)}) copy-start(bf16[4,4,32,256]{3,2,1,0:T(8,128)(2,1)} %fields.1) | copy-start | bytes 786436
  1.7 0.9 copy-start.7
  2.7 29.7 %copy-start.9 = (f32[256]{0:T(256)S(1)}, f32[256]{0:T(256)}, u32[]{:S(2)}) copy-start(f32[256]{0:T(256)} %param.11) | copy-start | bytes 3076
  3.8 31.6 %copy-start.8 = (f32[3,3,256]{2,1,0:T(4,128)S(1)}, f32[3,3,256]{2,1,0:T(4,128)}, u32[]{:S(2)}) copy-start(f32[3,3,256]{2,1,0:T(4,128)} %mix.1) | copy-start | bytes 27652
  3.8 16.3 %all-to-all-start = ((bf16[8,128,256]{2,1,0:T(8,128)(2,1)}), bf16[8,128,256]{2,1,0:T(8,128)(2,1)S(1)}, u32[]{:S(2)}, u32[]{:S(2)}) async-start(bf16[8,128,256]{2,1,0:T(8,128)(2,1)} %pack.1), calls=%async_computation | async-start | bytes 1048576 | tf_op jit(solution)/shard_map/to_cells/all_to_all | solution.py:360
  20.4 7.5 %collective-permute-start.1 = (bf16[4,32,256]{2,1,0:T(8,128)(2,1)S(1)}, bf16[4,32,256]{2,1,0:T(8,128)(2,1)S(1)}, u32[]{:S(2)}, u32[]{:S(2)}) collective-permute-start(bf16[4,32,256]{2,1,0:T(8,128)(2,1)S(1)} %get-tuple-element.51), channel_id=1, source_target_pairs={{0,64},{64,0},{128,192},{192,128},{224,160},{160,224},{96,32},{32,... | collective-permute-start | bytes 196616 | tf_op jit(solution)/shard_map/halo_cols/ppermute | solution.py:329
  20.8 9.0 %collective-permute-start = (bf16[4,32,256]{2,1,0:T(8,128)(2,1)S(1)}, bf16[4,32,256]{2,1,0:T(8,128)(2,1)S(1)}, u32[]{:S(2)}, u32[]{:S(2)}) collective-permute-start(bf16[4,32,256]{2,1,0:T(8,128)(2,1)S(1)} %get-tuple-element.52), channel_id=1, source_target_pairs={{64,128},{128,64},{192,224},{224,192},{160,96},{96,160},{32,1},{1,... | collective-permute-start | bytes 196616 | tf_op jit(solution)/shard_map/halo_cols/ppermute | solution.py:329
  29.9 5.5 %collective-permute-start.3 = (bf16[6,32,256]{2,1,0:T(8,128)(2,1)S(1)}, bf16[6,32,256]{2,1,0:T(8,128)(2,1)S(1)}, u32[]{:S(2)}, u32[]{:S(2)}) collective-permute-start(bf16[6,32,256]{2,1,0:T(8,128)(2,1)S(1)} %get-tuple-element.55), channel_id=1, source_target_pairs={{0,8},{8,0},{16,24},{24,16},{1,9},{9,1},{17,25},{25,17},{2,10},{10... | collective-permute-start | bytes 294920 | tf_op jit(solution)/shard_map/halo_rows/ppermute | solution.py:329
  31.6 3.7 %collective-permute-start.2 = (bf16[6,32,256]{2,1,0:T(8,128)(2,1)S(1)}, bf16[6,32,256]{2,1,0:T(8,128)(2,1)S(1)}, u32[]{:S(2)}, u32[]{:S(2)}) collective-permute-start(bf16[6,32,256]{2,1,0:T(8,128)(2,1)S(1)} %get-tuple-element.56), channel_id=1, source_target_pairs={{8,16},{16,8},{9,17},{17,9},{10,18},{18,10},{11,19},{19,11},{12,20... | collective-permute-start | bytes 294920 | tf_op jit(solution)/shard_map/halo_rows/ppermute | solution.py:329
  56.8 6.7 %collective-permute-start.6 = (bf16[144,256]{1,0:T(8,128)(2,1)S(1)}, bf16[144,256]{1,0:T(8,128)(2,1)S(1)}, u32[]{:S(2)}, u32[]{:S(2)}) collective-permute-start(bf16[144,256]{1,0:T(8,128)(2,1)S(1)} %slice_reduce_fusion), channel_id=1, source_target_pairs={{0,24},{8,16},{16,8},{24,0},{1,25},{9,17},{17,9},{25,1},{2,26},{10... | collective-permute-start | bytes 221192 | tf_op jit(solution)/shard_map/reduce/ppermute | solution.py:310
  61.6 4.8 %collective-permute-start.5 = (bf16[144,256]{1,0:T(8,128)(2,1)S(1)}, bf16[144,256]{1,0:T(8,128)(2,1)S(1)}, u32[]{:S(2)}, u32[]{:S(2)}) collective-permute-start(bf16[144,256]{1,0:T(8,128)(2,1)S(1)} %slice_reduce_fusion), channel_id=1, source_target_pairs={{0,16},{8,24},{16,0},{24,8},{1,17},{9,25},{17,1},{25,9},{2,18},{10... | collective-permute-start | bytes 221192 | tf_op jit(solution)/shard_map/reduce/ppermute | solution.py:310
  63.5 3.4 %collective-permute-start.4 = (bf16[144,256]{1,0:T(8,128)(2,1)S(1)}, bf16[144,256]{1,0:T(8,128)(2,1)S(1)}, u32[]{:S(2)}, u32[]{:S(2)}) collective-permute-start(bf16[144,256]{1,0:T(8,128)(2,1)S(1)} %slice_reduce_fusion), channel_id=1, source_target_pairs={{0,8},{8,0},{16,24},{24,16},{1,9},{9,1},{17,25},{25,17},{2,10},{10... | collective-permute-start | bytes 221192 | tf_op jit(solution)/shard_map/reduce/ppermute | solution.py:310
  67.0 4.5 %collective-permute-start.9 = (bf16[144,256]{1,0:T(8,128)(2,1)S(1)}, bf16[144,256]{1,0:T(8,128)(2,1)S(1)}, u32[]{:S(2)}, u32[]{:S(2)}) collective-permute-start(bf16[144,256]{1,0:T(8,128)(2,1)S(1)} %add_convert_fusion.2), channel_id=1, source_target_pairs={{0,6},{1,7},{2,4},{3,5},{4,2},{5,3},{6,0},{7,1},{8,14},{9,15},{10,... | collective-permute-start | bytes 221192 | tf_op jit(solution)/shard_map/reduce/ppermute | solution.py:310
  68.0 4.7 %collective-permute-start.8 = (bf16[144,256]{1,0:T(8,128)(2,1)S(1)}, bf16[144,256]{1,0:T(8,128)(2,1)S(1)}, u32[]{:S(2)}, u32[]{:S(2)}) collective-permute-start(bf16[144,256]{1,0:T(8,128)(2,1)S(1)} %add_convert_fusion.2), channel_id=1, source_target_pairs={{0,4},{1,5},{2,6},{3,7},{4,0},{5,1},{6,2},{7,3},{8,12},{9,13},{10,... | collective-permute-start | bytes 221192 | tf_op jit(solution)/shard_map/reduce/ppermute | solution.py:310
  68.3 4.5 %collective-permute-start.7 = (bf16[144,256]{1,0:T(8,128)(2,1)S(1)}, bf16[144,256]{1,0:T(8,128)(2,1)S(1)}, u32[]{:S(2)}, u32[]{:S(2)}) collective-permute-start(bf16[144,256]{1,0:T(8,128)(2,1)S(1)} %add_convert_fusion.2), channel_id=1, source_target_pairs={{0,2},{1,3},{2,0},{3,1},{4,6},{5,7},{6,4},{7,5},{8,10},{9,11},{10,... | collective-permute-start | bytes 221192 | tf_op jit(solution)/shard_map/reduce/ppermute | solution.py:310
  72.9 9.9 %collective-permute-start.10 = (bf16[144,256]{1,0:T(8,128)(2,1)S(1)}, bf16[144,256]{1,0:T(8,128)(2,1)S(1)}, u32[]{:S(2)}, u32[]{:S(2)}) collective-permute-start(bf16[144,256]{1,0:T(8,128)(2,1)S(1)} %add_convert_fusion.1), channel_id=1, source_target_pairs={{0,1},{1,0},{2,3},{3,2},{4,5},{5,4},{6,7},{7,6},{8,9},{9,8},{10,11... | collective-permute-start | bytes 221192 | tf_op jit(solution)/shard_map/reduce/ppermute | solution.py:310
  82.8 4.7 %collective-permute-start.12 = (bf16[128,256]{1,0:T(8,128)(2,1)S(1)}, bf16[128,256]{1,0:T(8,128)(2,1)S(1)}, u32[]{:S(2)}, u32[]{:S(2)}) collective-permute-start(bf16[128,256]{1,0:T(8,128)(2,1)S(1)} %get-tuple-element.60), channel_id=1, source_target_pairs={{0,128},{32,160},{64,192},{96,224},{128,0},{160,32},{192,64},{224,... | collective-permute-start | bytes 196616 | tf_op jit(solution)/shard_map/reduce/ppermute | solution.py:428
  83.5 4.0 %collective-permute-start.11 = (bf16[128,256]{1,0:T(8,128)(2,1)S(1)}, bf16[128,256]{1,0:T(8,128)(2,1)S(1)}, u32[]{:S(2)}, u32[]{:S(2)}) collective-permute-start(bf16[128,256]{1,0:T(8,128)(2,1)S(1)} %get-tuple-element.60), channel_id=1, source_target_pairs={{0,64},{32,96},{64,0},{96,32},{128,192},{160,224},{192,128},{224,1... | collective-permute-start | bytes 196616 | tf_op jit(solution)/shard_map/reduce/ppermute | solution.py:428
  84.4 4.3 %collective-permute-start.13 = (bf16[128,256]{1,0:T(8,128)(2,1)S(1)}, bf16[128,256]{1,0:T(8,128)(2,1)S(1)}, u32[]{:S(2)}, u32[]{:S(2)}) collective-permute-start(bf16[128,256]{1,0:T(8,128)(2,1)S(1)} %get-tuple-element.60), channel_id=1, source_target_pairs={{0,192},{32,224},{64,128},{96,160},{128,64},{160,96},{192,0},{224,... | collective-permute-start | bytes 196616 | tf_op jit(solution)/shard_map/reduce/ppermute | solution.py:428
  88.7 6.7 %collective-permute-start.14 = (bf16[4,128,256]{2,1,0:T(8,128)(2,1)S(1)}, bf16[4,128,256]{2,1,0:T(8,128)(2,1)S(1)}, u32[]{:S(2)}, u32[]{:S(2)}) collective-permute-start(bf16[4,128,256]{2,1,0:T(8,128)(2,1)S(1)} %pad_maximum_fusion.same_core), channel_id=1, source_target_pairs={{0,32},{32,0},{64,96},{96,64},{128,160},{160,128},{192,224},{224,1... | collective-permute-start | bytes 786440 | tf_op jit(solution)/shard_map/reduce/ppermute | solution.py:430

commit v10 on v9

--- a/solution.py
+++ b/solution.py
@@ -151,72 +151,52 @@
     mixed_out[...] = dot(att_out[...], wo[...]).astype(BF)
 
 
-def backward_kernel(
-    sizes,
-    place,
-    cot,
-    left,
-    right,
-    above,
-    below,
-    x_in,
-    q_in,
-    prob_in,
-    att_in,
-    mixed_in,
-    mat_k,
-    mat_v,
-    gain,
-    mix,
-    wq,
-    wk,
-    wv,
-    wo,
-    gather8,
-    headsum,
-    send,
-    padded,
-    sums,
-):
-    parts = send.shape[0]
+def backward_kernel(picked, sizes, ends, place, cot, left, right, *refs):
+    if ends:
+        above, below, part_in, grads_in, extra_in = refs[:5]
+        refs = refs[5:]
+    x_in, q_in, prob_in, att_in, mixed_in, mat_k, mat_v, gain, mix, wq, wk, wv, wo, gather8, headsum = refs[:15]
+    outs, (padded, sums) = refs[15:-2], refs[-2:]
     tile_rows, tile_cols, all_members, width = cot.shape
-    members = all_members // parts
     head_dim = width // HEADS
     scale = 1.0 / math.sqrt(head_dim)
-    cells = tile_rows * tile_cols
-    tokens = cells * all_members
     pad_cols = tile_cols + 2
-    base = cells * members
+    line = tile_cols * all_members
+    cells = [r * tile_cols + c for r in picked for c in range(tile_cols)]
+    tokens = len(cells) * all_members
     row, block = place[0], place[1]
+
+    def pick(ref):
+        return jnp.concatenate([ref[r * line : (r + 1) * line, :] for r in picked], axis=0)
 
     def side(inside, x):
         x = x.astype(F32)
         return jnp.where(inside, x, jnp.zeros_like(x))
 
     in_left, in_right = block > 0, block < sizes[1] - 1
-    edges = {0: (above, row > 0), tile_rows + 1: (below, row < sizes[0] - 1)}
     for r in range(tile_rows + 2):
         start = r * pad_cols
-        if r in edges:
-            source, inside = edges[r]
+        if 0 < r <= tile_rows:
+            padded[start] = side(in_left, left[r - 1])
+            padded[start + 1 : start + 1 + tile_cols] = cot[r - 1].astype(F32)
+            padded[start + 1 + tile_cols] = side(in_right, right[r - 1])
+        elif ends:
+            source, inside = (above, row > 0) if r == 0 else (below, row < sizes[0] - 1)
             padded[start] = side(inside & in_left, source[0])
             padded[start + 1 : start + 1 + tile_cols] = side(inside, source[1 : 1 + tile_cols])
             padded[start + 1 + tile_cols] = side(inside & in_right, source[1 + tile_cols])
-        else:
-            padded[start] = side(in_left, left[r - 1])
-            padded[start + 1 : start + 1 + tile_cols] = cot[r - 1].astype(F32)
-            padded[start + 1 + tile_cols] = side(in_right, right[r - 1])
 
     def shifted(i, j):
-        picked = [
-            padded[(r + 2 - i) * pad_cols + 2 - j : (r + 2 - i) * pad_cols + 2 - j + tile_cols]
-            for r in range(tile_rows)
+        moved = [
+            padded[(r + 2 - i) * pad_cols + 2 - j : (r + 2 - i) * pad_cols + 2 - j + tile_cols] for r in picked
         ]
-        return jnp.concatenate(picked, axis=0).reshape(tokens, width)
-
-    inv, normed = norm(x_in[...].astype(F32))
+        return jnp.concatenate(moved, axis=0).reshape(tokens, width)
+
+    inv, normed = norm(pick(x_in).astype(F32))
     inputs = (normed * gain[...]).astype(BF)
-    mixed = mixed_in[...].astype(F32)
+    queries = pick(q_in)
+    attended = pick(att_in)
+    mixed = pick(mixed_in).astype(F32)
     extra = []
     conv = jnp.zeros((tokens, width), F32)
     for i in range(3):
@@ -226,11 +206,11 @@
             extra.append(jnp.sum(mixed * moved, axis=0, keepdims=True))
     grad_mixed = conv.astype(BF)
     grad_att = dot(grad_mixed, wo[...], NT).astype(BF)
-    for c in range(cells):
-        rows = slice(c * all_members, (c + 1) * all_members)
+    for k, c in enumerate(cells):
+        rows = slice(k * all_members, (k + 1) * all_members)
         sums[rows, :] = dot(grad_att[rows], mat_v[c], NT)
 
-    prob = prob_in[...]
+    prob = pick(prob_in)
     prob_b = prob.astype(BF)
     grad_prob = sums[...]
     inner = head_sums(prob * grad_prob, headsum)
@@ -244,10 +224,10 @@
         return out
 
     gq_l, gk_l, gv_l = [], [], []
-    for c in range(cells):
-        rows = slice(c * all_members, (c + 1) * all_members)
+    for k, c in enumerate(cells):
+        rows = slice(k * all_members, (k + 1) * all_members)
         gq_l.append(dot(grad_score[rows], mat_k[c]).astype(BF))
-        gk_l.append(diagonal(dot(grad_score[rows], q_in[rows, :], TN)).astype(BF))
+        gk_l.append(diagonal(dot(grad_score[rows], queries[rows], TN)).astype(BF))
         gv_l.append(diagonal(dot(prob_b[rows], grad_att[rows], TN)).astype(BF))
     grad_q = jnp.concatenate(gq_l, axis=0)
     grad_k = jnp.concatenate(gk_l, axis=0)
@@ -258,23 +238,36 @@
     grad_normed = grad_in * gain[...]
     mean = jnp.mean(grad_normed * normed, axis=-1, keepdims=True)
     grad = (shifted(1, 1) + inv * (grad_normed - normed * mean)).astype(BF)
-    for g in range(cells // 8):
-        back = dot(gather8[...], grad[g * 256 : (g + 1) * 256], TN).astype(BF)
-        send[:, g * 32 : (g + 1) * 32, :] = back.reshape(parts, 32, width)
-
+    back = dot(gather8[...], grad, TN).astype(BF)
     weights = [
         dot(inputs, grad_q, TN),
         dot(inputs, grad_k, TN),
         dot(inputs, grad_v, TN),
-        dot(att_in[...], grad_mixed, TN),
+        dot(attended, grad_mixed, TN),
     ]
+    extras = jnp.concatenate(extra + [jnp.zeros((16 - len(extra), width), F32)], axis=0)
+    if not ends:
+        part_out, grads_out, extra_out = outs
+        part_out[...] = back.reshape(part_out.shape)
+        for k in range(4):
+            grads_out[k] = weights[k]
+        extra_out[...] = extras
+        return
+    (send,) = outs
+    parts = send.shape[0]
+    members = all_members // parts
+    base = tile_rows * tile_cols * members
     shard = 4 * width // parts
+    step = tile_cols * members
+    back = back.reshape(parts, len(picked) * step, width)
+    for k, r in enumerate(picked):
+        send[:, r * step : (r + 1) * step, :] = back[:, k * step : (k + 1) * step]
+    send[:, step : base - step, :] = part_in[...]
     for j in range(parts):
         which, start = divmod(j * shard, width)
-        send[j, base : base + shard, :] = weights[which][start : start + shard].astype(BF)
-    extras = jnp.concatenate(extra + [jnp.zeros((16 - len(extra), width), F32)], axis=0).astype(BF)
-    for j in range(parts):
-        send[j, base + shard : base + shard + 16, :] = extras
+        total = weights[which][start : start + shard] + grads_in[which, start : start + shard, :]
+        send[j, base : base + shard, :] = total.astype(BF)
+        send[j, base + shard : base + shard + 16, :] = (extras + extra_in[...]).astype(BF)
 
 
 def unpack_kernel(recv, out):
@@ -382,32 +375,39 @@
             scratch_shapes=[pltpu.VMEM((tokens, width), F32)],
             compiler_params=params,
         )(near(x), gain, w_query, w_key, w_value, w_out, headsum)
+    left, right, *kept = lax.optimization_barrier((left, right, *kept))
     with jax.named_scope("halo_rows"):
         top, bottom = [jnp.concatenate([left[r : r + 1], cot[r], right[r : r + 1]], axis=0) for r in (0, rows - 1)]
         rows_at = {r: r for r in range(grid[0])}
         below, above = swap(bottom, top, lax.axis_index("row"), "row", rows_at, False)
-    with jax.named_scope("backward"):
+
+    half = tokens // 2
+    scratch = [
+        pltpu.VMEM(((rows + 2) * (per + 2), members * parts, width), F32),
+        pltpu.VMEM((half, width), F32),
+    ]
+    halo = [near(a) for a in (cot, left, right)]
+    rest = [near(a) for a in (x, *kept)] + [gain, mix_kernel, w_query, w_key, w_value, w_out, gather8, headsum]
+    with jax.named_scope("backward_inner"):
+        inner = pl.pallas_call(
+            functools.partial(backward_kernel, tuple(range(1, rows - 1)), (grid[0], blocks), False),
+            in_specs=[smem] + [vmem] * 18,
+            out_shape=(
+                pltpu.VMEM((parts, base // 2, width), BF),
+                pltpu.VMEM((4, width, width), F32),
+                pltpu.VMEM((16, width), F32),
+            ),
+            scratch_shapes=scratch,
+            compiler_params=params,
+        )(place, *halo, *rest)
+    with jax.named_scope("backward_ends"):
         back = pl.pallas_call(
-            functools.partial(backward_kernel, (grid[0], blocks)),
-            in_specs=[smem] + [vmem] * 20,
+            functools.partial(backward_kernel, (0, rows - 1), (grid[0], blocks), True),
+            in_specs=[smem] + [vmem] * 23,
             out_shape=pltpu.VMEM((parts, base + shard + 16, width), BF),
-            scratch_shapes=[
-                pltpu.VMEM(((rows + 2) * (per + 2), members * parts, width), F32),
-                pltpu.VMEM((tokens, width), F32),
-            ],
-            compiler_params=params,
-        )(
-            place,
-            *[near(a) for a in (cot, left, right, above, below, x, *kept)],
-            gain,
-            mix_kernel,
-            w_query,
-            w_key,
-            w_value,
-            w_out,
-            gather8,
-            headsum,
-        )
+            scratch_shapes=scratch,
+            compiler_params=params,
+        )(place, *halo, *[near(a) for a in (above, below, *inner)], *rest)
     with jax.named_scope("to_members"):
         landed = lax.all_to_all(back, "mem", 0, 0)
     with jax.named_scope("unpack"):

time: 96.8 us -> 95.2 us (0.983)
  starting transfers between devices: 43.7 us -> 41.3 us
  waiting for transfers between devices: 21.8 us -> 20.5 us
  Pallas kernels: 10.9 us -> 12.1 us
    ppermute x4, waiting for transfers between devices: 1.93 us -> 0.01 us  [swap(): lax.ppermute(jnp.where(spot % 2 == odd, last, first), axis, pairs)]
    ppermute x7, starting transfers between devices: 18.2 us -> 16.7 us  [meet(): lax.ppermute(values, axis, partner(axis, k))]
    pallas_call x1 -> x2, Pallas kernels: 4.51 us -> 5.79 us  [the longest x1 2.92 us: local(): pl.pallas_call(functools.partial(backward_kernel, (0, rows - 1), (grid[0]...]
  transfers between devices with their start and end apart: 16 -> 16, of which waited for: 11 -> 9; matrix products, arithmetic and copies ran while one was open for 0% -> 0% of each run, Pallas kernels for 4% -> 7%
where the time goes in v10:
time: 95.2 us; the launch traced here: 94.9 us
  starting transfers between devices  41.3 us (43%)
  waiting for transfers between devices  20.5 us (22%)
  blocking collectives  17.7 us (19%)
  Pallas kernels  12.1 us (13%)
  local copies, waits for them, and re-layouts  2.04 us (2%)
    all_to_all x1, blocking collectives, local(): landed = lax.all_to_all(back, 'mem', 0, 0)  17.7 us
    ppermute x7, starting transfers between devices, meet(): lax.ppermute(values, axis, partner(axis, k))  16.7 us
    all_to_all x1, waiting for transfers between devices, local(): recv = lax.all_to_all(send, 'mem', 0, 0)  9.5 us
    ppermute x4, starting transfers between devices, swap(): lax.ppermute(jnp.where(spot % 2 == odd, last, first), axis, pairs)  8.94 us
    ppermute x7, waiting for transfers between devices, meet(): lax.ppermute(values, axis, partner(axis, k))  7.25 us
    all_to_all x1, starting transfers between devices, local(): recv = lax.all_to_all(send, 'mem', 0, 0)  6.77 us
    ppermute x1, starting transfers between devices, local(): other_core = lax.ppermute(same_core, 'mem', partner('mem', 1))  5.62 us
    ppermute x3, starting transfers between devices, local(): lax.ppermute(piece, 'mem', partner('mem', k))  3.34 us
  transfers between devices with their start and end apart: 16, of which 9 were waited for; matrix products, arithmetic and copies ran while one was open for 0% of the time, Pallas kernels for 7%

profile of v10, /device:TPU:1, one launch (start us, length us, event | category | flops | bytes accessed | tf_op | source)
XLA Modules:
  0.0 94.9 jit_solution(8794233407169222485)
XLA Ops:
  0.6 0.0 copy-start
  0.6 0.0 copy-start.5
  0.7 0.0 copy-start.4
  0.7 0.0 copy-start.3
  0.7 1.0 %copy-done.6 = bf16[4,4,32,256]{3,2,1,0:T(8,128)(2,1)S(1)} copy-done((bf16[4,4,32,256]{3,2,1,0:T(8,128)(2,1)S(1)}, bf16[4,4,32,256]{3,2,1,0:T(8,128)(2,1)}, u32[]{:S(2)}) %copy-start.6) | copy-done | bytes 262168
  1.7 0.9 copy-done.7
  2.7 1.1 %pack.1 = bf16[8,128,256]{2,1,0:T(8,128)(2,1)} custom-call(bf16[4,4,32,256]{3,2,1,0:T(8,128)(2,1)S(1)} %copy-done.6, bf16[4,4,32,256]{3,2,1,0:T(8,128)(2,1)S(1)} %copy-done.7), custom_call_target="tpu_custom_call" | custom-call | tf_op jit(solution)/shard_map/pack/pallas_call | solution.py:347
  3.8 6.8 %all-to-all-start = ((bf16[8,128,256]{2,1,0:T(8,128)(2,1)}), bf16[8,128,256]{2,1,0:T(8,128)(2,1)S(1)}, u32[]{:S(2)}, u32[]{:S(2)}) async-start(bf16[8,128,256]{2,1,0:T(8,128)(2,1)} %pack.1), calls=%async_computation | async-start | bytes 1048576 | tf_op jit(solution)/shard_map/to_cells/all_to_all | solution.py:353
  10.5 9.5 %all-to-all-done.recv = bf16[8,128,256]{2,1,0:T(8,128)(2,1)S(1)} async-done(((bf16[8,128,256]{2,1,0:T(8,128)(2,1)}), bf16[8,128,256]{2,1,0:T(8,128)(2,1)S(1)}, u32[]{:S(2)}, u32[]{:S(2)}) %all-to-all-start) | async-done | bytes 524320 | tf_op jit(solution)/shard_map/to_cells/all_to_all | solution.py:353
  20.0 0.3 order.1
  20.4 0.4 collective-permute-start.1
  20.8 7.1 %collective-permute-start = (bf16[4,32,256]{2,1,0:T(8,128)(2,1)S(1)}, bf16[4,32,256]{2,1,0:T(8,128)(2,1)S(1)}, u32[]{:S(2)}, u32[]{:S(2)}) collective-permute-start(bf16[4,32,256]{2,1,0:T(8,128)(2,1)S(1)} %get-tuple-element.74), channel_id=1, source_target_pairs={{64,128},{128,64},{192,224},{224,192},{160,96},{96,160},{32,1},{1,... | collective-permute-start | bytes 196616 | tf_op jit(solution)/shard_map/halo_cols/ppermute | solution.py:322
  27.9 3.0 %forward.1 = (bf16[512,256]{1,0:T(8,128)(2,1)S(1)}, f32[512,256]{1,0:T(8,128)S(1)}, bf16[512,256]{1,0:T(8,128)(2,1)S(1)}, bf16[512,256]{1,0:T(8,128)(2,1)S(1)}, ...) custom-call(bf16[512,256]{1,0:T(8,128)(2,1)S(1)} %get-tuple-element.41.x_in.refs_0_.refs_5_, ...), custom_call_target="tpu_custom_call" | custom-call | tf_op jit(solution)/shard_map/forward/pallas_call | solution.py:372
  30.9 0.0 collective-permute-done.1
  30.9 0.0 collective-permute-done
  31.0 0.8 collective-permute-start.3
  31.8 0.7 collective-permute-start.2
  32.5 0.1 pad_add_fusion.place
  32.5 2.9 %backward_inner.1 = (bf16[8,32,256]{2,1,0:T(8,128)(2,1)S(1)}, f32[4,256,256]{2,1,0:T(8,128)S(1)}, f32[16,256]{1,0:T(8,128)S(1)}) custom-call(s32[2]{0:T(128)S(1)} %pad_add_fusion.place, bf16[4,4,32,256]{3,2,1,0:T(8,128)(2,1)S(1)} %get-tuple-element.39.cot, bf16[4,32,256]{2,1,0:T(8,128)(2,1)S(1)} %get-tuple-element.52.left, ...), custom_call_target="tpu_custom_call" | custom-call | tf_op jit(solution)/shard_map/backward_inner/pallas_call | solution.py:392
  35.4 0.0 collective-permute-done.3
  35.4 0.0 collective-permute-done.2
  35.5 2.9 %backward_ends.1 = bf16[8,208,256]{2,1,0:T(8,128)(2,1)S(1)} custom-call(s32[2]{0:T(128)S(1)} %pad_add_fusion.place, bf16[4,4,32,256]{3,2,1,0:T(8,128)(2,1)S(1)} %get-tuple-element.39.cot, bf16[4,32,256]{2,1,0:T(8,128)(2,1)S(1)} %get-tuple-element.52.left, bf16[4,32,256]{2,1,0:T(8,128)(2,1)S(1)} %get-tuple-element.53.right, ...), custom_call_target="tpu_custom_call" | custom-call | tf_op jit(solution)/shard_map/backward_ends/pallas_call | solution.py:404
  38.4 17.7 %all_to_all.10.recv = bf16[8,208,256]{2,1,0:T(8,128)(2,1)S(1)} all-to-all(bf16[8,208,256]{2,1,0:T(8,128)(2,1)S(1)} %backward_ends.1), channel_id=1, replica_groups=mesh['mem'=8,'row'=4,'col'=8] {'mem'}, dimensions={0} | all-to-all | bytes 1703936 | tf_op jit(solution)/shard_map/to_members/all_to_all | solution.py:412
  56.1 0.1 slice_reduce_fusion
  56.1 3.7 %collective-permute-start.6 = (bf16[144,256]{1,0:T(8,128)(2,1)S(1)}, bf16[144,256]{1,0:T(8,128)(2,1)S(1)}, u32[]{:S(2)}, u32[]{:S(2)}) collective-permute-start(bf16[144,256]{1,0:T(8,128)(2,1)S(1)} %slice_reduce_fusion), channel_id=1, source_target_pairs={{0,24},{8,16},{16,8},{24,0},{1,25},{9,17},{17,9},{25,1},{2,26},{10... | collective-permute-start | bytes 221192 | tf_op jit(solution)/shard_map/reduce/ppermute | solution.py:303
  59.8 1.9 %collective-permute-start.5 = (bf16[144,256]{1,0:T(8,128)(2,1)S(1)}, bf16[144,256]{1,0:T(8,128)(2,1)S(1)}, u32[]{:S(2)}, u32[]{:S(2)}) collective-permute-start(bf16[144,256]{1,0:T(8,128)(2,1)S(1)} %slice_reduce_fusion), channel_id=1, source_target_pairs={{0,16},{8,24},{16,0},{24,8},{1,17},{9,25},{17,1},{25,9},{2,18},{10... | collective-permute-start | bytes 221192 | tf_op jit(solution)/shard_map/reduce/ppermute | solution.py:303
  61.7 0.2 collective-permute-start.4
  61.9 0.0 collective-permute-done.6
  61.9 2.7 %collective-permute-done.5 = bf16[144,256]{1,0:T(8,128)(2,1)S(1)} collective-permute-done((bf16[144,256]{1,0:T(8,128)(2,1)S(1)}, bf16[144,256]{1,0:T(8,128)(2,1)S(1)}, u32[]{:S(2)}, u32[]{:S(2)}) %collective-permute-start.5) | collective-permute-done | bytes 73760 | tf_op jit(solution)/shard_map/reduce/ppermute | solution.py:303
  64.6 0.6 collective-permute-done.4
  65.2 1.8 %collective-permute-start.9 = (bf16[144,256]{1,0:T(8,128)(2,1)S(1)}, bf16[144,256]{1,0:T(8,128)(2,1)S(1)}, u32[]{:S(2)}, u32[]{:S(2)}) collective-permute-start(bf16[144,256]{1,0:T(8,128)(2,1)S(1)} %add_convert_fusion.2), channel_id=1, source_target_pairs={{0,6},{1,7},{2,4},{3,5},{4,2},{5,3},{6,0},{7,1},{8,14},{9,15},{10,... | collective-permute-start | bytes 221192 | tf_op jit(solution)/shard_map/reduce/ppermute | solution.py:303
  67.1 0.0 collective-permute-start.8
  67.1 1.5 %collective-permute-start.7 = (bf16[144,256]{1,0:T(8,128)(2,1)S(1)}, bf16[144,256]{1,0:T(8,128)(2,1)S(1)}, u32[]{:S(2)}, u32[]{:S(2)}) collective-permute-start(bf16[144,256]{1,0:T(8,128)(2,1)S(1)} %add_convert_fusion.2), channel_id=1, source_target_pairs={{0,2},{1,3},{2,0},{3,1},{4,6},{5,7},{6,4},{7,5},{8,10},{9,11},{10,... | collective-permute-start | bytes 221192 | tf_op jit(solution)/shard_map/reduce/ppermute | solution.py:303
  68.6 1.2 %collective-permute-done.9 = bf16[144,256]{1,0:T(8,128)(2,1)S(1)} collective-permute-done((bf16[144,256]{1,0:T(8,128)(2,1)S(1)}, bf16[144,256]{1,0:T(8,128)(2,1)S(1)}, u32[]{:S(2)}, u32[]{:S(2)}) %collective-permute-start.9) | collective-permute-done | bytes 73760 | tf_op jit(solution)/shard_map/reduce/ppermute | solution.py:303
  69.7 2.0 %collective-permute-done.8 = bf16[144,256]{1,0:T(8,128)(2,1)S(1)} collective-permute-done((bf16[144,256]{1,0:T(8,128)(2,1)S(1)}, bf16[144,256]{1,0:T(8,128)(2,1)S(1)}, u32[]{:S(2)}, u32[]{:S(2)}) %collective-permute-start.8) | collective-permute-done | bytes 73760 | tf_op jit(solution)/shard_map/reduce/ppermute | solution.py:303
  71.8 0.0 collective-permute-done.7
  71.8 7.6 %collective-permute-start.10 = (bf16[144,256]{1,0:T(8,128)(2,1)S(1)}, bf16[144,256]{1,0:T(8,128)(2,1)S(1)}, u32[]{:S(2)}, u32[]{:S(2)}) collective-permute-start(bf16[144,256]{1,0:T(8,128)(2,1)S(1)} %add_convert_fusion.1), channel_id=1, source_target_pairs={{0,1},{1,0},{2,3},{3,2},{4,5},{5,4},{6,7},{7,6},{8,9},{9,8},{10,11... | collective-permute-start | bytes 221192 | tf_op jit(solution)/shard_map/reduce/ppermute | solution.py:303
  79.4 1.0 %unpack.1 = bf16[4,4,32,256]{3,2,1,0:T(8,128)(2,1)} custom-call(bf16[8,208,256]{2,1,0:T(8,128)(2,1)S(1)} %all_to_all.10.recv), custom_call_target="tpu_custom_call" | custom-call | tf_op jit(solution)/shard_map/unpack/pallas_call | solution.py:416
  80.4 0.8 collective-permute-done.10
  81.2 0.7 collective-permute-start.12
  81.9 0.8 collective-permute-start.11
  82.7 1.8 %collective-permute-start.13 = (bf16[128,256]{1,0:T(8,128)(2,1)S(1)}, bf16[128,256]{1,0:T(8,128)(2,1)S(1)}, u32[]{:S(2)}, u32[]{:S(2)}) collective-permute-start(bf16[128,256]{1,0:T(8,128)(2,1)S(1)} %get-tuple-element.82), channel_id=1, source_target_pairs={{0,192},{32,224},{64,128},{96,160},{128,64},{160,96},{192,0},{224,... | collective-permute-start | bytes 196616 | tf_op jit(solution)/shard_map/reduce/ppermute | solution.py:428
  84.5 1.4 %collective-permute-done.12 = bf16[128,256]{1,0:T(8,128)(2,1)S(1)} collective-permute-done((bf16[128,256]{1,0:T(8,128)(2,1)S(1)}, bf16[128,256]{1,0:T(8,128)(2,1)S(1)}, u32[]{:S(2)}, u32[]{:S(2)}) %collective-permute-start.12) | collective-permute-done | bytes 65568 | tf_op jit(solution)/shard_map/reduce/ppermute | solution.py:428
  85.9 0.0 collective-permute-done.11
  85.9 1.2 %collective-permute-done.13 = bf16[128,256]{1,0:T(8,128)(2,1)S(1)} collective-permute-done((bf16[128,256]{1,0:T(8,128)(2,1)S(1)}, bf16[128,256]{1,0:T(8,128)(2,1)S(1)}, u32[]{:S(2)}, u32[]{:S(2)}) %collective-permute-start.13) | collective-permute-done | bytes 65568 | tf_op jit(solution)/shard_map/reduce/ppermute | solution.py:428
  87.1 5.6 %collective-permute-start.14 = (bf16[4,128,256]{2,1,0:T(8,128)(2,1)S(1)}, bf16[4,128,256]{2,1,0:T(8,128)(2,1)S(1)}, u32[]{:S(2)}, u32[]{:S(2)}) collective-permute-start(bf16[4,128,256]{2,1,0:T(8,128)(2,1)S(1)} %pad_maximum_fusion.same_core), channel_id=1, source_target_pairs={{0,32},{32,0},{64,96},{96,64},{128,160},{160,128},{192,224},{224,1... | collective-permute-start | bytes 786440 | tf_op jit(solution)/shard_map/reduce/ppermute | solution.py:430
  92.7 1.2 %collective-permute-done.14.other_core = bf16[4,128,256]{2,1,0:T(8,128)(2,1)S(1)} collective-permute-done((bf16[4,128,256]{2,1,0:T(8,128)(2,1)S(1)}, bf16[4,128,256]{2,1,0:T(8,128)(2,1)S(1)}, u32[]{:S(2)}, u32[]{:S(2)}) %collective-permute-start.14) | collective-permute-done | bytes 262176 | tf_op jit(solution)/shard_map/reduce/ppermute | solution.py:430
  93.9 1.0 %finish.1 = (f32[256,256]{1,0:T(8,128)}, f32[256,256]{1,0:T(8,128)}, f32[256,256]{1,0:T(8,128)}, f32[256,256]{1,0:T(8,128)}, f32[3,3,256]{2,1,0:T(4,128)}, /*index=5*/f32[1,256]{1,0:T(1,128)}) custom-call(s32[1]{0:T(128)} %bitcast.7.place, bf16[4,128,256]{2,1,0:T(8,128)(2,1)S(1)} %pad_maximum_fusion.same_core, ...), custom_call_target="tpu_custom_call" | custom-call | tf_op jit(solution)/shard_map/finish/pallas_call | solution.py:436
  (25 shorter events, 0.3 us)
Async XLA Ops:
  0.6 19.4 %copy-start = (bf16[256,256]{1,0:T(8,128)(2,1)S(1)}, bf16[256,256]{1,0:T(8,128)(2,1)}, u32[]{:S(2)}) copy-start(bf16[256,256]{1,0:T(8,128)(2,1)} %constant.67.clone.gather8.refs_13_.refs_18_) | copy-start | bytes 393220
  0.6 27.2 %copy-start.5 = (bf16[256,256]{1,0:T(8,128)(2,1)S(1)}, bf16[256,256]{1,0:T(8,128)(2,1)}, u32[]{:S(2)}) copy-start(bf16[256,256]{1,0:T(8,128)(2,1)} %constant.68.clone.headsum.refs_14_.refs_19_) | copy-start | bytes 393220
  0.7 27.2 %copy-start.4 = (bf16[256,256]{1,0:T(8,128)(2,1)S(1)}, bf16[256,256]{1,0:T(8,128)(2,1)}, u32[]{:S(2)}) copy-start(bf16[256,256]{1,0:T(8,128)(2,1)} %refs_17_) | copy-start | bytes 393220
  0.7 27.2 %copy-start.3 = (bf16[256,256]{1,0:T(8,128)(2,1)S(1)}, bf16[256,256]{1,0:T(8,128)(2,1)}, u32[]{:S(2)}) copy-start(bf16[256,256]{1,0:T(8,128)(2,1)} %refs_16_) | copy-start | bytes 393220
  0.7 27.2 %copy-start.2 = (bf16[256,256]{1,0:T(8,128)(2,1)S(1)}, bf16[256,256]{1,0:T(8,128)(2,1)}, u32[]{:S(2)}) copy-start(bf16[256,256]{1,0:T(8,128)(2,1)} %refs_15_) | copy-start | bytes 393220
  0.7 27.2 %copy-start.1 = (bf16[256,256]{1,0:T(8,128)(2,1)S(1)}, bf16[256,256]{1,0:T(8,128)(2,1)}, u32[]{:S(2)}) copy-start(bf16[256,256]{1,0:T(8,128)(2,1)} %refs_14_.1) | copy-start | bytes 393220
  0.7 1.0 %copy-start.6 = (bf16[4,4,32,256]{3,2,1,0:T(8,128)(2,1)S(1)}, bf16[4,4,32,256]{3,2,1,0:T(8,128)(2,1)}, u32[]{:S(2)}) copy-start(bf16[4,4,32,256]{3,2,1,0:T(8,128)(2,1)} %fields.1) | copy-start | bytes 786436
  1.7 0.9 %copy-start.7 = (bf16[4,4,32,256]{3,2,1,0:T(8,128)(2,1)S(1)}, bf16[4,4,32,256]{3,2,1,0:T(8,128)(2,1)}, u32[]{:S(2)}) copy-start(bf16[4,4,32,256]{3,2,1,0:T(8,128)(2,1)} %cot.1) | copy-start | bytes 786436
  2.7 25.2 %copy-start.9 = (f32[256]{0:T(256)S(1)}, f32[256]{0:T(256)}, u32[]{:S(2)}) copy-start(f32[256]{0:T(256)} %param.11) | copy-start | bytes 3076
  3.8 28.8 %copy-start.8 = (f32[3,3,256]{2,1,0:T(4,128)S(1)}, f32[3,3,256]{2,1,0:T(4,128)}, u32[]{:S(2)}) copy-start(f32[3,3,256]{2,1,0:T(4,128)} %refs_13_.2) | copy-start | bytes 27652
  3.8 16.3 %all-to-all-start = ((bf16[8,128,256]{2,1,0:T(8,128)(2,1)}), bf16[8,128,256]{2,1,0:T(8,128)(2,1)S(1)}, u32[]{:S(2)}, u32[]{:S(2)}) async-start(bf16[8,128,256]{2,1,0:T(8,128)(2,1)} %pack.1), calls=%async_computation | async-start | bytes 1048576 | tf_op jit(solution)/shard_map/to_cells/all_to_all | solution.py:353
  20.4 10.5 %collective-permute-start.1 = (bf16[4,32,256]{2,1,0:T(8,128)(2,1)S(1)}, bf16[4,32,256]{2,1,0:T(8,128)(2,1)S(1)}, u32[]{:S(2)}, u32[]{:S(2)}) collective-permute-start(bf16[4,32,256]{2,1,0:T(8,128)(2,1)S(1)} %get-tuple-element.73), channel_id=1, source_target_pairs={{0,64},{64,0},{128,192},{192,128},{224,160},{160,224},{96,32},{32,... | collective-permute-start | bytes 196616 | tf_op jit(solution)/shard_map/halo_cols/ppermute | solution.py:322
  20.8 10.1 %collective-permute-start = (bf16[4,32,256]{2,1,0:T(8,128)(2,1)S(1)}, bf16[4,32,256]{2,1,0:T(8,128)(2,1)S(1)}, u32[]{:S(2)}, u32[]{:S(2)}) collective-permute-start(bf16[4,32,256]{2,1,0:T(8,128)(2,1)S(1)} %get-tuple-element.74), channel_id=1, source_target_pairs={{64,128},{128,64},{192,224},{224,192},{160,96},{96,160},{32,1},{1,... | collective-permute-start | bytes 196616 | tf_op jit(solution)/shard_map/halo_cols/ppermute | solution.py:322
  31.0 4.4 %collective-permute-start.3 = (bf16[6,32,256]{2,1,0:T(8,128)(2,1)S(1)}, bf16[6,32,256]{2,1,0:T(8,128)(2,1)S(1)}, u32[]{:S(2)}, u32[]{:S(2)}) collective-permute-start(bf16[6,32,256]{2,1,0:T(8,128)(2,1)S(1)} %get-tuple-element.77), channel_id=1, source_target_pairs={{0,8},{8,0},{16,24},{24,16},{1,9},{9,1},{17,25},{25,17},{2,10},{10... | collective-permute-start | bytes 294920 | tf_op jit(solution)/shard_map/halo_rows/ppermute | solution.py:322
  31.8 3.6 %collective-permute-start.2 = (bf16[6,32,256]{2,1,0:T(8,128)(2,1)S(1)}, bf16[6,32,256]{2,1,0:T(8,128)(2,1)S(1)}, u32[]{:S(2)}, u32[]{:S(2)}) collective-permute-start(bf16[6,32,256]{2,1,0:T(8,128)(2,1)S(1)} %get-tuple-element.78), channel_id=1, source_target_pairs={{8,16},{16,8},{9,17},{17,9},{10,18},{18,10},{11,19},{19,11},{12,20... | collective-permute-start | bytes 294920 | tf_op jit(solution)/shard_map/halo_rows/ppermute | solution.py:322
  56.1 5.7 %collective-permute-start.6 = (bf16[144,256]{1,0:T(8,128)(2,1)S(1)}, bf16[144,256]{1,0:T(8,128)(2,1)S(1)}, u32[]{:S(2)}, u32[]{:S(2)}) collective-permute-start(bf16[144,256]{1,0:T(8,128)(2,1)S(1)} %slice_reduce_fusion), channel_id=1, source_target_pairs={{0,24},{8,16},{16,8},{24,0},{1,25},{9,17},{17,9},{25,1},{2,26},{10... | collective-permute-start | bytes 221192 | tf_op jit(solution)/shard_map/reduce/ppermute | solution.py:303
  59.8 4.8 %collective-permute-start.5 = (bf16[144,256]{1,0:T(8,128)(2,1)S(1)}, bf16[144,256]{1,0:T(8,128)(2,1)S(1)}, u32[]{:S(2)}, u32[]{:S(2)}) collective-permute-start(bf16[144,256]{1,0:T(8,128)(2,1)S(1)} %slice_reduce_fusion), channel_id=1, source_target_pairs={{0,16},{8,24},{16,0},{24,8},{1,17},{9,25},{17,1},{25,9},{2,18},{10... | collective-permute-start | bytes 221192 | tf_op jit(solution)/shard_map/reduce/ppermute | solution.py:303
  61.7 3.4 %collective-permute-start.4 = (bf16[144,256]{1,0:T(8,128)(2,1)S(1)}, bf16[144,256]{1,0:T(8,128)(2,1)S(1)}, u32[]{:S(2)}, u32[]{:S(2)}) collective-permute-start(bf16[144,256]{1,0:T(8,128)(2,1)S(1)} %slice_reduce_fusion), channel_id=1, source_target_pairs={{0,8},{8,0},{16,24},{24,16},{1,9},{9,1},{17,25},{25,17},{2,10},{10... | collective-permute-start | bytes 221192 | tf_op jit(solution)/shard_map/reduce/ppermute | solution.py:303
  65.2 4.5 %collective-permute-start.9 = (bf16[144,256]{1,0:T(8,128)(2,1)S(1)}, bf16[144,256]{1,0:T(8,128)(2,1)S(1)}, u32[]{:S(2)}, u32[]{:S(2)}) collective-permute-start(bf16[144,256]{1,0:T(8,128)(2,1)S(1)} %add_convert_fusion.2), channel_id=1, source_target_pairs={{0,6},{1,7},{2,4},{3,5},{4,2},{5,3},{6,0},{7,1},{8,14},{9,15},{10,... | collective-permute-start | bytes 221192 | tf_op jit(solution)/shard_map/reduce/ppermute | solution.py:303
  67.1 4.7 %collective-permute-start.8 = (bf16[144,256]{1,0:T(8,128)(2,1)S(1)}, bf16[144,256]{1,0:T(8,128)(2,1)S(1)}, u32[]{:S(2)}, u32[]{:S(2)}) collective-permute-start(bf16[144,256]{1,0:T(8,128)(2,1)S(1)} %add_convert_fusion.2), channel_id=1, source_target_pairs={{0,4},{1,5},{2,6},{3,7},{4,0},{5,1},{6,2},{7,3},{8,12},{9,13},{10,... | collective-permute-start | bytes 221192 | tf_op jit(solution)/shard_map/reduce/ppermute | solution.py:303
  67.1 4.7 %collective-permute-start.7 = (bf16[144,256]{1,0:T(8,128)(2,1)S(1)}, bf16[144,256]{1,0:T(8,128)(2,1)S(1)}, u32[]{:S(2)}, u32[]{:S(2)}) collective-permute-start(bf16[144,256]{1,0:T(8,128)(2,1)S(1)} %add_convert_fusion.2), channel_id=1, source_target_pairs={{0,2},{1,3},{2,0},{3,1},{4,6},{5,7},{6,4},{7,5},{8,10},{9,11},{10,... | collective-permute-start | bytes 221192 | tf_op jit(solution)/shard_map/reduce/ppermute | solution.py:303
  71.8 9.3 %collective-permute-start.10 = (bf16[144,256]{1,0:T(8,128)(2,1)S(1)}, bf16[144,256]{1,0:T(8,128)(2,1)S(1)}, u32[]{:S(2)}, u32[]{:S(2)}) collective-permute-start(bf16[144,256]{1,0:T(8,128)(2,1)S(1)} %add_convert_fusion.1), channel_id=1, source_target_pairs={{0,1},{1,0},{2,3},{3,2},{4,5},{5,4},{6,7},{7,6},{8,9},{9,8},{10,11... | collective-permute-start | bytes 221192 | tf_op jit(solution)/shard_map/reduce/ppermute | solution.py:303
  81.2 4.7 %collective-permute-start.12 = (bf16[128,256]{1,0:T(8,128)(2,1)S(1)}, bf16[128,256]{1,0:T(8,128)(2,1)S(1)}, u32[]{:S(2)}, u32[]{:S(2)}) collective-permute-start(bf16[128,256]{1,0:T(8,128)(2,1)S(1)} %get-tuple-element.82), channel_id=1, source_target_pairs={{0,128},{32,160},{64,192},{96,224},{128,0},{160,32},{192,64},{224,... | collective-permute-start | bytes 196616 | tf_op jit(solution)/shard_map/reduce/ppermute | solution.py:428
  81.9 4.0 %collective-permute-start.11 = (bf16[128,256]{1,0:T(8,128)(2,1)S(1)}, bf16[128,256]{1,0:T(8,128)(2,1)S(1)}, u32[]{:S(2)}, u32[]{:S(2)}) collective-permute-start(bf16[128,256]{1,0:T(8,128)(2,1)S(1)} %get-tuple-element.82), channel_id=1, source_target_pairs={{0,64},{32,96},{64,0},{96,32},{128,192},{160,224},{192,128},{224,1... | collective-permute-start | bytes 196616 | tf_op jit(solution)/shard_map/reduce/ppermute | solution.py:428
  82.7 4.3 %collective-permute-start.13 = (bf16[128,256]{1,0:T(8,128)(2,1)S(1)}, bf16[128,256]{1,0:T(8,128)(2,1)S(1)}, u32[]{:S(2)}, u32[]{:S(2)}) collective-permute-start(bf16[128,256]{1,0:T(8,128)(2,1)S(1)} %get-tuple-element.82), channel_id=1, source_target_pairs={{0,192},{32,224},{64,128},{96,160},{128,64},{160,96},{192,0},{224,... | collective-permute-start | bytes 196616 | tf_op jit(solution)/shard_map/reduce/ppermute | solution.py:428
  87.1 6.8 %collective-permute-start.14 = (bf16[4,128,256]{2,1,0:T(8,128)(2,1)S(1)}, bf16[4,128,256]{2,1,0:T(8,128)(2,1)S(1)}, u32[]{:S(2)}, u32[]{:S(2)}) collective-permute-start(bf16[4,128,256]{2,1,0:T(8,128)(2,1)S(1)} %pad_maximum_fusion.same_core), channel_id=1, source_target_pairs={{0,32},{32,0},{64,96},{96,64},{128,160},{160,128},{192,224},{224,1... | collective-permute-start | bytes 786440 | tf_op jit(solution)/shard_map/reduce/ppermute | solution.py:430

commit v11 on v10

--- a/solution.py
+++ b/solution.py
@@ -46,14 +46,21 @@
     return out.reshape(cells * parts * members, -1)
 
 
-def pack_kernel(fields, cot, send):
+def pack_kernel(fields, cot, send, held, sems):
     members, rows, cols, width = fields.shape
     parts = send.shape[0]
     per = cols // parts * members
-    split = split_matrix(parts, members, cols)
+    copies = []
     for k, source in enumerate((fields, cot)):
         for r in range(rows):
-            tokens = source[:, r].reshape(members * cols, width)
+            copies.append(pltpu.make_async_copy(source.at[:, r], held.at[k, r], sems.at[k, r]))
+    for copy in copies:
+        copy.start()
+    split = split_matrix(parts, members, cols)
+    for k in range(2):
+        for r in range(rows):
+            copies[k * rows + r].wait()
+            tokens = held[k, r].reshape(members * cols, width)
             moved = dot(split, tokens).astype(BF).reshape(parts, per, width)
             start = (k * rows + r) * per
             send[:, start : start + per, :] = moved
@@ -151,9 +158,9 @@
     mixed_out[...] = dot(att_out[...], wo[...]).astype(BF)
 
 
-def backward_kernel(picked, sizes, ends, place, cot, left, right, *refs):
-    if ends:
-        above, below, part_in, grads_in, extra_in = refs[:5]
+def backward_kernel(picked, sizes, outer, place, cot, above, below, *refs):
+    if outer:
+        left, right, part_in, grads_in, extra_in = refs[:5]
         refs = refs[5:]
     x_in, q_in, prob_in, att_in, mixed_in, mat_k, mat_v, gain, mix, wq, wk, wv, wo, gather8, headsum = refs[:15]
     outs, (padded, sums) = refs[15:-2], refs[-2:]
@@ -161,36 +168,37 @@
     head_dim = width // HEADS
     scale = 1.0 / math.sqrt(head_dim)
     pad_cols = tile_cols + 2
-    line = tile_cols * all_members
-    cells = [r * tile_cols + c for r in picked for c in range(tile_cols)]
+    spots = [(r, c) for r in range(tile_rows) for c in picked]
+    cells = [r * tile_cols + c for r, c in spots]
     tokens = len(cells) * all_members
     row, block = place[0], place[1]
 
     def pick(ref):
-        return jnp.concatenate([ref[r * line : (r + 1) * line, :] for r in picked], axis=0)
+        return jnp.concatenate([ref[c * all_members : (c + 1) * all_members, :] for c in cells], axis=0)
 
     def side(inside, x):
         x = x.astype(F32)
         return jnp.where(inside, x, jnp.zeros_like(x))
 
     in_left, in_right = block > 0, block < sizes[1] - 1
-    for r in range(tile_rows + 2):
-        start = r * pad_cols
-        if 0 < r <= tile_rows:
-            padded[start] = side(in_left, left[r - 1])
-            padded[start + 1 : start + 1 + tile_cols] = cot[r - 1].astype(F32)
-            padded[start + 1 + tile_cols] = side(in_right, right[r - 1])
-        elif ends:
-            source, inside = (above, row > 0) if r == 0 else (below, row < sizes[0] - 1)
-            padded[start] = side(inside & in_left, source[0])
-            padded[start + 1 : start + 1 + tile_cols] = side(inside, source[1 : 1 + tile_cols])
-            padded[start + 1 + tile_cols] = side(inside & in_right, source[1 + tile_cols])
+    in_above, in_below = row > 0, row < sizes[0] - 1
+    padded[1 : 1 + tile_cols] = side(in_above, above[...])
+    padded[(tile_rows + 1) * pad_cols + 1 : (tile_rows + 1) * pad_cols + 1 + tile_cols] = side(in_below, below[...])
+    for r in range(tile_rows):
+        padded[(r + 1) * pad_cols + 1 : (r + 1) * pad_cols + 1 + tile_cols] = cot[r].astype(F32)
+    if outer:
+        for r in range(tile_rows + 2):
+            near_l, near_r = in_left, in_right
+            if r == 0:
+                near_l, near_r = in_left & in_above, in_right & in_above
+            elif r == tile_rows + 1:
+                near_l, near_r = in_left & in_below, in_right & in_below
+            padded[r * pad_cols] = side(near_l, left[r])
+            padded[r * pad_cols + 1 + tile_cols] = side(near_r, right[r])
 
     def shifted(i, j):
-        moved = [
-            padded[(r + 2 - i) * pad_cols + 2 - j : (r + 2 - i) * pad_cols + 2 - j + tile_cols] for r in picked
-        ]
-        return jnp.concatenate(moved, axis=0).reshape(tokens, width)
+        moved = [padded[(r + 2 - i) * pad_cols + c + 2 - j] for r, c in spots]
+        return jnp.concatenate(moved, axis=0)
 
     inv, normed = norm(pick(x_in).astype(F32))
     inputs = (normed * gain[...]).astype(BF)
@@ -238,7 +246,6 @@
     grad_normed = grad_in * gain[...]
     mean = jnp.mean(grad_normed * normed, axis=-1, keepdims=True)
     grad = (shifted(1, 1) + inv * (grad_normed - normed * mean)).astype(BF)
-    back = dot(gather8[...], grad, TN).astype(BF)
     weights = [
         dot(inputs, grad_q, TN),
         dot(inputs, grad_k, TN),
@@ -246,9 +253,9 @@
         dot(attended, grad_mixed, TN),
     ]
     extras = jnp.concatenate(extra + [jnp.zeros((16 - len(extra), width), F32)], axis=0)
-    if not ends:
+    if not outer:
         part_out, grads_out, extra_out = outs
-        part_out[...] = back.reshape(part_out.shape)
+        part_out[...] = grad
         for k in range(4):
             grads_out[k] = weights[k]
         extra_out[...] = extras
@@ -258,11 +265,14 @@
     members = all_members // parts
     base = tile_rows * tile_cols * members
     shard = 4 * width // parts
-    step = tile_cols * members
-    back = back.reshape(parts, len(picked) * step, width)
-    for k, r in enumerate(picked):
-        send[:, r * step : (r + 1) * step, :] = back[:, k * step : (k + 1) * step]
-    send[:, step : base - step, :] = part_in[...]
+    done = {c: grad[k * all_members : (k + 1) * all_members] for k, c in enumerate(cells)}
+    others = [c for c in range(tile_rows * tile_cols) if c not in done]
+    for k, c in enumerate(others):
+        done[c] = part_in[k * all_members : (k + 1) * all_members, :]
+    for g in range(len(done) // 8):
+        group = jnp.concatenate([done[c] for c in range(g * 8, (g + 1) * 8)], axis=0)
+        back = dot(gather8[...], group, TN).astype(BF)
+        send[:, g * 8 * members : (g + 1) * 8 * members, :] = back.reshape(parts, 8 * members, width)
     for j in range(parts):
         which, start = divmod(j * shard, width)
         total = weights[which][start : start + shard] + grads_in[which, start : start + shard, :]
@@ -346,9 +356,11 @@
     with jax.named_scope("pack"):
         send = pl.pallas_call(
             pack_kernel,
+            in_specs=[pl.BlockSpec(memory_space=pltpu.MemorySpace.HBM)] * 2,
+            scratch_shapes=[pltpu.VMEM((2, rows, members, cols, width), BF), pltpu.SemaphoreType.DMA((2, rows))],
             out_shape=pltpu.VMEM((parts, 2 * base, width), BF),
             compiler_params=params,
-        )(fields, cotangent)
+        )(*[pltpu.with_memory_space_constraint(a, pltpu.MemorySpace.HBM) for a in (fields, cotangent)])
     with jax.named_scope("to_cells"):
         recv = lax.all_to_all(send, "mem", 0, 0)
     with jax.named_scope("order"):
@@ -358,13 +370,9 @@
             compiler_params=params,
         )(near(recv), gather8)
         x, w_query, w_key, w_value, w_out = lax.optimization_barrier((x, w_query, w_key, w_value, w_out))
-    with jax.named_scope("halo_cols"):
-        where = {}
-        for mem in range(parts):
-            inner = mem // 2 if mem % 2 == 0 else parts - 1 - mem // 2
-            for c in range(grid[1]):
-                where[c * parts + inner] = mem * grid[1] + c
-        right, left = swap(cot[:, per - 1], cot[:, 0], block, ("mem", "col"), where, True)
+    with jax.named_scope("halo_rows"):
+        rows_at = {r: r for r in range(grid[0])}
+        below, above = swap(cot[rows - 1], cot[0], lax.axis_index("row"), "row", rows_at, False)
     with jax.named_scope("forward"):
         token = pltpu.VMEM((tokens, width), BF)
         token_f = pltpu.VMEM((tokens, width), F32)
@@ -375,39 +383,45 @@
             scratch_shapes=[pltpu.VMEM((tokens, width), F32)],
             compiler_params=params,
         )(near(x), gain, w_query, w_key, w_value, w_out, headsum)
-    left, right, *kept = lax.optimization_barrier((left, right, *kept))
-    with jax.named_scope("halo_rows"):
-        top, bottom = [jnp.concatenate([left[r : r + 1], cot[r], right[r : r + 1]], axis=0) for r in (0, rows - 1)]
-        rows_at = {r: r for r in range(grid[0])}
-        below, above = swap(bottom, top, lax.axis_index("row"), "row", rows_at, False)
+    above, below, *kept = lax.optimization_barrier((above, below, *kept))
+    with jax.named_scope("halo_cols"):
+        where = {}
+        for mem in range(parts):
+            inner = mem // 2 if mem % 2 == 0 else parts - 1 - mem // 2
+            for c in range(grid[1]):
+                where[c * parts + inner] = mem * grid[1] + c
+        last, first = [
+            jnp.concatenate([above[c : c + 1], cot[:, c], below[c : c + 1]], axis=0) for c in (per - 1, 0)
+        ]
+        right, left = swap(last, first, block, ("mem", "col"), where, True)
 
     half = tokens // 2
     scratch = [
         pltpu.VMEM(((rows + 2) * (per + 2), members * parts, width), F32),
         pltpu.VMEM((half, width), F32),
     ]
-    halo = [near(a) for a in (cot, left, right)]
+    halo = [near(a) for a in (cot, above, below)]
     rest = [near(a) for a in (x, *kept)] + [gain, mix_kernel, w_query, w_key, w_value, w_out, gather8, headsum]
     with jax.named_scope("backward_inner"):
         inner = pl.pallas_call(
-            functools.partial(backward_kernel, tuple(range(1, rows - 1)), (grid[0], blocks), False),
+            functools.partial(backward_kernel, tuple(range(1, per - 1)), (grid[0], blocks), False),
             in_specs=[smem] + [vmem] * 18,
             out_shape=(
-                pltpu.VMEM((parts, base // 2, width), BF),
+                pltpu.VMEM((half, width), BF),
                 pltpu.VMEM((4, width, width), F32),
                 pltpu.VMEM((16, width), F32),
             ),
             scratch_shapes=scratch,
             compiler_params=params,
         )(place, *halo, *rest)
-    with jax.named_scope("backward_ends"):
+    with jax.named_scope("backward_outer"):
         back = pl.pallas_call(
-            functools.partial(backward_kernel, (0, rows - 1), (grid[0], blocks), True),
+            functools.partial(backward_kernel, (0, per - 1), (grid[0], blocks), True),
             in_specs=[smem] + [vmem] * 23,
             out_shape=pltpu.VMEM((parts, base + shard + 16, width), BF),
             scratch_shapes=scratch,
             compiler_params=params,
-        )(place, *halo, *[near(a) for a in (above, below, *inner)], *rest)
+        )(place, *halo, *[near(a) for a in (left, right, *inner)], *rest)
     with jax.named_scope("to_members"):
         landed = lax.all_to_all(back, "mem", 0, 0)
     with jax.named_scope("unpack"):

time: 95.2 us -> 95.1 us (level)
  local copies, waits for them, and re-layouts: 2.04 us -> 0.07 us
  Pallas kernels: 12.1 us -> 13.7 us
  waiting for transfers between devices: 20.5 us -> 22 us
  starting transfers between devices: 41.3 us -> 40 us
    unnamed x20 -> x16, local copies, waits for them, and re-layouts: 2.02 us -> 0.04 us
    pallas_call x3, Pallas kernels: 6.86 us -> 8.38 us  [the longest x1 3.13 us: local(): pl.pallas_call(pack_kernel, in_specs=[pl.BlockSpec(memory_space=pltpu.Mem...]
    ppermute x7, starting transfers between devices: 16.7 us -> 15.3 us  [meet(): lax.ppermute(values, axis, partner(axis, k))]
    ppermute x4, waiting for transfers between devices: 0.01 us -> 1.01 us  [swap(): lax.ppermute(jnp.where(spot % 2 == odd, last, first), axis, pairs)]
where the time goes in v11:
time: 95.1 us; the launch traced here: 94.8 us
  starting transfers between devices  40 us (42%)
  waiting for transfers between devices  22 us (23%)
  blocking collectives  17.8 us (19%)
  Pallas kernels  13.7 us (14%)
    all_to_all x1, blocking collectives, local(): landed = lax.all_to_all(back, 'mem', 0, 0)  17.8 us
    ppermute x7, starting transfers between devices, meet(): lax.ppermute(values, axis, partner(axis, k))  15.3 us
    all_to_all x1, waiting for transfers between devices, local(): recv = lax.all_to_all(send, 'mem', 0, 0)  9.5 us
    ppermute x4, starting transfers between devices, swap(): lax.ppermute(jnp.where(spot % 2 == odd, last, first), axis, pairs)  9.22 us
    ppermute x7, waiting for transfers between devices, meet(): lax.ppermute(values, axis, partner(axis, k))  7.79 us
    all_to_all x1, starting transfers between devices, local(): recv = lax.all_to_all(send, 'mem', 0, 0)  6.65 us
    ppermute x1, starting transfers between devices, local(): other_core = lax.ppermute(same_core, 'mem', partner('mem', 1))  5.55 us
    ppermute x3, starting transfers between devices, local(): lax.ppermute(piece, 'mem', partner('mem', k))  3.34 us
  transfers between devices with their start and end apart: 16, of which 9 were waited for; matrix products, arithmetic and copies ran while one was open for 0% of the time, Pallas kernels for 7%

profile of v11, /device:TPU:1, one launch (start us, length us, event | category | flops | bytes accessed | tf_op | source)
XLA Modules:
  0.0 94.8 jit_solution(8585700274885080807)
XLA Ops:
  0.6 0.0 copy-start
  0.6 0.0 copy-start.5
  0.7 3.1 %pack.1 = bf16[8,128,256]{2,1,0:T(8,128)(2,1)} custom-call(bf16[4,4,32,256]{3,2,1,0:T(8,128)(2,1)} %fields.1, bf16[4,4,32,256]{3,2,1,0:T(8,128)(2,1)} %cot.1), custom_call_target="tpu_custom_call" | custom-call | tf_op jit(solution)/shard_map/pack/pallas_call | solution.py:357
  3.8 0.0 copy-start.6
  3.9 6.6 %all-to-all-start = ((bf16[8,128,256]{2,1,0:T(8,128)(2,1)}), bf16[8,128,256]{2,1,0:T(8,128)(2,1)S(1)}, u32[]{:S(2)}, u32[]{:S(2)}) async-start(bf16[8,128,256]{2,1,0:T(8,128)(2,1)} %pack.1), calls=%async_computation | async-start | bytes 1048576 | tf_op jit(solution)/shard_map/to_cells/all_to_all | solution.py:365
  10.5 9.5 %all-to-all-done.recv = bf16[8,128,256]{2,1,0:T(8,128)(2,1)S(1)} async-done(((bf16[8,128,256]{2,1,0:T(8,128)(2,1)}), bf16[8,128,256]{2,1,0:T(8,128)(2,1)S(1)}, u32[]{:S(2)}, u32[]{:S(2)}) %all-to-all-start) | async-done | bytes 524320 | tf_op jit(solution)/shard_map/to_cells/all_to_all | solution.py:365
  20.0 0.3 order.1
  20.3 0.9 collective-permute-start.1
  21.2 0.7 collective-permute-start
  21.9 0.0 copy-done.5
  21.9 0.0 copy-done.4
  21.9 0.0 copy-done.3
  22.0 3.0 %forward.1 = (bf16[512,256]{1,0:T(8,128)(2,1)S(1)}, f32[512,256]{1,0:T(8,128)S(1)}, bf16[512,256]{1,0:T(8,128)(2,1)S(1)}, bf16[512,256]{1,0:T(8,128)(2,1)S(1)}, ...) custom-call(bf16[512,256]{1,0:T(8,128)(2,1)S(1)} %get-tuple-element.41.x_in.refs_0_.refs_5_, ...), custom_call_target="tpu_custom_call" | custom-call | tf_op jit(solution)/shard_map/forward/pallas_call | solution.py:380
  24.9 0.0 collective-permute-done.1
  24.9 0.0 collective-permute-done
  25.0 0.4 collective-permute-start.3
  25.4 7.3 %collective-permute-start.2 = (bf16[6,32,256]{2,1,0:T(8,128)(2,1)S(1)}, bf16[6,32,256]{2,1,0:T(8,128)(2,1)S(1)}, u32[]{:S(2)}, u32[]{:S(2)}) collective-permute-start(bf16[6,32,256]{2,1,0:T(8,128)(2,1)S(1)} %get-tuple-element.78), channel_id=1, source_target_pairs={{64,128},{128,64},{192,224},{224,192},{160,96},{96,160},{32,1},{1,... | collective-permute-start | bytes 294920 | tf_op jit(solution)/shard_map/halo_cols/ppermute | solution.py:332
  32.7 0.1 pad_add_fusion.place
  32.8 2.5 %backward_inner.1 = (bf16[256,256]{1,0:T(8,128)(2,1)S(1)}, f32[4,256,256]{2,1,0:T(8,128)S(1)}, f32[16,256]{1,0:T(8,128)S(1)}) custom-call(s32[2]{0:T(128)S(1)} %pad_add_fusion.place, bf16[4,4,32,256]{3,2,1,0:T(8,128)(2,1)S(1)} %get-tuple-element.39.cot, bf16[4,32,256]{2,1,0:T(8,128)(2,1)S(1)} %get-tuple-element.52.above, ...), custom_call_target="tpu_custom_call" | custom-call | tf_op jit(solution)/shard_map/backward_inner/pallas_call | solution.py:406
  35.3 0.0 collective-permute-done.3
  35.3 1.0 %collective-permute-done.2 = bf16[6,32,256]{2,1,0:T(8,128)(2,1)S(1)} collective-permute-done((bf16[6,32,256]{2,1,0:T(8,128)(2,1)S(1)}, bf16[6,32,256]{2,1,0:T(8,128)(2,1)S(1)}, u32[]{:S(2)}, u32[]{:S(2)}) %collective-permute-start.2) | collective-permute-done | bytes 98336 | tf_op jit(solution)/shard_map/halo_cols/ppermute | solution.py:332
  36.3 2.8 %backward_outer.1 = bf16[8,208,256]{2,1,0:T(8,128)(2,1)S(1)} custom-call(s32[2]{0:T(128)S(1)} %pad_add_fusion.place, bf16[4,4,32,256]{3,2,1,0:T(8,128)(2,1)S(1)} %get-tuple-element.39.cot, bf16[4,32,256]{2,1,0:T(8,128)(2,1)S(1)} %get-tuple-element.52.above, bf16[4,32,256]{2,1,0:T(8,128)(2,1)S(1)} %get-tuple-element.53.below, ...), custom_call_target="tpu_custom_call" | custom-call | tf_op jit(solution)/shard_map/backward_outer/pallas_call | solution.py:418
  39.1 17.8 %all_to_all.10.recv = bf16[8,208,256]{2,1,0:T(8,128)(2,1)S(1)} all-to-all(bf16[8,208,256]{2,1,0:T(8,128)(2,1)S(1)} %backward_outer.1), channel_id=1, replica_groups=mesh['mem'=8,'row'=4,'col'=8] {'mem'}, dimensions={0} | all-to-all | bytes 1703936 | tf_op jit(solution)/shard_map/to_members/all_to_all | solution.py:426
  56.9 0.1 slice_reduce_fusion
  57.0 2.5 %collective-permute-start.6 = (bf16[144,256]{1,0:T(8,128)(2,1)S(1)}, bf16[144,256]{1,0:T(8,128)(2,1)S(1)}, u32[]{:S(2)}, u32[]{:S(2)}) collective-permute-start(bf16[144,256]{1,0:T(8,128)(2,1)S(1)} %slice_reduce_fusion), channel_id=1, source_target_pairs={{0,24},{8,16},{16,8},{24,0},{1,25},{9,17},{17,9},{25,1},{2,26},{10... | collective-permute-start | bytes 221192 | tf_op jit(solution)/shard_map/reduce/ppermute | solution.py:313
  59.5 3.2 %collective-permute-start.5 = (bf16[144,256]{1,0:T(8,128)(2,1)S(1)}, bf16[144,256]{1,0:T(8,128)(2,1)S(1)}, u32[]{:S(2)}, u32[]{:S(2)}) collective-permute-start(bf16[144,256]{1,0:T(8,128)(2,1)S(1)} %slice_reduce_fusion), channel_id=1, source_target_pairs={{0,16},{8,24},{16,0},{24,8},{1,17},{9,25},{17,1},{25,9},{2,18},{10... | collective-permute-start | bytes 221192 | tf_op jit(solution)/shard_map/reduce/ppermute | solution.py:313
  62.7 0.0 collective-permute-start.4
  62.7 0.0 collective-permute-done.6
  62.7 4.5 %collective-permute-done.5 = bf16[144,256]{1,0:T(8,128)(2,1)S(1)} collective-permute-done((bf16[144,256]{1,0:T(8,128)(2,1)S(1)}, bf16[144,256]{1,0:T(8,128)(2,1)S(1)}, u32[]{:S(2)}, u32[]{:S(2)}) %collective-permute-start.5) | collective-permute-done | bytes 73760 | tf_op jit(solution)/shard_map/reduce/ppermute | solution.py:313
  67.2 0.0 collective-permute-done.4
  67.2 0.1 collective-permute-start.9
  67.3 0.3 collective-permute-start.8
  67.6 3.0 %collective-permute-start.7 = (bf16[144,256]{1,0:T(8,128)(2,1)S(1)}, bf16[144,256]{1,0:T(8,128)(2,1)S(1)}, u32[]{:S(2)}, u32[]{:S(2)}) collective-permute-start(bf16[144,256]{1,0:T(8,128)(2,1)S(1)} %add_convert_fusion.2), channel_id=1, source_target_pairs={{0,2},{1,3},{2,0},{3,1},{4,6},{5,7},{6,4},{7,5},{8,10},{9,11},{10,... | collective-permute-start | bytes 221192 | tf_op jit(solution)/shard_map/reduce/ppermute | solution.py:313
  70.6 1.9 %collective-permute-done.9 = bf16[144,256]{1,0:T(8,128)(2,1)S(1)} collective-permute-done((bf16[144,256]{1,0:T(8,128)(2,1)S(1)}, bf16[144,256]{1,0:T(8,128)(2,1)S(1)}, u32[]{:S(2)}, u32[]{:S(2)}) %collective-permute-start.9) | collective-permute-done | bytes 73760 | tf_op jit(solution)/shard_map/reduce/ppermute | solution.py:313
  72.5 0.0 collective-permute-done.8
  72.5 0.6 collective-permute-done.7
  73.1 6.2 %collective-permute-start.10 = (bf16[144,256]{1,0:T(8,128)(2,1)S(1)}, bf16[144,256]{1,0:T(8,128)(2,1)S(1)}, u32[]{:S(2)}, u32[]{:S(2)}) collective-permute-start(bf16[144,256]{1,0:T(8,128)(2,1)S(1)} %add_convert_fusion.1), channel_id=1, source_target_pairs={{0,1},{1,0},{2,3},{3,2},{4,5},{5,4},{6,7},{7,6},{8,9},{9,8},{10,11... | collective-permute-start | bytes 221192 | tf_op jit(solution)/shard_map/reduce/ppermute | solution.py:313
  79.4 1.0 %unpack.1 = bf16[4,4,32,256]{3,2,1,0:T(8,128)(2,1)} custom-call(bf16[8,208,256]{2,1,0:T(8,128)(2,1)S(1)} %all_to_all.10.recv), custom_call_target="tpu_custom_call" | custom-call | tf_op jit(solution)/shard_map/unpack/pallas_call | solution.py:430
  80.4 0.8 collective-permute-done.10
  81.2 0.7 collective-permute-start.12
  81.9 0.8 collective-permute-start.11
  82.7 1.8 %collective-permute-start.13 = (bf16[128,256]{1,0:T(8,128)(2,1)S(1)}, bf16[128,256]{1,0:T(8,128)(2,1)S(1)}, u32[]{:S(2)}, u32[]{:S(2)}) collective-permute-start(bf16[128,256]{1,0:T(8,128)(2,1)S(1)} %get-tuple-element.82), channel_id=1, source_target_pairs={{0,192},{32,224},{64,128},{96,160},{128,64},{160,96},{192,0},{224,... | collective-permute-start | bytes 196616 | tf_op jit(solution)/shard_map/reduce/ppermute | solution.py:442
  84.5 1.4 %collective-permute-done.12 = bf16[128,256]{1,0:T(8,128)(2,1)S(1)} collective-permute-done((bf16[128,256]{1,0:T(8,128)(2,1)S(1)}, bf16[128,256]{1,0:T(8,128)(2,1)S(1)}, u32[]{:S(2)}, u32[]{:S(2)}) %collective-permute-start.12) | collective-permute-done | bytes 65568 | tf_op jit(solution)/shard_map/reduce/ppermute | solution.py:442
  85.9 0.0 collective-permute-done.11
  85.9 1.2 %collective-permute-done.13 = bf16[128,256]{1,0:T(8,128)(2,1)S(1)} collective-permute-done((bf16[128,256]{1,0:T(8,128)(2,1)S(1)}, bf16[128,256]{1,0:T(8,128)(2,1)S(1)}, u32[]{:S(2)}, u32[]{:S(2)}) %collective-permute-start.13) | collective-permute-done | bytes 65568 | tf_op jit(solution)/shard_map/reduce/ppermute | solution.py:442
  87.1 5.6 %collective-permute-start.14 = (bf16[4,128,256]{2,1,0:T(8,128)(2,1)S(1)}, bf16[4,128,256]{2,1,0:T(8,128)(2,1)S(1)}, u32[]{:S(2)}, u32[]{:S(2)}) collective-permute-start(bf16[4,128,256]{2,1,0:T(8,128)(2,1)S(1)} %pad_maximum_fusion.same_core), channel_id=1, source_target_pairs={{0,32},{32,0},{64,96},{96,64},{128,160},{160,128},{192,224},{224,1... | collective-permute-start | bytes 786440 | tf_op jit(solution)/shard_map/reduce/ppermute | solution.py:444
  92.6 1.2 %collective-permute-done.14.other_core = bf16[4,128,256]{2,1,0:T(8,128)(2,1)S(1)} collective-permute-done((bf16[4,128,256]{2,1,0:T(8,128)(2,1)S(1)}, bf16[4,128,256]{2,1,0:T(8,128)(2,1)S(1)}, u32[]{:S(2)}, u32[]{:S(2)}) %collective-permute-start.14) | collective-permute-done | bytes 262176 | tf_op jit(solution)/shard_map/reduce/ppermute | solution.py:444
  93.8 1.0 %finish.1 = (f32[256,256]{1,0:T(8,128)}, f32[256,256]{1,0:T(8,128)}, f32[256,256]{1,0:T(8,128)}, f32[256,256]{1,0:T(8,128)}, f32[3,3,256]{2,1,0:T(4,128)}, /*index=5*/f32[1,256]{1,0:T(1,128)}) custom-call(s32[1]{0:T(128)} %bitcast.7.place, bf16[4,128,256]{2,1,0:T(8,128)(2,1)S(1)} %pad_maximum_fusion.same_core, ...), custom_call_target="tpu_custom_call" | custom-call | tf_op jit(solution)/shard_map/finish/pallas_call | solution.py:450
  (21 shorter events, 0.3 us)
Async XLA Ops:
  0.6 19.4 %copy-start = (bf16[256,256]{1,0:T(8,128)(2,1)S(1)}, bf16[256,256]{1,0:T(8,128)(2,1)}, u32[]{:S(2)}) copy-start(bf16[256,256]{1,0:T(8,128)(2,1)} %constant.67.clone.gather8.refs_13_.refs_18_) | copy-start | bytes 393220
  0.6 21.2 %copy-start.5 = (bf16[256,256]{1,0:T(8,128)(2,1)S(1)}, bf16[256,256]{1,0:T(8,128)(2,1)}, u32[]{:S(2)}) copy-start(bf16[256,256]{1,0:T(8,128)(2,1)} %constant.68.clone.headsum.refs_14_.refs_19_) | copy-start | bytes 393220
  0.7 21.2 %copy-start.4 = (bf16[256,256]{1,0:T(8,128)(2,1)S(1)}, bf16[256,256]{1,0:T(8,128)(2,1)}, u32[]{:S(2)}) copy-start(bf16[256,256]{1,0:T(8,128)(2,1)} %refs_17_) | copy-start | bytes 393220
  0.7 21.2 %copy-start.3 = (bf16[256,256]{1,0:T(8,128)(2,1)S(1)}, bf16[256,256]{1,0:T(8,128)(2,1)}, u32[]{:S(2)}) copy-start(bf16[256,256]{1,0:T(8,128)(2,1)} %refs_16_) | copy-start | bytes 393220
  0.7 21.2 %copy-start.2 = (bf16[256,256]{1,0:T(8,128)(2,1)S(1)}, bf16[256,256]{1,0:T(8,128)(2,1)}, u32[]{:S(2)}) copy-start(bf16[256,256]{1,0:T(8,128)(2,1)} %refs_15_) | copy-start | bytes 393220
  0.7 21.2 %copy-start.1 = (bf16[256,256]{1,0:T(8,128)(2,1)S(1)}, bf16[256,256]{1,0:T(8,128)(2,1)}, u32[]{:S(2)}) copy-start(bf16[256,256]{1,0:T(8,128)(2,1)} %refs_14_.1) | copy-start | bytes 393220
  0.7 21.2 %copy-start.7 = (f32[256]{0:T(256)S(1)}, f32[256]{0:T(256)}, u32[]{:S(2)}) copy-start(f32[256]{0:T(256)} %param.11) | copy-start | bytes 3076
  3.8 28.9 %copy-start.6 = (f32[3,3,256]{2,1,0:T(4,128)S(1)}, f32[3,3,256]{2,1,0:T(4,128)}, u32[]{:S(2)}) copy-start(f32[3,3,256]{2,1,0:T(4,128)} %refs_13_.2) | copy-start | bytes 27652
  3.9 16.1 %all-to-all-start = ((bf16[8,128,256]{2,1,0:T(8,128)(2,1)}), bf16[8,128,256]{2,1,0:T(8,128)(2,1)S(1)}, u32[]{:S(2)}, u32[]{:S(2)}) async-start(bf16[8,128,256]{2,1,0:T(8,128)(2,1)} %pack.1), calls=%async_computation | async-start | bytes 1048576 | tf_op jit(solution)/shard_map/to_cells/all_to_all | solution.py:365
  20.3 4.6 %collective-permute-start.1 = (bf16[4,32,256]{2,1,0:T(8,128)(2,1)S(1)}, bf16[4,32,256]{2,1,0:T(8,128)(2,1)S(1)}, u32[]{:S(2)}, u32[]{:S(2)}) collective-permute-start(bf16[4,32,256]{2,1,0:T(8,128)(2,1)S(1)} %get-tuple-element.73), channel_id=1, source_target_pairs={{0,8},{8,0},{16,24},{24,16},{1,9},{9,1},{17,25},{25,17},{2,10},{10... | collective-permute-start | bytes 196616 | tf_op jit(solution)/shard_map/halo_rows/ppermute | solution.py:332
  21.2 3.7 %collective-permute-start = (bf16[4,32,256]{2,1,0:T(8,128)(2,1)S(1)}, bf16[4,32,256]{2,1,0:T(8,128)(2,1)S(1)}, u32[]{:S(2)}, u32[]{:S(2)}) collective-permute-start(bf16[4,32,256]{2,1,0:T(8,128)(2,1)S(1)} %get-tuple-element.74), channel_id=1, source_target_pairs={{8,16},{16,8},{9,17},{17,9},{10,18},{18,10},{11,19},{19,11},{12,20... | collective-permute-start | bytes 196616 | tf_op jit(solution)/shard_map/halo_rows/ppermute | solution.py:332
  25.0 10.3 %collective-permute-start.3 = (bf16[6,32,256]{2,1,0:T(8,128)(2,1)S(1)}, bf16[6,32,256]{2,1,0:T(8,128)(2,1)S(1)}, u32[]{:S(2)}, u32[]{:S(2)}) collective-permute-start(bf16[6,32,256]{2,1,0:T(8,128)(2,1)S(1)} %get-tuple-element.77), channel_id=1, source_target_pairs={{0,64},{64,0},{128,192},{192,128},{224,160},{160,224},{96,32},{32,... | collective-permute-start | bytes 294920 | tf_op jit(solution)/shard_map/halo_cols/ppermute | solution.py:332
  25.4 10.9 %collective-permute-start.2 = (bf16[6,32,256]{2,1,0:T(8,128)(2,1)S(1)}, bf16[6,32,256]{2,1,0:T(8,128)(2,1)S(1)}, u32[]{:S(2)}, u32[]{:S(2)}) collective-permute-start(bf16[6,32,256]{2,1,0:T(8,128)(2,1)S(1)} %get-tuple-element.78), channel_id=1, source_target_pairs={{64,128},{128,64},{192,224},{224,192},{160,96},{96,160},{32,1},{1,... | collective-permute-start | bytes 294920 | tf_op jit(solution)/shard_map/halo_cols/ppermute | solution.py:332
  57.0 5.7 %collective-permute-start.6 = (bf16[144,256]{1,0:T(8,128)(2,1)S(1)}, bf16[144,256]{1,0:T(8,128)(2,1)S(1)}, u32[]{:S(2)}, u32[]{:S(2)}) collective-permute-start(bf16[144,256]{1,0:T(8,128)(2,1)S(1)} %slice_reduce_fusion), channel_id=1, source_target_pairs={{0,24},{8,16},{16,8},{24,0},{1,25},{9,17},{17,9},{25,1},{2,26},{10... | collective-permute-start | bytes 221192 | tf_op jit(solution)/shard_map/reduce/ppermute | solution.py:313
  59.5 7.7 %collective-permute-start.5 = (bf16[144,256]{1,0:T(8,128)(2,1)S(1)}, bf16[144,256]{1,0:T(8,128)(2,1)S(1)}, u32[]{:S(2)}, u32[]{:S(2)}) collective-permute-start(bf16[144,256]{1,0:T(8,128)(2,1)S(1)} %slice_reduce_fusion), channel_id=1, source_target_pairs={{0,16},{8,24},{16,0},{24,8},{1,17},{9,25},{17,1},{25,9},{2,18},{10... | collective-permute-start | bytes 221192 | tf_op jit(solution)/shard_map/reduce/ppermute | solution.py:313
  62.7 4.5 %collective-permute-start.4 = (bf16[144,256]{1,0:T(8,128)(2,1)S(1)}, bf16[144,256]{1,0:T(8,128)(2,1)S(1)}, u32[]{:S(2)}, u32[]{:S(2)}) collective-permute-start(bf16[144,256]{1,0:T(8,128)(2,1)S(1)} %slice_reduce_fusion), channel_id=1, source_target_pairs={{0,8},{8,0},{16,24},{24,16},{1,9},{9,1},{17,25},{25,17},{2,10},{10... | collective-permute-start | bytes 221192 | tf_op jit(solution)/shard_map/reduce/ppermute | solution.py:313
  67.2 5.3 %collective-permute-start.9 = (bf16[144,256]{1,0:T(8,128)(2,1)S(1)}, bf16[144,256]{1,0:T(8,128)(2,1)S(1)}, u32[]{:S(2)}, u32[]{:S(2)}) collective-permute-start(bf16[144,256]{1,0:T(8,128)(2,1)S(1)} %add_convert_fusion.2), channel_id=1, source_target_pairs={{0,6},{1,7},{2,4},{3,5},{4,2},{5,3},{6,0},{7,1},{8,14},{9,15},{10,... | collective-permute-start | bytes 221192 | tf_op jit(solution)/shard_map/reduce/ppermute | solution.py:313
  67.3 5.2 %collective-permute-start.8 = (bf16[144,256]{1,0:T(8,128)(2,1)S(1)}, bf16[144,256]{1,0:T(8,128)(2,1)S(1)}, u32[]{:S(2)}, u32[]{:S(2)}) collective-permute-start(bf16[144,256]{1,0:T(8,128)(2,1)S(1)} %add_convert_fusion.2), channel_id=1, source_target_pairs={{0,4},{1,5},{2,6},{3,7},{4,0},{5,1},{6,2},{7,3},{8,12},{9,13},{10,... | collective-permute-start | bytes 221192 | tf_op jit(solution)/shard_map/reduce/ppermute | solution.py:313
  67.6 5.5 %collective-permute-start.7 = (bf16[144,256]{1,0:T(8,128)(2,1)S(1)}, bf16[144,256]{1,0:T(8,128)(2,1)S(1)}, u32[]{:S(2)}, u32[]{:S(2)}) collective-permute-start(bf16[144,256]{1,0:T(8,128)(2,1)S(1)} %add_convert_fusion.2), channel_id=1, source_target_pairs={{0,2},{1,3},{2,0},{3,1},{4,6},{5,7},{6,4},{7,5},{8,10},{9,11},{10,... | collective-permute-start | bytes 221192 | tf_op jit(solution)/shard_map/reduce/ppermute | solution.py:313
  73.1 8.0 %collective-permute-start.10 = (bf16[144,256]{1,0:T(8,128)(2,1)S(1)}, bf16[144,256]{1,0:T(8,128)(2,1)S(1)}, u32[]{:S(2)}, u32[]{:S(2)}) collective-permute-start(bf16[144,256]{1,0:T(8,128)(2,1)S(1)} %add_convert_fusion.1), channel_id=1, source_target_pairs={{0,1},{1,0},{2,3},{3,2},{4,5},{5,4},{6,7},{7,6},{8,9},{9,8},{10,11... | collective-permute-start | bytes 221192 | tf_op jit(solution)/shard_map/reduce/ppermute | solution.py:313
  81.2 4.7 %collective-permute-start.12 = (bf16[128,256]{1,0:T(8,128)(2,1)S(1)}, bf16[128,256]{1,0:T(8,128)(2,1)S(1)}, u32[]{:S(2)}, u32[]{:S(2)}) collective-permute-start(bf16[128,256]{1,0:T(8,128)(2,1)S(1)} %get-tuple-element.82), channel_id=1, source_target_pairs={{0,128},{32,160},{64,192},{96,224},{128,0},{160,32},{192,64},{224,... | collective-permute-start | bytes 196616 | tf_op jit(solution)/shard_map/reduce/ppermute | solution.py:442
  81.9 4.0 %collective-permute-start.11 = (bf16[128,256]{1,0:T(8,128)(2,1)S(1)}, bf16[128,256]{1,0:T(8,128)(2,1)S(1)}, u32[]{:S(2)}, u32[]{:S(2)}) collective-permute-start(bf16[128,256]{1,0:T(8,128)(2,1)S(1)} %get-tuple-element.82), channel_id=1, source_target_pairs={{0,64},{32,96},{64,0},{96,32},{128,192},{160,224},{192,128},{224,1... | collective-permute-start | bytes 196616 | tf_op jit(solution)/shard_map/reduce/ppermute | solution.py:442
  82.7 4.3 %collective-permute-start.13 = (bf16[128,256]{1,0:T(8,128)(2,1)S(1)}, bf16[128,256]{1,0:T(8,128)(2,1)S(1)}, u32[]{:S(2)}, u32[]{:S(2)}) collective-permute-start(bf16[128,256]{1,0:T(8,128)(2,1)S(1)} %get-tuple-element.82), channel_id=1, source_target_pairs={{0,192},{32,224},{64,128},{96,160},{128,64},{160,96},{192,0},{224,... | collective-permute-start | bytes 196616 | tf_op jit(solution)/shard_map/reduce/ppermute | solution.py:442
  87.1 6.7 %collective-permute-start.14 = (bf16[4,128,256]{2,1,0:T(8,128)(2,1)S(1)}, bf16[4,128,256]{2,1,0:T(8,128)(2,1)S(1)}, u32[]{:S(2)}, u32[]{:S(2)}) collective-permute-start(bf16[4,128,256]{2,1,0:T(8,128)(2,1)S(1)} %pad_maximum_fusion.same_core), channel_id=1, source_target_pairs={{0,32},{32,0},{64,96},{96,64},{128,160},{160,128},{192,224},{224,1... | collective-permute-start | bytes 786440 | tf_op jit(solution)/shard_map/reduce/ppermute | solution.py:444

commit v12 on v11

--- a/solution.py
+++ b/solution.py
@@ -64,6 +64,12 @@
             moved = dot(split, tokens).astype(BF).reshape(parts, per, width)
             start = (k * rows + r) * per
             send[:, start : start + per, :] = moved
+
+
+def hold_kernel(after, *refs):
+    count = len(refs) // 2
+    for source, held in zip(refs[:count], refs[count:]):
+        held[...] = source[...]
 
 
 def order_kernel(members, recv, gather8, x_out, cot_out):
@@ -290,14 +296,18 @@
         out[:, r] = dot(split, tokens, TN).astype(BF).reshape(members, cols, width)
 
 
-def finish_kernel(scale, place, same_core, other_core, total, g_q, g_k, g_v, g_o, g_mix, g_gain):
-    count, shard, width = same_core.shape
+def finish_kernel(scale, place, pair, pair_far, other, other_far, total, g_q, g_k, g_v, g_o, g_mix, g_gain):
+    _, shard, width = pair.shape
     per = width // shard
     outs = (g_q, g_k, g_v, g_o)
-    for p in range(2 * count):
+    for p in range(8):
         code = lax.bitwise_xor(place[0], p)
-        spot = lax.shift_right_logical(code, 1)
-        got = jnp.where(code == 2 * spot, same_core[spot], other_core[spot]).astype(F32)
+        step = lax.shift_right_logical(code, 1)
+        distant = step >= 2
+        spot = jnp.where(distant, 3 - step, step)
+        same = jnp.where(distant, pair_far[spot], pair[spot])
+        cross = jnp.where(distant, other_far[spot], other[spot])
+        got = jnp.where(code == 2 * step, same, cross).astype(F32)
         outs[p // per][p % per * shard : (p % per + 1) * shard, :] = got * scale
     rest = total[shard:, :].astype(F32) * scale
     for i in range(3):
@@ -315,6 +325,10 @@
     while len(got) > 1:
         got = [a + b for a, b in zip(got[::2], got[1::2])]
     return lax.optimization_barrier(got[0].astype(BF))
+
+
+def far(x):
+    return pltpu.with_memory_space_constraint(x, pltpu.MemorySpace.HBM)
 
 
 def near(x):
@@ -360,7 +374,16 @@
             scratch_shapes=[pltpu.VMEM((2, rows, members, cols, width), BF), pltpu.SemaphoreType.DMA((2, rows))],
             out_shape=pltpu.VMEM((parts, 2 * base, width), BF),
             compiler_params=params,
-        )(*[pltpu.with_memory_space_constraint(a, pltpu.MemorySpace.HBM) for a in (fields, cotangent)])
+        )(far(fields), far(cotangent))
+    with jax.named_scope("hold"):
+        kinds = (w_query, w_key, w_value, w_out, gather8, headsum)
+        held = pl.pallas_call(
+            hold_kernel,
+            in_specs=[pl.BlockSpec(memory_space=pl.ANY)] + [vmem] * len(kinds),
+            out_shape=tuple(pltpu.VMEM(a.shape, a.dtype) for a in kinds),
+            compiler_params=params,
+        )(near(send), *[far(a) for a in kinds])
+        w_query, w_key, w_value, w_out, gather8, headsum = [near(a) for a in held]
     with jax.named_scope("to_cells"):
         recv = lax.all_to_all(send, "mem", 0, 0)
     with jax.named_scope("order"):
@@ -369,7 +392,6 @@
             out_shape=(pltpu.VMEM((tokens, width), BF), pltpu.VMEM((rows, per, parts * members, width), BF)),
             compiler_params=params,
         )(near(recv), gather8)
-        x, w_query, w_key, w_value, w_out = lax.optimization_barrier((x, w_query, w_key, w_value, w_out))
     with jax.named_scope("halo_rows"):
         rows_at = {r: r for r in range(grid[0])}
         below, above = swap(cot[rows - 1], cot[0], lax.axis_index("row"), "row", rows_at, False)
@@ -439,9 +461,11 @@
         total = meet(total, "col", (1,))
         total, grad_fields = lax.optimization_barrier((total, grad_fields))
         piece = total[:shard]
-        same_core = jnp.stack([piece] + [lax.ppermute(piece, "mem", partner("mem", k)) for k in (2, 4, 6)])
-        same_core = lax.optimization_barrier(same_core)
-        other_core = lax.ppermute(same_core, "mem", partner("mem", 1))
+        next_x = lax.ppermute(piece, "mem", partner("mem", 2))
+        pair = lax.optimization_barrier(jnp.stack([piece, next_x]))
+        pair_far = lax.ppermute(pair, "mem", partner("mem", 6))
+        other = lax.ppermute(pair, "mem", partner("mem", 1))
+        other_far = lax.ppermute(pair_far, "mem", partner("mem", 1))
 
     scale_all = 1.0 / math.sqrt(tokens * grid[0] * grid[1] * parts)
     with jax.named_scope("finish"):
@@ -449,10 +473,10 @@
         own = lax.axis_index("mem").astype(jnp.int32).reshape(1)
         grads = pl.pallas_call(
             functools.partial(finish_kernel, scale_all),
-            in_specs=[smem] + [vmem] * 3,
+            in_specs=[smem] + [vmem] * 5,
             out_shape=(square,) * 4 + (jax.ShapeDtypeStruct((3, 3, width), F32), jax.ShapeDtypeStruct((1, width), F32)),
             compiler_params=params,
-        )(own, near(same_core), near(other_core), near(total))
+        )(own, *[near(a) for a in (pair, pair_far, other, other_far, total)])
     return (grad_fields, grads[5].reshape(width)) + tuple(grads[:5])
 
 

time: 95.1 us -> 97.7 us (1.027)
  starting transfers between devices: 40 us -> 43.4 us
  waiting for transfers between devices: 22 us -> 20.2 us
  Pallas kernels: 13.7 us -> 14.9 us
    ppermute x4, starting transfers between devices: 8.89 us -> 11.4 us  [the longest x1 5.07 us: local(): other = lax.ppermute(pair, 'mem', partner('mem', 1))]
    all_to_all x1, waiting for transfers between devices: 9.5 us -> 8.23 us  [local(): recv = lax.all_to_all(send, 'mem', 0, 0)]
    pallas_call x0 -> x1, Pallas kernels: none -> 1.26 us  [local(): pl.pallas_call(hold_kernel, in_specs=[pl.BlockSpec(memory_space=pl.ANY)]...]
  transfers between devices with their start and end apart: 16 -> 16, of which waited for: 9 -> 9; matrix products, arithmetic and copies ran while one was open for 0% -> 0% of each run, Pallas kernels for 7% -> 8%
where the time goes in v12:
time: 97.7 us; the launch traced here: 97.4 us
  starting transfers between devices  43.4 us (44%)
  waiting for transfers between devices  20.2 us (21%)
  blocking collectives  17.8 us (18%)
  Pallas kernels  14.9 us (15%)
    all_to_all x1, blocking collectives, local(): landed = lax.all_to_all(back, 'mem', 0, 0)  17.8 us
    ppermute x7, starting transfers between devices, meet(): lax.ppermute(values, axis, partner(axis, k))  16.1 us
    ppermute x4, starting transfers between devices, swap(): lax.ppermute(jnp.where(spot % 2 == odd, last, first), axis, pairs)  9.22 us
    all_to_all x1, waiting for transfers between devices, local(): recv = lax.all_to_all(send, 'mem', 0, 0)  8.23 us
    ppermute x7, waiting for transfers between devices, meet(): lax.ppermute(values, axis, partner(axis, k))  7.01 us
    all_to_all x1, starting transfers between devices, local(): recv = lax.all_to_all(send, 'mem', 0, 0)  6.64 us
    ppermute x1, starting transfers between devices, local(): other = lax.ppermute(pair, 'mem', partner('mem', 1))  5.07 us
    ppermute x1, starting transfers between devices, local(): other_far = lax.ppermute(pair_far, 'mem', partner('mem', 1))  5.01 us
  transfers between devices with their start and end apart: 16, of which 9 were waited for; matrix products, arithmetic and copies ran while one was open for 0% of the time, Pallas kernels for 8%

profile of v12, /device:TPU:1, one launch (start us, length us, event | category | flops | bytes accessed | tf_op | source)
XLA Modules:
  0.0 97.4 jit_solution(16407132441034860074)
XLA Ops:
  0.6 3.1 %pack.1.after = bf16[8,128,256]{2,1,0:T(8,128)(2,1)} custom-call(bf16[4,4,32,256]{3,2,1,0:T(8,128)(2,1)} %fields.1, bf16[4,4,32,256]{3,2,1,0:T(8,128)(2,1)} %cot.1), custom_call_target="tpu_custom_call" | custom-call | tf_op jit(solution)/shard_map/pack/pallas_call | solution.py:371
  3.7 0.0 copy-start.1
  3.7 6.6 %all-to-all-start = ((bf16[8,128,256]{2,1,0:T(8,128)(2,1)}), bf16[8,128,256]{2,1,0:T(8,128)(2,1)S(1)}, u32[]{:S(2)}, u32[]{:S(2)}) async-start(bf16[8,128,256]{2,1,0:T(8,128)(2,1)} %pack.1.after), calls=%async_computation | async-start | bytes 1048576 | tf_op jit(solution)/shard_map/to_cells/all_to_all | solution.py:388
  10.3 0.0 copy-start
  10.3 1.3 %hold.1 = (bf16[256,256]{1,0:T(8,128)(2,1)S(1)}, bf16[256,256]{1,0:T(8,128)(2,1)S(1)}, bf16[256,256]{1,0:T(8,128)(2,1)S(1)}, bf16[256,256]{1,0:T(8,128)(2,1)S(1)...) custom-call(bf16[8,128,256]{2,1,0:T(8,128)(2,1)} %pack.1.after, bf16[256,256]{1,0:T(8,128)(2,1)} %refs_0_.1, ...), custom_call_target="tpu_custom_call" | custom-call | tf_op jit(solution)/shard_map/hold/pallas_call | solution.py:380
  11.6 8.2 %all-to-all-done.recv = bf16[8,128,256]{2,1,0:T(8,128)(2,1)S(1)} async-done(((bf16[8,128,256]{2,1,0:T(8,128)(2,1)}), bf16[8,128,256]{2,1,0:T(8,128)(2,1)S(1)}, u32[]{:S(2)}, u32[]{:S(2)}) %all-to-all-start) | async-done | bytes 524320 | tf_op jit(solution)/shard_map/to_cells/all_to_all | solution.py:388
  19.8 0.3 order.1
  20.2 0.9 collective-permute-start.1
  21.1 0.7 collective-permute-start
  21.7 0.0 copy-done.1
  21.7 3.0 %forward.1 = (bf16[512,256]{1,0:T(8,128)(2,1)S(1)}, f32[512,256]{1,0:T(8,128)S(1)}, bf16[512,256]{1,0:T(8,128)(2,1)S(1)}, bf16[512,256]{1,0:T(8,128)(2,1)S(1)}, ...) custom-call(bf16[512,256]{1,0:T(8,128)(2,1)S(1)} %get-tuple-element.42.x_in.refs_0_.refs_5_, ...), custom_call_target="tpu_custom_call" | custom-call | tf_op jit(solution)/shard_map/forward/pallas_call | solution.py:402
  24.7 0.0 collective-permute-done.1
  24.7 0.0 collective-permute-done
  24.8 0.4 collective-permute-start.3
  25.2 7.3 %collective-permute-start.2 = (bf16[6,32,256]{2,1,0:T(8,128)(2,1)S(1)}, bf16[6,32,256]{2,1,0:T(8,128)(2,1)S(1)}, u32[]{:S(2)}, u32[]{:S(2)}) collective-permute-start(bf16[6,32,256]{2,1,0:T(8,128)(2,1)S(1)} %get-tuple-element.80), channel_id=1, source_target_pairs={{64,128},{128,64},{192,224},{224,192},{160,96},{96,160},{32,1},{1,... | collective-permute-start | bytes 294920 | tf_op jit(solution)/shard_map/halo_cols/ppermute | solution.py:346
  32.5 0.1 pad_add_fusion.place
  32.6 0.0 copy-done
  32.6 2.5 %backward_inner.1 = (bf16[256,256]{1,0:T(8,128)(2,1)S(1)}, f32[4,256,256]{2,1,0:T(8,128)S(1)}, f32[16,256]{1,0:T(8,128)S(1)}) custom-call(s32[2]{0:T(128)S(1)} %pad_add_fusion.place, bf16[4,4,32,256]{3,2,1,0:T(8,128)(2,1)S(1)} %get-tuple-element.41.cot, bf16[4,32,256]{2,1,0:T(8,128)(2,1)S(1)} %get-tuple-element.54.above, ...), custom_call_target="tpu_custom_call" | custom-call | tf_op jit(solution)/shard_map/backward_inner/pallas_call | solution.py:428
  35.1 0.0 collective-permute-done.3
  35.1 1.0 %collective-permute-done.2 = bf16[6,32,256]{2,1,0:T(8,128)(2,1)S(1)} collective-permute-done((bf16[6,32,256]{2,1,0:T(8,128)(2,1)S(1)}, bf16[6,32,256]{2,1,0:T(8,128)(2,1)S(1)}, u32[]{:S(2)}, u32[]{:S(2)}) %collective-permute-start.2) | collective-permute-done | bytes 98336 | tf_op jit(solution)/shard_map/halo_cols/ppermute | solution.py:346
  36.1 2.8 %backward_outer.1 = bf16[8,208,256]{2,1,0:T(8,128)(2,1)S(1)} custom-call(s32[2]{0:T(128)S(1)} %pad_add_fusion.place, bf16[4,4,32,256]{3,2,1,0:T(8,128)(2,1)S(1)} %get-tuple-element.41.cot, bf16[4,32,256]{2,1,0:T(8,128)(2,1)S(1)} %get-tuple-element.54.above, bf16[4,32,256]{2,1,0:T(8,128)(2,1)S(1)} %get-tuple-element.55.below, ...), custom_call_target="tpu_custom_call" | custom-call | tf_op jit(solution)/shard_map/backward_outer/pallas_call | solution.py:440
  38.9 17.8 %all_to_all.10.recv = bf16[8,208,256]{2,1,0:T(8,128)(2,1)S(1)} all-to-all(bf16[8,208,256]{2,1,0:T(8,128)(2,1)S(1)} %backward_outer.1), channel_id=1, replica_groups=mesh['mem'=8,'row'=4,'col'=8] {'mem'}, dimensions={0} | all-to-all | bytes 1703936 | tf_op jit(solution)/shard_map/to_members/all_to_all | solution.py:448
  56.7 0.1 slice_reduce_fusion
  56.8 2.5 %collective-permute-start.6 = (bf16[144,256]{1,0:T(8,128)(2,1)S(1)}, bf16[144,256]{1,0:T(8,128)(2,1)S(1)}, u32[]{:S(2)}, u32[]{:S(2)}) collective-permute-start(bf16[144,256]{1,0:T(8,128)(2,1)S(1)} %slice_reduce_fusion), channel_id=1, source_target_pairs={{0,24},{8,16},{16,8},{24,0},{1,25},{9,17},{17,9},{25,1},{2,26},{10... | collective-permute-start | bytes 221192 | tf_op jit(solution)/shard_map/reduce/ppermute | solution.py:323
  59.2 3.2 %collective-permute-start.5 = (bf16[144,256]{1,0:T(8,128)(2,1)S(1)}, bf16[144,256]{1,0:T(8,128)(2,1)S(1)}, u32[]{:S(2)}, u32[]{:S(2)}) collective-permute-start(bf16[144,256]{1,0:T(8,128)(2,1)S(1)} %slice_reduce_fusion), channel_id=1, source_target_pairs={{0,16},{8,24},{16,0},{24,8},{1,17},{9,25},{17,1},{25,9},{2,18},{10... | collective-permute-start | bytes 221192 | tf_op jit(solution)/shard_map/reduce/ppermute | solution.py:323
  62.5 0.0 collective-permute-start.4
  62.5 0.0 collective-permute-done.6
  62.5 3.7 %collective-permute-done.5 = bf16[144,256]{1,0:T(8,128)(2,1)S(1)} collective-permute-done((bf16[144,256]{1,0:T(8,128)(2,1)S(1)}, bf16[144,256]{1,0:T(8,128)(2,1)S(1)}, u32[]{:S(2)}, u32[]{:S(2)}) %collective-permute-start.5) | collective-permute-done | bytes 73760 | tf_op jit(solution)/shard_map/reduce/ppermute | solution.py:323
  66.2 0.0 collective-permute-done.4
  66.2 0.6 collective-permute-start.9
  66.9 0.5 collective-permute-start.8
  67.3 2.3 %collective-permute-start.7 = (bf16[144,256]{1,0:T(8,128)(2,1)S(1)}, bf16[144,256]{1,0:T(8,128)(2,1)S(1)}, u32[]{:S(2)}, u32[]{:S(2)}) collective-permute-start(bf16[144,256]{1,0:T(8,128)(2,1)S(1)} %add_convert_fusion.2), channel_id=1, source_target_pairs={{0,2},{1,3},{2,0},{3,1},{4,6},{5,7},{6,4},{7,5},{8,10},{9,11},{10,... | collective-permute-start | bytes 221192 | tf_op jit(solution)/shard_map/reduce/ppermute | solution.py:323
  69.6 1.2 %collective-permute-done.9 = bf16[144,256]{1,0:T(8,128)(2,1)S(1)} collective-permute-done((bf16[144,256]{1,0:T(8,128)(2,1)S(1)}, bf16[144,256]{1,0:T(8,128)(2,1)S(1)}, u32[]{:S(2)}, u32[]{:S(2)}) %collective-permute-start.9) | collective-permute-done | bytes 73760 | tf_op jit(solution)/shard_map/reduce/ppermute | solution.py:323
  70.7 0.8 collective-permute-done.8
  71.6 0.5 collective-permute-done.7
  72.1 7.0 %collective-permute-start.10 = (bf16[144,256]{1,0:T(8,128)(2,1)S(1)}, bf16[144,256]{1,0:T(8,128)(2,1)S(1)}, u32[]{:S(2)}, u32[]{:S(2)}) collective-permute-start(bf16[144,256]{1,0:T(8,128)(2,1)S(1)} %add_convert_fusion.1), channel_id=1, source_target_pairs={{0,1},{1,0},{2,3},{3,2},{4,5},{5,4},{6,7},{7,6},{8,9},{9,8},{10,11... | collective-permute-start | bytes 221192 | tf_op jit(solution)/shard_map/reduce/ppermute | solution.py:323
  79.2 1.0 unpack.1
  80.2 0.8 collective-permute-done.10
  81.0 0.4 collective-permute-start.11
  81.3 2.9 %collective-permute-done.11 = bf16[128,256]{1,0:T(8,128)(2,1)S(1)} collective-permute-done((bf16[128,256]{1,0:T(8,128)(2,1)S(1)}, bf16[128,256]{1,0:T(8,128)(2,1)S(1)}, u32[]{:S(2)}, u32[]{:S(2)}) %collective-permute-start.11) | collective-permute-done | bytes 65568 | tf_op jit(solution)/shard_map/reduce/ppermute | solution.py:464
  84.3 1.0 collective-permute-start.12
  85.3 5.1 %collective-permute-start.13 = (bf16[2,128,256]{2,1,0:T(8,128)(2,1)S(1)}, bf16[2,128,256]{2,1,0:T(8,128)(2,1)S(1)}, u32[]{:S(2)}, u32[]{:S(2)}) collective-permute-start(bf16[2,128,256]{2,1,0:T(8,128)(2,1)S(1)} %pad_maximum_fusion.pair), channel_id=1, source_target_pairs={{0,32},{32,0},{64,96},{96,64},{128,160},{160,128},{192,224},{224,1... | collective-permute-start | bytes 393224 | tf_op jit(solution)/shard_map/reduce/ppermute | solution.py:467
  90.3 0.0 collective-permute-done.12.pair_far
  90.3 5.0 %collective-permute-start.14 = (bf16[2,128,256]{2,1,0:T(8,128)(2,1)S(1)}, bf16[2,128,256]{2,1,0:T(8,128)(2,1)S(1)}, u32[]{:S(2)}, u32[]{:S(2)}) collective-permute-start(bf16[2,128,256]{2,1,0:T(8,128)(2,1)S(1)} %collective-permute-done.12.pair_far), channel_id=1, source_target_pairs={{0,32},{32,0},{64,96},{96,64},{128,160},{160,128},{192,224},{224,1... | collective-permute-start | bytes 393224 | tf_op jit(solution)/shard_map/reduce/ppermute | solution.py:468
  95.3 0.0 collective-permute-done.13.other
  95.4 1.0 %collective-permute-done.14.other_far = bf16[2,128,256]{2,1,0:T(8,128)(2,1)S(1)} collective-permute-done((bf16[2,128,256]{2,1,0:T(8,128)(2,1)S(1)}, bf16[2,128,256]{2,1,0:T(8,128)(2,1)S(1)}, u32[]{:S(2)}, u32[]{:S(2)}) %collective-permute-start.14) | collective-permute-done | bytes 131104 | tf_op jit(solution)/shard_map/reduce/ppermute | solution.py:468
  96.3 1.1 %finish.1 = (f32[256,256]{1,0:T(8,128)}, f32[256,256]{1,0:T(8,128)}, f32[256,256]{1,0:T(8,128)}, f32[256,256]{1,0:T(8,128)}, f32[3,3,256]{2,1,0:T(4,128)}, /*index=5*/f32[1,256]{1,0:T(1,128)}) custom-call(s32[1]{0:T(128)} %bitcast.7.place, bf16[2,128,256]{2,1,0:T(8,128)(2,1)S(1)} %pad_maximum_fusion.pair, ...), custom_call_target="tpu_custom_call" | custom-call | tf_op jit(solution)/shard_map/finish/pallas_call | solution.py:474
  (11 shorter events, 0.2 us)
Async XLA Ops:
  3.7 18.0 %copy-start.1 = (f32[256]{0:T(256)S(1)}, f32[256]{0:T(256)}, u32[]{:S(2)}) copy-start(f32[256]{0:T(256)} %param.11) | copy-start | bytes 3076
  3.7 16.1 %all-to-all-start = ((bf16[8,128,256]{2,1,0:T(8,128)(2,1)}), bf16[8,128,256]{2,1,0:T(8,128)(2,1)S(1)}, u32[]{:S(2)}, u32[]{:S(2)}) async-start(bf16[8,128,256]{2,1,0:T(8,128)(2,1)} %pack.1.after), calls=%async_computation | async-start | bytes 1048576 | tf_op jit(solution)/shard_map/to_cells/all_to_all | solution.py:388
  10.3 22.2 %copy-start = (f32[3,3,256]{2,1,0:T(4,128)S(1)}, f32[3,3,256]{2,1,0:T(4,128)}, u32[]{:S(2)}) copy-start(f32[3,3,256]{2,1,0:T(4,128)} %refs_13_.1) | copy-start | bytes 27652
  20.2 4.5 %collective-permute-start.1 = (bf16[4,32,256]{2,1,0:T(8,128)(2,1)S(1)}, bf16[4,32,256]{2,1,0:T(8,128)(2,1)S(1)}, u32[]{:S(2)}, u32[]{:S(2)}) collective-permute-start(bf16[4,32,256]{2,1,0:T(8,128)(2,1)S(1)} %get-tuple-element.75), channel_id=1, source_target_pairs={{0,8},{8,0},{16,24},{24,16},{1,9},{9,1},{17,25},{25,17},{2,10},{10... | collective-permute-start | bytes 196616 | tf_op jit(solution)/shard_map/halo_rows/ppermute | solution.py:346
  21.1 3.7 %collective-permute-start = (bf16[4,32,256]{2,1,0:T(8,128)(2,1)S(1)}, bf16[4,32,256]{2,1,0:T(8,128)(2,1)S(1)}, u32[]{:S(2)}, u32[]{:S(2)}) collective-permute-start(bf16[4,32,256]{2,1,0:T(8,128)(2,1)S(1)} %get-tuple-element.76), channel_id=1, source_target_pairs={{8,16},{16,8},{9,17},{17,9},{10,18},{18,10},{11,19},{19,11},{12,20... | collective-permute-start | bytes 196616 | tf_op jit(solution)/shard_map/halo_rows/ppermute | solution.py:346
  24.8 10.3 %collective-permute-start.3 = (bf16[6,32,256]{2,1,0:T(8,128)(2,1)S(1)}, bf16[6,32,256]{2,1,0:T(8,128)(2,1)S(1)}, u32[]{:S(2)}, u32[]{:S(2)}) collective-permute-start(bf16[6,32,256]{2,1,0:T(8,128)(2,1)S(1)} %get-tuple-element.79), channel_id=1, source_target_pairs={{0,64},{64,0},{128,192},{192,128},{224,160},{160,224},{96,32},{32,... | collective-permute-start | bytes 294920 | tf_op jit(solution)/shard_map/halo_cols/ppermute | solution.py:346
  25.2 10.9 %collective-permute-start.2 = (bf16[6,32,256]{2,1,0:T(8,128)(2,1)S(1)}, bf16[6,32,256]{2,1,0:T(8,128)(2,1)S(1)}, u32[]{:S(2)}, u32[]{:S(2)}) collective-permute-start(bf16[6,32,256]{2,1,0:T(8,128)(2,1)S(1)} %get-tuple-element.80), channel_id=1, source_target_pairs={{64,128},{128,64},{192,224},{224,192},{160,96},{96,160},{32,1},{1,... | collective-permute-start | bytes 294920 | tf_op jit(solution)/shard_map/halo_cols/ppermute | solution.py:346
  56.8 5.7 %collective-permute-start.6 = (bf16[144,256]{1,0:T(8,128)(2,1)S(1)}, bf16[144,256]{1,0:T(8,128)(2,1)S(1)}, u32[]{:S(2)}, u32[]{:S(2)}) collective-permute-start(bf16[144,256]{1,0:T(8,128)(2,1)S(1)} %slice_reduce_fusion), channel_id=1, source_target_pairs={{0,24},{8,16},{16,8},{24,0},{1,25},{9,17},{17,9},{25,1},{2,26},{10... | collective-permute-start | bytes 221192 | tf_op jit(solution)/shard_map/reduce/ppermute | solution.py:323
  59.2 6.9 %collective-permute-start.5 = (bf16[144,256]{1,0:T(8,128)(2,1)S(1)}, bf16[144,256]{1,0:T(8,128)(2,1)S(1)}, u32[]{:S(2)}, u32[]{:S(2)}) collective-permute-start(bf16[144,256]{1,0:T(8,128)(2,1)S(1)} %slice_reduce_fusion), channel_id=1, source_target_pairs={{0,16},{8,24},{16,0},{24,8},{1,17},{9,25},{17,1},{25,9},{2,18},{10... | collective-permute-start | bytes 221192 | tf_op jit(solution)/shard_map/reduce/ppermute | solution.py:323
  62.5 3.7 %collective-permute-start.4 = (bf16[144,256]{1,0:T(8,128)(2,1)S(1)}, bf16[144,256]{1,0:T(8,128)(2,1)S(1)}, u32[]{:S(2)}, u32[]{:S(2)}) collective-permute-start(bf16[144,256]{1,0:T(8,128)(2,1)S(1)} %slice_reduce_fusion), channel_id=1, source_target_pairs={{0,8},{8,0},{16,24},{24,16},{1,9},{9,1},{17,25},{25,17},{2,10},{10... | collective-permute-start | bytes 221192 | tf_op jit(solution)/shard_map/reduce/ppermute | solution.py:323
  66.2 4.5 %collective-permute-start.9 = (bf16[144,256]{1,0:T(8,128)(2,1)S(1)}, bf16[144,256]{1,0:T(8,128)(2,1)S(1)}, u32[]{:S(2)}, u32[]{:S(2)}) collective-permute-start(bf16[144,256]{1,0:T(8,128)(2,1)S(1)} %add_convert_fusion.2), channel_id=1, source_target_pairs={{0,6},{1,7},{2,4},{3,5},{4,2},{5,3},{6,0},{7,1},{8,14},{9,15},{10,... | collective-permute-start | bytes 221192 | tf_op jit(solution)/shard_map/reduce/ppermute | solution.py:323
  66.9 4.7 %collective-permute-start.8 = (bf16[144,256]{1,0:T(8,128)(2,1)S(1)}, bf16[144,256]{1,0:T(8,128)(2,1)S(1)}, u32[]{:S(2)}, u32[]{:S(2)}) collective-permute-start(bf16[144,256]{1,0:T(8,128)(2,1)S(1)} %add_convert_fusion.2), channel_id=1, source_target_pairs={{0,4},{1,5},{2,6},{3,7},{4,0},{5,1},{6,2},{7,3},{8,12},{9,13},{10,... | collective-permute-start | bytes 221192 | tf_op jit(solution)/shard_map/reduce/ppermute | solution.py:323
  67.3 4.8 %collective-permute-start.7 = (bf16[144,256]{1,0:T(8,128)(2,1)S(1)}, bf16[144,256]{1,0:T(8,128)(2,1)S(1)}, u32[]{:S(2)}, u32[]{:S(2)}) collective-permute-start(bf16[144,256]{1,0:T(8,128)(2,1)S(1)} %add_convert_fusion.2), channel_id=1, source_target_pairs={{0,2},{1,3},{2,0},{3,1},{4,6},{5,7},{6,4},{7,5},{8,10},{9,11},{10,... | collective-permute-start | bytes 221192 | tf_op jit(solution)/shard_map/reduce/ppermute | solution.py:323
  72.1 8.8 %collective-permute-start.10 = (bf16[144,256]{1,0:T(8,128)(2,1)S(1)}, bf16[144,256]{1,0:T(8,128)(2,1)S(1)}, u32[]{:S(2)}, u32[]{:S(2)}) collective-permute-start(bf16[144,256]{1,0:T(8,128)(2,1)S(1)} %add_convert_fusion.1), channel_id=1, source_target_pairs={{0,1},{1,0},{2,3},{3,2},{4,5},{5,4},{6,7},{7,6},{8,9},{9,8},{10,11... | collective-permute-start | bytes 221192 | tf_op jit(solution)/shard_map/reduce/ppermute | solution.py:323
  81.0 3.3 %collective-permute-start.11 = (bf16[128,256]{1,0:T(8,128)(2,1)S(1)}, bf16[128,256]{1,0:T(8,128)(2,1)S(1)}, u32[]{:S(2)}, u32[]{:S(2)}) collective-permute-start(bf16[128,256]{1,0:T(8,128)(2,1)S(1)} %get-tuple-element.84), channel_id=1, source_target_pairs={{0,64},{32,96},{64,0},{96,32},{128,192},{160,224},{192,128},{224,1... | collective-permute-start | bytes 196616 | tf_op jit(solution)/shard_map/reduce/ppermute | solution.py:464
  84.3 6.0 %collective-permute-start.12 = (bf16[2,128,256]{2,1,0:T(8,128)(2,1)S(1)}, bf16[2,128,256]{2,1,0:T(8,128)(2,1)S(1)}, u32[]{:S(2)}, u32[]{:S(2)}) collective-permute-start(bf16[2,128,256]{2,1,0:T(8,128)(2,1)S(1)} %pad_maximum_fusion.pair), channel_id=1, source_target_pairs={{0,192},{32,224},{64,128},{96,160},{128,64},{160,96},{192,0},{224,... | collective-permute-start | bytes 393224 | tf_op jit(solution)/shard_map/reduce/ppermute | solution.py:466
  85.3 10.1 %collective-permute-start.13 = (bf16[2,128,256]{2,1,0:T(8,128)(2,1)S(1)}, bf16[2,128,256]{2,1,0:T(8,128)(2,1)S(1)}, u32[]{:S(2)}, u32[]{:S(2)}) collective-permute-start(bf16[2,128,256]{2,1,0:T(8,128)(2,1)S(1)} %pad_maximum_fusion.pair), channel_id=1, source_target_pairs={{0,32},{32,0},{64,96},{96,64},{128,160},{160,128},{192,224},{224,1... | collective-permute-start | bytes 393224 | tf_op jit(solution)/shard_map/reduce/ppermute | solution.py:467
  90.3 6.0 %collective-permute-start.14 = (bf16[2,128,256]{2,1,0:T(8,128)(2,1)S(1)}, bf16[2,128,256]{2,1,0:T(8,128)(2,1)S(1)}, u32[]{:S(2)}, u32[]{:S(2)}) collective-permute-start(bf16[2,128,256]{2,1,0:T(8,128)(2,1)S(1)} %collective-permute-done.12.pair_far), channel_id=1, source_target_pairs={{0,32},{32,0},{64,96},{96,64},{128,160},{160,128},{192,224},{224,1... | collective-permute-start | bytes 393224 | tf_op jit(solution)/shard_map/reduce/ppermute | solution.py:468

commit v13 on v11

--- a/solution.py
+++ b/solution.py
@@ -323,15 +323,17 @@
 
 def swap(last, first, spot, axis, where, wrap):
     size = len(where)
-    got = []
-    for odd in (0, 1):
+    got = {}
+    for odd in (1, 0):
         pairs = []
         for a in range(odd, size if wrap else size - 1, 2):
             b = (a + 1) % size
             pairs += [(where[a], where[b]), (where[b], where[a])]
-        got.append(lax.ppermute(jnp.where(spot % 2 == odd, last, first), axis, pairs))
-    even = spot % 2 == 0
-    return jnp.where(even, got[0], got[1]), jnp.where(even, got[1], got[0])
+        got[odd] = lax.ppermute(jnp.where(spot % 2 == odd, last, first), axis, pairs)
+    odd = spot % 2 == 1
+    before = jnp.where(odd, got[0], got[1])
+    after = jnp.where(odd, got[1], got[0])
+    return after, before
 
 
 def local(fields, norm_gain, w_query, w_key, w_value, w_out, mix_kernel, cotangent):
@@ -390,8 +392,8 @@
             inner = mem // 2 if mem % 2 == 0 else parts - 1 - mem // 2
             for c in range(grid[1]):
                 where[c * parts + inner] = mem * grid[1] + c
-        last, first = [
-            jnp.concatenate([above[c : c + 1], cot[:, c], below[c : c + 1]], axis=0) for c in (per - 1, 0)
+        first, last = [
+            jnp.concatenate([above[c : c + 1], cot[:, c], below[c : c + 1]], axis=0) for c in (0, per - 1)
         ]
         right, left = swap(last, first, block, ("mem", "col"), where, True)
 
@@ -435,7 +437,7 @@
 
     with jax.named_scope("reduce"):
         total = meet(total, "row", (1, 2, 3))
-        total = meet(total, "col", (2, 4, 6))
+        total = meet(total, "col", (2, 6, 4))
         total = meet(total, "col", (1,))
         total, grad_fields = lax.optimization_barrier((total, grad_fields))
         piece = total[:shard]

time: 95.1 us -> 96 us (level)
  waiting for transfers between devices: 22 us -> 26.8 us
  starting transfers between devices: 40 us -> 36 us
    ppermute x7, waiting for transfers between devices: 7.79 us -> 12.4 us  [meet(): lax.ppermute(values, axis, partner(axis, k))]
    ppermute x7, starting transfers between devices: 15.3 us -> 10.7 us  [meet(): lax.ppermute(values, axis, partner(axis, k))]
    ppermute x4, starting transfers between devices: 9.22 us -> 10.9 us  [swap(): lax.ppermute(jnp.where(spot % 2 == odd, last, first), axis, pairs)]
    ppermute x1, starting transfers between devices: 5.55 us -> 4.43 us  [local(): other_core = lax.ppermute(same_core, 'mem', partner('mem', 1))]
  transfers between devices with their start and end apart: 16 -> 16, of which waited for: 9 -> 10; matrix products, arithmetic and copies ran while one was open for 0% -> 0% of each run, Pallas kernels for 7% -> 7%
where the time goes in v13:
time: 96 us; the launch traced here: 95.8 us
  starting transfers between devices  36 us (38%)
  waiting for transfers between devices  26.8 us (28%)
  blocking collectives  18 us (19%)
  Pallas kernels  13.7 us (14%)
    all_to_all x1, blocking collectives, local(): landed = lax.all_to_all(back, 'mem', 0, 0)  18 us
    ppermute x7, waiting for transfers between devices, meet(): lax.ppermute(values, axis, partner(axis, k))  12.4 us
    ppermute x4, starting transfers between devices, swap(): lax.ppermute(jnp.where(spot % 2 == odd, last, first), axis, pairs)  10.9 us
    ppermute x7, starting transfers between devices, meet(): lax.ppermute(values, axis, partner(axis, k))  10.7 us
    all_to_all x1, waiting for transfers between devices, local(): recv = lax.all_to_all(send, 'mem', 0, 0)  9.5 us
    all_to_all x1, starting transfers between devices, local(): recv = lax.all_to_all(send, 'mem', 0, 0)  6.65 us
    ppermute x1, starting transfers between devices, local(): other_core = lax.ppermute(same_core, 'mem', partner('mem', 1))  4.43 us
    ppermute x3, starting transfers between devices, local(): lax.ppermute(piece, 'mem', partner('mem', k))  3.34 us
  transfers between devices with their start and end apart: 16, of which 10 were waited for; matrix products, arithmetic and copies ran while one was open for 0% of the time, Pallas kernels for 7%

profile of v13, /device:TPU:1, one launch (start us, length us, event | category | flops | bytes accessed | tf_op | source)
XLA Modules:
  0.0 95.8 jit_solution(5480284222546665263)
XLA Ops:
  0.6 0.0 copy-start
  0.6 0.0 copy-start.5
  0.7 0.0 copy-start.4
  0.7 0.0 copy-start.3
  0.7 0.0 copy-start.2
  0.7 3.1 %pack.1 = bf16[8,128,256]{2,1,0:T(8,128)(2,1)} custom-call(bf16[4,4,32,256]{3,2,1,0:T(8,128)(2,1)} %fields.1, bf16[4,4,32,256]{3,2,1,0:T(8,128)(2,1)} %cot.1), custom_call_target="tpu_custom_call" | custom-call | tf_op jit(solution)/shard_map/pack/pallas_call | solution.py:359
  3.8 0.0 copy-start.6
  3.9 6.6 %all-to-all-start = ((bf16[8,128,256]{2,1,0:T(8,128)(2,1)}), bf16[8,128,256]{2,1,0:T(8,128)(2,1)S(1)}, u32[]{:S(2)}, u32[]{:S(2)}) async-start(bf16[8,128,256]{2,1,0:T(8,128)(2,1)} %pack.1), calls=%async_computation | async-start | bytes 1048576 | tf_op jit(solution)/shard_map/to_cells/all_to_all | solution.py:367
  10.5 9.5 %all-to-all-done.recv = bf16[8,128,256]{2,1,0:T(8,128)(2,1)S(1)} async-done(((bf16[8,128,256]{2,1,0:T(8,128)(2,1)}), bf16[8,128,256]{2,1,0:T(8,128)(2,1)S(1)}, u32[]{:S(2)}, u32[]{:S(2)}) %all-to-all-start) | async-done | bytes 524320 | tf_op jit(solution)/shard_map/to_cells/all_to_all | solution.py:367
  20.0 0.3 order.1
  20.3 0.7 collective-permute-start.1
  21.0 3.8 %collective-permute-start = (bf16[4,32,256]{2,1,0:T(8,128)(2,1)S(1)}, bf16[4,32,256]{2,1,0:T(8,128)(2,1)S(1)}, u32[]{:S(2)}, u32[]{:S(2)}) collective-permute-start(bf16[4,32,256]{2,1,0:T(8,128)(2,1)S(1)} %get-tuple-element.74), channel_id=1, source_target_pairs={{0,8},{8,0},{16,24},{24,16},{1,9},{9,1},{17,25},{25,17},{2,10},{10... | collective-permute-start | bytes 196616 | tf_op jit(solution)/shard_map/halo_rows/ppermute | solution.py:332
  24.8 3.0 %forward.1 = (bf16[512,256]{1,0:T(8,128)(2,1)S(1)}, f32[512,256]{1,0:T(8,128)S(1)}, bf16[512,256]{1,0:T(8,128)(2,1)S(1)}, bf16[512,256]{1,0:T(8,128)(2,1)S(1)}, ...) custom-call(bf16[512,256]{1,0:T(8,128)(2,1)S(1)} %get-tuple-element.41.x_in.refs_0_.refs_5_, ...), custom_call_target="tpu_custom_call" | custom-call | tf_op jit(solution)/shard_map/forward/pallas_call | solution.py:382
  27.8 0.0 collective-permute-done.1
  27.8 0.0 collective-permute-done
  27.9 6.5 %collective-permute-start.3 = (bf16[6,32,256]{2,1,0:T(8,128)(2,1)S(1)}, bf16[6,32,256]{2,1,0:T(8,128)(2,1)S(1)}, u32[]{:S(2)}, u32[]{:S(2)}) collective-permute-start(bf16[6,32,256]{2,1,0:T(8,128)(2,1)S(1)} %get-tuple-element.77), channel_id=1, source_target_pairs={{64,128},{128,64},{192,224},{224,192},{160,96},{96,160},{32,1},{1,... | collective-permute-start | bytes 294920 | tf_op jit(solution)/shard_map/halo_cols/ppermute | solution.py:332
  34.4 0.0 collective-permute-start.2
  34.4 0.1 pad_add_fusion.place
  34.5 2.5 %backward_inner.1 = (bf16[256,256]{1,0:T(8,128)(2,1)S(1)}, f32[4,256,256]{2,1,0:T(8,128)S(1)}, f32[16,256]{1,0:T(8,128)S(1)}) custom-call(s32[2]{0:T(128)S(1)} %pad_add_fusion.place, bf16[4,4,32,256]{3,2,1,0:T(8,128)(2,1)S(1)} %get-tuple-element.39.cot, bf16[4,32,256]{2,1,0:T(8,128)(2,1)S(1)} %get-tuple-element.52.above, ...), custom_call_target="tpu_custom_call" | custom-call | tf_op jit(solution)/shard_map/backward_inner/pallas_call | solution.py:408
  37.0 0.0 collective-permute-done.3
  37.0 1.2 %collective-permute-done.2 = bf16[6,32,256]{2,1,0:T(8,128)(2,1)S(1)} collective-permute-done((bf16[6,32,256]{2,1,0:T(8,128)(2,1)S(1)}, bf16[6,32,256]{2,1,0:T(8,128)(2,1)S(1)}, u32[]{:S(2)}, u32[]{:S(2)}) %collective-permute-start.2) | collective-permute-done | bytes 98336 | tf_op jit(solution)/shard_map/halo_cols/ppermute | solution.py:332
  38.2 2.8 %backward_outer.1 = bf16[8,208,256]{2,1,0:T(8,128)(2,1)S(1)} custom-call(s32[2]{0:T(128)S(1)} %pad_add_fusion.place, bf16[4,4,32,256]{3,2,1,0:T(8,128)(2,1)S(1)} %get-tuple-element.39.cot, bf16[4,32,256]{2,1,0:T(8,128)(2,1)S(1)} %get-tuple-element.52.above, bf16[4,32,256]{2,1,0:T(8,128)(2,1)S(1)} %get-tuple-element.53.below, ...), custom_call_target="tpu_custom_call" | custom-call | tf_op jit(solution)/shard_map/backward_outer/pallas_call | solution.py:420
  41.0 18.0 %all_to_all.10.recv = bf16[8,208,256]{2,1,0:T(8,128)(2,1)S(1)} all-to-all(bf16[8,208,256]{2,1,0:T(8,128)(2,1)S(1)} %backward_outer.1), channel_id=1, replica_groups=mesh['mem'=8,'row'=4,'col'=8] {'mem'}, dimensions={0} | all-to-all | bytes 1703936 | tf_op jit(solution)/shard_map/to_members/all_to_all | solution.py:428
  58.9 0.1 slice_reduce_fusion
  59.0 1.7 %collective-permute-start.6 = (bf16[144,256]{1,0:T(8,128)(2,1)S(1)}, bf16[144,256]{1,0:T(8,128)(2,1)S(1)}, u32[]{:S(2)}, u32[]{:S(2)}) collective-permute-start(bf16[144,256]{1,0:T(8,128)(2,1)S(1)} %slice_reduce_fusion), channel_id=1, source_target_pairs={{0,24},{8,16},{16,8},{24,0},{1,25},{9,17},{17,9},{25,1},{2,26},{10... | collective-permute-start | bytes 221192 | tf_op jit(solution)/shard_map/reduce/ppermute | solution.py:313
  60.7 2.4 %collective-permute-start.5 = (bf16[144,256]{1,0:T(8,128)(2,1)S(1)}, bf16[144,256]{1,0:T(8,128)(2,1)S(1)}, u32[]{:S(2)}, u32[]{:S(2)}) collective-permute-start(bf16[144,256]{1,0:T(8,128)(2,1)S(1)} %slice_reduce_fusion), channel_id=1, source_target_pairs={{0,16},{8,24},{16,0},{24,8},{1,17},{9,25},{17,1},{25,9},{2,18},{10... | collective-permute-start | bytes 221192 | tf_op jit(solution)/shard_map/reduce/ppermute | solution.py:313
  63.2 0.0 collective-permute-start.4
  63.2 0.9 collective-permute-done.6
  64.1 5.3 %collective-permute-done.5 = bf16[144,256]{1,0:T(8,128)(2,1)S(1)} collective-permute-done((bf16[144,256]{1,0:T(8,128)(2,1)S(1)}, bf16[144,256]{1,0:T(8,128)(2,1)S(1)}, u32[]{:S(2)}, u32[]{:S(2)}) %collective-permute-start.5) | collective-permute-done | bytes 73760 | tf_op jit(solution)/shard_map/reduce/ppermute | solution.py:313
  69.4 0.0 collective-permute-done.4
  69.5 1.0 %collective-permute-start.9 = (bf16[144,256]{1,0:T(8,128)(2,1)S(1)}, bf16[144,256]{1,0:T(8,128)(2,1)S(1)}, u32[]{:S(2)}, u32[]{:S(2)}) collective-permute-start(bf16[144,256]{1,0:T(8,128)(2,1)S(1)} %add_convert_fusion.2), channel_id=1, source_target_pairs={{0,4},{1,5},{2,6},{3,7},{4,0},{5,1},{6,2},{7,3},{8,12},{9,13},{10,... | collective-permute-start | bytes 221192 | tf_op jit(solution)/shard_map/reduce/ppermute | solution.py:313
  70.5 0.9 collective-permute-start.8
  71.4 0.8 collective-permute-start.7
  72.2 2.1 %collective-permute-done.9 = bf16[144,256]{1,0:T(8,128)(2,1)S(1)} collective-permute-done((bf16[144,256]{1,0:T(8,128)(2,1)S(1)}, bf16[144,256]{1,0:T(8,128)(2,1)S(1)}, u32[]{:S(2)}, u32[]{:S(2)}) %collective-permute-start.9) | collective-permute-done | bytes 73760 | tf_op jit(solution)/shard_map/reduce/ppermute | solution.py:313
  74.3 1.6 %collective-permute-done.8 = bf16[144,256]{1,0:T(8,128)(2,1)S(1)} collective-permute-done((bf16[144,256]{1,0:T(8,128)(2,1)S(1)}, bf16[144,256]{1,0:T(8,128)(2,1)S(1)}, u32[]{:S(2)}, u32[]{:S(2)}) %collective-permute-start.8) | collective-permute-done | bytes 73760 | tf_op jit(solution)/shard_map/reduce/ppermute | solution.py:313
  75.8 0.0 collective-permute-done.7
  75.9 3.8 %collective-permute-start.10 = (bf16[144,256]{1,0:T(8,128)(2,1)S(1)}, bf16[144,256]{1,0:T(8,128)(2,1)S(1)}, u32[]{:S(2)}, u32[]{:S(2)}) collective-permute-start(bf16[144,256]{1,0:T(8,128)(2,1)S(1)} %add_convert_fusion.1), channel_id=1, source_target_pairs={{0,1},{1,0},{2,3},{3,2},{4,5},{5,4},{6,7},{7,6},{8,9},{9,8},{10,11... | collective-permute-start | bytes 221192 | tf_op jit(solution)/shard_map/reduce/ppermute | solution.py:313
  79.6 1.0 %unpack.1 = bf16[4,4,32,256]{3,2,1,0:T(8,128)(2,1)} custom-call(bf16[8,208,256]{2,1,0:T(8,128)(2,1)S(1)} %all_to_all.10.recv), custom_call_target="tpu_custom_call" | custom-call | tf_op jit(solution)/shard_map/unpack/pallas_call | solution.py:432
  80.6 2.5 %collective-permute-done.10 = bf16[144,256]{1,0:T(8,128)(2,1)S(1)} collective-permute-done((bf16[144,256]{1,0:T(8,128)(2,1)S(1)}, bf16[144,256]{1,0:T(8,128)(2,1)S(1)}, u32[]{:S(2)}, u32[]{:S(2)}) %collective-permute-start.10) | collective-permute-done | bytes 73760 | tf_op jit(solution)/shard_map/reduce/ppermute | solution.py:313
  83.2 0.7 collective-permute-start.12
  83.9 0.8 collective-permute-start.11
  84.8 1.8 %collective-permute-start.13 = (bf16[128,256]{1,0:T(8,128)(2,1)S(1)}, bf16[128,256]{1,0:T(8,128)(2,1)S(1)}, u32[]{:S(2)}, u32[]{:S(2)}) collective-permute-start(bf16[128,256]{1,0:T(8,128)(2,1)S(1)} %get-tuple-element.82), channel_id=1, source_target_pairs={{0,192},{32,224},{64,128},{96,160},{128,64},{160,96},{192,0},{224,... | collective-permute-start | bytes 196616 | tf_op jit(solution)/shard_map/reduce/ppermute | solution.py:444
  86.6 1.4 %collective-permute-done.12 = bf16[128,256]{1,0:T(8,128)(2,1)S(1)} collective-permute-done((bf16[128,256]{1,0:T(8,128)(2,1)S(1)}, bf16[128,256]{1,0:T(8,128)(2,1)S(1)}, u32[]{:S(2)}, u32[]{:S(2)}) %collective-permute-start.12) | collective-permute-done | bytes 65568 | tf_op jit(solution)/shard_map/reduce/ppermute | solution.py:444
  87.9 0.0 collective-permute-done.11
  87.9 1.2 %collective-permute-done.13 = bf16[128,256]{1,0:T(8,128)(2,1)S(1)} collective-permute-done((bf16[128,256]{1,0:T(8,128)(2,1)S(1)}, bf16[128,256]{1,0:T(8,128)(2,1)S(1)}, u32[]{:S(2)}, u32[]{:S(2)}) %collective-permute-start.13) | collective-permute-done | bytes 65568 | tf_op jit(solution)/shard_map/reduce/ppermute | solution.py:444
  89.1 4.4 %collective-permute-start.14 = (bf16[4,128,256]{2,1,0:T(8,128)(2,1)S(1)}, bf16[4,128,256]{2,1,0:T(8,128)(2,1)S(1)}, u32[]{:S(2)}, u32[]{:S(2)}) collective-permute-start(bf16[4,128,256]{2,1,0:T(8,128)(2,1)S(1)} %pad_maximum_fusion.same_core), channel_id=1, source_target_pairs={{0,32},{32,0},{64,96},{96,64},{128,160},{160,128},{192,224},{224,1... | collective-permute-start | bytes 786440 | tf_op jit(solution)/shard_map/reduce/ppermute | solution.py:446
  93.6 1.2 %collective-permute-done.14.other_core = bf16[4,128,256]{2,1,0:T(8,128)(2,1)S(1)} collective-permute-done((bf16[4,128,256]{2,1,0:T(8,128)(2,1)S(1)}, bf16[4,128,256]{2,1,0:T(8,128)(2,1)S(1)}, u32[]{:S(2)}, u32[]{:S(2)}) %collective-permute-start.14) | collective-permute-done | bytes 262176 | tf_op jit(solution)/shard_map/reduce/ppermute | solution.py:446
  94.7 1.0 %finish.1 = (f32[256,256]{1,0:T(8,128)}, f32[256,256]{1,0:T(8,128)}, f32[256,256]{1,0:T(8,128)}, f32[256,256]{1,0:T(8,128)}, f32[3,3,256]{2,1,0:T(4,128)}, /*index=5*/f32[1,256]{1,0:T(1,128)}) custom-call(s32[1]{0:T(128)} %bitcast.7.place, bf16[4,128,256]{2,1,0:T(8,128)(2,1)S(1)} %pad_maximum_fusion.same_core, ...), custom_call_target="tpu_custom_call" | custom-call | tf_op jit(solution)/shard_map/finish/pallas_call | solution.py:452
  (21 shorter events, 0.3 us)
Async XLA Ops:
  0.6 19.4 %copy-start = (bf16[256,256]{1,0:T(8,128)(2,1)S(1)}, bf16[256,256]{1,0:T(8,128)(2,1)}, u32[]{:S(2)}) copy-start(bf16[256,256]{1,0:T(8,128)(2,1)} %constant.67.clone.gather8.refs_13_.refs_18_) | copy-start | bytes 393220
  0.6 24.1 %copy-start.5 = (bf16[256,256]{1,0:T(8,128)(2,1)S(1)}, bf16[256,256]{1,0:T(8,128)(2,1)}, u32[]{:S(2)}) copy-start(bf16[256,256]{1,0:T(8,128)(2,1)} %constant.68.clone.headsum.refs_14_.refs_19_) | copy-start | bytes 393220
  0.7 24.1 %copy-start.4 = (bf16[256,256]{1,0:T(8,128)(2,1)S(1)}, bf16[256,256]{1,0:T(8,128)(2,1)}, u32[]{:S(2)}) copy-start(bf16[256,256]{1,0:T(8,128)(2,1)} %refs_17_) | copy-start | bytes 393220
  0.7 24.1 %copy-start.3 = (bf16[256,256]{1,0:T(8,128)(2,1)S(1)}, bf16[256,256]{1,0:T(8,128)(2,1)}, u32[]{:S(2)}) copy-start(bf16[256,256]{1,0:T(8,128)(2,1)} %refs_16_) | copy-start | bytes 393220
  0.7 24.1 %copy-start.2 = (bf16[256,256]{1,0:T(8,128)(2,1)S(1)}, bf16[256,256]{1,0:T(8,128)(2,1)}, u32[]{:S(2)}) copy-start(bf16[256,256]{1,0:T(8,128)(2,1)} %refs_15_) | copy-start | bytes 393220
  0.7 24.1 %copy-start.1 = (bf16[256,256]{1,0:T(8,128)(2,1)S(1)}, bf16[256,256]{1,0:T(8,128)(2,1)}, u32[]{:S(2)}) copy-start(bf16[256,256]{1,0:T(8,128)(2,1)} %refs_14_.1) | copy-start | bytes 393220
  0.7 24.1 %copy-start.7 = (f32[256]{0:T(256)S(1)}, f32[256]{0:T(256)}, u32[]{:S(2)}) copy-start(f32[256]{0:T(256)} %param.11) | copy-start | bytes 3076
  3.8 30.6 %copy-start.6 = (f32[3,3,256]{2,1,0:T(4,128)S(1)}, f32[3,3,256]{2,1,0:T(4,128)}, u32[]{:S(2)}) copy-start(f32[3,3,256]{2,1,0:T(4,128)} %refs_13_.2) | copy-start | bytes 27652
  3.9 16.1 %all-to-all-start = ((bf16[8,128,256]{2,1,0:T(8,128)(2,1)}), bf16[8,128,256]{2,1,0:T(8,128)(2,1)S(1)}, u32[]{:S(2)}, u32[]{:S(2)}) async-start(bf16[8,128,256]{2,1,0:T(8,128)(2,1)} %pack.1), calls=%async_computation | async-start | bytes 1048576 | tf_op jit(solution)/shard_map/to_cells/all_to_all | solution.py:367
  20.3 7.5 %collective-permute-start.1 = (bf16[4,32,256]{2,1,0:T(8,128)(2,1)S(1)}, bf16[4,32,256]{2,1,0:T(8,128)(2,1)S(1)}, u32[]{:S(2)}, u32[]{:S(2)}) collective-permute-start(bf16[4,32,256]{2,1,0:T(8,128)(2,1)S(1)} %get-tuple-element.73), channel_id=1, source_target_pairs={{8,16},{16,8},{9,17},{17,9},{10,18},{18,10},{11,19},{19,11},{12,20... | collective-permute-start | bytes 196616 | tf_op jit(solution)/shard_map/halo_rows/ppermute | solution.py:332
  21.0 6.8 %collective-permute-start = (bf16[4,32,256]{2,1,0:T(8,128)(2,1)S(1)}, bf16[4,32,256]{2,1,0:T(8,128)(2,1)S(1)}, u32[]{:S(2)}, u32[]{:S(2)}) collective-permute-start(bf16[4,32,256]{2,1,0:T(8,128)(2,1)S(1)} %get-tuple-element.74), channel_id=1, source_target_pairs={{0,8},{8,0},{16,24},{24,16},{1,9},{9,1},{17,25},{25,17},{2,10},{10... | collective-permute-start | bytes 196616 | tf_op jit(solution)/shard_map/halo_rows/ppermute | solution.py:332
  27.9 9.1 %collective-permute-start.3 = (bf16[6,32,256]{2,1,0:T(8,128)(2,1)S(1)}, bf16[6,32,256]{2,1,0:T(8,128)(2,1)S(1)}, u32[]{:S(2)}, u32[]{:S(2)}) collective-permute-start(bf16[6,32,256]{2,1,0:T(8,128)(2,1)S(1)} %get-tuple-element.77), channel_id=1, source_target_pairs={{64,128},{128,64},{192,224},{224,192},{160,96},{96,160},{32,1},{1,... | collective-permute-start | bytes 294920 | tf_op jit(solution)/shard_map/halo_cols/ppermute | solution.py:332
  34.4 3.8 %collective-permute-start.2 = (bf16[6,32,256]{2,1,0:T(8,128)(2,1)S(1)}, bf16[6,32,256]{2,1,0:T(8,128)(2,1)S(1)}, u32[]{:S(2)}, u32[]{:S(2)}) collective-permute-start(bf16[6,32,256]{2,1,0:T(8,128)(2,1)S(1)} %get-tuple-element.78), channel_id=1, source_target_pairs={{0,64},{64,0},{128,192},{192,128},{224,160},{160,224},{96,32},{32,... | collective-permute-start | bytes 294920 | tf_op jit(solution)/shard_map/halo_cols/ppermute | solution.py:332
  59.0 5.1 %collective-permute-start.6 = (bf16[144,256]{1,0:T(8,128)(2,1)S(1)}, bf16[144,256]{1,0:T(8,128)(2,1)S(1)}, u32[]{:S(2)}, u32[]{:S(2)}) collective-permute-start(bf16[144,256]{1,0:T(8,128)(2,1)S(1)} %slice_reduce_fusion), channel_id=1, source_target_pairs={{0,24},{8,16},{16,8},{24,0},{1,25},{9,17},{17,9},{25,1},{2,26},{10... | collective-permute-start | bytes 221192 | tf_op jit(solution)/shard_map/reduce/ppermute | solution.py:313
  60.7 8.7 %collective-permute-start.5 = (bf16[144,256]{1,0:T(8,128)(2,1)S(1)}, bf16[144,256]{1,0:T(8,128)(2,1)S(1)}, u32[]{:S(2)}, u32[]{:S(2)}) collective-permute-start(bf16[144,256]{1,0:T(8,128)(2,1)S(1)} %slice_reduce_fusion), channel_id=1, source_target_pairs={{0,16},{8,24},{16,0},{24,8},{1,17},{9,25},{17,1},{25,9},{2,18},{10... | collective-permute-start | bytes 221192 | tf_op jit(solution)/shard_map/reduce/ppermute | solution.py:313
  63.2 6.2 %collective-permute-start.4 = (bf16[144,256]{1,0:T(8,128)(2,1)S(1)}, bf16[144,256]{1,0:T(8,128)(2,1)S(1)}, u32[]{:S(2)}, u32[]{:S(2)}) collective-permute-start(bf16[144,256]{1,0:T(8,128)(2,1)S(1)} %slice_reduce_fusion), channel_id=1, source_target_pairs={{0,8},{8,0},{16,24},{24,16},{1,9},{9,1},{17,25},{25,17},{2,10},{10... | collective-permute-start | bytes 221192 | tf_op jit(solution)/shard_map/reduce/ppermute | solution.py:313
  69.5 4.8 %collective-permute-start.9 = (bf16[144,256]{1,0:T(8,128)(2,1)S(1)}, bf16[144,256]{1,0:T(8,128)(2,1)S(1)}, u32[]{:S(2)}, u32[]{:S(2)}) collective-permute-start(bf16[144,256]{1,0:T(8,128)(2,1)S(1)} %add_convert_fusion.2), channel_id=1, source_target_pairs={{0,4},{1,5},{2,6},{3,7},{4,0},{5,1},{6,2},{7,3},{8,12},{9,13},{10,... | collective-permute-start | bytes 221192 | tf_op jit(solution)/shard_map/reduce/ppermute | solution.py:313
  70.5 5.3 %collective-permute-start.8 = (bf16[144,256]{1,0:T(8,128)(2,1)S(1)}, bf16[144,256]{1,0:T(8,128)(2,1)S(1)}, u32[]{:S(2)}, u32[]{:S(2)}) collective-permute-start(bf16[144,256]{1,0:T(8,128)(2,1)S(1)} %add_convert_fusion.2), channel_id=1, source_target_pairs={{0,6},{1,7},{2,4},{3,5},{4,2},{5,3},{6,0},{7,1},{8,14},{9,15},{10,... | collective-permute-start | bytes 221192 | tf_op jit(solution)/shard_map/reduce/ppermute | solution.py:313
  71.4 4.5 %collective-permute-start.7 = (bf16[144,256]{1,0:T(8,128)(2,1)S(1)}, bf16[144,256]{1,0:T(8,128)(2,1)S(1)}, u32[]{:S(2)}, u32[]{:S(2)}) collective-permute-start(bf16[144,256]{1,0:T(8,128)(2,1)S(1)} %add_convert_fusion.2), channel_id=1, source_target_pairs={{0,2},{1,3},{2,0},{3,1},{4,6},{5,7},{6,4},{7,5},{8,10},{9,11},{10,... | collective-permute-start | bytes 221192 | tf_op jit(solution)/shard_map/reduce/ppermute | solution.py:313
  75.9 7.3 %collective-permute-start.10 = (bf16[144,256]{1,0:T(8,128)(2,1)S(1)}, bf16[144,256]{1,0:T(8,128)(2,1)S(1)}, u32[]{:S(2)}, u32[]{:S(2)}) collective-permute-start(bf16[144,256]{1,0:T(8,128)(2,1)S(1)} %add_convert_fusion.1), channel_id=1, source_target_pairs={{0,1},{1,0},{2,3},{3,2},{4,5},{5,4},{6,7},{7,6},{8,9},{9,8},{10,11... | collective-permute-start | bytes 221192 | tf_op jit(solution)/shard_map/reduce/ppermute | solution.py:313
  83.2 4.7 %collective-permute-start.12 = (bf16[128,256]{1,0:T(8,128)(2,1)S(1)}, bf16[128,256]{1,0:T(8,128)(2,1)S(1)}, u32[]{:S(2)}, u32[]{:S(2)}) collective-permute-start(bf16[128,256]{1,0:T(8,128)(2,1)S(1)} %get-tuple-element.82), channel_id=1, source_target_pairs={{0,128},{32,160},{64,192},{96,224},{128,0},{160,32},{192,64},{224,... | collective-permute-start | bytes 196616 | tf_op jit(solution)/shard_map/reduce/ppermute | solution.py:444
  83.9 4.0 %collective-permute-start.11 = (bf16[128,256]{1,0:T(8,128)(2,1)S(1)}, bf16[128,256]{1,0:T(8,128)(2,1)S(1)}, u32[]{:S(2)}, u32[]{:S(2)}) collective-permute-start(bf16[128,256]{1,0:T(8,128)(2,1)S(1)} %get-tuple-element.82), channel_id=1, source_target_pairs={{0,64},{32,96},{64,0},{96,32},{128,192},{160,224},{192,128},{224,1... | collective-permute-start | bytes 196616 | tf_op jit(solution)/shard_map/reduce/ppermute | solution.py:444
  84.8 4.3 %collective-permute-start.13 = (bf16[128,256]{1,0:T(8,128)(2,1)S(1)}, bf16[128,256]{1,0:T(8,128)(2,1)S(1)}, u32[]{:S(2)}, u32[]{:S(2)}) collective-permute-start(bf16[128,256]{1,0:T(8,128)(2,1)S(1)} %get-tuple-element.82), channel_id=1, source_target_pairs={{0,192},{32,224},{64,128},{96,160},{128,64},{160,96},{192,0},{224,... | collective-permute-start | bytes 196616 | tf_op jit(solution)/shard_map/reduce/ppermute | solution.py:444
  89.1 5.6 %collective-permute-start.14 = (bf16[4,128,256]{2,1,0:T(8,128)(2,1)S(1)}, bf16[4,128,256]{2,1,0:T(8,128)(2,1)S(1)}, u32[]{:S(2)}, u32[]{:S(2)}) collective-permute-start(bf16[4,128,256]{2,1,0:T(8,128)(2,1)S(1)} %pad_maximum_fusion.same_core), channel_id=1, source_target_pairs={{0,32},{32,0},{64,96},{96,64},{128,160},{160,128},{192,224},{224,1... | collective-permute-start | bytes 786440 | tf_op jit(solution)/shard_map/reduce/ppermute | solution.py:446

commit v14 on v9

--- a/solution.py
+++ b/solution.py
@@ -382,6 +382,7 @@
             scratch_shapes=[pltpu.VMEM((tokens, width), F32)],
             compiler_params=params,
         )(near(x), gain, w_query, w_key, w_value, w_out, headsum)
+    left, right, *kept = lax.optimization_barrier((left, right, *kept))
     with jax.named_scope("halo_rows"):
         top, bottom = [jnp.concatenate([left[r : r + 1], cot[r], right[r : r + 1]], axis=0) for r in (0, rows - 1)]
         rows_at = {r: r for r in range(grid[0])}
@@ -421,7 +422,7 @@
 
     with jax.named_scope("reduce"):
         total = meet(total, "row", (1, 2, 3))
-        total = meet(total, "col", (2, 4, 6))
+        total = meet(total, "col", (2, 6, 4))
         total = meet(total, "col", (1,))
         total, grad_fields = lax.optimization_barrier((total, grad_fields))
         piece = total[:shard]

time: 96.8 us -> 97.1 us (level)
  starting transfers between devices: 43.7 us -> 41.4 us
  blocking collectives: 16.8 us -> 18.6 us
    all_to_all x1, blocking collectives: 16.8 us -> 18.6 us  [local(): landed = lax.all_to_all(back, 'mem', 0, 0)]
    ppermute x7, starting transfers between devices: 18.2 us -> 16.9 us  [meet(): lax.ppermute(values, axis, partner(axis, k))]
  transfers between devices with their start and end apart: 16 -> 16, of which waited for: 11 -> 10; matrix products, arithmetic and copies ran while one was open for 0% -> 0% of each run, Pallas kernels for 4% -> 4%
where the time goes in v14:
time: 97.1 us; the launch traced here: 96.8 us
  starting transfers between devices  41.4 us (43%)
  waiting for transfers between devices  22.6 us (23%)
  blocking collectives  18.6 us (19%)
  Pallas kernels  10.9 us (11%)
  local copies, waits for them, and re-layouts  2.04 us (2%)
    all_to_all x1, blocking collectives, local(): landed = lax.all_to_all(back, 'mem', 0, 0)  18.6 us
    ppermute x7, starting transfers between devices, meet(): lax.ppermute(values, axis, partner(axis, k))  16.9 us
    all_to_all x1, waiting for transfers between devices, local(): recv = lax.all_to_all(send, 'mem', 0, 0)  9.5 us
    ppermute x4, starting transfers between devices, swap(): lax.ppermute(jnp.where(spot % 2 == odd, last, first), axis, pairs)  8.94 us
    ppermute x7, waiting for transfers between devices, meet(): lax.ppermute(values, axis, partner(axis, k))  7.44 us
    all_to_all x1, starting transfers between devices, local(): recv = lax.all_to_all(send, 'mem', 0, 0)  6.77 us
    ppermute x1, starting transfers between devices, local(): other_core = lax.ppermute(same_core, 'mem', partner('mem', 1))  5.45 us
    pallas_call x1, Pallas kernels, local(): pl.pallas_call(functools.partial(backward_kernel, (grid[0], blocks)), in_...  4.51 us
  transfers between devices with their start and end apart: 16, of which 10 were waited for; matrix products, arithmetic and copies ran while one was open for 0% of the time, Pallas kernels for 4%

profile of v14, /device:TPU:1, one launch (start us, length us, event | category | flops | bytes accessed | tf_op | source)
XLA Modules:
  0.0 96.8 jit_solution(13684676203186486636)
XLA Ops:
  0.6 0.0 copy-start
  0.6 0.0 copy-start.5
  0.7 0.0 copy-start.4
  0.7 0.0 copy-start.3
  0.7 0.0 copy-start.2
  0.7 1.0 %copy-done.6 = bf16[4,4,32,256]{3,2,1,0:T(8,128)(2,1)S(1)} copy-done((bf16[4,4,32,256]{3,2,1,0:T(8,128)(2,1)S(1)}, bf16[4,4,32,256]{3,2,1,0:T(8,128)(2,1)}, u32[]{:S(2)}) %copy-start.6) | copy-done | bytes 262168
  1.7 0.9 copy-done.7
  2.7 1.1 %pack.1 = bf16[8,128,256]{2,1,0:T(8,128)(2,1)} custom-call(bf16[4,4,32,256]{3,2,1,0:T(8,128)(2,1)S(1)} %copy-done.6, bf16[4,4,32,256]{3,2,1,0:T(8,128)(2,1)S(1)} %copy-done.7), custom_call_target="tpu_custom_call" | custom-call | tf_op jit(solution)/shard_map/pack/pallas_call | solution.py:354
  3.8 6.8 %all-to-all-start = ((bf16[8,128,256]{2,1,0:T(8,128)(2,1)}), bf16[8,128,256]{2,1,0:T(8,128)(2,1)S(1)}, u32[]{:S(2)}, u32[]{:S(2)}) async-start(bf16[8,128,256]{2,1,0:T(8,128)(2,1)} %pack.1), calls=%async_computation | async-start | bytes 1048576 | tf_op jit(solution)/shard_map/to_cells/all_to_all | solution.py:360
  10.5 9.5 %all-to-all-done.recv = bf16[8,128,256]{2,1,0:T(8,128)(2,1)S(1)} async-done(((bf16[8,128,256]{2,1,0:T(8,128)(2,1)}), bf16[8,128,256]{2,1,0:T(8,128)(2,1)S(1)}, u32[]{:S(2)}, u32[]{:S(2)}) %all-to-all-start) | async-done | bytes 524320 | tf_op jit(solution)/shard_map/to_cells/all_to_all | solution.py:360
  20.0 0.3 order.1
  20.4 0.4 collective-permute-start.1
  20.8 7.1 %collective-permute-start = (bf16[4,32,256]{2,1,0:T(8,128)(2,1)S(1)}, bf16[4,32,256]{2,1,0:T(8,128)(2,1)S(1)}, u32[]{:S(2)}, u32[]{:S(2)}) collective-permute-start(bf16[4,32,256]{2,1,0:T(8,128)(2,1)S(1)} %get-tuple-element.68), channel_id=1, source_target_pairs={{64,128},{128,64},{192,224},{224,192},{160,96},{96,160},{32,1},{1,... | collective-permute-start | bytes 196616 | tf_op jit(solution)/shard_map/halo_cols/ppermute | solution.py:329
  27.9 3.0 %forward.1 = (bf16[512,256]{1,0:T(8,128)(2,1)S(1)}, f32[512,256]{1,0:T(8,128)S(1)}, bf16[512,256]{1,0:T(8,128)(2,1)S(1)}, bf16[512,256]{1,0:T(8,128)(2,1)S(1)}, ...) custom-call(bf16[512,256]{1,0:T(8,128)(2,1)S(1)} %get-tuple-element.38.x_in, f32[1,256]{1,0:T(1,128)S(1)} %bitcast.18, ...), custom_call_target="tpu_custom_call" | custom-call | tf_op jit(solution)/shard_map/forward/pallas_call | solution.py:379
  30.9 0.0 collective-permute-done.1
  30.9 0.0 collective-permute-done
  31.0 0.8 collective-permute-start.3
  31.8 0.7 collective-permute-start.2
  32.5 0.1 pad_add_fusion.place
  32.6 2.0 %collective-permute-done.3 = bf16[6,32,256]{2,1,0:T(8,128)(2,1)S(1)} collective-permute-done((bf16[6,32,256]{2,1,0:T(8,128)(2,1)S(1)}, bf16[6,32,256]{2,1,0:T(8,128)(2,1)S(1)}, u32[]{:S(2)}, u32[]{:S(2)}) %collective-permute-start.3) | collective-permute-done | bytes 98336 | tf_op jit(solution)/shard_map/halo_rows/ppermute | solution.py:329
  34.5 0.0 collective-permute-done.2
  34.6 4.5 %backward.1 = bf16[8,208,256]{2,1,0:T(8,128)(2,1)S(1)} custom-call(s32[2]{0:T(128)S(1)} %pad_add_fusion.place, bf16[4,4,32,256]{3,2,1,0:T(8,128)(2,1)S(1)} %get-tuple-element.36.cot, bf16[4,32,256]{2,1,0:T(8,128)(2,1)S(1)} %get-tuple-element.49.left, bf16[4,32,256]{2,1,0:T(8,128)(2,1)S(1)} %get-tuple-element.50.right, ...), custom_call_target="tpu_custom_call" | custom-call | tf_op jit(solution)/shard_map/backward/pallas_call | solution.py:391
  39.1 18.6 %all_to_all.10.recv = bf16[8,208,256]{2,1,0:T(8,128)(2,1)S(1)} all-to-all(bf16[8,208,256]{2,1,0:T(8,128)(2,1)S(1)} %backward.1), channel_id=1, replica_groups=mesh['mem'=8,'row'=4,'col'=8] {'mem'}, dimensions={0} | all-to-all | bytes 1703936 | tf_op jit(solution)/shard_map/to_members/all_to_all | solution.py:413
  57.7 0.1 slice_reduce_fusion
  57.7 3.0 %collective-permute-start.6 = (bf16[144,256]{1,0:T(8,128)(2,1)S(1)}, bf16[144,256]{1,0:T(8,128)(2,1)S(1)}, u32[]{:S(2)}, u32[]{:S(2)}) collective-permute-start(bf16[144,256]{1,0:T(8,128)(2,1)S(1)} %slice_reduce_fusion), channel_id=1, source_target_pairs={{0,24},{8,16},{16,8},{24,0},{1,25},{9,17},{17,9},{25,1},{2,26},{10... | collective-permute-start | bytes 221192 | tf_op jit(solution)/shard_map/reduce/ppermute | solution.py:310
  60.8 2.5 %collective-permute-start.5 = (bf16[144,256]{1,0:T(8,128)(2,1)S(1)}, bf16[144,256]{1,0:T(8,128)(2,1)S(1)}, u32[]{:S(2)}, u32[]{:S(2)}) collective-permute-start(bf16[144,256]{1,0:T(8,128)(2,1)S(1)} %slice_reduce_fusion), channel_id=1, source_target_pairs={{0,16},{8,24},{16,0},{24,8},{1,17},{9,25},{17,1},{25,9},{2,18},{10... | collective-permute-start | bytes 221192 | tf_op jit(solution)/shard_map/reduce/ppermute | solution.py:310
  63.3 0.2 collective-permute-start.4
  63.5 0.0 collective-permute-done.6
  63.5 2.9 %collective-permute-done.5 = bf16[144,256]{1,0:T(8,128)(2,1)S(1)} collective-permute-done((bf16[144,256]{1,0:T(8,128)(2,1)S(1)}, bf16[144,256]{1,0:T(8,128)(2,1)S(1)}, u32[]{:S(2)}, u32[]{:S(2)}) %collective-permute-start.5) | collective-permute-done | bytes 73760 | tf_op jit(solution)/shard_map/reduce/ppermute | solution.py:310
  66.4 0.8 collective-permute-done.4
  67.3 1.2 %collective-permute-start.9 = (bf16[144,256]{1,0:T(8,128)(2,1)S(1)}, bf16[144,256]{1,0:T(8,128)(2,1)S(1)}, u32[]{:S(2)}, u32[]{:S(2)}) collective-permute-start(bf16[144,256]{1,0:T(8,128)(2,1)S(1)} %add_convert_fusion.2), channel_id=1, source_target_pairs={{0,4},{1,5},{2,6},{3,7},{4,0},{5,1},{6,2},{7,3},{8,12},{9,13},{10,... | collective-permute-start | bytes 221192 | tf_op jit(solution)/shard_map/reduce/ppermute | solution.py:310
  68.5 1.0 %collective-permute-start.8 = (bf16[144,256]{1,0:T(8,128)(2,1)S(1)}, bf16[144,256]{1,0:T(8,128)(2,1)S(1)}, u32[]{:S(2)}, u32[]{:S(2)}) collective-permute-start(bf16[144,256]{1,0:T(8,128)(2,1)S(1)} %add_convert_fusion.2), channel_id=1, source_target_pairs={{0,6},{1,7},{2,4},{3,5},{4,2},{5,3},{6,0},{7,1},{8,14},{9,15},{10,... | collective-permute-start | bytes 221192 | tf_op jit(solution)/shard_map/reduce/ppermute | solution.py:310
  69.5 0.5 collective-permute-start.7
  70.0 2.1 %collective-permute-done.9 = bf16[144,256]{1,0:T(8,128)(2,1)S(1)} collective-permute-done((bf16[144,256]{1,0:T(8,128)(2,1)S(1)}, bf16[144,256]{1,0:T(8,128)(2,1)S(1)}, u32[]{:S(2)}, u32[]{:S(2)}) %collective-permute-start.9) | collective-permute-done | bytes 73760 | tf_op jit(solution)/shard_map/reduce/ppermute | solution.py:310
  72.1 0.8 collective-permute-done.8
  72.9 0.0 collective-permute-done.7
  73.0 8.4 %collective-permute-start.10 = (bf16[144,256]{1,0:T(8,128)(2,1)S(1)}, bf16[144,256]{1,0:T(8,128)(2,1)S(1)}, u32[]{:S(2)}, u32[]{:S(2)}) collective-permute-start(bf16[144,256]{1,0:T(8,128)(2,1)S(1)} %add_convert_fusion.1), channel_id=1, source_target_pairs={{0,1},{1,0},{2,3},{3,2},{4,5},{5,4},{6,7},{7,6},{8,9},{9,8},{10,11... | collective-permute-start | bytes 221192 | tf_op jit(solution)/shard_map/reduce/ppermute | solution.py:310
  81.4 1.0 %unpack.1 = bf16[4,4,32,256]{3,2,1,0:T(8,128)(2,1)} custom-call(bf16[8,208,256]{2,1,0:T(8,128)(2,1)S(1)} %all_to_all.10.recv), custom_call_target="tpu_custom_call" | custom-call | tf_op jit(solution)/shard_map/unpack/pallas_call | solution.py:417
  82.3 0.8 collective-permute-done.10
  83.2 0.8 collective-permute-start.12
  84.0 0.7 collective-permute-start.11
  84.7 1.8 %collective-permute-start.13 = (bf16[128,256]{1,0:T(8,128)(2,1)S(1)}, bf16[128,256]{1,0:T(8,128)(2,1)S(1)}, u32[]{:S(2)}, u32[]{:S(2)}) collective-permute-start(bf16[128,256]{1,0:T(8,128)(2,1)S(1)} %get-tuple-element.76), channel_id=1, source_target_pairs={{0,192},{32,224},{64,128},{96,160},{128,64},{160,96},{192,0},{224,... | collective-permute-start | bytes 196616 | tf_op jit(solution)/shard_map/reduce/ppermute | solution.py:429
  86.5 1.4 %collective-permute-done.12 = bf16[128,256]{1,0:T(8,128)(2,1)S(1)} collective-permute-done((bf16[128,256]{1,0:T(8,128)(2,1)S(1)}, bf16[128,256]{1,0:T(8,128)(2,1)S(1)}, u32[]{:S(2)}, u32[]{:S(2)}) %collective-permute-start.12) | collective-permute-done | bytes 65568 | tf_op jit(solution)/shard_map/reduce/ppermute | solution.py:429
  87.9 0.0 collective-permute-done.11
  87.9 1.2 %collective-permute-done.13 = bf16[128,256]{1,0:T(8,128)(2,1)S(1)} collective-permute-done((bf16[128,256]{1,0:T(8,128)(2,1)S(1)}, bf16[128,256]{1,0:T(8,128)(2,1)S(1)}, u32[]{:S(2)}, u32[]{:S(2)}) %collective-permute-start.13) | collective-permute-done | bytes 65568 | tf_op jit(solution)/shard_map/reduce/ppermute | solution.py:429
  89.1 5.5 %collective-permute-start.14 = (bf16[4,128,256]{2,1,0:T(8,128)(2,1)S(1)}, bf16[4,128,256]{2,1,0:T(8,128)(2,1)S(1)}, u32[]{:S(2)}, u32[]{:S(2)}) collective-permute-start(bf16[4,128,256]{2,1,0:T(8,128)(2,1)S(1)} %pad_maximum_fusion.same_core), channel_id=1, source_target_pairs={{0,32},{32,0},{64,96},{96,64},{128,160},{160,128},{192,224},{224,1... | collective-permute-start | bytes 786440 | tf_op jit(solution)/shard_map/reduce/ppermute | solution.py:431
  94.6 1.2 %collective-permute-done.14.other_core = bf16[4,128,256]{2,1,0:T(8,128)(2,1)S(1)} collective-permute-done((bf16[4,128,256]{2,1,0:T(8,128)(2,1)S(1)}, bf16[4,128,256]{2,1,0:T(8,128)(2,1)S(1)}, u32[]{:S(2)}, u32[]{:S(2)}) %collective-permute-start.14) | collective-permute-done | bytes 262176 | tf_op jit(solution)/shard_map/reduce/ppermute | solution.py:431
  95.7 1.0 %finish.1 = (f32[256,256]{1,0:T(8,128)}, f32[256,256]{1,0:T(8,128)}, f32[256,256]{1,0:T(8,128)}, f32[256,256]{1,0:T(8,128)}, f32[3,3,256]{2,1,0:T(4,128)}, /*index=5*/f32[1,256]{1,0:T(1,128)}) custom-call(s32[1]{0:T(128)} %bitcast.7.place, bf16[4,128,256]{2,1,0:T(8,128)(2,1)S(1)} %pad_maximum_fusion.same_core, ...), custom_call_target="tpu_custom_call" | custom-call | tf_op jit(solution)/shard_map/finish/pallas_call | solution.py:437
  (24 shorter events, 0.3 us)
Async XLA Ops:
  0.6 19.4 %copy-start = (bf16[256,256]{1,0:T(8,128)(2,1)S(1)}, bf16[256,256]{1,0:T(8,128)(2,1)}, u32[]{:S(2)}) copy-start(bf16[256,256]{1,0:T(8,128)(2,1)} %constant.67.clone.gather8) | copy-start | bytes 393220
  0.6 27.2 %copy-start.5 = (bf16[256,256]{1,0:T(8,128)(2,1)S(1)}, bf16[256,256]{1,0:T(8,128)(2,1)}, u32[]{:S(2)}) copy-start(bf16[256,256]{1,0:T(8,128)(2,1)} %constant.68.clone.headsum) | copy-start | bytes 393220
  0.7 27.2 %copy-start.4 = (bf16[256,256]{1,0:T(8,128)(2,1)S(1)}, bf16[256,256]{1,0:T(8,128)(2,1)}, u32[]{:S(2)}) copy-start(bf16[256,256]{1,0:T(8,128)(2,1)} %wo.1) | copy-start | bytes 393220
  0.7 27.2 %copy-start.3 = (bf16[256,256]{1,0:T(8,128)(2,1)S(1)}, bf16[256,256]{1,0:T(8,128)(2,1)}, u32[]{:S(2)}) copy-start(bf16[256,256]{1,0:T(8,128)(2,1)} %wv.1) | copy-start | bytes 393220
  0.7 27.2 %copy-start.2 = (bf16[256,256]{1,0:T(8,128)(2,1)S(1)}, bf16[256,256]{1,0:T(8,128)(2,1)}, u32[]{:S(2)}) copy-start(bf16[256,256]{1,0:T(8,128)(2,1)} %wk.1) | copy-start | bytes 393220
  0.7 27.2 %copy-start.1 = (bf16[256,256]{1,0:T(8,128)(2,1)S(1)}, bf16[256,256]{1,0:T(8,128)(2,1)}, u32[]{:S(2)}) copy-start(bf16[256,256]{1,0:T(8,128)(2,1)} %wq.1) | copy-start | bytes 393220
  0.7 1.0 %copy-start.6 = (bf16[4,4,32,256]{3,2,1,0:T(8,128)(2,1)S(1)}, bf16[4,4,32,256]{3,2,1,0:T(8,128)(2,1)}, u32[]{:S(2)}) copy-start(bf16[4,4,32,256]{3,2,1,0:T(8,128)(2,1)} %fields.1) | copy-start | bytes 786436
  1.7 0.9 copy-start.7
  2.7 25.2 %copy-start.9 = (f32[256]{0:T(256)S(1)}, f32[256]{0:T(256)}, u32[]{:S(2)}) copy-start(f32[256]{0:T(256)} %param.11) | copy-start | bytes 3076
  3.8 30.8 %copy-start.8 = (f32[3,3,256]{2,1,0:T(4,128)S(1)}, f32[3,3,256]{2,1,0:T(4,128)}, u32[]{:S(2)}) copy-start(f32[3,3,256]{2,1,0:T(4,128)} %mix.1) | copy-start | bytes 27652
  3.8 16.3 %all-to-all-start = ((bf16[8,128,256]{2,1,0:T(8,128)(2,1)}), bf16[8,128,256]{2,1,0:T(8,128)(2,1)S(1)}, u32[]{:S(2)}, u32[]{:S(2)}) async-start(bf16[8,128,256]{2,1,0:T(8,128)(2,1)} %pack.1), calls=%async_computation | async-start | bytes 1048576 | tf_op jit(solution)/shard_map/to_cells/all_to_all | solution.py:360
  20.4 10.5 %collective-permute-start.1 = (bf16[4,32,256]{2,1,0:T(8,128)(2,1)S(1)}, bf16[4,32,256]{2,1,0:T(8,128)(2,1)S(1)}, u32[]{:S(2)}, u32[]{:S(2)}) collective-permute-start(bf16[4,32,256]{2,1,0:T(8,128)(2,1)S(1)} %get-tuple-element.67), channel_id=1, source_target_pairs={{0,64},{64,0},{128,192},{192,128},{224,160},{160,224},{96,32},{32,... | collective-permute-start | bytes 196616 | tf_op jit(solution)/shard_map/halo_cols/ppermute | solution.py:329
  20.8 10.1 %collective-permute-start = (bf16[4,32,256]{2,1,0:T(8,128)(2,1)S(1)}, bf16[4,32,256]{2,1,0:T(8,128)(2,1)S(1)}, u32[]{:S(2)}, u32[]{:S(2)}) collective-permute-start(bf16[4,32,256]{2,1,0:T(8,128)(2,1)S(1)} %get-tuple-element.68), channel_id=1, source_target_pairs={{64,128},{128,64},{192,224},{224,192},{160,96},{96,160},{32,1},{1,... | collective-permute-start | bytes 196616 | tf_op jit(solution)/shard_map/halo_cols/ppermute | solution.py:329
  31.0 3.6 %collective-permute-start.3 = (bf16[6,32,256]{2,1,0:T(8,128)(2,1)S(1)}, bf16[6,32,256]{2,1,0:T(8,128)(2,1)S(1)}, u32[]{:S(2)}, u32[]{:S(2)}) collective-permute-start(bf16[6,32,256]{2,1,0:T(8,128)(2,1)S(1)} %get-tuple-element.71), channel_id=1, source_target_pairs={{0,8},{8,0},{16,24},{24,16},{1,9},{9,1},{17,25},{25,17},{2,10},{10... | collective-permute-start | bytes 294920 | tf_op jit(solution)/shard_map/halo_rows/ppermute | solution.py:329
  31.8 2.7 %collective-permute-start.2 = (bf16[6,32,256]{2,1,0:T(8,128)(2,1)S(1)}, bf16[6,32,256]{2,1,0:T(8,128)(2,1)S(1)}, u32[]{:S(2)}, u32[]{:S(2)}) collective-permute-start(bf16[6,32,256]{2,1,0:T(8,128)(2,1)S(1)} %get-tuple-element.72), channel_id=1, source_target_pairs={{8,16},{16,8},{9,17},{17,9},{10,18},{18,10},{11,19},{19,11},{12,20... | collective-permute-start | bytes 294920 | tf_op jit(solution)/shard_map/halo_rows/ppermute | solution.py:329
  57.7 5.8 %collective-permute-start.6 = (bf16[144,256]{1,0:T(8,128)(2,1)S(1)}, bf16[144,256]{1,0:T(8,128)(2,1)S(1)}, u32[]{:S(2)}, u32[]{:S(2)}) collective-permute-start(bf16[144,256]{1,0:T(8,128)(2,1)S(1)} %slice_reduce_fusion), channel_id=1, source_target_pairs={{0,24},{8,16},{16,8},{24,0},{1,25},{9,17},{17,9},{25,1},{2,26},{10... | collective-permute-start | bytes 221192 | tf_op jit(solution)/shard_map/reduce/ppermute | solution.py:310
  60.8 5.6 %collective-permute-start.5 = (bf16[144,256]{1,0:T(8,128)(2,1)S(1)}, bf16[144,256]{1,0:T(8,128)(2,1)S(1)}, u32[]{:S(2)}, u32[]{:S(2)}) collective-permute-start(bf16[144,256]{1,0:T(8,128)(2,1)S(1)} %slice_reduce_fusion), channel_id=1, source_target_pairs={{0,16},{8,24},{16,0},{24,8},{1,17},{9,25},{17,1},{25,9},{2,18},{10... | collective-permute-start | bytes 221192 | tf_op jit(solution)/shard_map/reduce/ppermute | solution.py:310
  63.3 3.9 %collective-permute-start.4 = (bf16[144,256]{1,0:T(8,128)(2,1)S(1)}, bf16[144,256]{1,0:T(8,128)(2,1)S(1)}, u32[]{:S(2)}, u32[]{:S(2)}) collective-permute-start(bf16[144,256]{1,0:T(8,128)(2,1)S(1)} %slice_reduce_fusion), channel_id=1, source_target_pairs={{0,8},{8,0},{16,24},{24,16},{1,9},{9,1},{17,25},{25,17},{2,10},{10... | collective-permute-start | bytes 221192 | tf_op jit(solution)/shard_map/reduce/ppermute | solution.py:310
  67.3 4.8 %collective-permute-start.9 = (bf16[144,256]{1,0:T(8,128)(2,1)S(1)}, bf16[144,256]{1,0:T(8,128)(2,1)S(1)}, u32[]{:S(2)}, u32[]{:S(2)}) collective-permute-start(bf16[144,256]{1,0:T(8,128)(2,1)S(1)} %add_convert_fusion.2), channel_id=1, source_target_pairs={{0,4},{1,5},{2,6},{3,7},{4,0},{5,1},{6,2},{7,3},{8,12},{9,13},{10,... | collective-permute-start | bytes 221192 | tf_op jit(solution)/shard_map/reduce/ppermute | solution.py:310
  68.5 4.4 %collective-permute-start.8 = (bf16[144,256]{1,0:T(8,128)(2,1)S(1)}, bf16[144,256]{1,0:T(8,128)(2,1)S(1)}, u32[]{:S(2)}, u32[]{:S(2)}) collective-permute-start(bf16[144,256]{1,0:T(8,128)(2,1)S(1)} %add_convert_fusion.2), channel_id=1, source_target_pairs={{0,6},{1,7},{2,4},{3,5},{4,2},{5,3},{6,0},{7,1},{8,14},{9,15},{10,... | collective-permute-start | bytes 221192 | tf_op jit(solution)/shard_map/reduce/ppermute | solution.py:310
  69.5 3.4 %collective-permute-start.7 = (bf16[144,256]{1,0:T(8,128)(2,1)S(1)}, bf16[144,256]{1,0:T(8,128)(2,1)S(1)}, u32[]{:S(2)}, u32[]{:S(2)}) collective-permute-start(bf16[144,256]{1,0:T(8,128)(2,1)S(1)} %add_convert_fusion.2), channel_id=1, source_target_pairs={{0,2},{1,3},{2,0},{3,1},{4,6},{5,7},{6,4},{7,5},{8,10},{9,11},{10,... | collective-permute-start | bytes 221192 | tf_op jit(solution)/shard_map/reduce/ppermute | solution.py:310
  73.0 10.2 %collective-permute-start.10 = (bf16[144,256]{1,0:T(8,128)(2,1)S(1)}, bf16[144,256]{1,0:T(8,128)(2,1)S(1)}, u32[]{:S(2)}, u32[]{:S(2)}) collective-permute-start(bf16[144,256]{1,0:T(8,128)(2,1)S(1)} %add_convert_fusion.1), channel_id=1, source_target_pairs={{0,1},{1,0},{2,3},{3,2},{4,5},{5,4},{6,7},{7,6},{8,9},{9,8},{10,11... | collective-permute-start | bytes 221192 | tf_op jit(solution)/shard_map/reduce/ppermute | solution.py:310
  83.2 4.7 %collective-permute-start.12 = (bf16[128,256]{1,0:T(8,128)(2,1)S(1)}, bf16[128,256]{1,0:T(8,128)(2,1)S(1)}, u32[]{:S(2)}, u32[]{:S(2)}) collective-permute-start(bf16[128,256]{1,0:T(8,128)(2,1)S(1)} %get-tuple-element.76), channel_id=1, source_target_pairs={{0,128},{32,160},{64,192},{96,224},{128,0},{160,32},{192,64},{224,... | collective-permute-start | bytes 196616 | tf_op jit(solution)/shard_map/reduce/ppermute | solution.py:429
  84.0 3.9 %collective-permute-start.11 = (bf16[128,256]{1,0:T(8,128)(2,1)S(1)}, bf16[128,256]{1,0:T(8,128)(2,1)S(1)}, u32[]{:S(2)}, u32[]{:S(2)}) collective-permute-start(bf16[128,256]{1,0:T(8,128)(2,1)S(1)} %get-tuple-element.76), channel_id=1, source_target_pairs={{0,64},{32,96},{64,0},{96,32},{128,192},{160,224},{192,128},{224,1... | collective-permute-start | bytes 196616 | tf_op jit(solution)/shard_map/reduce/ppermute | solution.py:429
  84.7 4.3 %collective-permute-start.13 = (bf16[128,256]{1,0:T(8,128)(2,1)S(1)}, bf16[128,256]{1,0:T(8,128)(2,1)S(1)}, u32[]{:S(2)}, u32[]{:S(2)}) collective-permute-start(bf16[128,256]{1,0:T(8,128)(2,1)S(1)} %get-tuple-element.76), channel_id=1, source_target_pairs={{0,192},{32,224},{64,128},{96,160},{128,64},{160,96},{192,0},{224,... | collective-permute-start | bytes 196616 | tf_op jit(solution)/shard_map/reduce/ppermute | solution.py:429
  89.1 6.6 %collective-permute-start.14 = (bf16[4,128,256]{2,1,0:T(8,128)(2,1)S(1)}, bf16[4,128,256]{2,1,0:T(8,128)(2,1)S(1)}, u32[]{:S(2)}, u32[]{:S(2)}) collective-permute-start(bf16[4,128,256]{2,1,0:T(8,128)(2,1)S(1)} %pad_maximum_fusion.same_core), channel_id=1, source_target_pairs={{0,32},{32,0},{64,96},{96,64},{128,160},{160,128},{192,224},{224,1... | collective-permute-start | bytes 786440 | tf_op jit(solution)/shard_map/reduce/ppermute | solution.py:431
